TPU v7x, 512 devices: a whole 4x8x8 slice. The times are simulated.
512 devices in a mesh: row: 32 (over z, x), rep: 16 (over y, core).
Axes of the slice: x: 4, y: 8, z: 8, core: 2. Of those that a mesh axis runs over, the one named last changes fastest.
Arguments:
- features: bfloat16 [65536, 512], P(('row', 'rep')), may hold values from -24 to 24
- edge_weights: bfloat16 [65536, 16], P(('row', 'rep')), may hold values from 0.25 to 2
- neighbours: int32 [65536, 16], P(('row', 'rep')), may hold values from 0 to 4095, as said below
- send_list: int32 [32, 16, 16, 2], P('row', 'rep'), may hold values from 0 to 31, as said below
- send_count: int32 [32, 16, 16], P('row', 'rep'), may hold values from 0 to 2, as said below
- w_agg: bfloat16 [512, 512], replicated, may hold values from -0.25 to 0.25
- w_self: bfloat16 [512, 512], replicated, may hold values from -0.25 to 0.25
- cotangent: bfloat16 [65536, 512], P(('row', 'rep')), may hold values from -6 to 6
Outputs:
- hidden: bfloat16 [65536, 512], P(('row', 'rep'))
- grad_agg: float32 [512, 512], P('row')
- grad_self: float32 [512, 512], P('row')
Inputs may be any that keep to these rules, and one draw needn't show every extreme that they name: The 16 codes of a node name 16 distinct neighbours, none the node itself. Codes of slots below 12 are below 4096; a code c of a later slot has c // 128 below the sum of send_count[o, s, g] over s for the node's owner index o and group g. `send_list`: entries of one (o, s, g) below its count are distinct positions of blocks in group s; entries at or past the count are unused. send_count[o, g, g] is 0. In every draw some device receives 2 blocks from every other group, and every device receives 2 from some group.
All inputs are finite; a program needn't handle non-finite values.
Results may differ from a plain program's by a relative error of at most 0.0051.
Values may be sent and summed in bfloat16 or wider, within the bound.
No kernel may reach another device: no remote copies, remote signals or barrier semaphores. Data moves between devices by JAX's collectives and lax.ppermute only.
A program may use at most 64 MiB of HBM per device.

v0:
```python
import jax
import jax.numpy as jnp
from jax import lax
from jax.sharding import PartitionSpec as P

TILE = 128
K_LOC = 12


def body(features, edge_weights, neighbours, send_list, send_count, w_agg, w_self, cotangent):
    owners = lax.axis_size("row")
    feature_width = features.shape[1]
    slot_count = send_list.shape[3]
    gathered = lax.all_gather(features, "row", axis=0, tiled=True)
    blocks = gathered.reshape(-1, TILE, feature_width)
    wanted = send_list[0, 0]
    counted = send_count[0, 0]
    positions = jnp.arange(slot_count, dtype=jnp.int32)[None, :]
    labels = jnp.where(positions < counted[:, None], wanted, -1)
    outgoing = jnp.take(blocks, wanted, axis=0)
    arrived, arrived_ids = (
        lax.all_to_all(outgoing, "rep", split_axis=0, concat_axis=0, tiled=True),
        lax.all_to_all(labels, "rep", split_axis=0, concat_axis=0, tiled=True),
    )
    filled = arrived_ids >= 0
    per_source = jnp.sum(filled.astype(jnp.int32), axis=1)
    inclusive = jnp.cumsum(per_source)
    before = inclusive - per_source
    arrived_rows = arrived.reshape(-1, feature_width)
    weights = edge_weights.astype(jnp.float32)
    summed = features.astype(jnp.float32)
    for slot_index in range(K_LOC):
        picked = jnp.take(gathered, neighbours[:, slot_index], axis=0)
        summed = summed + weights[:, slot_index : slot_index + 1] * picked.astype(jnp.float32)
    for slot_index in range(K_LOC, neighbours.shape[1]):
        codes_now = neighbours[:, slot_index]
        listed = codes_now // TILE
        source = jnp.sum((inclusive[None, :] <= listed[:, None]).astype(jnp.int32), axis=1)
        source_hot = (
            source[:, None] == jnp.arange(per_source.shape[0], dtype=jnp.int32)[None, :]
        ).astype(jnp.int32)
        start_of = jnp.sum(source_hot * before[None, :], axis=1)
        row_index = (source * slot_count + listed - start_of) * TILE + codes_now % TILE
        picked = jnp.take(arrived_rows, row_index, axis=0)
        summed = summed + weights[:, slot_index : slot_index + 1] * picked.astype(jnp.float32)
    degree = 1.0 + jnp.sum(weights, axis=1)
    aggregate = (summed / degree[:, None]).astype(jnp.bfloat16)
    preact = jnp.dot(aggregate, w_agg, preferred_element_type=jnp.float32) + jnp.dot(
        features, w_self, preferred_element_type=jnp.float32
    )
    hidden = jax.nn.silu(preact).astype(jnp.bfloat16)
    sigma = jax.nn.sigmoid(preact)
    grad_pre = (cotangent.astype(jnp.float32) * sigma * (1.0 + preact * (1.0 - sigma))).astype(
        jnp.bfloat16
    )
    contract = (((0,), (0,)), ((), ()))
    part_agg = lax.dot_general(aggregate, grad_pre, contract, preferred_element_type=jnp.float32)
    part_self = lax.dot_general(features, grad_pre, contract, preferred_element_type=jnp.float32)
    share_rows = feature_width // owners
    own_row = lax.axis_index("row")
    summed_agg, summed_self = lax.psum((part_agg, part_self), ("row", "rep"))
    grad_agg = lax.dynamic_slice_in_dim(summed_agg, own_row * share_rows, share_rows, 0)
    grad_self = lax.dynamic_slice_in_dim(summed_self, own_row * share_rows, share_rows, 0)
    return (hidden, grad_agg, grad_self)


def solution(mesh):
    in_specs = (
        P(("row", "rep"), None),
        P(("row", "rep"), None),
        P(("row", "rep"), None),
        P("row", "rep", None, None),
        P("row", "rep", None),
        P(),
        P(),
        P(("row", "rep"), None),
    )
    out_specs = (P(("row", "rep"), None), P("row", None), P("row", None))
    return jax.shard_map(body, mesh=mesh, in_specs=in_specs, out_specs=out_specs, check_vma=False)
```

profile of v0, /device:TPU:1, one launch (start us, length us, event | category | flops | bytes accessed | tf_op | source)
XLA Modules:
  0.0 519.9 jit_solution(7670536299032910332)
XLA Ops:
  7.2 0.0 all-gather.2.cloned.1.call-start
  7.2 0.7 all-gather.2.cloned.1.call-update
  7.9 0.7 compare_select_fusion.18
  8.6 0.7 copy.24
  9.3 10.1 %all-to-all-start.1 = ((s32[16,1,2]{2,1,0:T(1,128)}), s32[16,1,2]{2,1,0:T(1,128)S(1)}, u32[]{:S(2)}, u32[]{:S(2)}) async-start(s32[16,1,2]{2,1,0:T(1,128)} %copy.24), calls=%async_computation.1 | async-start | bytes 16384 | tf_op jit(solution)/shard_map/all_to_all | solution.py:23
  19.4 0.7 compare_and_fusion.16
  20.1 0.1 copy.26
  20.2 0.7 compare_select_fusion
  20.9 0.1 copy.27
  21.0 0.1 reshape.270
  21.1 80.7 %all-gather.2.cloned.1.call-done = bf16[4096,512]{1,0:T(8,128)(2,1)} async-done(((bf16[128,512]{1,0:T(8,128)(2,1)}), bf16[4096,512]{1,0:T(8,128)(2,1)}) %all-gather.2.cloned.1.call-update) | async-done | bytes 4194320 | tf_op jit(solution)/shard_map/all_gather | solution.py:14
  101.8 5.0 gather_fusion
  106.8 4.6 broadcast_select_fusion
  111.4 11.0 %all-to-all-start = ((bf16[16,2,128,512]{3,2,1,0:T(8,128)(2,1)}), bf16[16,2,128,512]{3,2,1,0:T(8,128)(2,1)}, u32[]{:S(2)}, u32[]{:S(2)}) async-start(bf16[16,2,128,512]{3,2,1,0:T(8,128)(2,1)} %broadcast_select_fusion), calls=%async_computation | async-start | bytes 8388608 | tf_op jit(solution)/shard_map/all_to_all | solution.py:22
  122.4 0.0 all-reduce.3.cloned.1.call-start
  122.5 0.4 fusion
  122.9 0.1 copy.25
  123.0 0.1 reduce.1
  123.1 0.1 convert_reduce_fusion.3
  123.2 0.1 select_reduce_fusion.3
  123.4 0.1 compare_and_fusion.15
  123.5 3.6 gather_fusion.4
  127.1 3.6 gather_fusion.6
  130.7 3.6 gather_fusion.8
  134.3 3.6 gather_fusion.10
  138.0 3.6 gather_fusion.12
  141.6 3.6 gather_fusion.2
  145.2 3.6 gather_fusion.3
  148.8 3.6 gather_fusion.5
  152.4 3.6 gather_fusion.7
  156.0 3.6 gather_fusion.9
  159.6 3.6 gather_fusion.11
  163.3 3.7 gather_fusion.1
  166.9 49.0 %all-to-all-done = bf16[16,2,128,512]{3,2,1,0:T(8,128)(2,1)} async-done(((bf16[16,2,128,512]{3,2,1,0:T(8,128)(2,1)}), bf16[16,2,128,512]{3,2,1,0:T(8,128)(2,1)}, u32[]{:S(2)}, u32[]{:S(2)}) %all-to-all-start) | async-done | bytes 4194336 | tf_op jit(solution)/shard_map/all_to_all | solution.py:22
  216.0 3.8 gather_fusion.16
  219.8 3.6 gather_fusion.15
  223.4 3.6 gather_fusion.14
  227.0 3.6 gather_fusion.13
  230.6 1.0 divide_convert_fusion
  231.6 0.2 fusion.10
  231.9 0.9 multiply_convert_fusion.1
  232.8 1.4 fusion.9
  234.2 1.3 convolution_bitcast_fusion
  235.5 0.0 all-reduce.3.cloned.1.call-update
  235.5 274.3 %all-reduce.3.cloned.1.call-done = (f32[512,512]{1,0:T(8,128)}, f32[512,512]{0,1:T(8,128)}) async-done(((f32[512,512]{1,0:T(8,128)}, f32[512,512]{0,1:T(8,128)}), (f32[512,512]{1,0:T(8,128)}, f32[512,512]{0,1:T(8,128)})) %all-reduce.3.cloned.1.call-update) | async-done | bytes 2097168 | tf_op jit(solution)/shard_map/psum | solution.py:61
  509.9 1.4 constant_dynamic-slice_fusion
  511.2 1.1 constant_dynamic-slice_fusion.1
  512.3 0.7 copy.28
  (30 shorter events, 0.2 us)
Async XLA Ops:
  7.2 224.7 %copy-start = (bf16[512,512]{1,0:T(8,128)(2,1)S(1)}, bf16[512,512]{1,0:T(8,128)(2,1)}, u32[]{:S(2)}) copy-start(bf16[512,512]{1,0:T(8,128)(2,1)} %param.16) | copy-start | bytes 1572868
  7.2 94.6 %all-gather.2.cloned.1.call-start = ((), (), s32[]{:S(2)}) async-start(), calls=%async_computation.2 | async-start | bytes 4325376 | tf_op jit(solution)/shard_map/all_gather | solution.py:14
  9.3 102.1 %all-to-all-start.1 = ((s32[16,1,2]{2,1,0:T(1,128)}), s32[16,1,2]{2,1,0:T(1,128)S(1)}, u32[]{:S(2)}, u32[]{:S(2)}) async-start(s32[16,1,2]{2,1,0:T(1,128)} %copy.24), calls=%async_computation.1 | async-start | bytes 16384 | tf_op jit(solution)/shard_map/all_to_all | solution.py:23
  111.4 11.0 %copy-start.3 = (bf16[128,16]{0,1:T(8,128)(2,1)S(1)}, bf16[128,16]{0,1:T(8,128)(2,1)}, u32[]{:S(2)}) copy-start(bf16[128,16]{0,1:T(8,128)(2,1)} %param.11) | copy-start | bytes 12292
  111.4 11.1 %copy-start.4 = (s32[128,16]{0,1:T(8,128)S(1)}, s32[128,16]{0,1:T(8,128)}, u32[]{:S(2)}) copy-start(s32[128,16]{0,1:T(8,128)} %param.12) | copy-start | bytes 24580
  111.4 104.6 %all-to-all-start = ((bf16[16,2,128,512]{3,2,1,0:T(8,128)(2,1)}), bf16[16,2,128,512]{3,2,1,0:T(8,128)(2,1)}, u32[]{:S(2)}, u32[]{:S(2)}) async-start(bf16[16,2,128,512]{3,2,1,0:T(8,128)(2,1)} %broadcast_select_fusion), calls=%async_computation | async-start | bytes 8388608 | tf_op jit(solution)/shard_map/all_to_all | solution.py:22
  122.4 387.5 %all-reduce.3.cloned.1.call-start = ((), (), s32[]{:S(2)}) async-start(), calls=%async_computation.3 | async-start | bytes 4194304 | tf_op jit(solution)/shard_map/psum | solution.py:61
  156.0 74.6 %copy-start.2 = (bf16[128,512]{1,0:T(8,128)(2,1)S(1)}, bf16[128,512]{1,0:T(8,128)(2,1)}, u32[]{:S(2)}) copy-start(bf16[128,512]{1,0:T(8,128)(2,1)} %param.10) | copy-start | bytes 393220
  163.2 68.4 %copy-start.1 = (bf16[512,512]{1,0:T(8,128)(2,1)S(1)}, bf16[512,512]{1,0:T(8,128)(2,1)}, u32[]{:S(2)}) copy-start(bf16[512,512]{1,0:T(8,128)(2,1)} %param.15) | copy-start | bytes 1572868
  219.7 13.1 %copy-start.5 = (bf16[128,512]{1,0:T(8,128)(2,1)S(1)}, bf16[128,512]{1,0:T(8,128)(2,1)}, u32[]{:S(2)}) copy-start(bf16[128,512]{1,0:T(8,128)(2,1)} %param.17) | copy-start | bytes 393220
Sparse Core Ops, SparseCore 0:
  11.2 90.5 all-gather.1
  235.7 274.1 all-reduce.2
where the time goes:
time: 521 us; the launch traced here: 520 us
  waiting for transfers between devices  405 us (78%)
  local copies, waits for them, and re-layouts  67.2 us (13%)
  starting transfers between devices  21.2 us (4%)
  between operations  14.3 us (3%)
  other arithmetic  8.57 us (2%)
    psum x1, waiting for transfers between devices, body(): summed_agg, summed_self = lax.psum((part_agg, part_self), ('row', 'rep'))  274 us
    all_gather x1, waiting for transfers between devices, body(): gathered = lax.all_gather(features, 'row', axis=0, tiled=True)  80.7 us
    all_to_all x1, waiting for transfers between devices, body(): lax.all_to_all(outgoing, 'rep', split_axis=0, concat_axis=0, tiled=True)  49 us
    gather x12, local copies, waits for them, and re-layouts, body(): picked = jnp.take(gathered, neighbours[:, slot_index], axis=0)  43.3 us
    gather x4, local copies, waits for them, and re-layouts, body(): picked = jnp.take(arrived_rows, row_index, axis=0)  14.6 us
    all_to_all x1, starting transfers between devices, body(): lax.all_to_all(outgoing, 'rep', split_axis=0, concat_axis=0, tiled=True)  11 us
  transfers between devices with their start and end apart: 4, of which 3 were waited for; matrix products, arithmetic and copies ran while one was open for 11% of the time, Pallas kernels for 0%

commit v1 on v0

v1 whole, which is shorter than its diff:
```python
import jax
import jax.numpy as jnp
from jax import lax
from jax.experimental import pallas as pl
from jax.experimental.pallas import tpu as pltpu
from jax.sharding import Mesh, PartitionSpec as P

NZ, NX, NY, NC = 8, 4, 8, 2
OWNERS = NZ * NX
GROUPS = NY * NC
T = 128
K_LOC = 12
K_REM = 4
CAP = 2
F32 = jnp.float32
BF16 = jnp.bfloat16
VMEM_LIMIT = 48 * 1024 * 1024


def build_kernel(scalars, local_ref, remote_ref, remote_hot, local_hot):
    g = pl.program_id(0)
    own_z = scalars[2 * NX * GROUPS]
    rows = lax.broadcasted_iota(jnp.int32, (T, T), 0).astype(F32)
    lanes = lax.broadcasted_iota(jnp.int32, (1, T), 1).astype(F32)
    for x in range(NX):
        start = scalars[x * GROUPS + g]
        count = scalars[NX * GROUPS + x * GROUPS + g]
        relative = remote_ref[0, x, 0:K_REM, :] - (start * T).astype(F32)
        relative = jnp.where(relative < (count * T).astype(F32), relative, -1.0)
        weight = remote_ref[0, x, K_REM : 2 * K_REM, :]
        for m in range(CAP):
            hot = jnp.zeros((T, T), F32)
            for k in range(K_REM):
                hot = jnp.where(rows == relative[k : k + 1] - float(m * T), weight[k : k + 1], hot)
            remote_hot[0, x, m * T : (m + 1) * T, :] = hot.astype(BF16)
    for q in range(2):
        p = 2 * g + q
        for x in range(NX):
            code = local_ref[x, 0:K_LOC, :] - (p * T).astype(F32)
            weight = local_ref[x, K_LOC : 2 * K_LOC, :]
            own = lanes - jnp.where(p == own_z * NX + x, 0.0, 1024.0)
            hot = jnp.where(rows == own, 1.0, 0.0)
            for k in range(K_LOC):
                hot = jnp.where(rows == code[k : k + 1], weight[k : k + 1], hot)
            local_hot[q * T : (q + 1) * T, x * T : (x + 1) * T] = hot.astype(BF16)


def build(scalars, local_data, remote_data):
    return pl.pallas_call(
        build_kernel,
        grid_spec=pltpu.PrefetchScalarGridSpec(
            num_scalar_prefetch=1,
            grid=(GROUPS,),
            in_specs=[
                pl.BlockSpec((NX, 40, T), lambda g, s: (0, 0, 0)),
                pl.BlockSpec((1, NX, 16, T), lambda g, s: (g, 0, 0, 0)),
            ],
            out_specs=[
                pl.BlockSpec((1, NX, CAP * T, T), lambda g, s: (g, 0, 0, 0)),
                pl.BlockSpec((2 * T, NX * T), lambda g, s: (g, 0)),
            ],
        ),
        out_shape=[
            jax.ShapeDtypeStruct((GROUPS, NX, CAP * T, T), BF16),
            jax.ShapeDtypeStruct((OWNERS * T, NX * T), BF16),
        ],
        compiler_params=pltpu.CompilerParams(vmem_limit_bytes=VMEM_LIMIT),
        cost_estimate=pl.CostEstimate(flops=200_000_000, bytes_accessed=10_000_000, transcendentals=0),
        name="build_hot",
    )(scalars, local_data, remote_data)


def partial_kernel(scalars, blocks_ref, remote_hot, local_hot, send_ref, keep_ref, total):
    i = pl.program_id(0)
    own_y = scalars[0]
    own_c = scalars[1]
    y = lax.rem(own_y + 1 + i, NY)

    @pl.when(i == 0)
    def _():
        total[...] = jnp.zeros_like(total)

    part = total[...]
    for j in range(2):
        pair = jnp.concatenate([blocks_ref[4 * i + 2 * j], blocks_ref[4 * i + 2 * j + 1]], axis=1)
        part = part + jnp.dot(pair, local_hot[2 * T * j : 2 * T * (j + 1), :], preferred_element_type=F32)
    total[...] = part

    def product(core, x):
        at = 2 + ((x * NY + y) * NC + core) * CAP
        first = jnp.clip(scalars[at], 0, OWNERS - 1)
        second = jnp.clip(scalars[at + 1], 0, OWNERS - 1)
        pair = jnp.concatenate([blocks_ref[first], blocks_ref[second]], axis=1)
        return jnp.dot(pair, remote_hot[0, core, x], preferred_element_type=F32)

    for x in range(NX):
        send_ref[x, 0] = product(1 - own_c, x).astype(BF16)
    last = jnp.where(i == NY - 1, 1.0, 0.0)
    for x in range(NX):
        keep_ref[x, 0] = (product(own_c, x) + last * total[:, x * T : (x + 1) * T]).astype(BF16)


def partials(scalars, blocks, remote_hot, local_hot):
    def turn(i, s):
        return lax.rem(s[0] + 1 + i, NY)

    shape = jax.ShapeDtypeStruct((NX, NY, T, T), BF16)
    return pl.pallas_call(
        partial_kernel,
        grid_spec=pltpu.PrefetchScalarGridSpec(
            num_scalar_prefetch=1,
            grid=(NY,),
            in_specs=[
                pl.BlockSpec((OWNERS, T, T), lambda i, s: (0, 0, 0)),
                pl.BlockSpec((1, NC, NX, CAP * T, T), lambda i, s: (turn(i, s), 0, 0, 0, 0)),
                pl.BlockSpec((4 * T, NX * T), lambda i, s: (i, 0)),
            ],
            out_specs=[
                pl.BlockSpec((NX, 1, T, T), lambda i, s: (0, turn(i, s), 0, 0)),
                pl.BlockSpec((NX, 1, T, T), lambda i, s: (0, turn(i, s), 0, 0)),
            ],
            scratch_shapes=[pltpu.VMEM((T, NX * T), F32)],
        ),
        out_shape=[shape, shape],
        compiler_params=pltpu.CompilerParams(vmem_limit_bytes=VMEM_LIMIT),
        cost_estimate=pl.CostEstimate(flops=1_000_000_000, bytes_accessed=11_000_000, transcendentals=0),
        name="partial_sums",
    )(scalars, blocks, remote_hot, local_hot)


def dense_kernel(scalars, arrived, weights_t, features, features_t, w_agg, w_self, cotangent, hidden_ref, send_ref, keep_ref, agg_t):
    own_c = scalars[0]
    degree = 1.0 + jnp.sum(weights_t[...], axis=0, keepdims=True)
    for x in range(NX):
        summed = arrived[x, 0].astype(F32)
        for y in range(1, NY):
            summed = summed + arrived[x, y].astype(F32)
        agg_t[x * T : (x + 1) * T, :] = (summed / degree).astype(BF16)
    contract = (((0,), (0,)), ((), ()))
    preact = lax.dot_general(agg_t[...], w_agg[...], contract, preferred_element_type=F32) + jnp.dot(
        features[...], w_self[...], preferred_element_type=F32
    )
    sigma = jax.nn.sigmoid(preact)
    hidden_ref[...] = (preact * sigma).astype(BF16)
    grad_pre = (cotangent[...].astype(F32) * sigma * (1.0 + preact * (1.0 - sigma))).astype(BF16)
    of_agg = jnp.dot(agg_t[...], grad_pre, preferred_element_type=F32)
    of_self = jnp.dot(features_t[...], grad_pre, preferred_element_type=F32)

    @pl.when(own_c == 0)
    def _():
        keep_ref[...] = of_agg
        send_ref[...] = of_self

    @pl.when(own_c != 0)
    def _():
        keep_ref[...] = of_self
        send_ref[...] = of_agg


def dense(scalars, *operands):
    width = NX * T
    vmem = pl.BlockSpec(memory_space=pltpu.VMEM)
    return pl.pallas_call(
        dense_kernel,
        in_specs=[pl.BlockSpec(memory_space=pltpu.SMEM)] + [vmem] * 7,
        out_specs=[vmem] * 3,
        out_shape=[
            jax.ShapeDtypeStruct((T, width), BF16),
            jax.ShapeDtypeStruct((width, width), F32),
            jax.ShapeDtypeStruct((width, width), F32),
        ],
        scratch_shapes=[pltpu.VMEM((width, T), BF16)],
        compiler_params=pltpu.CompilerParams(vmem_limit_bytes=VMEM_LIMIT),
        cost_estimate=pl.CostEstimate(flops=300_000_000, bytes_accessed=5_000_000, transcendentals=65536),
        name="dense",
    )(scalars, *operands)


def body(features, edge_weights, neighbours, send_list, send_count, w_agg, w_self, cotangent):
    width = features.shape[1]
    z, x, y, c = (lax.axis_index(a).astype(jnp.int32) for a in ("z", "x", "y", "c"))
    swap = [(0, 1), (1, 0)]

    features_t = features.T
    quarters = jnp.broadcast_to(features_t.reshape(1, NX, T, T), (NZ, NX, T, T)).reshape(OWNERS, T, T)
    blocks = lax.all_to_all(quarters, ("z", "x"), 0, 0, tiled=True)

    codes_t = neighbours.T.astype(F32)
    weights_t = edge_weights.T.astype(F32)
    counted = jnp.pad(send_count[0].astype(F32), ((0, 0), (0, T - GROUPS)))
    listed = jnp.pad(send_list[0].reshape(1, GROUPS * CAP).astype(F32), ((0, 0), (0, T - GROUPS * CAP)))
    small = jnp.concatenate(
        [codes_t[:K_LOC], weights_t[:K_LOC], codes_t[K_LOC:], weights_t[K_LOC:], counted, listed, jnp.zeros((6, T), F32)], axis=0
    )
    along_x = lax.all_gather(small, "x", axis=0)
    everyone = lax.all_gather(along_x[:, 24:40], ("y", "c"), axis=0)

    group = y * NC + c
    counts = everyone[:, :, 8, :GROUPS].astype(jnp.int32)
    sources = jnp.arange(GROUPS, dtype=jnp.int32)[:, None, None]
    start = jnp.sum(jnp.where(sources < group, counts, 0), axis=0)
    here = jnp.sum(jnp.where(sources == group, counts, 0), axis=0)
    build_scalars = jnp.concatenate([start.reshape(-1), here.reshape(-1), z[None]])
    remote_hot, local_hot = build(build_scalars, along_x, everyone)
    lists = along_x[:, 33, : GROUPS * CAP].astype(jnp.int32)
    partial_scalars = jnp.concatenate([y[None], c[None], lists.reshape(-1)])

    send, keep = partials(partial_scalars, blocks, remote_hot.reshape(NY, NC, NX, CAP * T, T), local_hot)
    received = lax.ppermute(send, "c", swap)
    chip_sum = (keep.astype(F32) + received.astype(F32)).astype(BF16)
    arrived = lax.all_to_all(chip_sum.reshape(NX * NY, T, T), ("x", "y"), 0, 0, tiled=True)

    hidden, send, keep = dense(
        c[None], arrived.reshape(NX, NY, T, T), weights_t, features, features_t, w_agg, w_self, cotangent
    )
    received = lax.ppermute(send, "c", swap)
    share = width // OWNERS
    chip_grad = (keep + received).astype(BF16).reshape(OWNERS, share, width)
    rows = lax.all_to_all(chip_grad, ("z", "x"), 0, 0, tiled=True)
    plane = jnp.sum(rows.astype(F32), axis=0)
    both = lax.all_gather(plane, ("y", "c"), axis=0).reshape(NY, NC, share, width)
    grads = jnp.sum(both, axis=0)
    return hidden, grads[0], grads[1]


def solution(mesh):
    fine = Mesh(mesh.devices.reshape(NZ, NX, NY, NC), ("z", "x", "y", "c"))
    row, rep = ("z", "x"), ("y", "c")
    nodes = P(row + rep, None)
    in_specs = (nodes, nodes, nodes, P(row, rep, None, None), P(row, rep, None), P(), P(), nodes)
    out_specs = (nodes, P(row, None), P(row, None))
    return jax.shard_map(body, mesh=fine, in_specs=in_specs, out_specs=out_specs, check_vma=False)
```

time: 521 us -> 163 us (0.31)
  waiting for transfers between devices: 405 us -> 4.74 us
  blocking collectives: 0 us -> 108 us
  local copies, waits for them, and re-layouts: 67.2 us -> 5.56 us
  Pallas kernels: 0 us -> 20.9 us
  between operations: 14.3 us -> 0.86 us
  other arithmetic: 8.57 us -> 1.07 us
    psum x1 -> x0, waiting for transfers between devices: 274 us -> none  [body(): summed_agg, summed_self = lax.psum((part_agg, part_self), ('row', 'rep'))]
    all_gather x1 -> x0, waiting for transfers between devices: 80.7 us -> none  [body(): gathered = lax.all_gather(features, 'row', axis=0, tiled=True)]
    gather x17 -> x0, local copies, waits for them, and re-layouts: 62.9 us -> none  [the longest x12 43.3 us: body(): picked = jnp.take(gathered, neighbours[:, slot_index], axis=0)]
    all_to_all x0 -> x2, blocking collectives: none -> 54.6 us  [the longest x1 31.1 us: body(): lax.all_to_all(chip_sum.reshape(NX * NY, T, T), ('x', 'y'), 0, 0, tiled=T...]
    all_gather x0 -> x3, blocking collectives: none -> 53.1 us  [the longest x1 21.4 us: body(): everyone = lax.all_gather(along_x[:, 24:40], ('y', 'c'), axis=0)]
    all_to_all x2 -> x1, waiting for transfers between devices: 49 us -> 0.01 us  [body(): blocks = lax.all_to_all(quarters, ('z', 'x'), 0, 0, tiled=True)]
    pallas_call x0 -> x3, Pallas kernels: none -> 20.9 us  [the longest x1 11.4 us: build(): pl.pallas_call(build_kernel, grid_spec=pltpu.PrefetchScalarGridSpec(num_s...]
    ppermute x0 -> x2, starting transfers between devices: none -> 8.2 us  [body(): received = lax.ppermute(send, 'c', swap)]
  transfers between devices with their start and end apart: 4 -> 3, of which waited for: 3 -> 2; matrix products, arithmetic and copies ran while one was open for 11% -> 1% of each run, Pallas kernels for 0% -> 7%
where the time goes in v1:
time: 163 us
  blocking collectives  108 us (66%)
  starting transfers between devices  21.9 us (13%)
  Pallas kernels  20.9 us (13%)
  local copies, waits for them, and re-layouts  5.56 us (3%)
  waiting for transfers between devices  4.74 us (3%)
    all_to_all x1, blocking collectives, body(): lax.all_to_all(chip_sum.reshape(NX * NY, T, T), ('x', 'y'), 0, 0, tiled=T...  31.1 us
    all_to_all x1, blocking collectives, body(): rows = lax.all_to_all(chip_grad, ('z', 'x'), 0, 0, tiled=True)  23.5 us
    all_gather x1, blocking collectives, body(): everyone = lax.all_gather(along_x[:, 24:40], ('y', 'c'), axis=0)  21.4 us
    all_gather x1, blocking collectives, body(): lax.all_gather(plane, ('y', 'c'), axis=0).reshape(NY, NC, share, width)  20.3 us
    all_to_all x1, starting transfers between devices, body(): blocks = lax.all_to_all(quarters, ('z', 'x'), 0, 0, tiled=True)  13.7 us
    all_gather x1, blocking collectives, body(): along_x = lax.all_gather(small, 'x', axis=0)  11.5 us
    pallas_call x1, Pallas kernels, build(): pl.pallas_call(build_kernel, grid_spec=pltpu.PrefetchScalarGridSpec(num_s...  11.4 us
    ppermute x2, starting transfers between devices, body(): received = lax.ppermute(send, 'c', swap)  8.2 us
  transfers between devices with their start and end apart: 3, of which 2 were waited for; matrix products, arithmetic and copies ran while one was open for 1% of the time, Pallas kernels for 7%

profile of v1, /device:TPU:1, one launch (start us, length us, event | category | flops | bytes accessed | tf_op | source)
XLA Modules:
  0.0 162.8 jit_solution(13051756769172483502)
XLA Ops:
  0.6 0.0 copy-start.7
  0.6 0.0 copy-start.8
  0.7 0.0 copy-start.6
  0.7 0.0 copy-start.5
  0.7 1.0 copy.18
  1.7 1.3 broadcast_in_dim.43
  3.0 13.7 %all-to-all-start = ((bf16[32,128,128]{2,1,0:T(8,128)(2,1)}), bf16[32,128,128]{2,1,0:T(8,128)(2,1)S(1)}, u32[]{:S(2)}, u32[]{:S(2)}) async-start(bf16[32,128,128]{2,1,0:T(8,128)(2,1)} %bitcast.8), calls=%async_computation | async-start | bytes 2097152 | tf_op jit(solution)/shard_map/all_to_all | solution.py:186
  16.7 0.0 copy-done.7
  16.8 0.1 copy.17
  16.8 0.1 convert_element_type.78
  16.9 0.0 copy-done.8
  17.0 0.0 copy-done.6
  17.0 0.0 copy-done.5
  17.1 0.2 concatenate.9
  17.2 11.5 %all-gather = f32[160,128]{1,0:T(8,128)S(1)} all-gather(f32[40,128]{1,0:T(8,128)S(1)} %concatenate.9), channel_id=2, replica_groups=mesh['z'=8,'x'=4,'y'=8,'c'=2] {'x'}, dimensions={0}, use_global_device_ids=true | all-gather | bytes 102400 | tf_op jit(solution)/shard_map/all_gather | solution.py:195
  28.7 0.1 convert_element_type.80
  28.8 21.4 %all-gather.1 = f32[64,16,128]{2,1,0:T(8,128)S(1)} all-gather(f32[4,16,128]{2,1,0:T(8,128)S(1)} %slice.41), channel_id=3, replica_groups=mesh['z'=8,'x'=4,'y'=8,'c'=2] {'y','c'}, dimensions={0}, use_global_device_ids=true | all-gather | bytes 557056 | tf_op jit(solution)/shard_map/all_gather | solution.py:196
  50.2 0.1 select_reduce_fusion.1
  50.3 0.1 reshape.73
  50.4 0.1 reshape.74
  50.5 0.1 pad_add_fusion.1.scalars
  50.6 11.4 %build_hot.1 = (bf16[16,4,256,128]{3,2,1,0:T(8,128)(2,1)S(1)}, bf16[4096,512]{1,0:T(8,128)(2,1)}) custom-call(s32[129]{0:T(256)S(1)} %pad_add_fusion.1.scalars, f32[4,40,128]{2,1,0:T(8,128)S(1)} %bitcast.37, f32[16,4,16,128]{3,2,1,0:T(8,128)S(1)} %bitcast.34), custom_call_target="tpu_custom_call" | custom-call | flops 200000000 | bytes 10000000 | tf_op jit(solution)/shard_map/build_hot/pallas_call | solution.py:49
  62.0 0.0 copy-start
  62.0 2.0 %copy-done = bf16[16,4,256,128]{3,2,1,0:T(8,128)(2,1)} copy-done((bf16[16,4,256,128]{3,2,1,0:T(8,128)(2,1)}, bf16[16,4,256,128]{3,2,1,0:T(8,128)(2,1)S(1)}, u32[]{:S(2)}) %copy-start) | copy-done | bytes 4194328
  63.9 0.1 pad_add_fusion.scalars
  64.0 0.0 all-to-all-done.blocks_ref
  64.0 7.7 %partial_sums.1 = (bf16[4,8,128,128]{3,2,1,0:T(8,128)(2,1)S(1)}, bf16[4,8,128,128]{3,2,1,0:T(8,128)(2,1)S(1)}) custom-call(s32[130]{0:T(256)S(1)} %pad_add_fusion.scalars, bf16[32,128,128]{2,1,0:T(8,128)(2,1)S(1)} %all-to-all-done.blocks_ref, bf16[8,2,4,256,128]{4,3,2,1,0:T(8,128)(2,1)} %bitcast.29, bf16[4096,512]{1,0:T(8,128)(2,1)} %get-tuple-element.11.local_hot), custom_call_target="tpu_custom_call" | custom-call | flops 1000000000 | bytes 11000000 | tf_op jit(solution)/shard_map/partial_sums/pallas_call | solution.py:108
  71.8 2.1 %collective-permute-start = (bf16[4,8,128,128]{3,2,1,0:T(8,128)(2,1)S(1)}, bf16[4,8,128,128]{3,2,1,0:T(8,128)(2,1)S(1)}, u32[]{:S(2)}, u32[]{:S(2)}) collective-permute-start(bf16[4,8,128,128]{3,2,1,0:T(8,128)(2,1)S(1)} %get-tuple-element.13), channel_id=1, source_target_pairs={{0,1},{1,0},{2,3},{3,2},{4,5},{5,4},{6,7},{7,6},{8,9},{9,8},{10,11... | collective-permute-start | bytes 3145736 | tf_op jit(solution)/shard_map/ppermute | solution.py:209
  73.8 2.5 %collective-permute-done = bf16[4,8,128,128]{3,2,1,0:T(8,128)(2,1)S(1)} collective-permute-done((bf16[4,8,128,128]{3,2,1,0:T(8,128)(2,1)S(1)}, bf16[4,8,128,128]{3,2,1,0:T(8,128)(2,1)S(1)}, u32[]{:S(2)}, u32[]{:S(2)}) %collective-permute-start) | collective-permute-done | bytes 1048608 | tf_op jit(solution)/shard_map/ppermute | solution.py:209
  76.3 0.0 copy-start.1
  76.3 0.0 copy-start.2
  76.3 0.0 copy-start.3
  76.3 0.0 copy-start.4
  76.3 0.4 add_convert_fusion
  76.7 31.1 %all_to_all.15 = bf16[32,128,128]{2,1,0:T(8,128)(2,1)S(1)} all-to-all(bf16[32,128,128]{2,1,0:T(8,128)(2,1)S(1)} %bitcast.39), channel_id=1, replica_groups=mesh['z'=8,'x'=4,'y'=8,'c'=2] {'x','y'}, dimensions={0} | all-to-all | bytes 2097152 | tf_op jit(solution)/shard_map/all_to_all | solution.py:211
  107.8 0.0 copy-done.1
  107.8 0.0 copy-done.2
  107.8 0.0 copy-done.3
  107.8 0.0 copy-done.4
  107.8 1.7 %dense.1 = (bf16[128,512]{1,0:T(8,128)(2,1)}, f32[512,512]{1,0:T(8,128)S(1)}, f32[512,512]{1,0:T(8,128)S(1)}) custom-call(s32[1]{0:T(128)} %bitcast.scalars, bf16[4,8,128,128]{3,2,1,0:T(8,128)(2,1)S(1)} %bitcast.30, f32[16,128]{1,0:T(8,128)S(1)} %convert_bitcast_fusion.weights_t, bf16[128,512]{1,0:T(8,128)(2,1)S(1)} %copy-done.1, ...), custom_call_target="tpu_custom_call" | custom-call | flops 300000000 | bytes 5000000 | tf_op jit(solution)/shard_map/dense/pallas_call | solution.py:163
  109.6 6.1 %collective-permute-start.1 = (f32[512,512]{1,0:T(8,128)S(1)}, f32[512,512]{1,0:T(8,128)S(1)}, u32[]{:S(2)}, u32[]{:S(2)}) collective-permute-start(f32[512,512]{1,0:T(8,128)S(1)} %get-tuple-element.16), channel_id=1, source_target_pairs={{0,1},{1,0},{2,3},{3,2},{4,5},{5,4},{6,7},{7,6},{8,9},{9,8},{10,11... | collective-permute-start | bytes 3145736 | tf_op jit(solution)/shard_map/ppermute | solution.py:216
  115.7 2.3 %collective-permute-done.1 = f32[512,512]{1,0:T(8,128)S(1)} collective-permute-done((f32[512,512]{1,0:T(8,128)S(1)}, f32[512,512]{1,0:T(8,128)S(1)}, u32[]{:S(2)}, u32[]{:S(2)}) %collective-permute-start.1) | collective-permute-done | bytes 1048608 | tf_op jit(solution)/shard_map/ppermute | solution.py:216
  118.0 0.3 add_convert_fusion.1
  118.2 23.5 %all_to_all.16 = bf16[32,16,512]{2,1,0:T(8,128)(2,1)S(1)} all-to-all(bf16[32,16,512]{2,1,0:T(8,128)(2,1)S(1)} %bitcast.40), channel_id=1, replica_groups=mesh['z'=8,'x'=4,'y'=8,'c'=2] {'z','x'}, dimensions={0} | all-to-all | bytes 1048576 | tf_op jit(solution)/shard_map/all_to_all | solution.py:219
  141.7 0.1 convert_reduce_fusion
  141.8 20.3 %all-gather.2 = f32[256,512]{1,0:T(8,128)S(1)} all-gather(f32[16,512]{1,0:T(8,128)S(1)} %convert_reduce_fusion), channel_id=4, replica_groups=mesh['z'=8,'x'=4,'y'=8,'c'=2] {'y','c'}, dimensions={0}, use_global_device_ids=true | all-gather | bytes 557056 | tf_op jit(solution)/shard_map/all_gather | solution.py:221
  162.1 0.6 slice_bitcast_fusion
  (14 shorter events, 0.1 us)
Async XLA Ops:
  0.6 16.1 %copy-start.7 = (s32[1,1,16,2]{2,3,1,0:T(2,128)S(1)}, s32[1,1,16,2]{2,3,1,0:T(2,128)}, u32[]{:S(2)}) copy-start(s32[1,1,16,2]{2,3,1,0:T(2,128)} %param.11) | copy-start | bytes 388
  0.6 16.3 %copy-start.8 = (s32[1,1,16]{2,1,0:T(1,128)S(1)}, s32[1,1,16]{2,1,0:T(1,128)}, u32[]{:S(2)}) copy-start(s32[1,1,16]{2,1,0:T(1,128)} %param.12) | copy-start | bytes 196
  0.7 16.3 %copy-start.6 = (bf16[128,16]{0,1:T(8,128)(2,1)S(1)}, bf16[128,16]{0,1:T(8,128)(2,1)}, u32[]{:S(2)}) copy-start(bf16[128,16]{0,1:T(8,128)(2,1)} %param.9) | copy-start | bytes 12292
  0.7 16.4 %copy-start.5 = (s32[128,16]{0,1:T(8,128)S(1)}, s32[128,16]{0,1:T(8,128)}, u32[]{:S(2)}) copy-start(s32[128,16]{0,1:T(8,128)} %param.10) | copy-start | bytes 24580
  3.0 61.0 %all-to-all-start = ((bf16[32,128,128]{2,1,0:T(8,128)(2,1)}), bf16[32,128,128]{2,1,0:T(8,128)(2,1)S(1)}, u32[]{:S(2)}, u32[]{:S(2)}) async-start(bf16[32,128,128]{2,1,0:T(8,128)(2,1)} %bitcast.8), calls=%async_computation | async-start | bytes 2097152 | tf_op jit(solution)/shard_map/all_to_all | solution.py:186
  62.0 2.0 %copy-start = (bf16[16,4,256,128]{3,2,1,0:T(8,128)(2,1)}, bf16[16,4,256,128]{3,2,1,0:T(8,128)(2,1)S(1)}, u32[]{:S(2)}) copy-start(bf16[16,4,256,128]{3,2,1,0:T(8,128)(2,1)S(1)} %get-tuple-element.10) | copy-start | bytes 12582916
  71.8 4.6 %collective-permute-start = (bf16[4,8,128,128]{3,2,1,0:T(8,128)(2,1)S(1)}, bf16[4,8,128,128]{3,2,1,0:T(8,128)(2,1)S(1)}, u32[]{:S(2)}, u32[]{:S(2)}) collective-permute-start(bf16[4,8,128,128]{3,2,1,0:T(8,128)(2,1)S(1)} %get-tuple-element.13), channel_id=1, source_target_pairs={{0,1},{1,0},{2,3},{3,2},{4,5},{5,4},{6,7},{7,6},{8,9},{9,8},{10,11... | collective-permute-start | bytes 3145736 | tf_op jit(solution)/shard_map/ppermute | solution.py:209
  76.3 31.5 %copy-start.1 = (bf16[128,512]{1,0:T(8,128)(2,1)S(1)}, bf16[128,512]{1,0:T(8,128)(2,1)}, u32[]{:S(2)}) copy-start(bf16[128,512]{1,0:T(8,128)(2,1)} %features.1) | copy-start | bytes 393220
  76.3 31.5 %copy-start.2 = (bf16[512,512]{1,0:T(8,128)(2,1)S(1)}, bf16[512,512]{1,0:T(8,128)(2,1)}, u32[]{:S(2)}) copy-start(bf16[512,512]{1,0:T(8,128)(2,1)} %w_agg.1) | copy-start | bytes 1572868
  76.3 31.5 %copy-start.3 = (bf16[512,512]{1,0:T(8,128)(2,1)S(1)}, bf16[512,512]{1,0:T(8,128)(2,1)}, u32[]{:S(2)}) copy-start(bf16[512,512]{1,0:T(8,128)(2,1)} %w_self.1) | copy-start | bytes 1572868
  76.3 31.5 %copy-start.4 = (bf16[128,512]{1,0:T(8,128)(2,1)S(1)}, bf16[128,512]{1,0:T(8,128)(2,1)}, u32[]{:S(2)}) copy-start(bf16[128,512]{1,0:T(8,128)(2,1)} %cotangent.1) | copy-start | bytes 393220
  109.6 8.4 %collective-permute-start.1 = (f32[512,512]{1,0:T(8,128)S(1)}, f32[512,512]{1,0:T(8,128)S(1)}, u32[]{:S(2)}, u32[]{:S(2)}) collective-permute-start(f32[512,512]{1,0:T(8,128)S(1)} %get-tuple-element.16), channel_id=1, source_target_pairs={{0,1},{1,0},{2,3},{3,2},{4,5},{5,4},{6,7},{7,6},{8,9},{9,8},{10,11... | collective-permute-start | bytes 3145736 | tf_op jit(solution)/shard_map/ppermute | solution.py:216

commit v2 on v0

v2 whole, which is shorter than its diff:
```python
import jax
import jax.numpy as jnp
from jax import lax
from jax.experimental import pallas as pl
from jax.experimental.pallas import tpu as pltpu
from jax.sharding import Mesh, PartitionSpec as P

NZ, NX, NY, NC = 8, 4, 8, 2
OWNERS = NZ * NX
GROUPS = NY * NC
T = 128
K_LOC = 12
K_REM = 4
CAP = 2
F32 = jnp.float32
BF16 = jnp.bfloat16
VMEM_LIMIT = 16 * 1024 * 1024


def vmem_call(kernel, name, scalar_inputs, array_inputs, outputs, scratch=(), flops=0, bytes_accessed=0, transcendentals=0):
    vmem = pl.BlockSpec(memory_space=pltpu.VMEM)
    return pl.pallas_call(
        kernel,
        in_specs=[pl.BlockSpec(memory_space=pltpu.SMEM)] * len(scalar_inputs) + [vmem] * len(array_inputs),
        out_specs=[vmem] * len(outputs),
        out_shape=[jax.ShapeDtypeStruct(shape, dtype) for shape, dtype in outputs],
        scratch_shapes=list(scratch),
        compiler_params=pltpu.CompilerParams(vmem_limit_bytes=VMEM_LIMIT),
        cost_estimate=pl.CostEstimate(flops=flops, bytes_accessed=bytes_accessed, transcendentals=transcendentals),
        name=name,
    )(*scalar_inputs, *array_inputs)


def remote_kernel(scalars, blocks_ref, remote_ref, sums_ref):
    core = scalars[0]
    rows = lax.broadcasted_iota(jnp.int32, (T, T), 0).astype(F32)

    def product(x, y):
        at = x * GROUPS + y * NC + core
        first = jnp.clip(scalars[1 + at * CAP], 0, OWNERS - 1)
        second = jnp.clip(scalars[2 + at * CAP], 0, OWNERS - 1)
        start = scalars[1 + NX * GROUPS * CAP + at].astype(F32)
        count = scalars[1 + NX * GROUPS * (CAP + 1) + at].astype(F32)
        told = remote_ref[y * NC + core, x].astype(F32)
        entry = told[0:K_REM] - start
        row = jnp.where(entry < count, entry * T + told[K_REM : 2 * K_REM], -1.0)
        weight = told[2 * K_REM : 3 * K_REM]
        halves = []
        for m in range(CAP):
            hot = jnp.zeros((T, T), F32)
            for k in range(K_REM):
                hot = jnp.where(rows == row[k : k + 1] - float(m * T), weight[k : k + 1], hot)
            halves.append(hot.astype(BF16))
        pair = jnp.concatenate([blocks_ref[first], blocks_ref[second]], axis=1)
        return jnp.dot(pair, jnp.concatenate(halves, axis=0), preferred_element_type=F32).astype(BF16)

    def of_y(y, carry):
        for x in range(NX):
            sums_ref[x, y] = product(x, y)
        return carry

    lax.fori_loop(0, NY, of_y, 0)


def local_kernel(scalars, blocks_ref, local_ref, out_0, out_1, out_2, out_3, hot_ref, total):
    own_z, own_x = scalars[0], scalars[1]
    rows = lax.broadcasted_iota(jnp.int32, (T, T), 0).astype(F32)
    lanes = lax.broadcasted_iota(jnp.int32, (1, T), 1).astype(F32)
    total[...] = jnp.zeros_like(total)

    def of_four(i, carry):
        for j in range(4):
            p = 4 * i + j
            for x in range(NX):
                code = local_ref[x, 16 : 16 + K_LOC, :].astype(F32) - p.astype(F32)
                code = code * T + local_ref[x, 32 : 32 + K_LOC, :].astype(F32)
                weight = local_ref[x, 48 : 48 + K_LOC, :].astype(F32)
                own = lanes - jnp.where(p == own_z * NX + x, 0.0, 1024.0)
                hot = jnp.where(rows == own, 1.0, 0.0)
                for k in range(K_LOC):
                    hot = jnp.where(rows == code[k : k + 1], weight[k : k + 1], hot)
                hot_ref[x, j * T : (j + 1) * T, :] = hot.astype(BF16)
        four = jnp.concatenate([blocks_ref[4 * i + j] for j in range(4)], axis=1)
        for x in range(NX):
            total[x] += jnp.dot(four, hot_ref[x], preferred_element_type=F32)
        return carry

    lax.fori_loop(0, OWNERS // 4, of_four, 0)
    for k, out in enumerate((out_0, out_1, out_2, out_3)):
        out[...] = total[lax.rem(own_x + k, NX)]


def dense_kernel(scalars, arrived, near_0, near_1, near_2, near_3, weights_t, features, features_t, w_agg, w_self, cotangent, hidden_ref, send_ref, keep_ref, agg_t):
    own_c, own_x = scalars[0], scalars[1]
    degree = 1.0 + jnp.sum(weights_t[...], axis=0, keepdims=True)
    for k, near in enumerate((near_0, near_1, near_2, near_3)):
        quarter = lax.rem(own_x + (NX - k), NX)
        summed = near[...]
        for y in range(NY):
            summed = summed + arrived[quarter, y].astype(F32)
        agg_t[pl.ds(pl.multiple_of(quarter * T, T), T), :] = (summed / degree).astype(BF16)
    contract = (((0,), (0,)), ((), ()))
    preact = lax.dot_general(agg_t[...], w_agg[...], contract, preferred_element_type=F32) + jnp.dot(
        features[...], w_self[...], preferred_element_type=F32
    )
    sigma = jax.nn.sigmoid(preact)
    hidden_ref[...] = (preact * sigma).astype(BF16)
    grad_pre = (cotangent[...].astype(F32) * sigma * (1.0 + preact * (1.0 - sigma))).astype(BF16)
    of_agg = jnp.dot(agg_t[...], grad_pre, preferred_element_type=F32)
    of_self = jnp.dot(features_t[...], grad_pre, preferred_element_type=F32)

    @pl.when(own_c == 0)
    def _():
        keep_ref[...] = of_agg
        send_ref[...] = of_self

    @pl.when(own_c != 0)
    def _():
        keep_ref[...] = of_self
        send_ref[...] = of_agg


def add_kernel(parts_ref, sum_ref):
    summed = parts_ref[0].astype(F32)
    for i in range(1, OWNERS):
        summed = summed + parts_ref[i].astype(F32)
    sum_ref[...] = summed


def body(features, edge_weights, neighbours, send_list, send_count, w_agg, w_self, cotangent):
    width = features.shape[1]
    z, x, y, c = (lax.axis_index(a).astype(jnp.int32) for a in ("z", "x", "y", "c"))
    swap = [(0, 1), (1, 0)]

    features_t = features.T
    quarters = jnp.broadcast_to(features_t.reshape(1, NX, T, T), (NZ, NX, T, T)).reshape(OWNERS, T, T)
    blocks = lax.all_to_all(quarters, ("z", "x"), 0, 0, tiled=True)

    codes_t = neighbours.T
    weights_t = edge_weights.T
    told = jnp.concatenate([send_count[0], send_list[0].reshape(1, GROUPS * CAP)], axis=1).astype(BF16)
    told = jnp.pad(told, ((0, 3), (0, T - GROUPS * (1 + CAP))))
    block, row = (codes_t // T).astype(BF16), (codes_t % T).astype(BF16)
    gap = jnp.zeros((16 - K_LOC, T), BF16)
    parts = [block[K_LOC:], row[K_LOC:], weights_t[K_LOC:], told]
    parts += [block[:K_LOC], gap, row[:K_LOC], gap, weights_t[:K_LOC], gap]
    along_x = lax.all_gather(jnp.concatenate(parts, axis=0), "x", axis=0)
    remote_data = lax.all_gather(along_x[:, :16], ("y", "c"), axis=0)
    told = remote_data[:, :, 12].astype(jnp.int32)
    sources = jnp.arange(GROUPS, dtype=jnp.int32)[:, None, None]
    group = y * NC + c
    here = jnp.sum(jnp.where(sources == group, told, 0), axis=0)
    start = jnp.sum(jnp.where(sources < group, told[:, :, :GROUPS], 0), axis=0)
    lists = here[:, GROUPS : GROUPS * (1 + CAP)]
    scalars = jnp.concatenate([lists.reshape(-1), start.reshape(-1), here[:, :GROUPS].reshape(-1)])

    def remote_sums(core, blocks):
        (sums,) = vmem_call(
            remote_kernel, "remote_sums", [jnp.concatenate([core[None], scalars])], [blocks, remote_data],
            [((NX, NY, T, T), BF16)], flops=300_000_000, bytes_accessed=2_500_000,
        )
        return sums

    received = lax.ppermute(remote_sums(1 - c, blocks), "c", swap)
    keep = remote_sums(c, blocks)
    chip_sum = (keep.astype(F32) + received.astype(F32)).astype(BF16)
    arrived = lax.all_to_all(chip_sum.reshape(NX * NY, T, T), ("x", "y"), 0, 0, tiled=True)

    near = vmem_call(
        local_kernel, "local_sums", [jnp.stack([z, x])], [blocks, along_x], [((T, T), F32)] * NX,
        scratch=[pltpu.VMEM((NX, 4 * T, T), BF16), pltpu.VMEM((NX, T, T), F32)],
        flops=600_000_000, bytes_accessed=1_500_000,
    )
    near = [near[0]] + [lax.ppermute(near[k], "x", [(i, (i + k) % NX) for i in range(NX)]) for k in range(1, NX)]

    hidden, send, keep = vmem_call(
        dense_kernel, "dense", [jnp.stack([c, x])],
        [arrived.reshape(NX, NY, T, T), *near, weights_t.astype(F32), features, features_t, w_agg, w_self, cotangent],
        [((T, width), BF16), ((width, width), F32), ((width, width), F32)],
        scratch=[pltpu.VMEM((width, T), BF16)], flops=300_000_000, bytes_accessed=5_000_000, transcendentals=65536,
    )
    received = lax.ppermute(send, "c", swap)
    share = width // OWNERS
    chip_grad = (keep + received).astype(BF16).reshape(OWNERS, share, width)
    rows = lax.all_to_all(chip_grad, ("z", "x"), 0, 0, tiled=True)
    (plane,) = vmem_call(add_kernel, "add_rows", [], [rows], [((share, width), F32)], flops=300_000, bytes_accessed=550_000)
    both = lax.all_gather(plane, ("y", "c"), axis=0).reshape(NY, NC, share, width)
    grads = jnp.sum(both, axis=0)
    return hidden, grads[0], grads[1]


def solution(mesh):
    fine = Mesh(mesh.devices.reshape(NZ, NX, NY, NC), ("z", "x", "y", "c"))
    row, rep = ("z", "x"), ("y", "c")
    nodes = P(row + rep, None)
    in_specs = (nodes, nodes, nodes, P(row, rep, None, None), P(row, rep, None), P(), P(), nodes)
    out_specs = (nodes, P(row, None), P(row, None))
    return jax.shard_map(body, mesh=fine, in_specs=in_specs, out_specs=out_specs, check_vma=False)
```

time: 521 us -> 149 us (0.29)
  waiting for transfers between devices: 405 us -> 5.15 us
  blocking collectives: 0 us -> 76 us
  local copies, waits for them, and re-layouts: 67.2 us -> 6.55 us
  Pallas kernels: 0 us -> 20.4 us
  starting transfers between devices: 21.2 us -> 37.5 us
  between operations: 14.3 us -> 0.88 us
  other arithmetic: 8.57 us -> 2.24 us
    psum x1 -> x0, waiting for transfers between devices: 274 us -> none  [body(): summed_agg, summed_self = lax.psum((part_agg, part_self), ('row', 'rep'))]
    all_gather x1 -> x0, waiting for transfers between devices: 80.7 us -> none  [body(): gathered = lax.all_gather(features, 'row', axis=0, tiled=True)]
    gather x17 -> x0, local copies, waits for them, and re-layouts: 62.9 us -> none  [the longest x12 43.3 us: body(): picked = jnp.take(gathered, neighbours[:, slot_index], axis=0)]
    all_gather x0 -> x3, blocking collectives: none -> 52 us  [the longest x1 20.4 us: body(): remote_data = lax.all_gather(along_x[:, :16], ('y', 'c'), axis=0)]
    all_to_all x2, waiting for transfers between devices: 49 us -> 0.01 us  [the longest x1 0.01 us: body(): blocks = lax.all_to_all(quarters, ('z', 'x'), 0, 0, tiled=True)]
    all_to_all x0 -> x1, blocking collectives: none -> 24.1 us  [body(): rows = lax.all_to_all(chip_grad, ('z', 'x'), 0, 0, tiled=True)]
    pallas_call x0 -> x5, Pallas kernels: none -> 20.4 us  [vmem_call(): pl.pallas_call(kernel, in_specs=[pl.BlockSpec(memory_space=pltpu.SMEM)] *...]
    ppermute x0 -> x5, starting transfers between devices: none -> 17.4 us  [the longest x3 10.5 us: body(): lax.ppermute(near[k], 'x', [(i, (i + k) % NX) for i in range(NX)])]
  transfers between devices with their start and end apart: 4 -> 7, of which waited for: 3 -> 3; matrix products, arithmetic and copies ran while one was open for 11% -> 1% of each run, Pallas kernels for 0% -> 10%
where the time goes in v2:
time: 149 us
  blocking collectives  76 us (51%)
  starting transfers between devices  37.5 us (25%)
  Pallas kernels  20.4 us (14%)
  local copies, waits for them, and re-layouts  6.55 us (4%)
  waiting for transfers between devices  5.15 us (3%)
  other arithmetic  2.24 us (2%)
    all_to_all x1, blocking collectives, body(): rows = lax.all_to_all(chip_grad, ('z', 'x'), 0, 0, tiled=True)  24.1 us
    pallas_call x5, Pallas kernels, vmem_call(): pl.pallas_call(kernel, in_specs=[pl.BlockSpec(memory_space=pltpu.SMEM)] *...  20.4 us
    all_gather x1, blocking collectives, body(): remote_data = lax.all_gather(along_x[:, :16], ('y', 'c'), axis=0)  20.4 us
    all_gather x1, blocking collectives, body(): lax.all_gather(plane, ('y', 'c'), axis=0).reshape(NY, NC, share, width)  20.3 us
    all_to_all x1, starting transfers between devices, body(): blocks = lax.all_to_all(quarters, ('z', 'x'), 0, 0, tiled=True)  13.9 us
    all_gather x1, blocking collectives, body(): along_x = lax.all_gather(jnp.concatenate(parts, axis=0), 'x', axis=0)  11.3 us
    ppermute x3, starting transfers between devices, body(): lax.ppermute(near[k], 'x', [(i, (i + k) % NX) for i in range(NX)])  10.5 us
    all_to_all x1, starting transfers between devices, body(): lax.all_to_all(chip_sum.reshape(NX * NY, T, T), ('x', 'y'), 0, 0, tiled=T...  6.16 us
  transfers between devices with their start and end apart: 7, of which 3 were waited for; matrix products, arithmetic and copies ran while one was open for 1% of the time, Pallas kernels for 10%

profile of v2, /device:TPU:1, one launch (start us, length us, event | category | flops | bytes accessed | tf_op | source)
XLA Modules:
  0.0 148.7 jit_solution(1421221313369627988)
XLA Ops:
  0.6 1.0 copy.16
  1.7 1.2 broadcast_in_dim.45
  2.9 13.9 %all-to-all-start = ((bf16[32,128,128]{2,1,0:T(8,128)(2,1)}), bf16[32,128,128]{2,1,0:T(8,128)(2,1)S(1)}, u32[]{:S(2)}, u32[]{:S(2)}) async-start(bf16[32,128,128]{2,1,0:T(8,128)(2,1)} %bitcast.10), calls=%async_computation | async-start | bytes 2097152 | tf_op jit(solution)/shard_map/all_to_all | solution.py:137
  16.9 0.1 copy.15
  17.0 0.1 concatenate.29
  17.1 0.1 fusion.10
  17.2 0.2 concatenate.31
  17.3 11.3 %all-gather = bf16[256,128]{1,0:T(8,128)(2,1)S(1)} all-gather(bf16[64,128]{1,0:T(8,128)(2,1)S(1)} %concatenate.31), channel_id=2, replica_groups=mesh['z'=8,'x'=4,'y'=8,'c'=2] {'x'}, dimensions={0}, use_global_device_ids=true | all-gather | bytes 81920 | tf_op jit(solution)/shard_map/all_gather | solution.py:147
  28.7 0.6 copy-done.4
  29.3 20.4 %all-gather.1 = bf16[64,16,128]{2,1,0:T(8,128)(2,1)S(1)} all-gather(bf16[4,16,128]{2,1,0:T(8,128)(2,1)S(1)} %slice.58), channel_id=3, replica_groups=mesh['z'=8,'x'=4,'y'=8,'c'=2] {'y','c'}, dimensions={0}, use_global_device_ids=true | all-gather | bytes 278528 | tf_op jit(solution)/shard_map/all_gather | solution.py:148
  49.7 0.1 slice_convert_fusion
  49.7 0.1 select_reduce_fusion
  49.8 0.1 slice.47
  49.9 0.1 reshape.82
  50.0 0.1 reshape.84
  50.1 0.1 fusion
  50.2 0.1 reshape.83
  50.3 0.1 pad_add_fusion.1
  50.3 0.0 all-to-all-done.blocks_ref
  50.3 3.3 %remote_sums.3 = bf16[4,8,128,128]{3,2,1,0:T(8,128)(2,1)S(1)} custom-call(s32[257]{0:T(512)S(1)} %get-tuple-element.22.scalars, bf16[32,128,128]{2,1,0:T(8,128)(2,1)S(1)} %all-to-all-done.blocks_ref, bf16[16,4,16,128]{3,2,1,0:T(8,128)(2,1)S(1)} %bitcast.57), custom_call_target="tpu_custom_call" | custom-call | flops 300000000 | bytes 2500000 | tf_op jit(solution)/shard_map/remote_sums/pallas_call | solution.py:22
  53.6 2.1 %collective-permute-start = (bf16[4,8,128,128]{3,2,1,0:T(8,128)(2,1)S(1)}, bf16[4,8,128,128]{3,2,1,0:T(8,128)(2,1)S(1)}, u32[]{:S(2)}, u32[]{:S(2)}) collective-permute-start(bf16[4,8,128,128]{3,2,1,0:T(8,128)(2,1)S(1)} %remote_sums.3), channel_id=1, source_target_pairs={{0,1},{1,0},{2,3},{3,2},{4,5},{5,4},{6,7},{7,6},{8,9},{9,8},{10,11... | collective-permute-start | bytes 3145736 | tf_op jit(solution)/shard_map/ppermute | solution.py:164
  55.7 3.3 %remote_sums.2 = bf16[4,8,128,128]{3,2,1,0:T(8,128)(2,1)S(1)} custom-call(s32[257]{0:T(512)S(1)} %get-tuple-element.21.scalars, bf16[32,128,128]{2,1,0:T(8,128)(2,1)S(1)} %all-to-all-done.blocks_ref, bf16[16,4,16,128]{3,2,1,0:T(8,128)(2,1)S(1)} %bitcast.58), custom_call_target="tpu_custom_call" | custom-call | flops 300000000 | bytes 2500000 | tf_op jit(solution)/shard_map/remote_sums/pallas_call | solution.py:22
  59.0 0.0 collective-permute-done
  59.0 1.4 add_convert_fusion
  60.4 6.2 %all-to-all-start.1 = ((bf16[32,128,128]{2,1,0:T(8,128)(2,1)}), bf16[32,128,128]{2,1,0:T(8,128)(2,1)S(1)}, u32[]{:S(2)}, u32[]{:S(2)}) async-start(bf16[32,128,128]{2,1,0:T(8,128)(2,1)} %bitcast.12), calls=%async_computation.1 | async-start | bytes 2097152 | tf_op jit(solution)/shard_map/all_to_all | solution.py:167
  66.5 0.1 pad_add_fusion.7.scalars
  66.6 0.8 copy-done.5
  67.5 11.5 %local_sums.1 = (f32[128,128]{1,0:T(8,128)S(1)}, f32[128,128]{1,0:T(8,128)S(1)}, f32[128,128]{1,0:T(8,128)S(1)}, f32[128,128]{1,0:T(8,128)S(1)}) custom-call(s32[2]{0:T(128)S(1)} %pad_add_fusion.7.scalars, bf16[32,128,128]{2,1,0:T(8,128)(2,1)S(1)} %all-to-all-done.blocks_ref, bf16[4,64,128]{2,1,0:T(8,128)(2,1)S(1)} %bitcast.62), custom_call_target="tpu_custom_call" | custom-call | flops 600000000 | bytes 1500000 | tf_op jit(solution)/shard_map/local_sums/pallas_call | solution.py:22
  78.9 0.0 copy-start.6
  78.9 0.6 copy-done.6
  79.6 3.1 %collective-permute-start.1 = (f32[128,128]{1,0:T(8,128)S(1)}, f32[128,128]{1,0:T(8,128)S(1)}, u32[]{:S(2)}, u32[]{:S(2)}) collective-permute-start(f32[128,128]{1,0:T(8,128)S(1)} %get-tuple-element.11), channel_id=1, source_target_pairs={{0,16},{16,32},{32,48},{48,0},{1,17},{17,33},{33,49},{49,1},{2,18}... | collective-permute-start | bytes 196616 | tf_op jit(solution)/shard_map/ppermute | solution.py:174
  82.7 4.3 %collective-permute-start.2 = (f32[128,128]{1,0:T(8,128)S(1)}, f32[128,128]{1,0:T(8,128)S(1)}, u32[]{:S(2)}, u32[]{:S(2)}) collective-permute-start(f32[128,128]{1,0:T(8,128)S(1)} %get-tuple-element.12), channel_id=1, source_target_pairs={{0,32},{16,48},{32,0},{48,16},{1,33},{17,49},{33,1},{49,17},{2,34}... | collective-permute-start | bytes 196616 | tf_op jit(solution)/shard_map/ppermute | solution.py:174
  87.0 3.1 %collective-permute-start.3 = (f32[128,128]{1,0:T(8,128)S(1)}, f32[128,128]{1,0:T(8,128)S(1)}, u32[]{:S(2)}, u32[]{:S(2)}) collective-permute-start(f32[128,128]{1,0:T(8,128)S(1)} %get-tuple-element.13), channel_id=1, source_target_pairs={{0,48},{16,0},{32,16},{48,32},{1,49},{17,1},{33,17},{49,33},{2,50}... | collective-permute-start | bytes 196616 | tf_op jit(solution)/shard_map/ppermute | solution.py:174
  90.1 0.1 pad_add_fusion.6.scalars
  90.2 0.0 collective-permute-done.1.near_1
  90.2 1.5 collective-permute-done.2.near_2
  91.6 1.4 collective-permute-done.3.near_3
  93.1 0.0 all-to-all-done.1
  93.1 0.0 copy-start.7
  93.1 0.8 copy-done.7
  93.9 2.3 %dense.1 = (bf16[128,512]{1,0:T(8,128)(2,1)}, f32[512,512]{1,0:T(8,128)S(1)}, f32[512,512]{1,0:T(8,128)S(1)}) custom-call(s32[2]{0:T(128)S(1)} %pad_add_fusion.6.scalars, bf16[4,8,128,128]{3,2,1,0:T(8,128)(2,1)S(1)} %bitcast.55, f32[128,128]{1,0:T(8,128)S(1)} %copy-done.7, f32[128,128]{1,0:T(8,128)S(1)} %collective-permute-done.1.near_1, ...), custom_call_target="tpu_custom_call" | custom-call | flops 300000000 | bytes 5000000 | tf_op jit(solution)/shard_map/dense/pallas_call | solution.py:22
  96.2 4.8 %collective-permute-start.4 = (f32[512,512]{1,0:T(8,128)S(1)}, f32[512,512]{1,0:T(8,128)S(1)}, u32[]{:S(2)}, u32[]{:S(2)}) collective-permute-start(f32[512,512]{1,0:T(8,128)S(1)} %get-tuple-element.16), channel_id=1, source_target_pairs={{0,1},{1,0},{2,3},{3,2},{4,5},{5,4},{6,7},{7,6},{8,9},{9,8},{10,11... | collective-permute-start | bytes 3145736 | tf_op jit(solution)/shard_map/ppermute | solution.py:182
  101.1 2.3 %collective-permute-done.4 = f32[512,512]{1,0:T(8,128)S(1)} collective-permute-done((f32[512,512]{1,0:T(8,128)S(1)}, f32[512,512]{1,0:T(8,128)S(1)}, u32[]{:S(2)}, u32[]{:S(2)}) %collective-permute-start.4) | collective-permute-done | bytes 1048608 | tf_op jit(solution)/shard_map/ppermute | solution.py:182
  103.3 0.3 add_convert_fusion.1
  103.6 24.1 %all_to_all.15.parts_ref = bf16[32,16,512]{2,1,0:T(8,128)(2,1)S(1)} all-to-all(bf16[32,16,512]{2,1,0:T(8,128)(2,1)S(1)} %bitcast.63), channel_id=1, replica_groups=mesh['z'=8,'x'=4,'y'=8,'c'=2] {'z','x'}, dimensions={0} | all-to-all | bytes 1048576 | tf_op jit(solution)/shard_map/all_to_all | solution.py:185
  127.6 0.1 add_rows.1
  127.7 20.3 %all-gather.2 = f32[256,512]{1,0:T(8,128)S(1)} all-gather(f32[16,512]{1,0:T(8,128)S(1)} %add_rows.1), channel_id=4, replica_groups=mesh['z'=8,'x'=4,'y'=8,'c'=2] {'y','c'}, dimensions={0}, use_global_device_ids=true | all-gather | bytes 557056 | tf_op jit(solution)/shard_map/all_gather | solution.py:187
  148.0 0.6 slice_bitcast_fusion
  (29 shorter events, 0.1 us)
Async XLA Ops:
  2.9 13.9 %copy-start.9 = (s32[128,16]{0,1:T(8,128)S(1)}, s32[128,16]{0,1:T(8,128)}, u32[]{:S(2)}) copy-start(s32[128,16]{0,1:T(8,128)} %param.10) | copy-start | bytes 24580
  2.9 13.9 %copy-start.8 = (bf16[128,16]{0,1:T(8,128)(2,1)S(1)}, bf16[128,16]{0,1:T(8,128)(2,1)}, u32[]{:S(2)}) copy-start(bf16[128,16]{0,1:T(8,128)(2,1)} %param.9) | copy-start | bytes 12292
  2.9 14.0 %copy-start.10 = (s32[1,1,16,2]{2,3,1,0:T(2,128)S(1)}, s32[1,1,16,2]{2,3,1,0:T(2,128)}, u32[]{:S(2)}) copy-start(s32[1,1,16,2]{2,3,1,0:T(2,128)} %param.11) | copy-start | bytes 388
  2.9 14.2 %copy-start.11 = (s32[1,1,16]{2,1,0:T(1,128)S(1)}, s32[1,1,16]{2,1,0:T(1,128)}, u32[]{:S(2)}) copy-start(s32[1,1,16]{2,1,0:T(1,128)} %param.12) | copy-start | bytes 196
  2.9 47.4 %all-to-all-start = ((bf16[32,128,128]{2,1,0:T(8,128)(2,1)}), bf16[32,128,128]{2,1,0:T(8,128)(2,1)S(1)}, u32[]{:S(2)}, u32[]{:S(2)}) async-start(bf16[32,128,128]{2,1,0:T(8,128)(2,1)} %bitcast.10), calls=%async_computation | async-start | bytes 2097152 | tf_op jit(solution)/shard_map/all_to_all | solution.py:137
  28.7 0.6 copy-start.4
  53.6 5.4 %collective-permute-start = (bf16[4,8,128,128]{3,2,1,0:T(8,128)(2,1)S(1)}, bf16[4,8,128,128]{3,2,1,0:T(8,128)(2,1)S(1)}, u32[]{:S(2)}, u32[]{:S(2)}) collective-permute-start(bf16[4,8,128,128]{3,2,1,0:T(8,128)(2,1)S(1)} %remote_sums.3), channel_id=1, source_target_pairs={{0,1},{1,0},{2,3},{3,2},{4,5},{5,4},{6,7},{7,6},{8,9},{9,8},{10,11... | collective-permute-start | bytes 3145736 | tf_op jit(solution)/shard_map/ppermute | solution.py:164
  60.4 32.7 %all-to-all-start.1 = ((bf16[32,128,128]{2,1,0:T(8,128)(2,1)}), bf16[32,128,128]{2,1,0:T(8,128)(2,1)S(1)}, u32[]{:S(2)}, u32[]{:S(2)}) async-start(bf16[32,128,128]{2,1,0:T(8,128)(2,1)} %bitcast.12), calls=%async_computation.1 | async-start | bytes 2097152 | tf_op jit(solution)/shard_map/all_to_all | solution.py:167
  66.6 0.8 copy-start.5
  67.4 25.6 %copy-start = (bf16[128,512]{1,0:T(8,128)(2,1)S(1)}, bf16[128,512]{1,0:T(8,128)(2,1)}, u32[]{:S(2)}) copy-start(bf16[128,512]{1,0:T(8,128)(2,1)} %features.1) | copy-start | bytes 393220
  67.4 25.6 %copy-start.1 = (bf16[512,512]{1,0:T(8,128)(2,1)S(1)}, bf16[512,512]{1,0:T(8,128)(2,1)}, u32[]{:S(2)}) copy-start(bf16[512,512]{1,0:T(8,128)(2,1)} %w_agg.1) | copy-start | bytes 1572868
  67.4 25.6 %copy-start.2 = (bf16[512,512]{1,0:T(8,128)(2,1)S(1)}, bf16[512,512]{1,0:T(8,128)(2,1)}, u32[]{:S(2)}) copy-start(bf16[512,512]{1,0:T(8,128)(2,1)} %w_self.1) | copy-start | bytes 1572868
  67.4 25.6 %copy-start.3 = (bf16[128,512]{1,0:T(8,128)(2,1)S(1)}, bf16[128,512]{1,0:T(8,128)(2,1)}, u32[]{:S(2)}) copy-start(bf16[128,512]{1,0:T(8,128)(2,1)} %cotangent.1) | copy-start | bytes 393220
  78.9 0.6 copy-start.6
  79.6 10.6 %collective-permute-start.1 = (f32[128,128]{1,0:T(8,128)S(1)}, f32[128,128]{1,0:T(8,128)S(1)}, u32[]{:S(2)}, u32[]{:S(2)}) collective-permute-start(f32[128,128]{1,0:T(8,128)S(1)} %get-tuple-element.11), channel_id=1, source_target_pairs={{0,16},{16,32},{32,48},{48,0},{1,17},{17,33},{33,49},{49,1},{2,18}... | collective-permute-start | bytes 196616 | tf_op jit(solution)/shard_map/ppermute | solution.py:174
  82.7 9.0 %collective-permute-start.2 = (f32[128,128]{1,0:T(8,128)S(1)}, f32[128,128]{1,0:T(8,128)S(1)}, u32[]{:S(2)}, u32[]{:S(2)}) collective-permute-start(f32[128,128]{1,0:T(8,128)S(1)} %get-tuple-element.12), channel_id=1, source_target_pairs={{0,32},{16,48},{32,0},{48,16},{1,33},{17,49},{33,1},{49,17},{2,34}... | collective-permute-start | bytes 196616 | tf_op jit(solution)/shard_map/ppermute | solution.py:174
  87.0 6.0 %collective-permute-start.3 = (f32[128,128]{1,0:T(8,128)S(1)}, f32[128,128]{1,0:T(8,128)S(1)}, u32[]{:S(2)}, u32[]{:S(2)}) collective-permute-start(f32[128,128]{1,0:T(8,128)S(1)} %get-tuple-element.13), channel_id=1, source_target_pairs={{0,48},{16,0},{32,16},{48,32},{1,49},{17,1},{33,17},{49,33},{2,50}... | collective-permute-start | bytes 196616 | tf_op jit(solution)/shard_map/ppermute | solution.py:174
  93.1 0.8 copy-start.7
  96.2 7.1 %collective-permute-start.4 = (f32[512,512]{1,0:T(8,128)S(1)}, f32[512,512]{1,0:T(8,128)S(1)}, u32[]{:S(2)}, u32[]{:S(2)}) collective-permute-start(f32[512,512]{1,0:T(8,128)S(1)} %get-tuple-element.16), channel_id=1, source_target_pairs={{0,1},{1,0},{2,3},{3,2},{4,5},{5,4},{6,7},{7,6},{8,9},{9,8},{10,11... | collective-permute-start | bytes 3145736 | tf_op jit(solution)/shard_map/ppermute | solution.py:182

commit v3 on v2

v3 whole, which is shorter than its diff:
```python
import jax
import jax.numpy as jnp
from jax import lax
from jax.experimental import pallas as pl
from jax.experimental.pallas import tpu as pltpu
from jax.sharding import Mesh, PartitionSpec as P

NZ, NX, NY, NC = 8, 4, 8, 2
OWNERS = NZ * NX
GROUPS = NY * NC
T = 128
K_LOC = 12
K_REM = 4
CAP = 2
TOLD = 16
F32 = jnp.float32
BF16 = jnp.bfloat16
VMEM_LIMIT = 16 * 1024 * 1024


def vmem_call(
    kernel, name, scalar_inputs, array_inputs, outputs, scratch=(), anywhere=(), flops=0, bytes_accessed=0, transcendentals=0
):
    vmem = pl.BlockSpec(memory_space=pltpu.VMEM)
    return pl.pallas_call(
        kernel,
        in_specs=[pl.BlockSpec(memory_space=pltpu.SMEM)] * len(scalar_inputs)
        + [pl.BlockSpec(memory_space=pl.ANY)] * len(anywhere)
        + [vmem] * len(array_inputs),
        out_specs=[vmem] * len(outputs),
        out_shape=[jax.ShapeDtypeStruct(shape, dtype) for shape, dtype in outputs],
        scratch_shapes=list(scratch),
        compiler_params=pltpu.CompilerParams(vmem_limit_bytes=VMEM_LIMIT),
        cost_estimate=pl.CostEstimate(flops=flops, bytes_accessed=bytes_accessed, transcendentals=transcendentals),
        name=name,
    )(*scalar_inputs, *anywhere, *array_inputs)


def spread_kernel(features_ref, quarters_ref, features_t, sems):
    features_t[...] = features_ref[...].astype(F32).T.astype(BF16).reshape(NX, T, T)
    copies = [pltpu.make_async_copy(features_t, quarters_ref.at[z], sems.at[z]) for z in range(NZ)]
    for copy in copies:
        copy.start()
    for copy in copies:
        copy.wait()


def spread(features):
    vmem, anywhere = pl.BlockSpec(memory_space=pltpu.VMEM), pl.BlockSpec(memory_space=pl.ANY)
    return pl.pallas_call(
        spread_kernel,
        in_specs=[vmem],
        out_specs=[anywhere, vmem],
        out_shape=[jax.ShapeDtypeStruct((NZ, NX, T, T), BF16), jax.ShapeDtypeStruct((NX, T, T), BF16)],
        scratch_shapes=[pltpu.SemaphoreType.DMA((NZ,))],
        compiler_params=pltpu.CompilerParams(vmem_limit_bytes=VMEM_LIMIT),
        name="spread",
    )(features)


def remote_kernel(scalars, blocks_ref, told_ref, sums_ref):
    core = scalars[0]
    rows = lax.broadcasted_iota(jnp.int16, (CAP * T, T), 0)

    def product(x, y):
        group = y * NC + core
        at = x * GROUPS + group
        first = jnp.clip(scalars[1 + at * CAP], 0, OWNERS - 1)
        second = jnp.clip(scalars[2 + at * CAP], 0, OWNERS - 1)
        start = scalars[1 + NX * GROUPS * CAP + at].astype(F32)
        count = scalars[1 + NX * GROUPS * (CAP + 1) + at].astype(F32)
        told = told_ref[x, pl.ds(pl.multiple_of(group * TOLD, TOLD), TOLD), :].astype(F32)
        entry = told[0:K_REM] - start
        row = jnp.where(entry < count, entry * T + told[K_REM : 2 * K_REM], -1.0).astype(jnp.int16)
        weight = told[2 * K_REM : 3 * K_REM].astype(BF16)
        hot = jnp.zeros((CAP * T, T), BF16)
        for k in range(K_REM):
            hot = jnp.where(rows == row[k : k + 1], weight[k : k + 1], hot)
        pair = jnp.concatenate([blocks_ref[first], blocks_ref[second]], axis=1)
        return jnp.dot(pair, hot, preferred_element_type=F32).astype(BF16)

    def of_y(y, carry):
        for x in range(NX):
            sums_ref[x, y] = product(x, y)
        return carry

    lax.fori_loop(0, NY, of_y, 0, unroll=True)


def local_kernel(scalars, blocks_ref, told_ref, out_0, out_1, out_2, out_3, hot_ref, total):
    own_z, own_x = scalars[0], scalars[1]
    rows = lax.broadcasted_iota(jnp.int16, (T, T), 0)
    lanes = lax.broadcasted_iota(jnp.int32, (1, T), 1).astype(F32)
    ones, zeros = jnp.ones((T, T), BF16), jnp.zeros((T, T), BF16)
    total[...] = jnp.zeros_like(total)

    def of_four(i, carry):
        for j in range(4):
            p = 4 * i + j
            for x in range(NX):
                block, row, weight = (
                    told_ref[x, GROUPS * TOLD + n * 16 : GROUPS * TOLD + n * 16 + 16, :].astype(F32) for n in range(3)
                )
                code = ((block - p.astype(F32)) * T + row).astype(jnp.int16)
                weight = weight.astype(BF16)
                own = (lanes - jnp.where(p == own_z * NX + x, 0.0, 1024.0)).astype(jnp.int16)
                hot = jnp.where(rows == own, ones, zeros)
                for k in range(K_LOC):
                    hot = jnp.where(rows == code[k : k + 1], weight[k : k + 1], hot)
                hot_ref[x, j * T : (j + 1) * T, :] = hot
        four = jnp.concatenate([blocks_ref[4 * i + j] for j in range(4)], axis=1)
        for x in range(NX):
            total[x] += jnp.dot(four, hot_ref[x], preferred_element_type=F32)
        return carry

    lax.fori_loop(0, OWNERS // 4, of_four, 0, unroll=2)
    for k, out in enumerate((out_0, out_1, out_2, out_3)):
        out[...] = total[lax.rem(own_x + k, NX)]


def dense_kernel(scalars, near_0, arrived, near_1, near_2, near_3, weights_t, features, features_t, w_agg, w_self, cotangent, hidden_ref, send_ref, keep_ref, agg_t, near, sem):
    own_c, own_x = scalars[0], scalars[1]
    degree = 1.0 + jnp.sum(weights_t[...], axis=0, keepdims=True)
    copy = pltpu.make_async_copy(near_0, near, sem)
    copy.start()

    def of_quarter(k, own):
        quarter = lax.rem(own_x + (NX - k), NX)
        summed = own[...]
        for y in range(NY):
            summed = summed + arrived[quarter, y].astype(F32)
        agg_t[pl.ds(pl.multiple_of(quarter * T, T), T), :] = (summed / degree).astype(BF16)

    of_quarter(1, near_1)
    of_quarter(2, near_2)
    of_quarter(3, near_3)
    copy.wait()
    of_quarter(0, near)
    contract = (((0,), (0,)), ((), ()))
    preact = lax.dot_general(agg_t[...], w_agg[...], contract, preferred_element_type=F32) + jnp.dot(
        features[...], w_self[...], preferred_element_type=F32
    )
    sigma = jax.nn.sigmoid(preact)
    hidden_ref[...] = (preact * sigma).astype(BF16)
    grad_pre = (cotangent[...].astype(F32) * sigma * (1.0 + preact * (1.0 - sigma))).astype(BF16)
    of_agg = jnp.dot(agg_t[...], grad_pre, preferred_element_type=F32)
    of_self = jnp.dot(features_t[...].reshape(NX * T, T), grad_pre, preferred_element_type=F32)

    @pl.when(own_c == 0)
    def _():
        keep_ref[...] = of_agg
        send_ref[...] = of_self.astype(BF16)

    @pl.when(own_c != 0)
    def _():
        keep_ref[...] = of_self
        send_ref[...] = of_agg.astype(BF16)


def add_kernel(parts_ref, sum_ref):
    summed = parts_ref[0].astype(F32)
    for i in range(1, parts_ref.shape[0]):
        summed = summed + parts_ref[i].astype(F32)
    sum_ref[...] = summed.astype(sum_ref.dtype)


def added(parts, dtype):
    (summed,) = vmem_call(
        add_kernel, "added", [], [parts], [(parts.shape[1:], dtype)], flops=parts.size, bytes_accessed=3 * parts.size
    )
    return summed


def body(features, edge_weights, neighbours, send_list, send_count, w_agg, w_self, cotangent):
    width = features.shape[1]
    z, x, y, c = (lax.axis_index(a).astype(jnp.int32) for a in ("z", "x", "y", "c"))
    swap = [(0, 1), (1, 0)]

    quarters, features_t = spread(features)
    blocks = lax.all_to_all(quarters.reshape(OWNERS, T, T), ("z", "x"), 0, 0, tiled=True)

    codes_t = neighbours.T
    weights_t = edge_weights.T
    told = jnp.concatenate([send_count[0], send_list[0].reshape(1, GROUPS * CAP)], axis=1).astype(BF16)
    told = jnp.pad(told, ((0, 3), (0, T - GROUPS * (1 + CAP))))
    block, row = (codes_t // T).astype(BF16), (codes_t % T).astype(BF16)
    of_remote = jnp.concatenate([block[K_LOC:], row[K_LOC:], weights_t[K_LOC:], told], axis=0)
    over_rep = lax.all_gather(of_remote, ("y", "c"), axis=0)
    gap = jnp.zeros((16 - K_LOC, T), BF16)
    of_both = [over_rep.reshape(GROUPS * TOLD, T), block[:K_LOC], gap, row[:K_LOC], gap, weights_t[:K_LOC], gap]
    over_all = lax.all_gather(jnp.concatenate(of_both, axis=0), "x", axis=0)
    told = over_all[:, : GROUPS * TOLD].reshape(NX, GROUPS, TOLD, T)[:, :, 12].astype(jnp.int32)
    sources = jnp.arange(GROUPS, dtype=jnp.int32)[None, :, None]
    group = y * NC + c
    here = jnp.sum(jnp.where(sources == group, told, 0), axis=1)
    start = jnp.sum(jnp.where(sources < group, told[:, :, :GROUPS], 0), axis=1)
    lists = here[:, GROUPS : GROUPS * (1 + CAP)]
    scalars = jnp.concatenate([lists.reshape(-1), start.reshape(-1), here[:, :GROUPS].reshape(-1)])

    def remote_sums(core, blocks):
        (sums,) = vmem_call(
            remote_kernel, "remote_sums", [jnp.concatenate([core[None], scalars])], [blocks, over_all],
            [((NX, NY, T, T), BF16)], flops=300_000_000, bytes_accessed=2_500_000,
        )
        return sums

    received = lax.ppermute(remote_sums(1 - c, blocks), "c", swap)
    keep = remote_sums(c, blocks)
    chip_sum = (keep.astype(F32) + received.astype(F32)).astype(BF16)
    arrived = lax.all_to_all(chip_sum.reshape(NX * NY, T, T), ("x", "y"), 0, 0, tiled=True)

    near = vmem_call(
        local_kernel, "local_sums", [jnp.stack([z, x])], [blocks, over_all], [((T, T), F32)] * NX,
        scratch=[pltpu.VMEM((NX, 4 * T, T), BF16), pltpu.VMEM((NX, T, T), F32)],
        flops=600_000_000, bytes_accessed=1_500_000,
    )
    moved = [lax.ppermute(near[k], "x", [(i, (i + k) % NX) for i in range(NX)]) for k in range(1, NX)]

    hidden, send, keep = vmem_call(
        dense_kernel, "dense", [jnp.stack([c, x])],
        [arrived.reshape(NX, NY, T, T), *moved, weights_t.astype(F32), features, features_t, w_agg, w_self, cotangent],
        [((T, width), BF16), ((width, width), BF16), ((width, width), F32)],
        scratch=[pltpu.VMEM((width, T), BF16), pltpu.VMEM((T, T), F32), pltpu.SemaphoreType.DMA], anywhere=[near[0]], flops=300_000_000, bytes_accessed=5_000_000, transcendentals=65536,
    )
    received = lax.ppermute(send, "c", swap)
    share = width // OWNERS
    chip_grad = (keep + received.astype(F32)).reshape(NZ, NX, share, width).swapaxes(0, 1).astype(BF16)
    along_x = added(lax.all_to_all(chip_grad, "x", 0, 0, tiled=True), BF16)
    plane = added(lax.all_to_all(along_x, "z", 0, 0, tiled=True), F32)
    both = lax.all_gather(plane, ("y", "c"), axis=0).reshape(NY, NC, share, width)
    grads = jnp.sum(both, axis=0)
    return hidden, grads[0], grads[1]


def solution(mesh):
    fine = Mesh(mesh.devices.reshape(NZ, NX, NY, NC), ("z", "x", "y", "c"))
    row, rep = ("z", "x"), ("y", "c")
    nodes = P(row + rep, None)
    in_specs = (nodes, nodes, nodes, P(row, rep, None, None), P(row, rep, None), P(), P(), nodes)
    out_specs = (nodes, P(row, None), P(row, None))
    return jax.shard_map(body, mesh=fine, in_specs=in_specs, out_specs=out_specs, check_vma=False)
```

time: 149 us -> 147 us (0.987)
  Pallas kernels: 20.4 us -> 14.3 us
  waiting for transfers between devices: 5.15 us -> 9.23 us
  local copies, waits for them, and re-layouts: 6.55 us -> 3.33 us
  starting transfers between devices: 37.5 us -> 39.5 us
    pallas_call x5 -> x6, Pallas kernels: 20.4 us -> 13.1 us  [vmem_call(): pl.pallas_call(kernel, in_specs=[pl.BlockSpec(memory_space=pltpu.SMEM)] *...]
    all_to_all x1, waiting for transfers between devices: 0.01 us -> 3 us  [body(): lax.all_to_all(chip_sum.reshape(NX * NY, T, T), ('x', 'y'), 0, 0, tiled=T...]
    unnamed x25 -> x18, local copies, waits for them, and re-layouts: 3.98 us -> 1.97 us
    all_to_all x1 -> x2, blocking collectives: 24.1 us -> 25.7 us  [the longest x1 14 us: body(): plane = added(lax.all_to_all(along_x, 'z', 0, 0, tiled=True), F32)]
  transfers between devices with their start and end apart: 7 -> 7, of which waited for: 3 -> 5; matrix products, arithmetic and copies ran while one was open for 1% -> 1% of each run, Pallas kernels for 10% -> 6%
where the time goes in v3:
time: 147 us; the launch traced here: 146 us
  blocking collectives  76.9 us (52%)
  starting transfers between devices  39.5 us (27%)
  Pallas kernels  14.3 us (10%)
  waiting for transfers between devices  9.23 us (6%)
  local copies, waits for them, and re-layouts  3.33 us (2%)
  other arithmetic  2.18 us (1%)
    all_gather x1, blocking collectives, body(): lax.all_gather(plane, ('y', 'c'), axis=0).reshape(NY, NC, share, width)  19.6 us
    all_gather x1, blocking collectives, body(): over_rep = lax.all_gather(of_remote, ('y', 'c'), axis=0)  18.5 us
    all_to_all x1, blocking collectives, body(): plane = added(lax.all_to_all(along_x, 'z', 0, 0, tiled=True), F32)  14 us
    all_to_all x1, starting transfers between devices, body(): lax.all_to_all(quarters.reshape(OWNERS, T, T), ('z', 'x'), 0, 0, tiled=True)  13.9 us
    all_gather x1, blocking collectives, body(): over_all = lax.all_gather(jnp.concatenate(of_both, axis=0), 'x', axis=0)  13.1 us
    pallas_call x6, Pallas kernels, vmem_call(): pl.pallas_call(kernel, in_specs=[pl.BlockSpec(memory_space=pltpu.SMEM)] *...  13.1 us
    all_to_all x1, blocking collectives, body(): along_x = added(lax.all_to_all(chip_grad, 'x', 0, 0, tiled=True), BF16)  11.6 us
    ppermute x3, starting transfers between devices, body(): lax.ppermute(near[k], 'x', [(i, (i + k) % NX) for i in range(NX)])  10.5 us
  transfers between devices with their start and end apart: 7, of which 5 were waited for; matrix products, arithmetic and copies ran while one was open for 1% of the time, Pallas kernels for 6%

profile of v3, /device:TPU:1, one launch (start us, length us, event | category | flops | bytes accessed | tf_op | source)
XLA Modules:
  0.0 146.3 jit_solution(4493636942608719358)
XLA Ops:
  0.6 0.0 copy-start
  0.6 0.9 copy-done
  1.5 1.1 spread.1
  2.7 0.0 copy-start.7
  2.7 0.0 copy-start.5
  2.7 0.0 copy-start.6
  2.7 0.0 copy-start.8
  2.7 13.9 %all-to-all-start = ((bf16[32,128,128]{2,1,0:T(8,128)(2,1)}), bf16[32,128,128]{2,1,0:T(8,128)(2,1)S(1)}, u32[]{:S(2)}, u32[]{:S(2)}) async-start(bf16[32,128,128]{2,1,0:T(8,128)(2,1)} %bitcast.3), calls=%async_computation | async-start | bytes 2097152 | tf_op jit(solution)/shard_map/all_to_all | solution.py:180
  16.7 0.1 copy.12
  16.8 0.1 concatenate.32
  16.9 0.1 fusion.10
  17.0 18.5 %all-gather = bf16[256,128]{1,0:T(8,128)(2,1)S(1)} all-gather(bf16[16,128]{1,0:T(8,128)(2,1)S(1)} %pad_maximum_fusion), channel_id=2, replica_groups=mesh['z'=8,'x'=4,'y'=8,'c'=2] {'y','c'}, dimensions={0}, use_global_device_ids=true | all-gather | bytes 69632 | tf_op jit(solution)/shard_map/all_gather | solution.py:188
  35.6 0.1 concatenate.35
  35.7 13.1 %all-gather.1 = bf16[1216,128]{1,0:T(8,128)(2,1)S(1)} all-gather(bf16[304,128]{1,0:T(8,128)(2,1)S(1)} %concatenate.35), channel_id=3, replica_groups=mesh['z'=8,'x'=4,'y'=8,'c'=2] {'x'}, dimensions={0}, use_global_device_ids=true | all-gather | bytes 389120 | tf_op jit(solution)/shard_map/all_gather | solution.py:191
  48.9 0.1 slice_convert_fusion
  48.9 0.1 fusion
  49.0 0.1 reshape.89
  49.1 0.1 select_reduce_fusion
  49.2 0.1 slice.47
  49.3 0.1 reshape.90
  49.4 0.1 reshape.88
  49.4 0.1 pad_add_fusion.1
  49.5 1.7 %remote_sums.3 = bf16[4,8,128,128]{3,2,1,0:T(8,128)(2,1)S(1)} custom-call(s32[257]{0:T(512)S(1)} %get-tuple-element.26.scalars, bf16[32,128,128]{2,1,0:T(8,128)(2,1)S(1)} %all-to-all-done.blocks_ref, bf16[4,304,128]{2,1,0:T(8,128)(2,1)S(1)} %bitcast.56), custom_call_target="tpu_custom_call" | custom-call | flops 300000000 | bytes 2500000 | tf_op jit(solution)/shard_map/remote_sums/pallas_call | solution.py:25
  51.2 3.5 %collective-permute-start = (bf16[4,8,128,128]{3,2,1,0:T(8,128)(2,1)S(1)}, bf16[4,8,128,128]{3,2,1,0:T(8,128)(2,1)S(1)}, u32[]{:S(2)}, u32[]{:S(2)}) collective-permute-start(bf16[4,8,128,128]{3,2,1,0:T(8,128)(2,1)S(1)} %remote_sums.3), channel_id=1, source_target_pairs={{0,1},{1,0},{2,3},{3,2},{4,5},{5,4},{6,7},{7,6},{8,9},{9,8},{10,11... | collective-permute-start | bytes 3145736 | tf_op jit(solution)/shard_map/ppermute | solution.py:207
  54.7 1.7 %remote_sums.2 = bf16[4,8,128,128]{3,2,1,0:T(8,128)(2,1)S(1)} custom-call(s32[257]{0:T(512)S(1)} %get-tuple-element.25.scalars, bf16[32,128,128]{2,1,0:T(8,128)(2,1)S(1)} %all-to-all-done.blocks_ref, bf16[4,304,128]{2,1,0:T(8,128)(2,1)S(1)} %bitcast.57), custom_call_target="tpu_custom_call" | custom-call | flops 300000000 | bytes 2500000 | tf_op jit(solution)/shard_map/remote_sums/pallas_call | solution.py:25
  56.4 0.6 collective-permute-done
  57.0 1.3 add_convert_fusion
  58.3 5.3 %all-to-all-start.1 = ((bf16[32,128,128]{2,1,0:T(8,128)(2,1)}), bf16[32,128,128]{2,1,0:T(8,128)(2,1)S(1)}, u32[]{:S(2)}, u32[]{:S(2)}) async-start(bf16[32,128,128]{2,1,0:T(8,128)(2,1)} %bitcast.60), calls=%async_computation.1 | async-start | bytes 2097152 | tf_op jit(solution)/shard_map/all_to_all | solution.py:210
  63.6 0.1 pad_add_fusion.7.scalars
  63.7 7.4 %local_sums.1 = (f32[128,128]{1,0:T(8,128)S(1)}, f32[128,128]{1,0:T(8,128)S(1)}, f32[128,128]{1,0:T(8,128)S(1)}, f32[128,128]{1,0:T(8,128)S(1)}) custom-call(s32[2]{0:T(128)S(1)} %pad_add_fusion.7.scalars, bf16[32,128,128]{2,1,0:T(8,128)(2,1)S(1)} %all-to-all-done.blocks_ref, bf16[4,304,128]{2,1,0:T(8,128)(2,1)S(1)} %bitcast.58), custom_call_target="tpu_custom_call" | custom-call | flops 600000000 | bytes 1500000 | tf_op jit(solution)/shard_map/local_sums/pallas_call | solution.py:25
  71.1 3.1 %collective-permute-start.1 = (f32[128,128]{1,0:T(8,128)S(1)}, f32[128,128]{1,0:T(8,128)S(1)}, u32[]{:S(2)}, u32[]{:S(2)}) collective-permute-start(f32[128,128]{1,0:T(8,128)S(1)} %get-tuple-element.14), channel_id=1, source_target_pairs={{0,16},{16,32},{32,48},{48,0},{1,17},{17,33},{33,49},{49,1},{2,18}... | collective-permute-start | bytes 196616 | tf_op jit(solution)/shard_map/ppermute | solution.py:217
  74.2 4.3 %collective-permute-start.2 = (f32[128,128]{1,0:T(8,128)S(1)}, f32[128,128]{1,0:T(8,128)S(1)}, u32[]{:S(2)}, u32[]{:S(2)}) collective-permute-start(f32[128,128]{1,0:T(8,128)S(1)} %get-tuple-element.15), channel_id=1, source_target_pairs={{0,32},{16,48},{32,0},{48,16},{1,33},{17,49},{33,1},{49,17},{2,34}... | collective-permute-start | bytes 196616 | tf_op jit(solution)/shard_map/ppermute | solution.py:217
  78.6 3.0 %collective-permute-start.3 = (f32[128,128]{1,0:T(8,128)S(1)}, f32[128,128]{1,0:T(8,128)S(1)}, u32[]{:S(2)}, u32[]{:S(2)}) collective-permute-start(f32[128,128]{1,0:T(8,128)S(1)} %get-tuple-element.16), channel_id=1, source_target_pairs={{0,48},{16,0},{32,16},{48,32},{1,49},{17,1},{33,17},{49,33},{2,50}... | collective-permute-start | bytes 196616 | tf_op jit(solution)/shard_map/ppermute | solution.py:217
  81.7 0.1 pad_add_fusion.6.scalars
  81.7 0.4 collective-permute-done.2.near_2
  82.1 3.7 %collective-permute-done.3.near_3 = f32[128,128]{1,0:T(8,128)S(1)} collective-permute-done((f32[128,128]{1,0:T(8,128)S(1)}, f32[128,128]{1,0:T(8,128)S(1)}, u32[]{:S(2)}, u32[]{:S(2)}) %collective-permute-start.3) | collective-permute-done | bytes 65568 | tf_op jit(solution)/shard_map/ppermute | solution.py:217
  85.8 3.0 %all-to-all-done.1 = bf16[32,128,128]{2,1,0:T(8,128)(2,1)S(1)} async-done(((bf16[32,128,128]{2,1,0:T(8,128)(2,1)}), bf16[32,128,128]{2,1,0:T(8,128)(2,1)S(1)}, u32[]{:S(2)}, u32[]{:S(2)}) %all-to-all-start.1) | async-done | bytes 1048608 | tf_op jit(solution)/shard_map/all_to_all | solution.py:210
  88.9 0.0 copy-start.3
  88.9 1.0 copy-done.3
  89.9 2.3 %dense.1 = (bf16[128,512]{1,0:T(8,128)(2,1)}, bf16[512,512]{1,0:T(8,128)(2,1)S(1)}, f32[512,512]{1,0:T(8,128)S(1)}) custom-call(s32[2]{0:T(128)S(1)} %pad_add_fusion.6.scalars, f32[128,128]{1,0:T(8,128)S(1)} %get-tuple-element.13.near_0, bf16[4,8,128,128]{3,2,1,0:T(8,128)(2,1)S(1)} %bitcast.59, f32[128,128]{1,0:T(8,128)S(1)} %collective-permute-done.1.near_1, ...), custom_call_target="tpu_custom_call" | custom-call | flops 300000000 | bytes 5000000 | tf_op jit(solution)/shard_map/dense/pallas_call | solution.py:25
  92.3 6.2 %collective-permute-start.4 = (bf16[512,512]{1,0:T(8,128)(2,1)S(1)}, bf16[512,512]{1,0:T(8,128)(2,1)S(1)}, u32[]{:S(2)}, u32[]{:S(2)}) collective-permute-start(bf16[512,512]{1,0:T(8,128)(2,1)S(1)} %get-tuple-element.20), channel_id=1, source_target_pairs={{0,1},{1,0},{2,3},{3,2},{4,5},{5,4},{6,7},{7,6},{8,9},{9,8},{10,11... | collective-permute-start | bytes 1572872 | tf_op jit(solution)/shard_map/ppermute | solution.py:225
  98.5 1.5 %collective-permute-done.4 = bf16[512,512]{1,0:T(8,128)(2,1)S(1)} collective-permute-done((bf16[512,512]{1,0:T(8,128)(2,1)S(1)}, bf16[512,512]{1,0:T(8,128)(2,1)S(1)}, u32[]{:S(2)}, u32[]{:S(2)}) %collective-permute-start.4) | collective-permute-done | bytes 524320 | tf_op jit(solution)/shard_map/ppermute | solution.py:225
  100.0 0.2 add_convert_fusion.1
  100.3 11.6 %all_to_all.20.parts_ref = bf16[4,8,16,512]{3,2,1,0:T(8,128)(2,1)S(1)} all-to-all(bf16[4,8,16,512]{3,2,1,0:T(8,128)(2,1)S(1)} %bitcast.62), channel_id=1, replica_groups=mesh['z'=8,'x'=4,'y'=8,'c'=2] {'x'}, dimensions={0} | all-to-all | bytes 1048576 | tf_op jit(solution)/shard_map/all_to_all | solution.py:228
  111.9 0.1 added.2
  112.0 14.0 %all_to_all.21.parts_ref = bf16[8,16,512]{2,1,0:T(8,128)(2,1)S(1)} all-to-all(bf16[8,16,512]{2,1,0:T(8,128)(2,1)S(1)} %added.2), channel_id=1, replica_groups=mesh['z'=8,'x'=4,'y'=8,'c'=2] {'z'}, dimensions={0} | all-to-all | bytes 262144 | tf_op jit(solution)/shard_map/all_to_all | solution.py:229
  126.0 19.6 %all-gather.2 = f32[256,512]{1,0:T(8,128)S(1)} all-gather(f32[16,512]{1,0:T(8,128)S(1)} %added.3), channel_id=4, replica_groups=mesh['z'=8,'x'=4,'y'=8,'c'=2] {'y','c'}, dimensions={0}, use_global_device_ids=true | all-gather | bytes 557056 | tf_op jit(solution)/shard_map/all_gather | solution.py:230
  145.7 0.6 slice_bitcast_fusion
  (26 shorter events, 0.2 us)
Async XLA Ops:
  0.6 0.9 copy-start
  2.7 13.9 %copy-start.7 = (s32[1,1,16,2]{2,3,1,0:T(2,128)S(1)}, s32[1,1,16,2]{2,3,1,0:T(2,128)}, u32[]{:S(2)}) copy-start(s32[1,1,16,2]{2,3,1,0:T(2,128)} %param.11) | copy-start | bytes 388
  2.7 13.9 %copy-start.5 = (bf16[128,16]{0,1:T(8,128)(2,1)S(1)}, bf16[128,16]{0,1:T(8,128)(2,1)}, u32[]{:S(2)}) copy-start(bf16[128,16]{0,1:T(8,128)(2,1)} %param.9) | copy-start | bytes 12292
  2.7 14.1 %copy-start.6 = (s32[128,16]{0,1:T(8,128)S(1)}, s32[128,16]{0,1:T(8,128)}, u32[]{:S(2)}) copy-start(s32[128,16]{0,1:T(8,128)} %param.10) | copy-start | bytes 24580
  2.7 14.2 %copy-start.8 = (s32[1,1,16]{2,1,0:T(1,128)S(1)}, s32[1,1,16]{2,1,0:T(1,128)}, u32[]{:S(2)}) copy-start(s32[1,1,16]{2,1,0:T(1,128)} %param.12) | copy-start | bytes 196
  2.7 46.8 %all-to-all-start = ((bf16[32,128,128]{2,1,0:T(8,128)(2,1)}), bf16[32,128,128]{2,1,0:T(8,128)(2,1)S(1)}, u32[]{:S(2)}, u32[]{:S(2)}) async-start(bf16[32,128,128]{2,1,0:T(8,128)(2,1)} %bitcast.3), calls=%async_computation | async-start | bytes 2097152 | tf_op jit(solution)/shard_map/all_to_all | solution.py:180
  51.2 5.8 %collective-permute-start = (bf16[4,8,128,128]{3,2,1,0:T(8,128)(2,1)S(1)}, bf16[4,8,128,128]{3,2,1,0:T(8,128)(2,1)S(1)}, u32[]{:S(2)}, u32[]{:S(2)}) collective-permute-start(bf16[4,8,128,128]{3,2,1,0:T(8,128)(2,1)S(1)} %remote_sums.3), channel_id=1, source_target_pairs={{0,1},{1,0},{2,3},{3,2},{4,5},{5,4},{6,7},{7,6},{8,9},{9,8},{10,11... | collective-permute-start | bytes 3145736 | tf_op jit(solution)/shard_map/ppermute | solution.py:207
  58.3 30.5 %all-to-all-start.1 = ((bf16[32,128,128]{2,1,0:T(8,128)(2,1)}), bf16[32,128,128]{2,1,0:T(8,128)(2,1)S(1)}, u32[]{:S(2)}, u32[]{:S(2)}) async-start(bf16[32,128,128]{2,1,0:T(8,128)(2,1)} %bitcast.60), calls=%async_computation.1 | async-start | bytes 2097152 | tf_op jit(solution)/shard_map/all_to_all | solution.py:210
  63.7 25.1 %copy-start.1 = (bf16[128,512]{1,0:T(8,128)(2,1)S(1)}, bf16[128,512]{1,0:T(8,128)(2,1)}, u32[]{:S(2)}) copy-start(bf16[128,512]{1,0:T(8,128)(2,1)} %features.1) | copy-start | bytes 393220
  63.7 25.1 %copy-start.2 = (bf16[512,512]{1,0:T(8,128)(2,1)S(1)}, bf16[512,512]{1,0:T(8,128)(2,1)}, u32[]{:S(2)}) copy-start(bf16[512,512]{1,0:T(8,128)(2,1)} %w_agg.1) | copy-start | bytes 1572868
  63.7 25.1 %copy-start.4 = (bf16[128,512]{1,0:T(8,128)(2,1)S(1)}, bf16[128,512]{1,0:T(8,128)(2,1)}, u32[]{:S(2)}) copy-start(bf16[128,512]{1,0:T(8,128)(2,1)} %cotangent.1) | copy-start | bytes 393220
  71.1 10.6 %collective-permute-start.1 = (f32[128,128]{1,0:T(8,128)S(1)}, f32[128,128]{1,0:T(8,128)S(1)}, u32[]{:S(2)}, u32[]{:S(2)}) collective-permute-start(f32[128,128]{1,0:T(8,128)S(1)} %get-tuple-element.14), channel_id=1, source_target_pairs={{0,16},{16,32},{32,48},{48,0},{1,17},{17,33},{33,49},{49,1},{2,18}... | collective-permute-start | bytes 196616 | tf_op jit(solution)/shard_map/ppermute | solution.py:217
  74.2 7.9 %collective-permute-start.2 = (f32[128,128]{1,0:T(8,128)S(1)}, f32[128,128]{1,0:T(8,128)S(1)}, u32[]{:S(2)}, u32[]{:S(2)}) collective-permute-start(f32[128,128]{1,0:T(8,128)S(1)} %get-tuple-element.15), channel_id=1, source_target_pairs={{0,32},{16,48},{32,0},{48,16},{1,33},{17,49},{33,1},{49,17},{2,34}... | collective-permute-start | bytes 196616 | tf_op jit(solution)/shard_map/ppermute | solution.py:217
  78.6 7.2 %collective-permute-start.3 = (f32[128,128]{1,0:T(8,128)S(1)}, f32[128,128]{1,0:T(8,128)S(1)}, u32[]{:S(2)}, u32[]{:S(2)}) collective-permute-start(f32[128,128]{1,0:T(8,128)S(1)} %get-tuple-element.16), channel_id=1, source_target_pairs={{0,48},{16,0},{32,16},{48,32},{1,49},{17,1},{33,17},{49,33},{2,50}... | collective-permute-start | bytes 196616 | tf_op jit(solution)/shard_map/ppermute | solution.py:217
  88.9 1.0 copy-start.3
  92.3 7.8 %collective-permute-start.4 = (bf16[512,512]{1,0:T(8,128)(2,1)S(1)}, bf16[512,512]{1,0:T(8,128)(2,1)S(1)}, u32[]{:S(2)}, u32[]{:S(2)}) collective-permute-start(bf16[512,512]{1,0:T(8,128)(2,1)S(1)} %get-tuple-element.20), channel_id=1, source_target_pairs={{0,1},{1,0},{2,3},{3,2},{4,5},{5,4},{6,7},{7,6},{8,9},{9,8},{10,11... | collective-permute-start | bytes 1572872 | tf_op jit(solution)/shard_map/ppermute | solution.py:225

commit v4 on v3

v4 whole, which is shorter than its diff:
```python
import jax
import jax.numpy as jnp
from jax import lax
from jax.experimental import pallas as pl
from jax.experimental.pallas import tpu as pltpu
from jax.sharding import Mesh, PartitionSpec as P

NZ, NX, NY, NC = 8, 4, 8, 2
OWNERS = NZ * NX
GROUPS = NY * NC
T = 128
K_LOC = 12
K_REM = 4
CAP = 2
TOLD = 16
CODES = 64
F32 = jnp.float32
BF16 = jnp.bfloat16
VMEM_LIMIT = 16 * 1024 * 1024


def vmem_call(
    kernel, name, scalar_inputs, array_inputs, outputs, scratch=(), anywhere=(), outside=0, flops=0, bytes_accessed=0, transcendentals=0
):
    vmem = pl.BlockSpec(memory_space=pltpu.VMEM)
    return pl.pallas_call(
        kernel,
        in_specs=[pl.BlockSpec(memory_space=pltpu.SMEM)] * len(scalar_inputs)
        + [pl.BlockSpec(memory_space=pltpu.HBM)] * len(anywhere)
        + [vmem] * len(array_inputs),
        out_specs=[vmem] * (len(outputs) - outside) + [pl.BlockSpec(memory_space=pltpu.HBM)] * outside,
        out_shape=[jax.ShapeDtypeStruct(*of) for of in outputs[: len(outputs) - outside]]
        + [pltpu.HBM(*of) for of in outputs[len(outputs) - outside :]],
        scratch_shapes=list(scratch),
        compiler_params=pltpu.CompilerParams(vmem_limit_bytes=VMEM_LIMIT),
        cost_estimate=pl.CostEstimate(flops=flops, bytes_accessed=bytes_accessed, transcendentals=transcendentals),
        name=name,
    )(*scalar_inputs, *anywhere, *array_inputs)


def quarters_kernel(features_ref, codes_ref, features_t, parts_ref):
    turned = features_ref[...].astype(F32).T.astype(BF16).reshape(NX, T, T)
    features_t[...] = turned
    for x in range(NX):
        parts_ref[x, 0:T, :] = turned[x]
        parts_ref[x, T : T + CODES, :] = codes_ref[...]


def copies_kernel(parts_ref, codes_ref, copies_ref, sems):
    copies = [pltpu.make_async_copy(parts_ref.at[:, 0:T, :], copies_ref.at[z], sems.at[z]) for z in range(NZ)]
    copies.append(pltpu.make_async_copy(parts_ref.at[:, T : T + CODES, :], codes_ref, sems.at[NZ]))
    for copy in copies:
        copy.start()
    for copy in copies:
        copy.wait()


def remote_kernel(scalars, blocks_ref, told_ref, sums_ref):
    core = scalars[0]
    rows = lax.broadcasted_iota(jnp.int16, (CAP * T, T), 0)

    def product(x, y):
        group = y * NC + core
        at = x * GROUPS + group
        first = jnp.clip(scalars[1 + at * CAP], 0, OWNERS - 1)
        second = jnp.clip(scalars[2 + at * CAP], 0, OWNERS - 1)
        start = scalars[1 + NX * GROUPS * CAP + at].astype(F32)
        count = scalars[1 + NX * GROUPS * (CAP + 1) + at].astype(F32)
        told = told_ref[group, x].astype(F32)
        entry = told[0:K_REM] - start
        row = jnp.where(entry < count, entry * T + told[K_REM : 2 * K_REM], -1.0).astype(jnp.int16)
        weight = told[2 * K_REM : 3 * K_REM].astype(BF16)
        hot = jnp.zeros((CAP * T, T), BF16)
        for k in range(K_REM):
            hot = jnp.where(rows == row[k : k + 1], weight[k : k + 1], hot)
        pair = jnp.concatenate([blocks_ref[first], blocks_ref[second]], axis=1)
        return jnp.dot(pair, hot, preferred_element_type=F32).astype(BF16)

    def of_y(y, carry):
        for x in range(NX):
            sums_ref[x, y] = product(x, y)
        return carry

    lax.fori_loop(0, NY, of_y, 0, unroll=True)


def local_kernel(scalars, blocks_ref, told_ref, out_1, out_2, out_3, out_0, hot_ref, total, sem):
    own_z, own_x = scalars[0], scalars[1]
    rows = lax.broadcasted_iota(jnp.int16, (T, T), 0)
    lanes = lax.broadcasted_iota(jnp.int32, (1, T), 1).astype(F32)
    ones, zeros = jnp.ones((T, T), BF16), jnp.zeros((T, T), BF16)
    total[...] = jnp.zeros_like(total)

    def of_four(i, carry):
        for j in range(4):
            p = 4 * i + j
            for x in range(NX):
                block, row, weight = (
                    told_ref[x, TOLD + n * 16 : TOLD + n * 16 + 16, :].astype(F32) for n in range(3)
                )
                code = ((block - p.astype(F32)) * T + row).astype(jnp.int16)
                weight = weight.astype(BF16)
                own = (lanes - jnp.where(p == own_z * NX + x, 0.0, 1024.0)).astype(jnp.int16)
                hot = jnp.where(rows == own, ones, zeros)
                for k in range(K_LOC):
                    hot = jnp.where(rows == code[k : k + 1], weight[k : k + 1], hot)
                hot_ref[x, j * T : (j + 1) * T, :] = hot
        four = jnp.concatenate([blocks_ref[4 * i + j] for j in range(4)], axis=1)
        for x in range(NX):
            total[x] += jnp.dot(four, hot_ref[x], preferred_element_type=F32)
        return carry

    lax.fori_loop(0, OWNERS // 4, of_four, 0, unroll=2)
    copy = pltpu.make_async_copy(total.at[own_x], out_0, sem)
    copy.start()
    for k, out in enumerate((out_1, out_2, out_3)):
        out[...] = total[lax.rem(own_x + k + 1, NX)]
    copy.wait()


def dense_kernel(scalars, near_0, w_self_in, arrived, near_1, near_2, near_3, weights_t, features, features_t, w_agg, cotangent, hidden_ref, send_ref, keep_ref, agg_t, near, w_self, sems):
    own_c, own_x = scalars[0], scalars[1]
    degree = 1.0 + jnp.sum(weights_t[...], axis=0, keepdims=True)
    copy = pltpu.make_async_copy(near_0, near, sems.at[0])
    copy.start()
    copy_w = pltpu.make_async_copy(w_self_in, w_self, sems.at[1])
    copy_w.start()

    def of_quarter(k, own):
        quarter = lax.rem(own_x + (NX - k), NX)
        summed = own[...]
        for y in range(NY):
            summed = summed + arrived[quarter, y].astype(F32)
        agg_t[pl.ds(pl.multiple_of(quarter * T, T), T), :] = (summed / degree).astype(BF16)

    of_quarter(1, near_1)
    of_quarter(2, near_2)
    of_quarter(3, near_3)
    copy.wait()
    of_quarter(0, near)
    copy_w.wait()
    contract = (((0,), (0,)), ((), ()))
    preact = lax.dot_general(agg_t[...], w_agg[...], contract, preferred_element_type=F32) + jnp.dot(
        features[...], w_self[...], preferred_element_type=F32
    )
    sigma = jax.nn.sigmoid(preact)
    hidden_ref[...] = (preact * sigma).astype(BF16)
    grad_pre = (cotangent[...].astype(F32) * sigma * (1.0 + preact * (1.0 - sigma))).astype(BF16)
    of_agg = jnp.dot(agg_t[...], grad_pre, preferred_element_type=F32)
    of_self = jnp.dot(features_t[...].reshape(NX * T, T), grad_pre, preferred_element_type=F32)

    @pl.when(own_c == 0)
    def _():
        keep_ref[...] = of_agg
        send_ref[...] = of_self.astype(BF16)

    @pl.when(own_c != 0)
    def _():
        keep_ref[...] = of_self
        send_ref[...] = of_agg.astype(BF16)


def add_kernel(parts_ref, sum_ref):
    summed = parts_ref[0].astype(F32)
    for i in range(1, parts_ref.shape[0]):
        summed = summed + parts_ref[i].astype(F32)
    sum_ref[...] = summed.astype(sum_ref.dtype)


def added(parts, dtype):
    (summed,) = vmem_call(
        add_kernel, "added", [], [parts], [(parts.shape[1:], dtype)], flops=parts.size, bytes_accessed=3 * parts.size
    )
    return summed


def body(features, edge_weights, neighbours, send_list, send_count, w_agg, w_self, cotangent):
    width = features.shape[1]
    z, x, y, c = (lax.axis_index(a).astype(jnp.int32) for a in ("z", "x", "y", "c"))
    swap = [(0, 1), (1, 0)]

    codes_t = neighbours.T
    weights_t = edge_weights.T
    told = jnp.concatenate([send_count[0], send_list[0].reshape(1, GROUPS * CAP)], axis=1).astype(BF16)
    told = jnp.pad(told, ((0, 3), (0, T - GROUPS * (1 + CAP))))
    block, row = (codes_t // T).astype(BF16), (codes_t % T).astype(BF16)
    gap = jnp.zeros((16 - K_LOC, T), BF16)
    codes = [block[K_LOC:], row[K_LOC:], weights_t[K_LOC:], told]
    codes += [block[:K_LOC], gap, row[:K_LOC], gap, weights_t[:K_LOC], gap]
    features_t, parts = vmem_call(
        quarters_kernel, "quarters", [], [features, jnp.concatenate(codes, axis=0)],
        [((NX, T, T), BF16), ((NX, T + CODES, T), BF16)], bytes_accessed=600_000,
    )
    parts = lax.all_to_all(parts, "x", 0, 0, tiled=True)
    codes, copies = vmem_call(
        copies_kernel, "copies", [], [parts], [((NX, CODES, T), BF16), ((NZ, NX, T, T), BF16)],
        scratch=[pltpu.SemaphoreType.DMA((NZ + 1,))], outside=2, bytes_accessed=1_500_000,
    )
    blocks = lax.all_to_all(copies, "z", 0, 0, tiled=True).reshape(OWNERS, T, T)
    remote_codes = lax.all_gather(codes[:, :TOLD], ("y", "c"), axis=0)
    told = remote_codes[:, :, 12].astype(jnp.int32)
    sources = jnp.arange(GROUPS, dtype=jnp.int32)[:, None, None]
    group = y * NC + c
    here = jnp.sum(jnp.where(sources == group, told, 0), axis=0)
    start = jnp.sum(jnp.where(sources < group, told[:, :, :GROUPS], 0), axis=0)
    lists = here[:, GROUPS : GROUPS * (1 + CAP)]
    scalars = jnp.concatenate([lists.reshape(-1), start.reshape(-1), here[:, :GROUPS].reshape(-1)])

    def remote_sums(core, blocks):
        (sums,) = vmem_call(
            remote_kernel, "remote_sums", [jnp.concatenate([core[None], scalars])], [blocks, remote_codes],
            [((NX, NY, T, T), BF16)], flops=300_000_000, bytes_accessed=2_500_000,
        )
        return sums

    received = lax.ppermute(remote_sums(1 - c, blocks), "c", swap)
    keep = remote_sums(c, blocks)
    chip_sum = (keep.astype(F32) + received.astype(F32)).astype(BF16)
    arrived = lax.all_to_all(chip_sum.reshape(NX * NY, T, T), ("x", "y"), 0, 0, tiled=True)

    *near, near_0 = vmem_call(
        local_kernel, "local_sums", [jnp.stack([z, x])], [blocks, codes], [((T, T), F32)] * NX,
        scratch=[pltpu.VMEM((NX, 4 * T, T), BF16), pltpu.VMEM((NX, T, T), F32), pltpu.SemaphoreType.DMA], outside=1,
        flops=600_000_000, bytes_accessed=1_500_000,
    )
    moved = [lax.ppermute(near[k - 1], "x", [(i, (i + k) % NX) for i in range(NX)]) for k in range(1, NX)]

    hidden, send, keep = vmem_call(
        dense_kernel, "dense", [jnp.stack([c, x])],
        [arrived.reshape(NX, NY, T, T), *moved, weights_t.astype(F32), features, features_t, w_agg, cotangent],
        [((T, width), BF16), ((width, width), BF16), ((width, width), F32)],
        scratch=[pltpu.VMEM((width, T), BF16), pltpu.VMEM((T, T), F32), pltpu.VMEM((width, width), BF16), pltpu.SemaphoreType.DMA((2,))],
        anywhere=[near_0, w_self], flops=300_000_000, bytes_accessed=5_000_000, transcendentals=65536,
    )
    received = lax.ppermute(send, "c", swap)
    share = width // OWNERS
    chip_grad = (keep + received.astype(F32)).astype(BF16).reshape(OWNERS, share, width)
    plane = added(lax.all_to_all(chip_grad, ("z", "x"), 0, 0, tiled=True), F32)
    both = lax.all_gather(plane, ("y", "c"), axis=0).reshape(NY, NC, share, width)
    grads = jnp.sum(both, axis=0)
    return hidden, grads[0], grads[1]


def solution(mesh):
    fine = Mesh(mesh.devices.reshape(NZ, NX, NY, NC), ("z", "x", "y", "c"))
    row, rep = ("z", "x"), ("y", "c")
    nodes = P(row + rep, None)
    in_specs = (nodes, nodes, nodes, P(row, rep, None, None), P(row, rep, None), P(), P(), nodes)
    out_specs = (nodes, P(row, None), P(row, None))
    return jax.shard_map(body, mesh=fine, in_specs=in_specs, out_specs=out_specs, check_vma=False)
```

time: 147 us -> 148 us (level)
  blocking collectives: 76.9 us -> 69.1 us
  waiting for transfers between devices: 9.23 us -> 13.4 us
  local copies, waits for them, and re-layouts: 3.33 us -> 6.02 us
  other arithmetic: 2.18 us -> 4.17 us
    all_gather x2 -> x1, blocking collectives: 31.7 us -> 20.5 us  [body(): remote_codes = lax.all_gather(codes[:, :TOLD], ('y', 'c'), axis=0)]
    all_to_all x1, waiting for transfers between devices: 0.01 us -> 5.68 us  [body(): blocks = lax.all_to_all(copies, 'z', 0, 0, tiled=True).reshape(OWNERS, T, T)]
    all_to_all x1, starting transfers between devices: 13.9 us -> 10 us  [body(): blocks = lax.all_to_all(copies, 'z', 0, 0, tiled=True).reshape(OWNERS, T, T)]
    all_to_all x2, blocking collectives: 25.7 us -> 29.5 us  [the longest x1 19.6 us: body(): plane = added(lax.all_to_all(chip_grad, ('z', 'x'), 0, 0, tiled=True), F32)]
    all_to_all x1, starting transfers between devices: 5.33 us -> 8.07 us  [body(): lax.all_to_all(chip_sum.reshape(NX * NY, T, T), ('x', 'y'), 0, 0, tiled=T...]
    pallas_call x6 -> x7, Pallas kernels: 13.1 us -> 14.9 us  [vmem_call(): pl.pallas_call(kernel, in_specs=[pl.BlockSpec(memory_space=pltpu.SMEM)] *...]
  transfers between devices with their start and end apart: 7 -> 7, of which waited for: 5 -> 6; matrix products, arithmetic and copies ran while one was open for 1% -> 1% of each run, Pallas kernels for 6% -> 7%
where the time goes in v4:
time: 148 us; the launch traced here: 147 us
  blocking collectives  69.1 us (47%)
  starting transfers between devices  38.9 us (26%)
  Pallas kernels  14.9 us (10%)
  waiting for transfers between devices  13.4 us (9%)
  local copies, waits for them, and re-layouts  6.02 us (4%)
  other arithmetic  4.17 us (3%)
    all_gather x1, blocking collectives, body(): remote_codes = lax.all_gather(codes[:, :TOLD], ('y', 'c'), axis=0)  20.5 us
    all_to_all x1, blocking collectives, body(): plane = added(lax.all_to_all(chip_grad, ('z', 'x'), 0, 0, tiled=True), F32)  19.6 us
    all_gather x1, blocking collectives, body(): lax.all_gather(plane, ('y', 'c'), axis=0).reshape(NY, NC, share, width)  19.1 us
    pallas_call x7, Pallas kernels, vmem_call(): pl.pallas_call(kernel, in_specs=[pl.BlockSpec(memory_space=pltpu.SMEM)] *...  14.9 us
    ppermute x3, starting transfers between devices, body(): lax.ppermute(near[k - 1], 'x', [(i, (i + k) % NX) for i in range(NX)])  10.5 us
    all_to_all x1, starting transfers between devices, body(): blocks = lax.all_to_all(copies, 'z', 0, 0, tiled=True).reshape(OWNERS, T, T)  10 us
    all_to_all x1, blocking collectives, body(): parts = lax.all_to_all(parts, 'x', 0, 0, tiled=True)  9.82 us
    all_to_all x1, starting transfers between devices, body(): lax.all_to_all(chip_sum.reshape(NX * NY, T, T), ('x', 'y'), 0, 0, tiled=T...  8.07 us
  transfers between devices with their start and end apart: 7, of which 6 were waited for; matrix products, arithmetic and copies ran while one was open for 1% of the time, Pallas kernels for 7%

profile of v4, /device:TPU:1, one launch (start us, length us, event | category | flops | bytes accessed | tf_op | source)
XLA Modules:
  0.0 147.3 jit_solution(17203067500093179717)
XLA Ops:
  0.6 0.7 convert.10
  1.3 0.7 convert_bitcast_fusion
  2.0 0.7 slice.54
  2.7 0.1 copy.13
  2.8 0.1 concatenate.29
  2.9 0.7 fusion.2
  3.6 0.1 fusion.10
  3.7 0.9 concatenate.31.codes_ref
  4.5 0.9 copy-done
  5.4 0.1 quarters.1
  5.5 9.8 %all_to_all.20.parts_ref = bf16[4,192,128]{2,1,0:T(8,128)(2,1)S(1)} all-to-all(bf16[4,192,128]{2,1,0:T(8,128)(2,1)S(1)} %get-tuple-element.14), channel_id=1, replica_groups=mesh['z'=8,'x'=4,'y'=8,'c'=2] {'x'}, dimensions={0} | all-to-all | bytes 393216 | tf_op jit(solution)/shard_map/all_to_all | solution.py:194
  15.4 1.1 copies.1
  16.4 10.0 %all-to-all-start.1 = ((bf16[8,4,128,128]{3,2,1,0:T(8,128)(2,1)}), bf16[8,4,128,128]{3,2,1,0:T(8,128)(2,1)S(1)}, u32[]{:S(2)}, u32[]{:S(2)}) async-start(bf16[8,4,128,128]{3,2,1,0:T(8,128)(2,1)} %get-tuple-element.15), calls=%async_computation.1 | async-start | bytes 2097152 | tf_op jit(solution)/shard_map/all_to_all | solution.py:199
  26.5 0.7 slice.45
  27.2 20.5 %all-gather = bf16[64,16,128]{2,1,0:T(8,128)(2,1)S(1)} all-gather(bf16[4,16,128]{2,1,0:T(8,128)(2,1)S(1)} %slice.45), channel_id=2, replica_groups=mesh['z'=8,'x'=4,'y'=8,'c'=2] {'y','c'}, dimensions={0}, use_global_device_ids=true | all-gather | bytes 278528 | tf_op jit(solution)/shard_map/all_gather | solution.py:200
  47.8 0.1 fusion
  47.9 0.1 reshape.82
  47.9 0.1 select_reduce_fusion
  48.0 0.1 slice.47
  48.1 0.1 reshape.83
  48.2 0.1 reshape.81
  48.3 0.1 pad_add_fusion.1
  48.4 5.7 %all-to-all-done.1 = bf16[8,4,128,128]{3,2,1,0:T(8,128)(2,1)S(1)} async-done(((bf16[8,4,128,128]{3,2,1,0:T(8,128)(2,1)}), bf16[8,4,128,128]{3,2,1,0:T(8,128)(2,1)S(1)}, u32[]{:S(2)}, u32[]{:S(2)}) %all-to-all-start.1) | async-done | bytes 1048608 | tf_op jit(solution)/shard_map/all_to_all | solution.py:199
  54.1 1.7 %remote_sums.3 = bf16[4,8,128,128]{3,2,1,0:T(8,128)(2,1)S(1)} custom-call(s32[257]{0:T(512)S(1)} %get-tuple-element.30.scalars, bf16[32,128,128]{2,1,0:T(8,128)(2,1)S(1)} %bitcast.51, bf16[16,4,16,128]{3,2,1,0:T(8,128)(2,1)S(1)} %bitcast.56), custom_call_target="tpu_custom_call" | custom-call | flops 300000000 | bytes 2500000 | tf_op jit(solution)/shard_map/remote_sums/pallas_call | solution.py:26
  55.7 4.0 %collective-permute-start = (bf16[4,8,128,128]{3,2,1,0:T(8,128)(2,1)S(1)}, bf16[4,8,128,128]{3,2,1,0:T(8,128)(2,1)S(1)}, u32[]{:S(2)}, u32[]{:S(2)}) collective-permute-start(bf16[4,8,128,128]{3,2,1,0:T(8,128)(2,1)S(1)} %remote_sums.3), channel_id=1, source_target_pairs={{0,1},{1,0},{2,3},{3,2},{4,5},{5,4},{6,7},{7,6},{8,9},{9,8},{10,11... | collective-permute-start | bytes 3145736 | tf_op jit(solution)/shard_map/ppermute | solution.py:216
  59.7 1.7 %remote_sums.2 = bf16[4,8,128,128]{3,2,1,0:T(8,128)(2,1)S(1)} custom-call(s32[257]{0:T(512)S(1)} %get-tuple-element.29.scalars, bf16[32,128,128]{2,1,0:T(8,128)(2,1)S(1)} %bitcast.52, bf16[16,4,16,128]{3,2,1,0:T(8,128)(2,1)S(1)} %bitcast.57), custom_call_target="tpu_custom_call" | custom-call | flops 300000000 | bytes 2500000 | tf_op jit(solution)/shard_map/remote_sums/pallas_call | solution.py:26
  61.4 0.6 collective-permute-done
  62.0 1.3 add_convert_fusion
  63.3 8.1 %all-to-all-start.2 = ((bf16[32,128,128]{2,1,0:T(8,128)(2,1)}), bf16[32,128,128]{2,1,0:T(8,128)(2,1)S(1)}, u32[]{:S(2)}, u32[]{:S(2)}) async-start(bf16[32,128,128]{2,1,0:T(8,128)(2,1)} %bitcast.10), calls=%async_computation.2 | async-start | bytes 2097152 | tf_op jit(solution)/shard_map/all_to_all | solution.py:219
  71.4 0.1 pad_add_fusion.7.scalars
  71.5 0.8 copy-done.6
  72.4 8.0 %local_sums.1 = (f32[128,128]{1,0:T(8,128)S(1)}, f32[128,128]{1,0:T(8,128)S(1)}, f32[128,128]{1,0:T(8,128)S(1)}, f32[128,128]{1,0:T(8,128)}) custom-call(s32[2]{0:T(128)S(1)} %pad_add_fusion.7.scalars, bf16[32,128,128]{2,1,0:T(8,128)(2,1)S(1)} %bitcast.53, bf16[4,64,128]{2,1,0:T(8,128)(2,1)S(1)} %copy-done.6), custom_call_target="tpu_custom_call" | custom-call | flops 600000000 | bytes 1500000 | tf_op jit(solution)/shard_map/local_sums/pallas_call | solution.py:26
  80.3 3.1 %collective-permute-start.1 = (f32[128,128]{1,0:T(8,128)S(1)}, f32[128,128]{1,0:T(8,128)S(1)}, u32[]{:S(2)}, u32[]{:S(2)}) collective-permute-start(f32[128,128]{1,0:T(8,128)S(1)} %get-tuple-element.18), channel_id=1, source_target_pairs={{0,16},{16,32},{32,48},{48,0},{1,17},{17,33},{33,49},{49,1},{2,18}... | collective-permute-start | bytes 196616 | tf_op jit(solution)/shard_map/ppermute | solution.py:226
  83.5 4.3 %collective-permute-start.2 = (f32[128,128]{1,0:T(8,128)S(1)}, f32[128,128]{1,0:T(8,128)S(1)}, u32[]{:S(2)}, u32[]{:S(2)}) collective-permute-start(f32[128,128]{1,0:T(8,128)S(1)} %get-tuple-element.19), channel_id=1, source_target_pairs={{0,32},{16,48},{32,0},{48,16},{1,33},{17,49},{33,1},{49,17},{2,34}... | collective-permute-start | bytes 196616 | tf_op jit(solution)/shard_map/ppermute | solution.py:226
  87.9 3.1 %collective-permute-start.3 = (f32[128,128]{1,0:T(8,128)S(1)}, f32[128,128]{1,0:T(8,128)S(1)}, u32[]{:S(2)}, u32[]{:S(2)}) collective-permute-start(f32[128,128]{1,0:T(8,128)S(1)} %get-tuple-element.20), channel_id=1, source_target_pairs={{0,48},{16,0},{32,16},{48,32},{1,49},{17,1},{33,17},{49,33},{2,50}... | collective-permute-start | bytes 196616 | tf_op jit(solution)/shard_map/ppermute | solution.py:226
  90.9 0.1 pad_add_fusion.6.scalars
  91.0 1.7 %collective-permute-done.2.near_2 = f32[128,128]{1,0:T(8,128)S(1)} collective-permute-done((f32[128,128]{1,0:T(8,128)S(1)}, f32[128,128]{1,0:T(8,128)S(1)}, u32[]{:S(2)}, u32[]{:S(2)}) %collective-permute-start.2) | collective-permute-done | bytes 65568 | tf_op jit(solution)/shard_map/ppermute | solution.py:226
  92.7 1.9 %collective-permute-done.3.near_3 = f32[128,128]{1,0:T(8,128)S(1)} collective-permute-done((f32[128,128]{1,0:T(8,128)S(1)}, f32[128,128]{1,0:T(8,128)S(1)}, u32[]{:S(2)}, u32[]{:S(2)}) %collective-permute-start.3) | collective-permute-done | bytes 65568 | tf_op jit(solution)/shard_map/ppermute | solution.py:226
  94.6 2.0 %all-to-all-done.2 = bf16[32,128,128]{2,1,0:T(8,128)(2,1)S(1)} async-done(((bf16[32,128,128]{2,1,0:T(8,128)(2,1)}), bf16[32,128,128]{2,1,0:T(8,128)(2,1)S(1)}, u32[]{:S(2)}, u32[]{:S(2)}) %all-to-all-start.2) | async-done | bytes 1048608 | tf_op jit(solution)/shard_map/all_to_all | solution.py:219
  96.7 0.8 copy-done.5
  97.5 2.4 %dense.1 = (bf16[128,512]{1,0:T(8,128)(2,1)}, bf16[512,512]{1,0:T(8,128)(2,1)S(1)}, f32[512,512]{1,0:T(8,128)S(1)}) custom-call(s32[2]{0:T(128)S(1)} %pad_add_fusion.6.scalars, f32[128,128]{1,0:T(8,128)S(1)} %copy-done.5, bf16[512,512]{1,0:T(8,128)(2,1)S(1)} %copy-done.2, bf16[4,8,128,128]{3,2,1,0:T(8,128)(2,1)S(1)} %bitcast.54, ...), custom_call_target="tpu_custom_call" | custom-call | flops 300000000 | bytes 5000000 | tf_op jit(solution)/shard_map/dense/pallas_call | solution.py:26
  99.9 6.2 %collective-permute-start.4 = (bf16[512,512]{1,0:T(8,128)(2,1)S(1)}, bf16[512,512]{1,0:T(8,128)(2,1)S(1)}, u32[]{:S(2)}, u32[]{:S(2)}) collective-permute-start(bf16[512,512]{1,0:T(8,128)(2,1)S(1)} %get-tuple-element.24), channel_id=1, source_target_pairs={{0,1},{1,0},{2,3},{3,2},{4,5},{5,4},{6,7},{7,6},{8,9},{9,8},{10,11... | collective-permute-start | bytes 1572872 | tf_op jit(solution)/shard_map/ppermute | solution.py:235
  106.2 1.5 %collective-permute-done.4 = bf16[512,512]{1,0:T(8,128)(2,1)S(1)} collective-permute-done((bf16[512,512]{1,0:T(8,128)(2,1)S(1)}, bf16[512,512]{1,0:T(8,128)(2,1)S(1)}, u32[]{:S(2)}, u32[]{:S(2)}) %collective-permute-start.4) | collective-permute-done | bytes 524320 | tf_op jit(solution)/shard_map/ppermute | solution.py:235
  107.7 0.2 add_convert_fusion.1
  107.8 19.6 %all_to_all.21.parts_ref = bf16[32,16,512]{2,1,0:T(8,128)(2,1)S(1)} all-to-all(bf16[32,16,512]{2,1,0:T(8,128)(2,1)S(1)} %bitcast.59), channel_id=1, replica_groups=mesh['z'=8,'x'=4,'y'=8,'c'=2] {'z','x'}, dimensions={0} | all-to-all | bytes 1048576 | tf_op jit(solution)/shard_map/all_to_all | solution.py:238
  127.5 0.1 added.1
  127.6 19.1 %all-gather.1 = f32[256,512]{1,0:T(8,128)S(1)} all-gather(f32[16,512]{1,0:T(8,128)S(1)} %added.1), channel_id=3, replica_groups=mesh['z'=8,'x'=4,'y'=8,'c'=2] {'y','c'}, dimensions={0}, use_global_device_ids=true | all-gather | bytes 557056 | tf_op jit(solution)/shard_map/all_gather | solution.py:239
  146.7 0.6 slice_bitcast_fusion
  (21 shorter events, 0.1 us)
Async XLA Ops:
  4.5 0.9 copy-start
  16.4 37.6 %all-to-all-start.1 = ((bf16[8,4,128,128]{3,2,1,0:T(8,128)(2,1)}), bf16[8,4,128,128]{3,2,1,0:T(8,128)(2,1)S(1)}, u32[]{:S(2)}, u32[]{:S(2)}) async-start(bf16[8,4,128,128]{3,2,1,0:T(8,128)(2,1)} %get-tuple-element.15), calls=%async_computation.1 | async-start | bytes 2097152 | tf_op jit(solution)/shard_map/all_to_all | solution.py:199
  55.7 6.3 %collective-permute-start = (bf16[4,8,128,128]{3,2,1,0:T(8,128)(2,1)S(1)}, bf16[4,8,128,128]{3,2,1,0:T(8,128)(2,1)S(1)}, u32[]{:S(2)}, u32[]{:S(2)}) collective-permute-start(bf16[4,8,128,128]{3,2,1,0:T(8,128)(2,1)S(1)} %remote_sums.3), channel_id=1, source_target_pairs={{0,1},{1,0},{2,3},{3,2},{4,5},{5,4},{6,7},{7,6},{8,9},{9,8},{10,11... | collective-permute-start | bytes 3145736 | tf_op jit(solution)/shard_map/ppermute | solution.py:216
  63.3 8.2 %copy-start.7 = (bf16[128,16]{0,1:T(8,128)(2,1)S(1)}, bf16[128,16]{0,1:T(8,128)(2,1)}, u32[]{:S(2)}) copy-start(bf16[128,16]{0,1:T(8,128)(2,1)} %param.9) | copy-start | bytes 12292
  63.3 33.3 %all-to-all-start.2 = ((bf16[32,128,128]{2,1,0:T(8,128)(2,1)}), bf16[32,128,128]{2,1,0:T(8,128)(2,1)S(1)}, u32[]{:S(2)}, u32[]{:S(2)}) async-start(bf16[32,128,128]{2,1,0:T(8,128)(2,1)} %bitcast.10), calls=%async_computation.2 | async-start | bytes 2097152 | tf_op jit(solution)/shard_map/all_to_all | solution.py:219
  71.5 0.8 copy-start.6
  72.4 24.3 %copy-start.1 = (bf16[128,512]{1,0:T(8,128)(2,1)S(1)}, bf16[128,512]{1,0:T(8,128)(2,1)}, u32[]{:S(2)}) copy-start(bf16[128,512]{1,0:T(8,128)(2,1)} %features.1) | copy-start | bytes 393220
  72.4 24.3 %copy-start.2 = (bf16[512,512]{1,0:T(8,128)(2,1)S(1)}, bf16[512,512]{1,0:T(8,128)(2,1)}, u32[]{:S(2)}) copy-start(bf16[512,512]{1,0:T(8,128)(2,1)} %w_self_in.1) | copy-start | bytes 1572868
  72.4 24.3 %copy-start.3 = (bf16[512,512]{1,0:T(8,128)(2,1)S(1)}, bf16[512,512]{1,0:T(8,128)(2,1)}, u32[]{:S(2)}) copy-start(bf16[512,512]{1,0:T(8,128)(2,1)} %w_agg.1) | copy-start | bytes 1572868
  72.4 24.3 %copy-start.4 = (bf16[128,512]{1,0:T(8,128)(2,1)S(1)}, bf16[128,512]{1,0:T(8,128)(2,1)}, u32[]{:S(2)}) copy-start(bf16[128,512]{1,0:T(8,128)(2,1)} %cotangent.1) | copy-start | bytes 393220
  80.3 10.6 %collective-permute-start.1 = (f32[128,128]{1,0:T(8,128)S(1)}, f32[128,128]{1,0:T(8,128)S(1)}, u32[]{:S(2)}, u32[]{:S(2)}) collective-permute-start(f32[128,128]{1,0:T(8,128)S(1)} %get-tuple-element.18), channel_id=1, source_target_pairs={{0,16},{16,32},{32,48},{48,0},{1,17},{17,33},{33,49},{49,1},{2,18}... | collective-permute-start | bytes 196616 | tf_op jit(solution)/shard_map/ppermute | solution.py:226
  83.5 9.2 %collective-permute-start.2 = (f32[128,128]{1,0:T(8,128)S(1)}, f32[128,128]{1,0:T(8,128)S(1)}, u32[]{:S(2)}, u32[]{:S(2)}) collective-permute-start(f32[128,128]{1,0:T(8,128)S(1)} %get-tuple-element.19), channel_id=1, source_target_pairs={{0,32},{16,48},{32,0},{48,16},{1,33},{17,49},{33,1},{49,17},{2,34}... | collective-permute-start | bytes 196616 | tf_op jit(solution)/shard_map/ppermute | solution.py:226
  87.9 6.8 %collective-permute-start.3 = (f32[128,128]{1,0:T(8,128)S(1)}, f32[128,128]{1,0:T(8,128)S(1)}, u32[]{:S(2)}, u32[]{:S(2)}) collective-permute-start(f32[128,128]{1,0:T(8,128)S(1)} %get-tuple-element.20), channel_id=1, source_target_pairs={{0,48},{16,0},{32,16},{48,32},{1,49},{17,1},{33,17},{49,33},{2,50}... | collective-permute-start | bytes 196616 | tf_op jit(solution)/shard_map/ppermute | solution.py:226
  96.7 0.8 copy-start.5
  99.9 7.8 %collective-permute-start.4 = (bf16[512,512]{1,0:T(8,128)(2,1)S(1)}, bf16[512,512]{1,0:T(8,128)(2,1)S(1)}, u32[]{:S(2)}, u32[]{:S(2)}) collective-permute-start(bf16[512,512]{1,0:T(8,128)(2,1)S(1)} %get-tuple-element.24), channel_id=1, source_target_pairs={{0,1},{1,0},{2,3},{3,2},{4,5},{5,4},{6,7},{7,6},{8,9},{9,8},{10,11... | collective-permute-start | bytes 1572872 | tf_op jit(solution)/shard_map/ppermute | solution.py:235

commit v5 on v4

--- a/solution.py
+++ b/solution.py
@@ -13,7 +13,7 @@
 K_REM = 4
 CAP = 2
 TOLD = 16
-CODES = 64
+X, Y = ("x1", "x0"), ("y2", "y1", "y0")
 F32 = jnp.float32
 BF16 = jnp.bfloat16
 VMEM_LIMIT = 16 * 1024 * 1024
@@ -38,17 +38,9 @@
     )(*scalar_inputs, *anywhere, *array_inputs)
 
 
-def quarters_kernel(features_ref, codes_ref, features_t, parts_ref):
-    turned = features_ref[...].astype(F32).T.astype(BF16).reshape(NX, T, T)
-    features_t[...] = turned
-    for x in range(NX):
-        parts_ref[x, 0:T, :] = turned[x]
-        parts_ref[x, T : T + CODES, :] = codes_ref[...]
-
-
-def copies_kernel(parts_ref, codes_ref, copies_ref, sems):
-    copies = [pltpu.make_async_copy(parts_ref.at[:, 0:T, :], copies_ref.at[z], sems.at[z]) for z in range(NZ)]
-    copies.append(pltpu.make_async_copy(parts_ref.at[:, T : T + CODES, :], codes_ref, sems.at[NZ]))
+def spread_kernel(features_ref, features_t, quarters_ref, sems):
+    features_t[...] = features_ref[...].astype(F32).T.astype(BF16).reshape(NX, T, T)
+    copies = [pltpu.make_async_copy(features_t, quarters_ref.at[z], sems.at[z]) for z in range(NZ)]
     for copy in copies:
         copy.start()
     for copy in copies:
@@ -66,7 +58,7 @@
         second = jnp.clip(scalars[2 + at * CAP], 0, OWNERS - 1)
         start = scalars[1 + NX * GROUPS * CAP + at].astype(F32)
         count = scalars[1 + NX * GROUPS * (CAP + 1) + at].astype(F32)
-        told = told_ref[group, x].astype(F32)
+        told = told_ref[core, y, x].astype(F32)
         entry = told[0:K_REM] - start
         row = jnp.where(entry < count, entry * T + told[K_REM : 2 * K_REM], -1.0).astype(jnp.int16)
         weight = told[2 * K_REM : 3 * K_REM].astype(BF16)
@@ -176,8 +168,14 @@
 
 def body(features, edge_weights, neighbours, send_list, send_count, w_agg, w_self, cotangent):
     width = features.shape[1]
-    z, x, y, c = (lax.axis_index(a).astype(jnp.int32) for a in ("z", "x", "y", "c"))
+    z, x, y, c = (lax.axis_index(a).astype(jnp.int32) for a in ("z", X, Y, "c"))
     swap = [(0, 1), (1, 0)]
+
+    features_t, quarters = vmem_call(
+        spread_kernel, "spread", [], [features], [((NX, T, T), BF16), ((NZ, NX, T, T), BF16)],
+        scratch=[pltpu.SemaphoreType.DMA((NZ,))], outside=1, bytes_accessed=1_500_000,
+    )
+    blocks = lax.all_to_all(quarters.reshape(OWNERS, T, T), ("z",) + X, 0, 0, tiled=True)
 
     codes_t = neighbours.T
     weights_t = edge_weights.T
@@ -187,18 +185,15 @@
     gap = jnp.zeros((16 - K_LOC, T), BF16)
     codes = [block[K_LOC:], row[K_LOC:], weights_t[K_LOC:], told]
     codes += [block[:K_LOC], gap, row[:K_LOC], gap, weights_t[:K_LOC], gap]
-    features_t, parts = vmem_call(
-        quarters_kernel, "quarters", [], [features, jnp.concatenate(codes, axis=0)],
-        [((NX, T, T), BF16), ((NX, T + CODES, T), BF16)], bytes_accessed=600_000,
-    )
-    parts = lax.all_to_all(parts, "x", 0, 0, tiled=True)
-    codes, copies = vmem_call(
-        copies_kernel, "copies", [], [parts], [((NX, CODES, T), BF16), ((NZ, NX, T, T), BF16)],
-        scratch=[pltpu.SemaphoreType.DMA((NZ + 1,))], outside=2, bytes_accessed=1_500_000,
-    )
-    blocks = lax.all_to_all(copies, "z", 0, 0, tiled=True).reshape(OWNERS, T, T)
-    remote_codes = lax.all_gather(codes[:, :TOLD], ("y", "c"), axis=0)
-    told = remote_codes[:, :, 12].astype(jnp.int32)
+    codes = jnp.concatenate(codes, axis=0)
+    for axis in reversed(X):
+        codes = lax.all_gather(codes, axis, axis=0)
+    codes = codes.reshape(NX, 64, T)
+    remote_codes = codes[:, :TOLD]
+    for axis in reversed(Y):
+        remote_codes = lax.all_gather(remote_codes, axis, axis=0)
+    remote_codes = lax.all_gather(remote_codes, "c", axis=0).reshape(NC, NY, NX, TOLD, T)
+    told = remote_codes[:, :, :, 12].swapaxes(0, 1).reshape(GROUPS, NX, T).astype(jnp.int32)
     sources = jnp.arange(GROUPS, dtype=jnp.int32)[:, None, None]
     group = y * NC + c
     here = jnp.sum(jnp.where(sources == group, told, 0), axis=0)
@@ -216,14 +211,14 @@
     received = lax.ppermute(remote_sums(1 - c, blocks), "c", swap)
     keep = remote_sums(c, blocks)
     chip_sum = (keep.astype(F32) + received.astype(F32)).astype(BF16)
-    arrived = lax.all_to_all(chip_sum.reshape(NX * NY, T, T), ("x", "y"), 0, 0, tiled=True)
+    arrived = lax.all_to_all(chip_sum.reshape(NX * NY, T, T), X + Y, 0, 0, tiled=True)
 
     *near, near_0 = vmem_call(
         local_kernel, "local_sums", [jnp.stack([z, x])], [blocks, codes], [((T, T), F32)] * NX,
         scratch=[pltpu.VMEM((NX, 4 * T, T), BF16), pltpu.VMEM((NX, T, T), F32), pltpu.SemaphoreType.DMA], outside=1,
         flops=600_000_000, bytes_accessed=1_500_000,
     )
-    moved = [lax.ppermute(near[k - 1], "x", [(i, (i + k) % NX) for i in range(NX)]) for k in range(1, NX)]
+    moved = [lax.ppermute(near[k - 1], X, [(i, (i + k) % NX) for i in range(NX)]) for k in range(1, NX)]
 
     hidden, send, keep = vmem_call(
         dense_kernel, "dense", [jnp.stack([c, x])],
@@ -235,15 +230,16 @@
     received = lax.ppermute(send, "c", swap)
     share = width // OWNERS
     chip_grad = (keep + received.astype(F32)).astype(BF16).reshape(OWNERS, share, width)
-    plane = added(lax.all_to_all(chip_grad, ("z", "x"), 0, 0, tiled=True), F32)
-    both = lax.all_gather(plane, ("y", "c"), axis=0).reshape(NY, NC, share, width)
-    grads = jnp.sum(both, axis=0)
+    plane = added(lax.all_to_all(chip_grad, ("z",) + X, 0, 0, tiled=True), BF16)
+    planes = lax.all_to_all(jnp.broadcast_to(plane, (NY, share, width)), Y, 0, 0, tiled=True)
+    grads = lax.all_gather(added(planes, F32), "c", axis=0)
     return hidden, grads[0], grads[1]
 
 
 def solution(mesh):
-    fine = Mesh(mesh.devices.reshape(NZ, NX, NY, NC), ("z", "x", "y", "c"))
-    row, rep = ("z", "x"), ("y", "c")
+    axes = ("z",) + X + Y + ("c",)
+    fine = Mesh(mesh.devices.reshape(NZ, 2, 2, 2, 2, 2, NC), axes)
+    row, rep = ("z",) + X, Y + ("c",)
     nodes = P(row + rep, None)
     in_specs = (nodes, nodes, nodes, P(row, rep, None, None), P(row, rep, None), P(), P(), nodes)
     out_specs = (nodes, P(row, None), P(row, None))

time: 148 us -> 147 us (level)
  waiting for transfers between devices: 13.4 us -> 7.75 us
  starting transfers between devices: 38.9 us -> 43.3 us
  blocking collectives: 69.1 us -> 73.4 us
  other arithmetic: 4.17 us -> 2.06 us
  local copies, waits for them, and re-layouts: 6.02 us -> 4.02 us
    all_to_all x2, starting transfers between devices: 18.1 us -> 24.3 us  [the longest x1 13.9 us: body(): lax.all_to_all(quarters.reshape(OWNERS, T, T), ('z',) + X, 0, 0, tiled=True)]
    all_to_all x2, waiting for transfers between devices: 7.71 us -> 2.01 us  [the longest x1 2 us: body(): lax.all_to_all(chip_sum.reshape(NX * NY, T, T), X + Y, 0, 0, tiled=True)]
    all_to_all x2, blocking collectives: 29.5 us -> 34.6 us  [the longest x1 22.6 us: body(): plane = added(lax.all_to_all(chip_grad, ('z',) + X, 0, 0, tiled=True), BF16)]
    ppermute x1, starting transfers between devices: 4.01 us -> 2.27 us  [body(): received = lax.ppermute(remote_sums(1 - c, blocks), 'c', swap)]
    all_gather x2 -> x7, blocking collectives: 39.6 us -> 38.8 us  [the longest x3 16.8 us: body(): remote_codes = lax.all_gather(remote_codes, axis, axis=0)]
  transfers between devices with their start and end apart: 7 -> 7, of which waited for: 6 -> 5; matrix products, arithmetic and copies ran while one was open for 1% -> 1% of each run, Pallas kernels for 7% -> 7%
where the time goes in v5:
time: 147 us; the launch traced here: 146 us
  blocking collectives  73.4 us (50%)
  starting transfers between devices  43.3 us (29%)
  Pallas kernels  15 us (10%)
  waiting for transfers between devices  7.75 us (5%)
  local copies, waits for them, and re-layouts  4.02 us (3%)
  other arithmetic  2.06 us (1%)
    all_to_all x1, blocking collectives, body(): plane = added(lax.all_to_all(chip_grad, ('z',) + X, 0, 0, tiled=True), BF16)  22.6 us
    all_gather x3, blocking collectives, body(): remote_codes = lax.all_gather(remote_codes, axis, axis=0)  16.8 us
    pallas_call x7, Pallas kernels, vmem_call(): pl.pallas_call(kernel, in_specs=[pl.BlockSpec(memory_space=pltpu.SMEM)] *...  15 us
    all_to_all x1, starting transfers between devices, body(): lax.all_to_all(quarters.reshape(OWNERS, T, T), ('z',) + X, 0, 0, tiled=True)  13.9 us
    all_to_all x1, blocking collectives, body(): lax.all_to_all(jnp.broadcast_to(plane, (NY, share, width)), Y, 0, 0, tile...  12 us
    ppermute x3, starting transfers between devices, body(): lax.ppermute(near[k - 1], X, [(i, (i + k) % NX) for i in range(NX)])  10.6 us
    all_to_all x1, starting transfers between devices, body(): lax.all_to_all(chip_sum.reshape(NX * NY, T, T), X + Y, 0, 0, tiled=True)  10.4 us
    all_gather x2, blocking collectives, body(): codes = lax.all_gather(codes, axis, axis=0)  8.79 us
  transfers between devices with their start and end apart: 7, of which 5 were waited for; matrix products, arithmetic and copies ran while one was open for 1% of the time, Pallas kernels for 7%

profile of v5, /device:TPU:1, one launch (start us, length us, event | category | flops | bytes accessed | tf_op | source)
XLA Modules:
  0.0 146.5 jit_solution(729550174479132398)
XLA Ops:
  0.6 0.9 copy-done
  1.5 1.2 spread.1
  2.7 0.0 copy-start.8
  2.7 0.0 copy-start.9
  2.8 13.9 %all-to-all-start = ((bf16[32,128,128]{2,1,0:T(8,128)(2,1)}), bf16[32,128,128]{2,1,0:T(8,128)(2,1)S(1)}, u32[]{:S(2)}, u32[]{:S(2)}) async-start(bf16[32,128,128]{2,1,0:T(8,128)(2,1)} %bitcast.60), calls=%async_computation | async-start | bytes 2097152 | tf_op jit(solution)/shard_map/all_to_all | solution.py:178
  16.7 0.1 copy.15
  16.8 0.1 concatenate.29
  17.0 0.1 fusion.9
  17.0 0.2 concatenate.31
  17.2 3.4 %all-gather = bf16[128,128]{1,0:T(8,128)(2,1)S(1)} all-gather(bf16[64,128]{1,0:T(8,128)(2,1)S(1)} %concatenate.31), channel_id=2, replica_groups=mesh['z'=8,'x1'=2,'x0'=2,'y2'=2,'y1'=2,'y0'=2,'c'=2] {'x0'}, dimensions={0}, use_global_device_ids=true | all-gather | bytes 49152 | tf_op jit(solution)/shard_map/all_gather | solution.py:190
  20.6 5.4 %all-gather.1.told_ref = bf16[4,64,128]{2,1,0:T(8,128)(2,1)S(1)} all-gather(bf16[2,64,128]{2,1,0:T(8,128)(2,1)S(1)} %bitcast.63), channel_id=3, replica_groups=mesh['z'=8,'x1'=2,'x0'=2,'y2'=2,'y1'=2,'y0'=2,'c'=2] {'x1'}, dimensions={0}, use_global_device_ids=true | all-gather | bytes 98304 | tf_op jit(solution)/shard_map/all_gather | solution.py:190
  26.0 3.5 %all-gather.2 = bf16[8,16,128]{2,1,0:T(8,128)(2,1)S(1)} all-gather(bf16[4,16,128]{2,1,0:T(8,128)(2,1)S(1)} %slice.64), channel_id=4, replica_groups=mesh['z'=8,'x1'=2,'x0'=2,'y2'=2,'y1'=2,'y0'=2,'c'=2] {'y0'}, dimensions={0}, use_global_device_ids=true | all-gather | bytes 49152 | tf_op jit(solution)/shard_map/all_gather | solution.py:194
  29.6 4.6 %all-gather.3 = bf16[4,4,16,128]{3,2,1,0:T(8,128)(2,1)S(1)} all-gather(bf16[2,4,16,128]{3,2,1,0:T(8,128)(2,1)S(1)} %bitcast.64), channel_id=5, replica_groups=mesh['z'=8,'x1'=2,'x0'=2,'y2'=2,'y1'=2,'y0'=2,'c'=2] {'y1'}, dimensions={0}, use_global_device_ids=true | all-gather | bytes 98304 | tf_op jit(solution)/shard_map/all_gather | solution.py:194
  34.2 8.6 %all-gather.4 = bf16[4,2,4,16,128]{4,3,2,1,0:T(8,128)(2,1)S(1)} all-gather(bf16[2,2,4,16,128]{4,3,2,1,0:T(8,128)(2,1)S(1)} %bitcast.62), channel_id=6, replica_groups=mesh['z'=8,'x1'=2,'x0'=2,'y2'=2,'y1'=2,'y0'=2,'c'=2] {'y2'}, dimensions={0}, use_global_device_ids=true | all-gather | bytes 196608 | tf_op jit(solution)/shard_map/all_gather | solution.py:194
  42.8 8.2 %all-gather.5 = bf16[4,2,2,4,16,128]{5,4,3,2,1,0:T(8,128)(2,1)S(1)} all-gather(bf16[2,2,2,4,16,128]{5,4,3,2,1,0:T(8,128)(2,1)S(1)} %bitcast.61), channel_id=7, replica_groups=mesh['z'=8,'x1'=2,'x0'=2,'y2'=2,'y1'=2,'y0'=2,'c'=2] {'c'}, dimensions={0}, use_global_device_ids=true | all-gather | bytes 393216 | tf_op jit(solution)/shard_map/all_gather | solution.py:195
  51.1 0.1 select_reduce_fusion.1
  51.2 0.1 select_reduce_fusion
  51.3 0.1 reshape.94
  51.4 0.1 slice.50
  51.5 0.1 reshape.95
  51.5 0.1 reshape.93
  51.6 0.1 pad_add_fusion.1
  51.7 1.7 %remote_sums.3 = bf16[4,8,128,128]{3,2,1,0:T(8,128)(2,1)S(1)} custom-call(s32[257]{0:T(512)S(1)} %get-tuple-element.28.scalars, bf16[32,128,128]{2,1,0:T(8,128)(2,1)S(1)} %all-to-all-done.blocks_ref, bf16[2,8,4,16,128]{4,3,2,1,0:T(8,128)(2,1)S(1)} %bitcast.57), custom_call_target="tpu_custom_call" | custom-call | flops 300000000 | bytes 2500000 | tf_op jit(solution)/shard_map/remote_sums/pallas_call | solution.py:26
  53.4 2.3 %collective-permute-start = (bf16[4,8,128,128]{3,2,1,0:T(8,128)(2,1)S(1)}, bf16[4,8,128,128]{3,2,1,0:T(8,128)(2,1)S(1)}, u32[]{:S(2)}, u32[]{:S(2)}) collective-permute-start(bf16[4,8,128,128]{3,2,1,0:T(8,128)(2,1)S(1)} %remote_sums.3), channel_id=1, source_target_pairs={{0,1},{1,0},{2,3},{3,2},{4,5},{5,4},{6,7},{7,6},{8,9},{9,8},{10,11... | collective-permute-start | bytes 3145736 | tf_op jit(solution)/shard_map/ppermute | solution.py:211
  55.6 1.7 %remote_sums.2 = bf16[4,8,128,128]{3,2,1,0:T(8,128)(2,1)S(1)} custom-call(s32[257]{0:T(512)S(1)} %get-tuple-element.27.scalars, bf16[32,128,128]{2,1,0:T(8,128)(2,1)S(1)} %all-to-all-done.blocks_ref, bf16[2,8,4,16,128]{4,3,2,1,0:T(8,128)(2,1)S(1)} %bitcast.58), custom_call_target="tpu_custom_call" | custom-call | flops 300000000 | bytes 2500000 | tf_op jit(solution)/shard_map/remote_sums/pallas_call | solution.py:26
  57.3 0.6 collective-permute-done
  57.9 1.4 add_convert_fusion
  59.3 10.4 %all-to-all-start.1 = ((bf16[32,128,128]{2,1,0:T(8,128)(2,1)}), bf16[32,128,128]{2,1,0:T(8,128)(2,1)S(1)}, u32[]{:S(2)}, u32[]{:S(2)}) async-start(bf16[32,128,128]{2,1,0:T(8,128)(2,1)} %bitcast.17), calls=%async_computation.1 | async-start | bytes 2097152 | tf_op jit(solution)/shard_map/all_to_all | solution.py:214
  69.7 0.1 pad_add_fusion.7.scalars
  69.8 0.8 copy-done.6
  70.7 8.0 %local_sums.1 = (f32[128,128]{1,0:T(8,128)S(1)}, f32[128,128]{1,0:T(8,128)S(1)}, f32[128,128]{1,0:T(8,128)S(1)}, f32[128,128]{1,0:T(8,128)}) custom-call(s32[2]{0:T(128)S(1)} %pad_add_fusion.7.scalars, bf16[32,128,128]{2,1,0:T(8,128)(2,1)S(1)} %all-to-all-done.blocks_ref, bf16[4,64,128]{2,1,0:T(8,128)(2,1)S(1)} %copy-done.6), custom_call_target="tpu_custom_call" | custom-call | flops 600000000 | bytes 1500000 | tf_op jit(solution)/shard_map/local_sums/pallas_call | solution.py:26
  78.6 3.1 %collective-permute-start.1 = (f32[128,128]{1,0:T(8,128)S(1)}, f32[128,128]{1,0:T(8,128)S(1)}, u32[]{:S(2)}, u32[]{:S(2)}) collective-permute-start(f32[128,128]{1,0:T(8,128)S(1)} %get-tuple-element.14), channel_id=1, source_target_pairs={{0,16},{16,32},{32,48},{48,0},{1,17},{17,33},{33,49},{49,1},{2,18}... | collective-permute-start | bytes 196616 | tf_op jit(solution)/shard_map/ppermute | solution.py:221
  81.8 4.4 %collective-permute-start.2 = (f32[128,128]{1,0:T(8,128)S(1)}, f32[128,128]{1,0:T(8,128)S(1)}, u32[]{:S(2)}, u32[]{:S(2)}) collective-permute-start(f32[128,128]{1,0:T(8,128)S(1)} %get-tuple-element.15), channel_id=1, source_target_pairs={{0,32},{16,48},{32,0},{48,16},{1,33},{17,49},{33,1},{49,17},{2,34}... | collective-permute-start | bytes 196616 | tf_op jit(solution)/shard_map/ppermute | solution.py:221
  86.1 3.1 %collective-permute-start.3 = (f32[128,128]{1,0:T(8,128)S(1)}, f32[128,128]{1,0:T(8,128)S(1)}, u32[]{:S(2)}, u32[]{:S(2)}) collective-permute-start(f32[128,128]{1,0:T(8,128)S(1)} %get-tuple-element.16), channel_id=1, source_target_pairs={{0,48},{16,0},{32,16},{48,32},{1,49},{17,1},{33,17},{49,33},{2,50}... | collective-permute-start | bytes 196616 | tf_op jit(solution)/shard_map/ppermute | solution.py:221
  89.2 0.1 pad_add_fusion.6.scalars
  89.3 1.7 %collective-permute-done.2.near_2 = f32[128,128]{1,0:T(8,128)S(1)} collective-permute-done((f32[128,128]{1,0:T(8,128)S(1)}, f32[128,128]{1,0:T(8,128)S(1)}, u32[]{:S(2)}, u32[]{:S(2)}) %collective-permute-start.2) | collective-permute-done | bytes 65568 | tf_op jit(solution)/shard_map/ppermute | solution.py:221
  91.0 1.9 %collective-permute-done.3.near_3 = f32[128,128]{1,0:T(8,128)S(1)} collective-permute-done((f32[128,128]{1,0:T(8,128)S(1)}, f32[128,128]{1,0:T(8,128)S(1)}, u32[]{:S(2)}, u32[]{:S(2)}) %collective-permute-start.3) | collective-permute-done | bytes 65568 | tf_op jit(solution)/shard_map/ppermute | solution.py:221
  92.9 2.0 %all-to-all-done.1 = bf16[32,128,128]{2,1,0:T(8,128)(2,1)S(1)} async-done(((bf16[32,128,128]{2,1,0:T(8,128)(2,1)}), bf16[32,128,128]{2,1,0:T(8,128)(2,1)S(1)}, u32[]{:S(2)}, u32[]{:S(2)}) %all-to-all-start.1) | async-done | bytes 1048608 | tf_op jit(solution)/shard_map/all_to_all | solution.py:214
  94.9 0.8 copy-done.7
  95.8 2.4 %dense.1 = (bf16[128,512]{1,0:T(8,128)(2,1)}, bf16[512,512]{1,0:T(8,128)(2,1)S(1)}, f32[512,512]{1,0:T(8,128)S(1)}) custom-call(s32[2]{0:T(128)S(1)} %pad_add_fusion.6.scalars, f32[128,128]{1,0:T(8,128)S(1)} %copy-done.7, bf16[512,512]{1,0:T(8,128)(2,1)S(1)} %copy-done.2, bf16[4,8,128,128]{3,2,1,0:T(8,128)(2,1)S(1)} %bitcast.55, ...), custom_call_target="tpu_custom_call" | custom-call | flops 300000000 | bytes 5000000 | tf_op jit(solution)/shard_map/dense/pallas_call | solution.py:26
  98.2 6.2 %collective-permute-start.4 = (bf16[512,512]{1,0:T(8,128)(2,1)S(1)}, bf16[512,512]{1,0:T(8,128)(2,1)S(1)}, u32[]{:S(2)}, u32[]{:S(2)}) collective-permute-start(bf16[512,512]{1,0:T(8,128)(2,1)S(1)} %get-tuple-element.20), channel_id=1, source_target_pairs={{0,1},{1,0},{2,3},{3,2},{4,5},{5,4},{6,7},{7,6},{8,9},{9,8},{10,11... | collective-permute-start | bytes 1572872 | tf_op jit(solution)/shard_map/ppermute | solution.py:230
  104.4 1.5 %collective-permute-done.4 = bf16[512,512]{1,0:T(8,128)(2,1)S(1)} collective-permute-done((bf16[512,512]{1,0:T(8,128)(2,1)S(1)}, bf16[512,512]{1,0:T(8,128)(2,1)S(1)}, u32[]{:S(2)}, u32[]{:S(2)}) %collective-permute-start.4) | collective-permute-done | bytes 524320 | tf_op jit(solution)/shard_map/ppermute | solution.py:230
  106.0 0.2 add_convert_fusion.1
  106.1 22.6 %all_to_all.20.parts_ref = bf16[32,16,512]{2,1,0:T(8,128)(2,1)S(1)} all-to-all(bf16[32,16,512]{2,1,0:T(8,128)(2,1)S(1)} %bitcast.59), channel_id=1, replica_groups=mesh['z'=8,'x1'=2,'x0'=2,'y2'=2,'y1'=2,'y0'=2,'c'=2] {'z','x1','x0'}, dimensions={0} | all-to-all | bytes 1048576 | tf_op jit(solution)/shard_map/all_to_all | solution.py:233
  128.7 0.1 added.2
  128.8 12.0 %all_to_all.21.parts_ref = bf16[8,16,512]{2,1,0:T(8,128)(2,1)S(1)} all-to-all(bf16[8,16,512]{2,1,0:T(8,128)(2,1)S(1)} %broadcast_in_dim.41), channel_id=1, replica_groups=mesh['z'=8,'x1'=2,'x0'=2,'y2'=2,'y1'=2,'y0'=2,'c'=2] {'y2','y1','y0'}, dimensions={0} | all-to-all | bytes 262144 | tf_op jit(solution)/shard_map/all_to_all | solution.py:234
  140.8 5.0 %all-gather.6 = f32[32,512]{1,0:T(8,128)S(1)} all-gather(f32[16,512]{1,0:T(8,128)S(1)} %added.3), channel_id=8, replica_groups=mesh['z'=8,'x1'=2,'x0'=2,'y2'=2,'y1'=2,'y0'=2,'c'=2] {'c'}, dimensions={0}, use_global_device_ids=true | all-gather | bytes 98304 | tf_op jit(solution)/shard_map/all_gather | solution.py:235
  145.8 0.6 fusion.11
  (36 shorter events, 0.2 us)
Async XLA Ops:
  0.6 0.9 copy-start
  2.7 13.9 %copy-start.10 = (s32[1,1,16,2]{2,3,1,0:T(2,128)S(1)}, s32[1,1,16,2]{2,3,1,0:T(2,128)}, u32[]{:S(2)}) copy-start(s32[1,1,16,2]{2,3,1,0:T(2,128)} %param.11) | copy-start | bytes 388
  2.7 13.9 %copy-start.8 = (bf16[128,16]{0,1:T(8,128)(2,1)S(1)}, bf16[128,16]{0,1:T(8,128)(2,1)}, u32[]{:S(2)}) copy-start(bf16[128,16]{0,1:T(8,128)(2,1)} %param.9) | copy-start | bytes 12292
  2.7 14.1 %copy-start.9 = (s32[128,16]{0,1:T(8,128)S(1)}, s32[128,16]{0,1:T(8,128)}, u32[]{:S(2)}) copy-start(s32[128,16]{0,1:T(8,128)} %param.10) | copy-start | bytes 24580
  2.8 14.2 %copy-start.11 = (s32[1,1,16]{2,1,0:T(1,128)S(1)}, s32[1,1,16]{2,1,0:T(1,128)}, u32[]{:S(2)}) copy-start(s32[1,1,16]{2,1,0:T(1,128)} %param.12) | copy-start | bytes 196
  2.8 48.9 %all-to-all-start = ((bf16[32,128,128]{2,1,0:T(8,128)(2,1)}), bf16[32,128,128]{2,1,0:T(8,128)(2,1)S(1)}, u32[]{:S(2)}, u32[]{:S(2)}) async-start(bf16[32,128,128]{2,1,0:T(8,128)(2,1)} %bitcast.60), calls=%async_computation | async-start | bytes 2097152 | tf_op jit(solution)/shard_map/all_to_all | solution.py:178
  26.0 16.8 %copy-start.5 = (bf16[4,64,128]{2,1,0:T(8,128)(2,1)}, bf16[4,64,128]{2,1,0:T(8,128)(2,1)S(1)}, u32[]{:S(2)}) copy-start(bf16[4,64,128]{2,1,0:T(8,128)(2,1)S(1)} %all-gather.1.told_ref) | copy-start | bytes 196612
  53.4 4.6 %collective-permute-start = (bf16[4,8,128,128]{3,2,1,0:T(8,128)(2,1)S(1)}, bf16[4,8,128,128]{3,2,1,0:T(8,128)(2,1)S(1)}, u32[]{:S(2)}, u32[]{:S(2)}) collective-permute-start(bf16[4,8,128,128]{3,2,1,0:T(8,128)(2,1)S(1)} %remote_sums.3), channel_id=1, source_target_pairs={{0,1},{1,0},{2,3},{3,2},{4,5},{5,4},{6,7},{7,6},{8,9},{9,8},{10,11... | collective-permute-start | bytes 3145736 | tf_op jit(solution)/shard_map/ppermute | solution.py:211
  59.3 35.6 %all-to-all-start.1 = ((bf16[32,128,128]{2,1,0:T(8,128)(2,1)}), bf16[32,128,128]{2,1,0:T(8,128)(2,1)S(1)}, u32[]{:S(2)}, u32[]{:S(2)}) async-start(bf16[32,128,128]{2,1,0:T(8,128)(2,1)} %bitcast.17), calls=%async_computation.1 | async-start | bytes 2097152 | tf_op jit(solution)/shard_map/all_to_all | solution.py:214
  69.8 0.8 copy-start.6
  70.6 24.3 %copy-start.1 = (bf16[128,512]{1,0:T(8,128)(2,1)S(1)}, bf16[128,512]{1,0:T(8,128)(2,1)}, u32[]{:S(2)}) copy-start(bf16[128,512]{1,0:T(8,128)(2,1)} %features.1) | copy-start | bytes 393220
  70.6 24.3 %copy-start.2 = (bf16[512,512]{1,0:T(8,128)(2,1)S(1)}, bf16[512,512]{1,0:T(8,128)(2,1)}, u32[]{:S(2)}) copy-start(bf16[512,512]{1,0:T(8,128)(2,1)} %w_self_in.1) | copy-start | bytes 1572868
  70.6 24.3 %copy-start.3 = (bf16[512,512]{1,0:T(8,128)(2,1)S(1)}, bf16[512,512]{1,0:T(8,128)(2,1)}, u32[]{:S(2)}) copy-start(bf16[512,512]{1,0:T(8,128)(2,1)} %w_agg.1) | copy-start | bytes 1572868
  70.6 24.3 %copy-start.4 = (bf16[128,512]{1,0:T(8,128)(2,1)S(1)}, bf16[128,512]{1,0:T(8,128)(2,1)}, u32[]{:S(2)}) copy-start(bf16[128,512]{1,0:T(8,128)(2,1)} %cotangent.1) | copy-start | bytes 393220
  78.6 10.7 %collective-permute-start.1 = (f32[128,128]{1,0:T(8,128)S(1)}, f32[128,128]{1,0:T(8,128)S(1)}, u32[]{:S(2)}, u32[]{:S(2)}) collective-permute-start(f32[128,128]{1,0:T(8,128)S(1)} %get-tuple-element.14), channel_id=1, source_target_pairs={{0,16},{16,32},{32,48},{48,0},{1,17},{17,33},{33,49},{49,1},{2,18}... | collective-permute-start | bytes 196616 | tf_op jit(solution)/shard_map/ppermute | solution.py:221
  81.8 9.2 %collective-permute-start.2 = (f32[128,128]{1,0:T(8,128)S(1)}, f32[128,128]{1,0:T(8,128)S(1)}, u32[]{:S(2)}, u32[]{:S(2)}) collective-permute-start(f32[128,128]{1,0:T(8,128)S(1)} %get-tuple-element.15), channel_id=1, source_target_pairs={{0,32},{16,48},{32,0},{48,16},{1,33},{17,49},{33,1},{49,17},{2,34}... | collective-permute-start | bytes 196616 | tf_op jit(solution)/shard_map/ppermute | solution.py:221
  86.1 6.8 %collective-permute-start.3 = (f32[128,128]{1,0:T(8,128)S(1)}, f32[128,128]{1,0:T(8,128)S(1)}, u32[]{:S(2)}, u32[]{:S(2)}) collective-permute-start(f32[128,128]{1,0:T(8,128)S(1)} %get-tuple-element.16), channel_id=1, source_target_pairs={{0,48},{16,0},{32,16},{48,32},{1,49},{17,1},{33,17},{49,33},{2,50}... | collective-permute-start | bytes 196616 | tf_op jit(solution)/shard_map/ppermute | solution.py:221
  94.9 0.8 copy-start.7
  98.2 7.8 %collective-permute-start.4 = (bf16[512,512]{1,0:T(8,128)(2,1)S(1)}, bf16[512,512]{1,0:T(8,128)(2,1)S(1)}, u32[]{:S(2)}, u32[]{:S(2)}) collective-permute-start(bf16[512,512]{1,0:T(8,128)(2,1)S(1)} %get-tuple-element.20), channel_id=1, source_target_pairs={{0,1},{1,0},{2,3},{3,2},{4,5},{5,4},{6,7},{7,6},{8,9},{9,8},{10,11... | collective-permute-start | bytes 1572872 | tf_op jit(solution)/shard_map/ppermute | solution.py:230

commit v6 on v5

--- a/solution.py
+++ b/solution.py
@@ -58,7 +58,7 @@
         second = jnp.clip(scalars[2 + at * CAP], 0, OWNERS - 1)
         start = scalars[1 + NX * GROUPS * CAP + at].astype(F32)
         count = scalars[1 + NX * GROUPS * (CAP + 1) + at].astype(F32)
-        told = told_ref[core, y, x].astype(F32)
+        told = told_ref[core, y % 2, y // 2 % 2, x % 2, x // 2, y // 4].astype(F32)
         entry = told[0:K_REM] - start
         row = jnp.where(entry < count, entry * T + told[K_REM : 2 * K_REM], -1.0).astype(jnp.int16)
         weight = told[2 * K_REM : 3 * K_REM].astype(BF16)
@@ -68,12 +68,9 @@
         pair = jnp.concatenate([blocks_ref[first], blocks_ref[second]], axis=1)
         return jnp.dot(pair, hot, preferred_element_type=F32).astype(BF16)
 
-    def of_y(y, carry):
+    for y in range(NY):
         for x in range(NX):
             sums_ref[x, y] = product(x, y)
-        return carry
-
-    lax.fori_loop(0, NY, of_y, 0, unroll=True)
 
 
 def local_kernel(scalars, blocks_ref, told_ref, out_1, out_2, out_3, out_0, hot_ref, total, sem):
@@ -88,7 +85,7 @@
             p = 4 * i + j
             for x in range(NX):
                 block, row, weight = (
-                    told_ref[x, TOLD + n * 16 : TOLD + n * 16 + 16, :].astype(F32) for n in range(3)
+                    told_ref[x % 2, x // 2, n * 16 : n * 16 + 16, :].astype(F32) for n in range(3)
                 )
                 code = ((block - p.astype(F32)) * T + row).astype(jnp.int16)
                 weight = weight.astype(BF16)
@@ -141,15 +138,19 @@
     of_agg = jnp.dot(agg_t[...], grad_pre, preferred_element_type=F32)
     of_self = jnp.dot(features_t[...].reshape(NX * T, T), grad_pre, preferred_element_type=F32)
 
+    def lay(ref, product):
+        for j in range(NX):
+            ref[:, j] = product[:, j * T : (j + 1) * T].reshape(OWNERS, ref.shape[2], T).astype(ref.dtype)
+
     @pl.when(own_c == 0)
     def _():
-        keep_ref[...] = of_agg
-        send_ref[...] = of_self.astype(BF16)
+        lay(keep_ref, of_agg)
+        lay(send_ref, of_self)
 
     @pl.when(own_c != 0)
     def _():
-        keep_ref[...] = of_self
-        send_ref[...] = of_agg.astype(BF16)
+        lay(keep_ref, of_self)
+        lay(send_ref, of_agg)
 
 
 def add_kernel(parts_ref, sum_ref):
@@ -183,17 +184,16 @@
     told = jnp.pad(told, ((0, 3), (0, T - GROUPS * (1 + CAP))))
     block, row = (codes_t // T).astype(BF16), (codes_t % T).astype(BF16)
     gap = jnp.zeros((16 - K_LOC, T), BF16)
-    codes = [block[K_LOC:], row[K_LOC:], weights_t[K_LOC:], told]
-    codes += [block[:K_LOC], gap, row[:K_LOC], gap, weights_t[:K_LOC], gap]
-    codes = jnp.concatenate(codes, axis=0)
-    for axis in reversed(X):
-        codes = lax.all_gather(codes, axis, axis=0)
-    codes = codes.reshape(NX, 64, T)
-    remote_codes = codes[:, :TOLD]
-    for axis in reversed(Y):
+    codes = jnp.concatenate([block[K_LOC:], row[K_LOC:], weights_t[K_LOC:], told], axis=0)
+    codes = lax.all_gather(codes, "y2", axis=0).reshape(2 * TOLD, T)
+    codes = jnp.concatenate([codes, block[:K_LOC], gap, row[:K_LOC], gap, weights_t[:K_LOC], gap], axis=0)
+    codes = lax.all_gather(lax.all_gather(codes, "x1", axis=0), "x0", axis=0)
+    remote_codes, local_codes = codes[:, :, : 2 * TOLD], codes[:, :, 2 * TOLD :]
+    for axis in ("y1", "y0", "c"):
         remote_codes = lax.all_gather(remote_codes, axis, axis=0)
-    remote_codes = lax.all_gather(remote_codes, "c", axis=0).reshape(NC, NY, NX, TOLD, T)
-    told = remote_codes[:, :, :, 12].swapaxes(0, 1).reshape(GROUPS, NX, T).astype(jnp.int32)
+    remote_codes = remote_codes.reshape(NC, 2, 2, 2, 2, 2, TOLD, T)
+    told = remote_codes[:, :, :, :, :, :, 12].transpose(5, 2, 1, 0, 4, 3, 6)
+    told = told.reshape(GROUPS, NX, T).astype(jnp.int32)
     sources = jnp.arange(GROUPS, dtype=jnp.int32)[:, None, None]
     group = y * NC + c
     here = jnp.sum(jnp.where(sources == group, told, 0), axis=0)
@@ -214,25 +214,27 @@
     arrived = lax.all_to_all(chip_sum.reshape(NX * NY, T, T), X + Y, 0, 0, tiled=True)
 
     *near, near_0 = vmem_call(
-        local_kernel, "local_sums", [jnp.stack([z, x])], [blocks, codes], [((T, T), F32)] * NX,
+        local_kernel, "local_sums", [jnp.stack([z, x])], [blocks, local_codes], [((T, T), F32)] * NX,
         scratch=[pltpu.VMEM((NX, 4 * T, T), BF16), pltpu.VMEM((NX, T, T), F32), pltpu.SemaphoreType.DMA], outside=1,
         flops=600_000_000, bytes_accessed=1_500_000,
     )
+    near_0 = pltpu.with_memory_space_constraint(near_0, pltpu.HBM)
     moved = [lax.ppermute(near[k - 1], X, [(i, (i + k) % NX) for i in range(NX)]) for k in range(1, NX)]
 
+    share = width // OWNERS
     hidden, send, keep = vmem_call(
         dense_kernel, "dense", [jnp.stack([c, x])],
         [arrived.reshape(NX, NY, T, T), *moved, weights_t.astype(F32), features, features_t, w_agg, cotangent],
-        [((T, width), BF16), ((width, width), BF16), ((width, width), F32)],
+        [((T, width), BF16), ((OWNERS, NX, share, T), BF16), ((OWNERS, NX, share, T), F32)],
         scratch=[pltpu.VMEM((width, T), BF16), pltpu.VMEM((T, T), F32), pltpu.VMEM((width, width), BF16), pltpu.SemaphoreType.DMA((2,))],
         anywhere=[near_0, w_self], flops=300_000_000, bytes_accessed=5_000_000, transcendentals=65536,
     )
     received = lax.ppermute(send, "c", swap)
-    share = width // OWNERS
-    chip_grad = (keep + received.astype(F32)).astype(BF16).reshape(OWNERS, share, width)
+    chip_grad = (keep + received.astype(F32)).astype(BF16).reshape(OWNERS, NX * share, T)
     plane = added(lax.all_to_all(chip_grad, ("z",) + X, 0, 0, tiled=True), BF16)
-    planes = lax.all_to_all(jnp.broadcast_to(plane, (NY, share, width)), Y, 0, 0, tiled=True)
+    planes = lax.all_to_all(jnp.broadcast_to(plane, (NY,) + plane.shape), Y, 0, 0, tiled=True)
     grads = lax.all_gather(added(planes, F32), "c", axis=0)
+    grads = grads.reshape(NC, NX, share, T).swapaxes(1, 2).reshape(NC, share, width)
     return hidden, grads[0], grads[1]
 
 

time: 147 us -> 147 us (level)
    all_to_all x1, blocking collectives: 22.6 us -> 24.1 us  [body(): plane = added(lax.all_to_all(chip_grad, ('z',) + X, 0, 0, tiled=True), BF16)]
where the time goes in v6:
time: 147 us; the launch traced here: 146 us
  blocking collectives  73.4 us (50%)
  starting transfers between devices  43.4 us (30%)
  Pallas kernels  15.6 us (11%)
  waiting for transfers between devices  7.23 us (5%)
  local copies, waits for them, and re-layouts  3.79 us (3%)
  other arithmetic  2.08 us (1%)
    all_to_all x1, blocking collectives, body(): plane = added(lax.all_to_all(chip_grad, ('z',) + X, 0, 0, tiled=True), BF16)  24.1 us
    all_gather x3, blocking collectives, body(): remote_codes = lax.all_gather(remote_codes, axis, axis=0)  15.9 us
    pallas_call x7, Pallas kernels, vmem_call(): pl.pallas_call(kernel, in_specs=[pl.BlockSpec(memory_space=pltpu.SMEM)] *...  15.6 us
    all_to_all x1, starting transfers between devices, body(): lax.all_to_all(quarters.reshape(OWNERS, T, T), ('z',) + X, 0, 0, tiled=True)  13.9 us
    all_to_all x1, blocking collectives, body(): lax.all_to_all(jnp.broadcast_to(plane, (NY,) + plane.shape), Y, 0, 0, til...  12 us
    all_to_all x1, starting transfers between devices, body(): lax.all_to_all(chip_sum.reshape(NX * NY, T, T), X + Y, 0, 0, tiled=True)  10.5 us
    ppermute x3, starting transfers between devices, body(): lax.ppermute(near[k - 1], X, [(i, (i + k) % NX) for i in range(NX)])  10.5 us
    all_gather x2, blocking collectives, body(): codes = lax.all_gather(lax.all_gather(codes, 'x1', axis=0), 'x0', axis=0)  9.16 us
  transfers between devices with their start and end apart: 7, of which 5 were waited for; matrix products, arithmetic and copies ran while one was open for 1% of the time, Pallas kernels for 7%

profile of v6, /device:TPU:1, one launch (start us, length us, event | category | flops | bytes accessed | tf_op | source)
XLA Modules:
  0.0 146.4 jit_solution(13871812813231562337)
XLA Ops:
  0.6 0.9 copy-done
  1.5 1.2 spread.1
  2.7 0.0 copy-start.6
  2.7 0.0 copy-start.7
  2.8 13.9 %all-to-all-start = ((bf16[32,128,128]{2,1,0:T(8,128)(2,1)}), bf16[32,128,128]{2,1,0:T(8,128)(2,1)S(1)}, u32[]{:S(2)}, u32[]{:S(2)}) async-start(bf16[32,128,128]{2,1,0:T(8,128)(2,1)} %bitcast.73), calls=%async_computation | async-start | bytes 2097152 | tf_op jit(solution)/shard_map/all_to_all | solution.py:179
  16.7 0.1 copy.22
  16.8 0.1 concatenate.32
  17.0 0.1 fusion.9
  17.1 7.2 %all-gather = bf16[32,128]{1,0:T(8,128)(2,1)S(1)} all-gather(bf16[16,128]{1,0:T(8,128)(2,1)S(1)} %pad_maximum_fusion), channel_id=2, replica_groups=mesh['z'=8,'x1'=2,'x0'=2,'y2'=2,'y1'=2,'y0'=2,'c'=2] {'y2'}, dimensions={0}, use_global_device_ids=true | all-gather | bytes 12288 | tf_op jit(solution)/shard_map/all_gather | solution.py:188
  24.3 0.1 concatenate.35
  24.4 5.1 %all-gather.1 = bf16[160,128]{1,0:T(8,128)(2,1)S(1)} all-gather(bf16[80,128]{1,0:T(8,128)(2,1)S(1)} %concatenate.35), channel_id=3, replica_groups=mesh['z'=8,'x1'=2,'x0'=2,'y2'=2,'y1'=2,'y0'=2,'c'=2] {'x1'}, dimensions={0}, use_global_device_ids=true | all-gather | bytes 61440 | tf_op jit(solution)/shard_map/all_gather | solution.py:190
  29.5 4.1 %all-gather.2 = bf16[4,80,128]{2,1,0:T(8,128)(2,1)S(1)} all-gather(bf16[2,80,128]{2,1,0:T(8,128)(2,1)S(1)} %bitcast.79), channel_id=4, replica_groups=mesh['z'=8,'x1'=2,'x0'=2,'y2'=2,'y1'=2,'y0'=2,'c'=2] {'x0'}, dimensions={0}, use_global_device_ids=true | all-gather | bytes 122880 | tf_op jit(solution)/shard_map/all_gather | solution.py:190
  33.6 4.6 %all-gather.3 = bf16[4,2,32,128]{3,2,1,0:T(8,128)(2,1)S(1)} all-gather(bf16[2,2,32,128]{3,2,1,0:T(8,128)(2,1)S(1)} %slice.69), channel_id=5, replica_groups=mesh['z'=8,'x1'=2,'x0'=2,'y2'=2,'y1'=2,'y0'=2,'c'=2] {'y1'}, dimensions={0}, use_global_device_ids=true | all-gather | bytes 98304 | tf_op jit(solution)/shard_map/all_gather | solution.py:193
  38.2 4.4 %all-gather.4 = bf16[4,2,2,32,128]{4,3,2,1,0:T(8,128)(2,1)S(1)} all-gather(bf16[2,2,2,32,128]{4,3,2,1,0:T(8,128)(2,1)S(1)} %bitcast.77), channel_id=6, replica_groups=mesh['z'=8,'x1'=2,'x0'=2,'y2'=2,'y1'=2,'y0'=2,'c'=2] {'y0'}, dimensions={0}, use_global_device_ids=true | all-gather | bytes 196608 | tf_op jit(solution)/shard_map/all_gather | solution.py:193
  42.6 6.8 %all-gather.5 = bf16[4,2,2,2,32,128]{5,4,3,2,1,0:T(8,128)(2,1)S(1)} all-gather(bf16[2,2,2,2,32,128]{5,4,3,2,1,0:T(8,128)(2,1)S(1)} %bitcast.74), channel_id=7, replica_groups=mesh['z'=8,'x1'=2,'x0'=2,'y2'=2,'y1'=2,'y0'=2,'c'=2] {'c'}, dimensions={0}, use_global_device_ids=true | all-gather | bytes 393216 | tf_op jit(solution)/shard_map/all_gather | solution.py:193
  49.6 0.1 select_reduce_fusion
  49.7 0.1 reshape.103
  49.8 0.1 select_reduce_fusion.1
  49.9 0.1 slice.56
  49.9 0.1 reshape.104
  50.0 0.1 reshape.102
  50.1 0.1 pad_add_fusion.1
  50.2 1.6 %remote_sums.3 = bf16[4,8,128,128]{3,2,1,0:T(8,128)(2,1)S(1)} custom-call(s32[257]{0:T(512)S(1)} %get-tuple-element.26.scalars, bf16[32,128,128]{2,1,0:T(8,128)(2,1)S(1)} %all-to-all-done.blocks_ref, bf16[2,2,2,2,2,2,16,128]{7,6,5,4,3,2,1,0:T(8,128)(2,1)S(1)} %bitcast.70), custom_call_target="tpu_custom_call" | custom-call | flops 300000000 | bytes 2500000 | tf_op jit(solution)/shard_map/remote_sums/pallas_call | solution.py:26
  51.8 2.3 %collective-permute-start = (bf16[4,8,128,128]{3,2,1,0:T(8,128)(2,1)S(1)}, bf16[4,8,128,128]{3,2,1,0:T(8,128)(2,1)S(1)}, u32[]{:S(2)}, u32[]{:S(2)}) collective-permute-start(bf16[4,8,128,128]{3,2,1,0:T(8,128)(2,1)S(1)} %remote_sums.3), channel_id=1, source_target_pairs={{0,1},{1,0},{2,3},{3,2},{4,5},{5,4},{6,7},{7,6},{8,9},{9,8},{10,11... | collective-permute-start | bytes 3145736 | tf_op jit(solution)/shard_map/ppermute | solution.py:211
  54.1 1.6 %remote_sums.2 = bf16[4,8,128,128]{3,2,1,0:T(8,128)(2,1)S(1)} custom-call(s32[257]{0:T(512)S(1)} %get-tuple-element.25.scalars, bf16[32,128,128]{2,1,0:T(8,128)(2,1)S(1)} %all-to-all-done.blocks_ref, bf16[2,2,2,2,2,2,16,128]{7,6,5,4,3,2,1,0:T(8,128)(2,1)S(1)} %bitcast.71), custom_call_target="tpu_custom_call" | custom-call | flops 300000000 | bytes 2500000 | tf_op jit(solution)/shard_map/remote_sums/pallas_call | solution.py:26
  55.7 0.6 collective-permute-done
  56.4 1.4 add_convert_fusion
  57.7 10.5 %all-to-all-start.1 = ((bf16[32,128,128]{2,1,0:T(8,128)(2,1)}), bf16[32,128,128]{2,1,0:T(8,128)(2,1)S(1)}, u32[]{:S(2)}, u32[]{:S(2)}) async-start(bf16[32,128,128]{2,1,0:T(8,128)(2,1)} %bitcast.16), calls=%async_computation.1 | async-start | bytes 2097152 | tf_op jit(solution)/shard_map/all_to_all | solution.py:214
  68.3 0.6 slice.68.told_ref
  68.9 0.1 pad_add_fusion.7.scalars
  69.0 0.8 copy-done.5
  69.8 8.0 %local_sums.1 = (f32[128,128]{1,0:T(8,128)S(1)}, f32[128,128]{1,0:T(8,128)S(1)}, f32[128,128]{1,0:T(8,128)S(1)}, f32[128,128]{1,0:T(8,128)}) custom-call(s32[2]{0:T(128)S(1)} %pad_add_fusion.7.scalars, bf16[32,128,128]{2,1,0:T(8,128)(2,1)S(1)} %all-to-all-done.blocks_ref, bf16[2,2,48,128]{3,2,1,0:T(8,128)(2,1)S(1)} %copy-done.5), custom_call_target="tpu_custom_call" | custom-call | flops 600000000 | bytes 1500000 | tf_op jit(solution)/shard_map/local_sums/pallas_call | solution.py:26
  77.8 3.1 %collective-permute-start.1 = (f32[128,128]{1,0:T(8,128)S(1)}, f32[128,128]{1,0:T(8,128)S(1)}, u32[]{:S(2)}, u32[]{:S(2)}) collective-permute-start(f32[128,128]{1,0:T(8,128)S(1)} %get-tuple-element.14), channel_id=1, source_target_pairs={{0,16},{16,32},{32,48},{48,0},{1,17},{17,33},{33,49},{49,1},{2,18}... | collective-permute-start | bytes 196616 | tf_op jit(solution)/shard_map/ppermute | solution.py:222
  80.9 4.3 %collective-permute-start.2 = (f32[128,128]{1,0:T(8,128)S(1)}, f32[128,128]{1,0:T(8,128)S(1)}, u32[]{:S(2)}, u32[]{:S(2)}) collective-permute-start(f32[128,128]{1,0:T(8,128)S(1)} %get-tuple-element.15), channel_id=1, source_target_pairs={{0,32},{16,48},{32,0},{48,16},{1,33},{17,49},{33,1},{49,17},{2,34}... | collective-permute-start | bytes 196616 | tf_op jit(solution)/shard_map/ppermute | solution.py:222
  85.3 3.1 %collective-permute-start.3 = (f32[128,128]{1,0:T(8,128)S(1)}, f32[128,128]{1,0:T(8,128)S(1)}, u32[]{:S(2)}, u32[]{:S(2)}) collective-permute-start(f32[128,128]{1,0:T(8,128)S(1)} %get-tuple-element.16), channel_id=1, source_target_pairs={{0,48},{16,0},{32,16},{48,32},{1,49},{17,1},{33,17},{49,33},{2,50}... | collective-permute-start | bytes 196616 | tf_op jit(solution)/shard_map/ppermute | solution.py:222
  88.3 0.1 pad_add_fusion.6.scalars
  88.4 1.6 %collective-permute-done.2.near_2 = f32[128,128]{1,0:T(8,128)S(1)} collective-permute-done((f32[128,128]{1,0:T(8,128)S(1)}, f32[128,128]{1,0:T(8,128)S(1)}, u32[]{:S(2)}, u32[]{:S(2)}) %collective-permute-start.2) | collective-permute-done | bytes 65568 | tf_op jit(solution)/shard_map/ppermute | solution.py:222
  90.0 1.5 %collective-permute-done.3.near_3 = f32[128,128]{1,0:T(8,128)S(1)} collective-permute-done((f32[128,128]{1,0:T(8,128)S(1)}, f32[128,128]{1,0:T(8,128)S(1)}, u32[]{:S(2)}, u32[]{:S(2)}) %collective-permute-start.3) | collective-permute-done | bytes 65568 | tf_op jit(solution)/shard_map/ppermute | solution.py:222
  91.5 2.0 %all-to-all-done.1 = bf16[32,128,128]{2,1,0:T(8,128)(2,1)S(1)} async-done(((bf16[32,128,128]{2,1,0:T(8,128)(2,1)}), bf16[32,128,128]{2,1,0:T(8,128)(2,1)S(1)}, u32[]{:S(2)}, u32[]{:S(2)}) %all-to-all-start.1) | async-done | bytes 1048608 | tf_op jit(solution)/shard_map/all_to_all | solution.py:214
  93.5 3.1 %dense.1 = (bf16[128,512]{1,0:T(8,128)(2,1)}, bf16[32,4,16,128]{3,2,1,0:T(8,128)(2,1)S(1)}, f32[32,4,16,128]{3,2,1,0:T(8,128)S(1)}) custom-call(s32[2]{0:T(128)S(1)} %pad_add_fusion.6.scalars, f32[128,128]{1,0:T(8,128)} %get-tuple-element.13.near_0, bf16[512,512]{1,0:T(8,128)(2,1)S(1)} %copy-done.2, bf16[4,8,128,128]{3,2,1,0:T(8,128)(2,1)S(1)} %bitcast.68, ...), custom_call_target="tpu_custom_call" | custom-call | flops 300000000 | bytes 5000000 | tf_op jit(solution)/shard_map/dense/pallas_call | solution.py:26
  96.6 6.2 %collective-permute-start.4 = (bf16[32,4,16,128]{3,2,1,0:T(8,128)(2,1)S(1)}, bf16[32,4,16,128]{3,2,1,0:T(8,128)(2,1)S(1)}, u32[]{:S(2)}, u32[]{:S(2)}) collective-permute-start(bf16[32,4,16,128]{3,2,1,0:T(8,128)(2,1)S(1)} %get-tuple-element.20), channel_id=1, source_target_pairs={{0,1},{1,0},{2,3},{3,2},{4,5},{5,4},{6,7},{7,6},{8,9},{9,8},{10,11... | collective-permute-start | bytes 1572872 | tf_op jit(solution)/shard_map/ppermute | solution.py:232
  102.8 1.5 %collective-permute-done.4 = bf16[32,4,16,128]{3,2,1,0:T(8,128)(2,1)S(1)} collective-permute-done((bf16[32,4,16,128]{3,2,1,0:T(8,128)(2,1)S(1)}, bf16[32,4,16,128]{3,2,1,0:T(8,128)(2,1)S(1)}, u32[]{:S(2)}, u32[]{:S(2)}) %collective-permute-start.4) | collective-permute-done | bytes 524320 | tf_op jit(solution)/shard_map/ppermute | solution.py:232
  104.3 0.2 add_convert_fusion.1
  104.4 24.1 %all_to_all.20.parts_ref = bf16[32,64,128]{2,1,0:T(8,128)(2,1)S(1)} all-to-all(bf16[32,64,128]{2,1,0:T(8,128)(2,1)S(1)} %bitcast.72), channel_id=1, replica_groups=mesh['z'=8,'x1'=2,'x0'=2,'y2'=2,'y1'=2,'y0'=2,'c'=2] {'z','x1','x0'}, dimensions={0} | all-to-all | bytes 1048576 | tf_op jit(solution)/shard_map/all_to_all | solution.py:234
  128.5 0.1 added.2
  128.6 12.0 %all_to_all.21.parts_ref = bf16[8,64,128]{2,1,0:T(8,128)(2,1)S(1)} all-to-all(bf16[8,64,128]{2,1,0:T(8,128)(2,1)S(1)} %broadcast_in_dim.41), channel_id=1, replica_groups=mesh['z'=8,'x1'=2,'x0'=2,'y2'=2,'y1'=2,'y0'=2,'c'=2] {'y2','y1','y0'}, dimensions={0} | all-to-all | bytes 262144 | tf_op jit(solution)/shard_map/all_to_all | solution.py:235
  140.7 5.0 %all-gather.6 = f32[128,128]{1,0:T(8,128)S(1)} all-gather(f32[64,128]{1,0:T(8,128)S(1)} %added.3), channel_id=8, replica_groups=mesh['z'=8,'x1'=2,'x0'=2,'y2'=2,'y1'=2,'y0'=2,'c'=2] {'c'}, dimensions={0}, use_global_device_ids=true | all-gather | bytes 98304 | tf_op jit(solution)/shard_map/all_gather | solution.py:236
  145.8 0.6 copy_bitcast_fusion
  (38 shorter events, 0.3 us)
Async XLA Ops:
  0.6 0.9 copy-start
  2.7 13.9 %copy-start.8 = (s32[1,1,16,2]{2,3,1,0:T(2,128)S(1)}, s32[1,1,16,2]{2,3,1,0:T(2,128)}, u32[]{:S(2)}) copy-start(s32[1,1,16,2]{2,3,1,0:T(2,128)} %param.11) | copy-start | bytes 388
  2.7 13.9 %copy-start.6 = (bf16[128,16]{0,1:T(8,128)(2,1)S(1)}, bf16[128,16]{0,1:T(8,128)(2,1)}, u32[]{:S(2)}) copy-start(bf16[128,16]{0,1:T(8,128)(2,1)} %param.9) | copy-start | bytes 12292
  2.7 14.1 %copy-start.7 = (s32[128,16]{0,1:T(8,128)S(1)}, s32[128,16]{0,1:T(8,128)}, u32[]{:S(2)}) copy-start(s32[128,16]{0,1:T(8,128)} %param.10) | copy-start | bytes 24580
  2.7 14.2 %copy-start.9 = (s32[1,1,16]{2,1,0:T(1,128)S(1)}, s32[1,1,16]{2,1,0:T(1,128)}, u32[]{:S(2)}) copy-start(s32[1,1,16]{2,1,0:T(1,128)} %param.12) | copy-start | bytes 196
  2.8 47.4 %all-to-all-start = ((bf16[32,128,128]{2,1,0:T(8,128)(2,1)}), bf16[32,128,128]{2,1,0:T(8,128)(2,1)S(1)}, u32[]{:S(2)}, u32[]{:S(2)}) async-start(bf16[32,128,128]{2,1,0:T(8,128)(2,1)} %bitcast.73), calls=%async_computation | async-start | bytes 2097152 | tf_op jit(solution)/shard_map/all_to_all | solution.py:179
  51.8 4.6 %collective-permute-start = (bf16[4,8,128,128]{3,2,1,0:T(8,128)(2,1)S(1)}, bf16[4,8,128,128]{3,2,1,0:T(8,128)(2,1)S(1)}, u32[]{:S(2)}, u32[]{:S(2)}) collective-permute-start(bf16[4,8,128,128]{3,2,1,0:T(8,128)(2,1)S(1)} %remote_sums.3), channel_id=1, source_target_pairs={{0,1},{1,0},{2,3},{3,2},{4,5},{5,4},{6,7},{7,6},{8,9},{9,8},{10,11... | collective-permute-start | bytes 3145736 | tf_op jit(solution)/shard_map/ppermute | solution.py:211
  57.7 35.8 %all-to-all-start.1 = ((bf16[32,128,128]{2,1,0:T(8,128)(2,1)}), bf16[32,128,128]{2,1,0:T(8,128)(2,1)S(1)}, u32[]{:S(2)}, u32[]{:S(2)}) async-start(bf16[32,128,128]{2,1,0:T(8,128)(2,1)} %bitcast.16), calls=%async_computation.1 | async-start | bytes 2097152 | tf_op jit(solution)/shard_map/all_to_all | solution.py:214
  69.0 0.8 copy-start.5
  69.8 23.7 %copy-start.1 = (bf16[128,512]{1,0:T(8,128)(2,1)S(1)}, bf16[128,512]{1,0:T(8,128)(2,1)}, u32[]{:S(2)}) copy-start(bf16[128,512]{1,0:T(8,128)(2,1)} %features.1) | copy-start | bytes 393220
  69.8 23.7 %copy-start.2 = (bf16[512,512]{1,0:T(8,128)(2,1)S(1)}, bf16[512,512]{1,0:T(8,128)(2,1)}, u32[]{:S(2)}) copy-start(bf16[512,512]{1,0:T(8,128)(2,1)} %w_self_in.1) | copy-start | bytes 1572868
  69.8 23.7 %copy-start.3 = (bf16[512,512]{1,0:T(8,128)(2,1)S(1)}, bf16[512,512]{1,0:T(8,128)(2,1)}, u32[]{:S(2)}) copy-start(bf16[512,512]{1,0:T(8,128)(2,1)} %w_agg.1) | copy-start | bytes 1572868
  69.8 23.7 %copy-start.4 = (bf16[128,512]{1,0:T(8,128)(2,1)S(1)}, bf16[128,512]{1,0:T(8,128)(2,1)}, u32[]{:S(2)}) copy-start(bf16[128,512]{1,0:T(8,128)(2,1)} %cotangent.1) | copy-start | bytes 393220
  77.8 10.6 %collective-permute-start.1 = (f32[128,128]{1,0:T(8,128)S(1)}, f32[128,128]{1,0:T(8,128)S(1)}, u32[]{:S(2)}, u32[]{:S(2)}) collective-permute-start(f32[128,128]{1,0:T(8,128)S(1)} %get-tuple-element.14), channel_id=1, source_target_pairs={{0,16},{16,32},{32,48},{48,0},{1,17},{17,33},{33,49},{49,1},{2,18}... | collective-permute-start | bytes 196616 | tf_op jit(solution)/shard_map/ppermute | solution.py:222
  80.9 9.1 %collective-permute-start.2 = (f32[128,128]{1,0:T(8,128)S(1)}, f32[128,128]{1,0:T(8,128)S(1)}, u32[]{:S(2)}, u32[]{:S(2)}) collective-permute-start(f32[128,128]{1,0:T(8,128)S(1)} %get-tuple-element.15), channel_id=1, source_target_pairs={{0,32},{16,48},{32,0},{48,16},{1,33},{17,49},{33,1},{49,17},{2,34}... | collective-permute-start | bytes 196616 | tf_op jit(solution)/shard_map/ppermute | solution.py:222
  85.3 6.2 %collective-permute-start.3 = (f32[128,128]{1,0:T(8,128)S(1)}, f32[128,128]{1,0:T(8,128)S(1)}, u32[]{:S(2)}, u32[]{:S(2)}) collective-permute-start(f32[128,128]{1,0:T(8,128)S(1)} %get-tuple-element.16), channel_id=1, source_target_pairs={{0,48},{16,0},{32,16},{48,32},{1,49},{17,1},{33,17},{49,33},{2,50}... | collective-permute-start | bytes 196616 | tf_op jit(solution)/shard_map/ppermute | solution.py:222
  96.6 7.7 %collective-permute-start.4 = (bf16[32,4,16,128]{3,2,1,0:T(8,128)(2,1)S(1)}, bf16[32,4,16,128]{3,2,1,0:T(8,128)(2,1)S(1)}, u32[]{:S(2)}, u32[]{:S(2)}) collective-permute-start(bf16[32,4,16,128]{3,2,1,0:T(8,128)(2,1)S(1)} %get-tuple-element.20), channel_id=1, source_target_pairs={{0,1},{1,0},{2,3},{3,2},{4,5},{5,4},{6,7},{7,6},{8,9},{9,8},{10,11... | collective-permute-start | bytes 1572872 | tf_op jit(solution)/shard_map/ppermute | solution.py:232

commit v7 on v6

--- a/solution.py
+++ b/solution.py
@@ -48,29 +48,29 @@
 
 
 def remote_kernel(scalars, blocks_ref, told_ref, sums_ref):
-    core = scalars[0]
+    core, own_x = scalars[0], scalars[1]
     rows = lax.broadcasted_iota(jnp.int16, (CAP * T, T), 0)
 
-    def product(x, y):
+    def product(k, y):
         group = y * NC + core
-        at = x * GROUPS + group
-        first = jnp.clip(scalars[1 + at * CAP], 0, OWNERS - 1)
-        second = jnp.clip(scalars[2 + at * CAP], 0, OWNERS - 1)
-        start = scalars[1 + NX * GROUPS * CAP + at].astype(F32)
-        count = scalars[1 + NX * GROUPS * (CAP + 1) + at].astype(F32)
-        told = told_ref[core, y % 2, y // 2 % 2, x % 2, x // 2, y // 4].astype(F32)
+        at = k * GROUPS + group
+        first = jnp.clip(scalars[2 + at * CAP], 0, OWNERS - 1)
+        second = jnp.clip(scalars[3 + at * CAP], 0, OWNERS - 1)
+        start = scalars[2 + NX * GROUPS * CAP + at].astype(F32)
+        count = scalars[2 + NX * GROUPS * (CAP + 1) + at].astype(F32)
+        told = told_ref[group, k].astype(F32)
         entry = told[0:K_REM] - start
         row = jnp.where(entry < count, entry * T + told[K_REM : 2 * K_REM], -1.0).astype(jnp.int16)
         weight = told[2 * K_REM : 3 * K_REM].astype(BF16)
         hot = jnp.zeros((CAP * T, T), BF16)
-        for k in range(K_REM):
-            hot = jnp.where(rows == row[k : k + 1], weight[k : k + 1], hot)
+        for slot in range(K_REM):
+            hot = jnp.where(rows == row[slot : slot + 1], weight[slot : slot + 1], hot)
         pair = jnp.concatenate([blocks_ref[first], blocks_ref[second]], axis=1)
         return jnp.dot(pair, hot, preferred_element_type=F32).astype(BF16)
 
     for y in range(NY):
-        for x in range(NX):
-            sums_ref[x, y] = product(x, y)
+        for k in range(NX):
+            sums_ref[lax.rem(own_x + (NX - k), NX), y] = product(k, y)
 
 
 def local_kernel(scalars, blocks_ref, told_ref, out_1, out_2, out_3, out_0, hot_ref, total, sem):
@@ -83,27 +83,26 @@
     def of_four(i, carry):
         for j in range(4):
             p = 4 * i + j
-            for x in range(NX):
-                block, row, weight = (
-                    told_ref[x % 2, x // 2, n * 16 : n * 16 + 16, :].astype(F32) for n in range(3)
-                )
+            for k in range(NX):
+                block, row, weight = (told_ref[k, n * 16 : n * 16 + 16, :].astype(F32) for n in range(1, 4))
                 code = ((block - p.astype(F32)) * T + row).astype(jnp.int16)
                 weight = weight.astype(BF16)
-                own = (lanes - jnp.where(p == own_z * NX + x, 0.0, 1024.0)).astype(jnp.int16)
+                here = p == own_z * NX + lax.rem(own_x + (NX - k), NX)
+                own = (lanes - jnp.where(here, 0.0, 1024.0)).astype(jnp.int16)
                 hot = jnp.where(rows == own, ones, zeros)
-                for k in range(K_LOC):
-                    hot = jnp.where(rows == code[k : k + 1], weight[k : k + 1], hot)
-                hot_ref[x, j * T : (j + 1) * T, :] = hot
+                for slot in range(K_LOC):
+                    hot = jnp.where(rows == code[slot : slot + 1], weight[slot : slot + 1], hot)
+                hot_ref[k, j * T : (j + 1) * T, :] = hot
         four = jnp.concatenate([blocks_ref[4 * i + j] for j in range(4)], axis=1)
-        for x in range(NX):
-            total[x] += jnp.dot(four, hot_ref[x], preferred_element_type=F32)
+        for k in range(NX):
+            total[k] += jnp.dot(four, hot_ref[k], preferred_element_type=F32)
         return carry
 
     lax.fori_loop(0, OWNERS // 4, of_four, 0, unroll=2)
-    copy = pltpu.make_async_copy(total.at[own_x], out_0, sem)
+    copy = pltpu.make_async_copy(total.at[0], out_0, sem)
     copy.start()
     for k, out in enumerate((out_1, out_2, out_3)):
-        out[...] = total[lax.rem(own_x + k + 1, NX)]
+        out[...] = total[NX - 1 - k]
     copy.wait()
 
 
@@ -184,16 +183,13 @@
     told = jnp.pad(told, ((0, 3), (0, T - GROUPS * (1 + CAP))))
     block, row = (codes_t // T).astype(BF16), (codes_t % T).astype(BF16)
     gap = jnp.zeros((16 - K_LOC, T), BF16)
-    codes = jnp.concatenate([block[K_LOC:], row[K_LOC:], weights_t[K_LOC:], told], axis=0)
-    codes = lax.all_gather(codes, "y2", axis=0).reshape(2 * TOLD, T)
-    codes = jnp.concatenate([codes, block[:K_LOC], gap, row[:K_LOC], gap, weights_t[:K_LOC], gap], axis=0)
-    codes = lax.all_gather(lax.all_gather(codes, "x1", axis=0), "x0", axis=0)
-    remote_codes, local_codes = codes[:, :, : 2 * TOLD], codes[:, :, 2 * TOLD :]
-    for axis in ("y1", "y0", "c"):
-        remote_codes = lax.all_gather(remote_codes, axis, axis=0)
-    remote_codes = remote_codes.reshape(NC, 2, 2, 2, 2, 2, TOLD, T)
-    told = remote_codes[:, :, :, :, :, :, 12].transpose(5, 2, 1, 0, 4, 3, 6)
-    told = told.reshape(GROUPS, NX, T).astype(jnp.int32)
+    codes = [block[K_LOC:], row[K_LOC:], weights_t[K_LOC:], told]
+    codes += [block[:K_LOC], gap, row[:K_LOC], gap, weights_t[:K_LOC], gap]
+    codes = jnp.concatenate(codes, axis=0)
+    forward = [[(i, (i + k) % NX) for i in range(NX)] for k in range(NX)]
+    codes = jnp.stack([codes] + [lax.ppermute(codes, X, forward[k]) for k in range(1, NX)])
+    remote_codes = lax.all_gather(codes[:, :TOLD], Y + ("c",), axis=0)
+    told = remote_codes[:, :, 12].astype(jnp.int32)
     sources = jnp.arange(GROUPS, dtype=jnp.int32)[:, None, None]
     group = y * NC + c
     here = jnp.sum(jnp.where(sources == group, told, 0), axis=0)
@@ -203,7 +199,7 @@
 
     def remote_sums(core, blocks):
         (sums,) = vmem_call(
-            remote_kernel, "remote_sums", [jnp.concatenate([core[None], scalars])], [blocks, remote_codes],
+            remote_kernel, "remote_sums", [jnp.concatenate([core[None], x[None], scalars])], [blocks, remote_codes],
             [((NX, NY, T, T), BF16)], flops=300_000_000, bytes_accessed=2_500_000,
         )
         return sums
@@ -214,12 +210,12 @@
     arrived = lax.all_to_all(chip_sum.reshape(NX * NY, T, T), X + Y, 0, 0, tiled=True)
 
     *near, near_0 = vmem_call(
-        local_kernel, "local_sums", [jnp.stack([z, x])], [blocks, local_codes], [((T, T), F32)] * NX,
+        local_kernel, "local_sums", [jnp.stack([z, x])], [blocks, codes], [((T, T), F32)] * NX,
         scratch=[pltpu.VMEM((NX, 4 * T, T), BF16), pltpu.VMEM((NX, T, T), F32), pltpu.SemaphoreType.DMA], outside=1,
         flops=600_000_000, bytes_accessed=1_500_000,
     )
     near_0 = pltpu.with_memory_space_constraint(near_0, pltpu.HBM)
-    moved = [lax.ppermute(near[k - 1], X, [(i, (i + k) % NX) for i in range(NX)]) for k in range(1, NX)]
+    moved = [lax.ppermute(near[k - 1], X, forward[k]) for k in range(1, NX)]
 
     share = width // OWNERS
     hidden, send, keep = vmem_call(

time: 147 us -> 145 us (0.986)
  blocking collectives: 73.4 us -> 61.7 us
  waiting for transfers between devices: 7.23 us -> 11.7 us
  starting transfers between devices: 43.4 us -> 46.9 us
    all_gather x6 -> x1, blocking collectives: 32.3 us -> 21.1 us  [body(): remote_codes = lax.all_gather(codes[:, :TOLD], Y + ('c',), axis=0)]
    ppermute x3 -> x6, starting transfers between devices: 10.5 us -> 19.8 us  [the longest x3 10.5 us: body(): moved = [lax.ppermute(near[k - 1], X, forward[k]) for k in range(1, NX)]]
    all_to_all x1, starting transfers between devices: 10.5 us -> 5 us  [body(): lax.all_to_all(chip_sum.reshape(NX * NY, T, T), X + Y, 0, 0, tiled=True)]
    ppermute x3 -> x6, waiting for transfers between devices: 3.1 us -> 7.11 us  [the longest x3 3.59 us: body(): moved = [lax.ppermute(near[k - 1], X, forward[k]) for k in range(1, NX)]]
    unnamed x20 -> x24, local copies, waits for them, and re-layouts: 1.74 us -> 3.64 us
  transfers between devices with their start and end apart: 7 -> 10, of which waited for: 5 -> 7; matrix products, arithmetic and copies ran while one was open for 1% -> 1% of each run, Pallas kernels for 7% -> 7%
where the time goes in v7:
time: 145 us
  blocking collectives  61.7 us (43%)
  starting transfers between devices  46.9 us (32%)
  Pallas kernels  15.5 us (11%)
  waiting for transfers between devices  11.7 us (8%)
  local copies, waits for them, and re-layouts  4.58 us (3%)
  other arithmetic  3.28 us (2%)
    all_to_all x1, blocking collectives, body(): plane = added(lax.all_to_all(chip_grad, ('z',) + X, 0, 0, tiled=True), BF16)  23.6 us
    all_gather x1, blocking collectives, body(): remote_codes = lax.all_gather(codes[:, :TOLD], Y + ('c',), axis=0)  21.1 us
    pallas_call x7, Pallas kernels, vmem_call(): pl.pallas_call(kernel, in_specs=[pl.BlockSpec(memory_space=pltpu.SMEM)] *...  15.5 us
    all_to_all x1, starting transfers between devices, body(): lax.all_to_all(quarters.reshape(OWNERS, T, T), ('z',) + X, 0, 0, tiled=True)  13.9 us
    all_to_all x1, blocking collectives, body(): lax.all_to_all(jnp.broadcast_to(plane, (NY,) + plane.shape), Y, 0, 0, til...  12 us
    ppermute x3, starting transfers between devices, body(): moved = [lax.ppermute(near[k - 1], X, forward[k]) for k in range(1, NX)]  10.5 us
    ppermute x3, starting transfers between devices, body(): lax.ppermute(codes, X, forward[k])  9.31 us
    ppermute x1, starting transfers between devices, body(): received = lax.ppermute(send, 'c', swap)  6.1 us
  transfers between devices with their start and end apart: 10, of which 7 were waited for; matrix products, arithmetic and copies ran while one was open for 1% of the time, Pallas kernels for 7%

profile of v7, /device:TPU:1, one launch (start us, length us, event | category | flops | bytes accessed | tf_op | source)
XLA Modules:
  0.0 144.6 jit_solution(16093795229476338203)
XLA Ops:
  0.6 0.9 copy-done
  1.5 1.2 spread.1
  2.8 13.9 %all-to-all-start = ((bf16[32,128,128]{2,1,0:T(8,128)(2,1)}), bf16[32,128,128]{2,1,0:T(8,128)(2,1)S(1)}, u32[]{:S(2)}, u32[]{:S(2)}) async-start(bf16[32,128,128]{2,1,0:T(8,128)(2,1)} %bitcast.68), calls=%async_computation | async-start | bytes 2097152 | tf_op jit(solution)/shard_map/all_to_all | solution.py:178
  16.7 0.1 copy.17
  16.8 0.1 concatenate.29
  16.9 0.1 fusion.10
  17.0 0.2 concatenate.31
  17.2 4.3 %collective-permute-start.2 = (bf16[64,128]{1,0:T(8,128)(2,1)S(1)}, bf16[64,128]{1,0:T(8,128)(2,1)S(1)}, u32[]{:S(2)}, u32[]{:S(2)}) collective-permute-start(bf16[64,128]{1,0:T(8,128)(2,1)S(1)} %concatenate.31), channel_id=1, source_target_pairs={{0,48},{16,0},{32,16},{48,32},{1,49},{17,1},{33,17},{49,33},{2,50}... | collective-permute-start | bytes 49160 | tf_op jit(solution)/shard_map/ppermute | solution.py:190
  21.6 2.5 %collective-permute-start.1 = (bf16[64,128]{1,0:T(8,128)(2,1)S(1)}, bf16[64,128]{1,0:T(8,128)(2,1)S(1)}, u32[]{:S(2)}, u32[]{:S(2)}) collective-permute-start(bf16[64,128]{1,0:T(8,128)(2,1)S(1)} %concatenate.31), channel_id=1, source_target_pairs={{0,32},{16,48},{32,0},{48,16},{1,33},{17,49},{33,1},{49,17},{2,34}... | collective-permute-start | bytes 49160 | tf_op jit(solution)/shard_map/ppermute | solution.py:190
  24.0 2.5 %collective-permute-start = (bf16[64,128]{1,0:T(8,128)(2,1)S(1)}, bf16[64,128]{1,0:T(8,128)(2,1)S(1)}, u32[]{:S(2)}, u32[]{:S(2)}) collective-permute-start(bf16[64,128]{1,0:T(8,128)(2,1)S(1)} %concatenate.31), channel_id=1, source_target_pairs={{0,16},{16,32},{32,48},{48,0},{1,17},{17,33},{33,49},{49,1},{2,18}... | collective-permute-start | bytes 49160 | tf_op jit(solution)/shard_map/ppermute | solution.py:190
  26.6 1.4 collective-permute-done.1
  27.9 2.2 %collective-permute-done = bf16[64,128]{1,0:T(8,128)(2,1)S(1)} collective-permute-done((bf16[64,128]{1,0:T(8,128)(2,1)S(1)}, bf16[64,128]{1,0:T(8,128)(2,1)S(1)}, u32[]{:S(2)}, u32[]{:S(2)}) %collective-permute-start) | collective-permute-done | bytes 16416 | tf_op jit(solution)/shard_map/ppermute | solution.py:190
  30.1 0.6 copy-done.5
  30.8 21.1 %all-gather = bf16[64,16,128]{2,1,0:T(8,128)(2,1)S(1)} all-gather(bf16[4,16,128]{2,1,0:T(8,128)(2,1)S(1)} %slice.60), channel_id=2, replica_groups=mesh['z'=8,'x1'=2,'x0'=2,'y2'=2,'y1'=2,'y0'=2,'c'=2] {'y2','y1','y0','c'}, dimensions={0}, use_global_device_ids=true | all-gather | bytes 278528 | tf_op jit(solution)/shard_map/all_gather | solution.py:191
  51.9 0.1 fusion
  52.0 0.1 reshape.87
  52.1 0.1 select_reduce_fusion
  52.2 0.1 slice.49
  52.3 0.1 reshape.88
  52.4 0.1 reshape.86
  52.5 0.1 concatenate.33.scalars
  52.6 1.6 %remote_sums.3 = bf16[4,8,128,128]{3,2,1,0:T(8,128)(2,1)S(1)} custom-call(s32[258]{0:T(512)S(1)} %concatenate.33.scalars, bf16[32,128,128]{2,1,0:T(8,128)(2,1)S(1)} %all-to-all-done.blocks_ref, bf16[16,4,16,128]{3,2,1,0:T(8,128)(2,1)S(1)} %bitcast.65), custom_call_target="tpu_custom_call" | custom-call | flops 300000000 | bytes 2500000 | tf_op jit(solution)/shard_map/remote_sums/pallas_call | solution.py:26
  54.2 2.1 %collective-permute-start.3 = (bf16[4,8,128,128]{3,2,1,0:T(8,128)(2,1)S(1)}, bf16[4,8,128,128]{3,2,1,0:T(8,128)(2,1)}, u32[]{:S(2)}, u32[]{:S(2)}) collective-permute-start(bf16[4,8,128,128]{3,2,1,0:T(8,128)(2,1)S(1)} %remote_sums.3), channel_id=1, source_target_pairs={{0,1},{1,0},{2,3},{3,2},{4,5},{5,4},{6,7},{7,6},{8,9},{9,8},{10,11... | collective-permute-start | bytes 3145736 | tf_op jit(solution)/shard_map/ppermute | solution.py:207
  56.2 0.1 concatenate.32.scalars
  56.3 1.6 %remote_sums.2 = bf16[4,8,128,128]{3,2,1,0:T(8,128)(2,1)S(1)} custom-call(s32[258]{0:T(512)S(1)} %concatenate.32.scalars, bf16[32,128,128]{2,1,0:T(8,128)(2,1)S(1)} %all-to-all-done.blocks_ref, bf16[16,4,16,128]{3,2,1,0:T(8,128)(2,1)S(1)} %bitcast.66), custom_call_target="tpu_custom_call" | custom-call | flops 300000000 | bytes 2500000 | tf_op jit(solution)/shard_map/remote_sums/pallas_call | solution.py:26
  57.9 0.9 collective-permute-done.3
  58.8 2.6 %add_convert_fusion = bf16[4,8,128,128]{3,2,1,0:T(8,128)(2,1)} fusion(bf16[4,8,128,128]{3,2,1,0:T(8,128)(2,1)} %collective-permute-done.3, bf16[4,8,128,128]{3,2,1,0:T(8,128)(2,1)S(1)} %remote_sums.2), kind=kLoop, calls=%fused_computation | loop fusion | flops 2097152 | bytes 3145728 | tf_op jit(solution)/shard_map/convert_element_type | solution.py:209
  61.4 5.0 %all-to-all-start.1 = ((bf16[32,128,128]{2,1,0:T(8,128)(2,1)}), bf16[32,128,128]{2,1,0:T(8,128)(2,1)S(1)}, u32[]{:S(2)}, u32[]{:S(2)}) async-start(bf16[32,128,128]{2,1,0:T(8,128)(2,1)} %bitcast.14), calls=%async_computation.1 | async-start | bytes 2097152 | tf_op jit(solution)/shard_map/all_to_all | solution.py:210
  66.5 0.1 pad_add_fusion.1.scalars
  66.5 0.8 copy-done.6
  67.4 8.0 %local_sums.1 = (f32[128,128]{1,0:T(8,128)S(1)}, f32[128,128]{1,0:T(8,128)S(1)}, f32[128,128]{1,0:T(8,128)S(1)}, f32[128,128]{1,0:T(8,128)}) custom-call(s32[2]{0:T(128)S(1)} %pad_add_fusion.1.scalars, bf16[32,128,128]{2,1,0:T(8,128)(2,1)S(1)} %all-to-all-done.blocks_ref, bf16[4,64,128]{2,1,0:T(8,128)(2,1)S(1)} %copy-done.6), custom_call_target="tpu_custom_call" | custom-call | flops 600000000 | bytes 1500000 | tf_op jit(solution)/shard_map/local_sums/pallas_call | solution.py:26
  75.4 3.1 %collective-permute-start.4 = (f32[128,128]{1,0:T(8,128)S(1)}, f32[128,128]{1,0:T(8,128)S(1)}, u32[]{:S(2)}, u32[]{:S(2)}) collective-permute-start(f32[128,128]{1,0:T(8,128)S(1)} %get-tuple-element.14), channel_id=1, source_target_pairs={{0,16},{16,32},{32,48},{48,0},{1,17},{17,33},{33,49},{49,1},{2,18}... | collective-permute-start | bytes 196616 | tf_op jit(solution)/shard_map/ppermute | solution.py:218
  78.5 4.3 %collective-permute-start.5 = (f32[128,128]{1,0:T(8,128)S(1)}, f32[128,128]{1,0:T(8,128)S(1)}, u32[]{:S(2)}, u32[]{:S(2)}) collective-permute-start(f32[128,128]{1,0:T(8,128)S(1)} %get-tuple-element.15), channel_id=1, source_target_pairs={{0,32},{16,48},{32,0},{48,16},{1,33},{17,49},{33,1},{49,17},{2,34}... | collective-permute-start | bytes 196616 | tf_op jit(solution)/shard_map/ppermute | solution.py:218
  82.9 3.0 %collective-permute-start.6 = (f32[128,128]{1,0:T(8,128)S(1)}, f32[128,128]{1,0:T(8,128)S(1)}, u32[]{:S(2)}, u32[]{:S(2)}) collective-permute-start(f32[128,128]{1,0:T(8,128)S(1)} %get-tuple-element.16), channel_id=1, source_target_pairs={{0,48},{16,0},{32,16},{48,32},{1,49},{17,1},{33,17},{49,33},{2,50}... | collective-permute-start | bytes 196616 | tf_op jit(solution)/shard_map/ppermute | solution.py:218
  85.9 0.1 pad_add_fusion.scalars
  86.0 1.8 %collective-permute-done.5.near_2 = f32[128,128]{1,0:T(8,128)S(1)} collective-permute-done((f32[128,128]{1,0:T(8,128)S(1)}, f32[128,128]{1,0:T(8,128)S(1)}, u32[]{:S(2)}, u32[]{:S(2)}) %collective-permute-start.5) | collective-permute-done | bytes 65568 | tf_op jit(solution)/shard_map/ppermute | solution.py:218
  87.8 1.8 %collective-permute-done.6.near_3 = f32[128,128]{1,0:T(8,128)S(1)} collective-permute-done((f32[128,128]{1,0:T(8,128)S(1)}, f32[128,128]{1,0:T(8,128)S(1)}, u32[]{:S(2)}, u32[]{:S(2)}) %collective-permute-start.6) | collective-permute-done | bytes 65568 | tf_op jit(solution)/shard_map/ppermute | solution.py:218
  89.6 2.1 %all-to-all-done.1 = bf16[32,128,128]{2,1,0:T(8,128)(2,1)S(1)} async-done(((bf16[32,128,128]{2,1,0:T(8,128)(2,1)}), bf16[32,128,128]{2,1,0:T(8,128)(2,1)S(1)}, u32[]{:S(2)}, u32[]{:S(2)}) %all-to-all-start.1) | async-done | bytes 1048608 | tf_op jit(solution)/shard_map/all_to_all | solution.py:210
  91.7 3.1 %dense.1 = (bf16[128,512]{1,0:T(8,128)(2,1)}, bf16[32,4,16,128]{3,2,1,0:T(8,128)(2,1)S(1)}, f32[32,4,16,128]{3,2,1,0:T(8,128)S(1)}) custom-call(s32[2]{0:T(128)S(1)} %pad_add_fusion.scalars, f32[128,128]{1,0:T(8,128)} %get-tuple-element.13.near_0, bf16[512,512]{1,0:T(8,128)(2,1)S(1)} %copy-done.2, bf16[4,8,128,128]{3,2,1,0:T(8,128)(2,1)S(1)} %bitcast.63, ...), custom_call_target="tpu_custom_call" | custom-call | flops 300000000 | bytes 5000000 | tf_op jit(solution)/shard_map/dense/pallas_call | solution.py:26
  94.8 6.1 %collective-permute-start.7 = (bf16[32,4,16,128]{3,2,1,0:T(8,128)(2,1)S(1)}, bf16[32,4,16,128]{3,2,1,0:T(8,128)(2,1)S(1)}, u32[]{:S(2)}, u32[]{:S(2)}) collective-permute-start(bf16[32,4,16,128]{3,2,1,0:T(8,128)(2,1)S(1)} %get-tuple-element.20), channel_id=1, source_target_pairs={{0,1},{1,0},{2,3},{3,2},{4,5},{5,4},{6,7},{7,6},{8,9},{9,8},{10,11... | collective-permute-start | bytes 1572872 | tf_op jit(solution)/shard_map/ppermute | solution.py:228
  100.9 1.5 %collective-permute-done.7 = bf16[32,4,16,128]{3,2,1,0:T(8,128)(2,1)S(1)} collective-permute-done((bf16[32,4,16,128]{3,2,1,0:T(8,128)(2,1)S(1)}, bf16[32,4,16,128]{3,2,1,0:T(8,128)(2,1)S(1)}, u32[]{:S(2)}, u32[]{:S(2)}) %collective-permute-start.7) | collective-permute-done | bytes 524320 | tf_op jit(solution)/shard_map/ppermute | solution.py:228
  102.4 0.2 add_convert_fusion.1
  102.6 23.6 %all_to_all.20.parts_ref = bf16[32,64,128]{2,1,0:T(8,128)(2,1)S(1)} all-to-all(bf16[32,64,128]{2,1,0:T(8,128)(2,1)S(1)} %bitcast.67), channel_id=1, replica_groups=mesh['z'=8,'x1'=2,'x0'=2,'y2'=2,'y1'=2,'y0'=2,'c'=2] {'z','x1','x0'}, dimensions={0} | all-to-all | bytes 1048576 | tf_op jit(solution)/shard_map/all_to_all | solution.py:230
  126.2 0.1 added.2
  126.3 12.0 %all_to_all.21.parts_ref = bf16[8,64,128]{2,1,0:T(8,128)(2,1)S(1)} all-to-all(bf16[8,64,128]{2,1,0:T(8,128)(2,1)S(1)} %broadcast_in_dim.43), channel_id=1, replica_groups=mesh['z'=8,'x1'=2,'x0'=2,'y2'=2,'y1'=2,'y0'=2,'c'=2] {'y2','y1','y0'}, dimensions={0} | all-to-all | bytes 262144 | tf_op jit(solution)/shard_map/all_to_all | solution.py:231
  138.3 5.0 %all-gather.1 = f32[128,128]{1,0:T(8,128)S(1)} all-gather(f32[64,128]{1,0:T(8,128)S(1)} %added.3), channel_id=3, replica_groups=mesh['z'=8,'x1'=2,'x0'=2,'y2'=2,'y1'=2,'y0'=2,'c'=2] {'c'}, dimensions={0}, use_global_device_ids=true | all-gather | bytes 98304 | tf_op jit(solution)/shard_map/all_gather | solution.py:232
  143.4 0.6 copy.24
  144.0 0.6 copy.25
  (39 shorter events, 0.3 us)
Async XLA Ops:
  0.6 0.9 copy-start
  2.7 13.9 %copy-start.9 = (s32[1,1,16,2]{2,3,1,0:T(2,128)S(1)}, s32[1,1,16,2]{2,3,1,0:T(2,128)}, u32[]{:S(2)}) copy-start(s32[1,1,16,2]{2,3,1,0:T(2,128)} %param.11) | copy-start | bytes 388
  2.7 13.9 %copy-start.7 = (bf16[128,16]{0,1:T(8,128)(2,1)S(1)}, bf16[128,16]{0,1:T(8,128)(2,1)}, u32[]{:S(2)}) copy-start(bf16[128,16]{0,1:T(8,128)(2,1)} %param.9) | copy-start | bytes 12292
  2.7 14.1 %copy-start.8 = (s32[128,16]{0,1:T(8,128)S(1)}, s32[128,16]{0,1:T(8,128)}, u32[]{:S(2)}) copy-start(s32[128,16]{0,1:T(8,128)} %param.10) | copy-start | bytes 24580
  2.8 14.2 %copy-start.10 = (s32[1,1,16]{2,1,0:T(1,128)S(1)}, s32[1,1,16]{2,1,0:T(1,128)}, u32[]{:S(2)}) copy-start(s32[1,1,16]{2,1,0:T(1,128)} %param.12) | copy-start | bytes 196
  2.8 49.8 %all-to-all-start = ((bf16[32,128,128]{2,1,0:T(8,128)(2,1)}), bf16[32,128,128]{2,1,0:T(8,128)(2,1)S(1)}, u32[]{:S(2)}, u32[]{:S(2)}) async-start(bf16[32,128,128]{2,1,0:T(8,128)(2,1)} %bitcast.68), calls=%async_computation | async-start | bytes 2097152 | tf_op jit(solution)/shard_map/all_to_all | solution.py:178
  17.2 9.4 %collective-permute-start.2 = (bf16[64,128]{1,0:T(8,128)(2,1)S(1)}, bf16[64,128]{1,0:T(8,128)(2,1)S(1)}, u32[]{:S(2)}, u32[]{:S(2)}) collective-permute-start(bf16[64,128]{1,0:T(8,128)(2,1)S(1)} %concatenate.31), channel_id=1, source_target_pairs={{0,48},{16,0},{32,16},{48,32},{1,49},{17,1},{33,17},{49,33},{2,50}... | collective-permute-start | bytes 49160 | tf_op jit(solution)/shard_map/ppermute | solution.py:190
  21.6 6.4 %collective-permute-start.1 = (bf16[64,128]{1,0:T(8,128)(2,1)S(1)}, bf16[64,128]{1,0:T(8,128)(2,1)S(1)}, u32[]{:S(2)}, u32[]{:S(2)}) collective-permute-start(bf16[64,128]{1,0:T(8,128)(2,1)S(1)} %concatenate.31), channel_id=1, source_target_pairs={{0,32},{16,48},{32,0},{48,16},{1,33},{17,49},{33,1},{49,17},{2,34}... | collective-permute-start | bytes 49160 | tf_op jit(solution)/shard_map/ppermute | solution.py:190
  24.0 6.1 %collective-permute-start = (bf16[64,128]{1,0:T(8,128)(2,1)S(1)}, bf16[64,128]{1,0:T(8,128)(2,1)S(1)}, u32[]{:S(2)}, u32[]{:S(2)}) collective-permute-start(bf16[64,128]{1,0:T(8,128)(2,1)S(1)} %concatenate.31), channel_id=1, source_target_pairs={{0,16},{16,32},{32,48},{48,0},{1,17},{17,33},{33,49},{49,1},{2,18}... | collective-permute-start | bytes 49160 | tf_op jit(solution)/shard_map/ppermute | solution.py:190
  30.1 0.6 copy-start.5
  54.2 4.7 %collective-permute-start.3 = (bf16[4,8,128,128]{3,2,1,0:T(8,128)(2,1)S(1)}, bf16[4,8,128,128]{3,2,1,0:T(8,128)(2,1)}, u32[]{:S(2)}, u32[]{:S(2)}) collective-permute-start(bf16[4,8,128,128]{3,2,1,0:T(8,128)(2,1)S(1)} %remote_sums.3), channel_id=1, source_target_pairs={{0,1},{1,0},{2,3},{3,2},{4,5},{5,4},{6,7},{7,6},{8,9},{9,8},{10,11... | collective-permute-start | bytes 3145736 | tf_op jit(solution)/shard_map/ppermute | solution.py:207
  61.4 30.3 %all-to-all-start.1 = ((bf16[32,128,128]{2,1,0:T(8,128)(2,1)}), bf16[32,128,128]{2,1,0:T(8,128)(2,1)S(1)}, u32[]{:S(2)}, u32[]{:S(2)}) async-start(bf16[32,128,128]{2,1,0:T(8,128)(2,1)} %bitcast.14), calls=%async_computation.1 | async-start | bytes 2097152 | tf_op jit(solution)/shard_map/all_to_all | solution.py:210
  66.5 0.8 copy-start.6
  67.4 24.4 %copy-start.1 = (bf16[128,512]{1,0:T(8,128)(2,1)S(1)}, bf16[128,512]{1,0:T(8,128)(2,1)}, u32[]{:S(2)}) copy-start(bf16[128,512]{1,0:T(8,128)(2,1)} %features.1) | copy-start | bytes 393220
  67.4 24.4 %copy-start.2 = (bf16[512,512]{1,0:T(8,128)(2,1)S(1)}, bf16[512,512]{1,0:T(8,128)(2,1)}, u32[]{:S(2)}) copy-start(bf16[512,512]{1,0:T(8,128)(2,1)} %w_self_in.1) | copy-start | bytes 1572868
  67.4 24.4 %copy-start.3 = (bf16[512,512]{1,0:T(8,128)(2,1)S(1)}, bf16[512,512]{1,0:T(8,128)(2,1)}, u32[]{:S(2)}) copy-start(bf16[512,512]{1,0:T(8,128)(2,1)} %w_agg.1) | copy-start | bytes 1572868
  67.4 24.4 %copy-start.4 = (bf16[128,512]{1,0:T(8,128)(2,1)S(1)}, bf16[128,512]{1,0:T(8,128)(2,1)}, u32[]{:S(2)}) copy-start(bf16[128,512]{1,0:T(8,128)(2,1)} %cotangent.1) | copy-start | bytes 393220
  75.4 10.6 %collective-permute-start.4 = (f32[128,128]{1,0:T(8,128)S(1)}, f32[128,128]{1,0:T(8,128)S(1)}, u32[]{:S(2)}, u32[]{:S(2)}) collective-permute-start(f32[128,128]{1,0:T(8,128)S(1)} %get-tuple-element.14), channel_id=1, source_target_pairs={{0,16},{16,32},{32,48},{48,0},{1,17},{17,33},{33,49},{49,1},{2,18}... | collective-permute-start | bytes 196616 | tf_op jit(solution)/shard_map/ppermute | solution.py:218
  78.5 9.3 %collective-permute-start.5 = (f32[128,128]{1,0:T(8,128)S(1)}, f32[128,128]{1,0:T(8,128)S(1)}, u32[]{:S(2)}, u32[]{:S(2)}) collective-permute-start(f32[128,128]{1,0:T(8,128)S(1)} %get-tuple-element.15), channel_id=1, source_target_pairs={{0,32},{16,48},{32,0},{48,16},{1,33},{17,49},{33,1},{49,17},{2,34}... | collective-permute-start | bytes 196616 | tf_op jit(solution)/shard_map/ppermute | solution.py:218
  82.9 6.7 %collective-permute-start.6 = (f32[128,128]{1,0:T(8,128)S(1)}, f32[128,128]{1,0:T(8,128)S(1)}, u32[]{:S(2)}, u32[]{:S(2)}) collective-permute-start(f32[128,128]{1,0:T(8,128)S(1)} %get-tuple-element.16), channel_id=1, source_target_pairs={{0,48},{16,0},{32,16},{48,32},{1,49},{17,1},{33,17},{49,33},{2,50}... | collective-permute-start | bytes 196616 | tf_op jit(solution)/shard_map/ppermute | solution.py:218
  94.8 7.6 %collective-permute-start.7 = (bf16[32,4,16,128]{3,2,1,0:T(8,128)(2,1)S(1)}, bf16[32,4,16,128]{3,2,1,0:T(8,128)(2,1)S(1)}, u32[]{:S(2)}, u32[]{:S(2)}) collective-permute-start(bf16[32,4,16,128]{3,2,1,0:T(8,128)(2,1)S(1)} %get-tuple-element.20), channel_id=1, source_target_pairs={{0,1},{1,0},{2,3},{3,2},{4,5},{5,4},{6,7},{7,6},{8,9},{9,8},{10,11... | collective-permute-start | bytes 1572872 | tf_op jit(solution)/shard_map/ppermute | solution.py:228

commit v8 on v7

--- a/solution.py
+++ b/solution.py
@@ -47,44 +47,68 @@
         copy.wait()
 
 
-def remote_kernel(scalars, blocks_ref, told_ref, sums_ref):
-    core, own_x = scalars[0], scalars[1]
+def split_kernel(codes_0, codes_1, codes_2, codes_3, remote_ref, local_ref, sems):
+    copies = []
+    for k, codes in enumerate((codes_0, codes_1, codes_2, codes_3)):
+        copies.append(pltpu.make_async_copy(codes.at[TOLD:], local_ref.at[k], sems.at[k]))
+        copies[-1].start()
+        remote_ref[k] = codes[0:TOLD]
+    for copy in copies:
+        copy.wait()
+
+
+def remote_product(scalars, blocks_ref, told_ref, k, y):
+    group = y * NC + scalars[0]
+    at = k * GROUPS + group
+    first = jnp.clip(scalars[2 + at * CAP], 0, OWNERS - 1)
+    second = jnp.clip(scalars[3 + at * CAP], 0, OWNERS - 1)
+    start = scalars[2 + NX * GROUPS * CAP + at].astype(F32)
+    count = scalars[2 + NX * GROUPS * (CAP + 1) + at].astype(F32)
+    told = told_ref[group, k].astype(F32)
+    entry = told[0:K_REM] - start
+    row = jnp.where(entry < count, entry * T + told[K_REM : 2 * K_REM], -1.0).astype(jnp.int16)
+    weight = told[2 * K_REM : 3 * K_REM].astype(BF16)
     rows = lax.broadcasted_iota(jnp.int16, (CAP * T, T), 0)
-
-    def product(k, y):
-        group = y * NC + core
-        at = k * GROUPS + group
-        first = jnp.clip(scalars[2 + at * CAP], 0, OWNERS - 1)
-        second = jnp.clip(scalars[3 + at * CAP], 0, OWNERS - 1)
-        start = scalars[2 + NX * GROUPS * CAP + at].astype(F32)
-        count = scalars[2 + NX * GROUPS * (CAP + 1) + at].astype(F32)
-        told = told_ref[group, k].astype(F32)
-        entry = told[0:K_REM] - start
-        row = jnp.where(entry < count, entry * T + told[K_REM : 2 * K_REM], -1.0).astype(jnp.int16)
-        weight = told[2 * K_REM : 3 * K_REM].astype(BF16)
-        hot = jnp.zeros((CAP * T, T), BF16)
-        for slot in range(K_REM):
-            hot = jnp.where(rows == row[slot : slot + 1], weight[slot : slot + 1], hot)
-        pair = jnp.concatenate([blocks_ref[first], blocks_ref[second]], axis=1)
-        return jnp.dot(pair, hot, preferred_element_type=F32).astype(BF16)
-
+    hot = jnp.zeros((CAP * T, T), BF16)
+    for slot in range(K_REM):
+        hot = jnp.where(rows == row[slot : slot + 1], weight[slot : slot + 1], hot)
+    pair = jnp.concatenate([blocks_ref[first], blocks_ref[second]], axis=1)
+    return jnp.dot(pair, hot, preferred_element_type=F32)
+
+
+def first_kernel(scalars, blocks_ref, told_ref, part_ref):
     for y in range(NY):
         for k in range(NX):
-            sums_ref[lax.rem(own_x + (NX - k), NX), y] = product(k, y)
-
-
-def local_kernel(scalars, blocks_ref, told_ref, out_1, out_2, out_3, out_0, hot_ref, total, sem):
+            part_ref[lax.rem(scalars[1] + (NX - k), NX), y] = remote_product(scalars, blocks_ref, told_ref, k, y)
+
+
+def second_kernel(scalars, blocks_ref, told_ref, part_ref, sums_ref, sums, sems):
+    copies = []
+    for y in range(NY):
+        for k in range(NX):
+            x = lax.rem(scalars[1] + (NX - k), NX)
+            sums[x, y] = (part_ref[x, y] + remote_product(scalars, blocks_ref, told_ref, k, y)).astype(BF16)
+        copies.append(pltpu.make_async_copy(sums.at[:, y], sums_ref.at[:, y], sems.at[y]))
+        copies[-1].start()
+    for copy in copies:
+        copy.wait()
+
+
+def local_kernel(scalars, codes_ref, blocks_ref, out_1, out_2, out_3, out_0, hot_ref, total, told_ref, sems):
     own_z, own_x = scalars[0], scalars[1]
+    copy = pltpu.make_async_copy(codes_ref, told_ref, sems.at[0])
+    copy.start()
     rows = lax.broadcasted_iota(jnp.int16, (T, T), 0)
     lanes = lax.broadcasted_iota(jnp.int32, (1, T), 1).astype(F32)
     ones, zeros = jnp.ones((T, T), BF16), jnp.zeros((T, T), BF16)
     total[...] = jnp.zeros_like(total)
+    copy.wait()
 
     def of_four(i, carry):
         for j in range(4):
             p = 4 * i + j
             for k in range(NX):
-                block, row, weight = (told_ref[k, n * 16 : n * 16 + 16, :].astype(F32) for n in range(1, 4))
+                block, row, weight = (told_ref[k, n * 16 : n * 16 + 16, :].astype(F32) for n in range(3))
                 code = ((block - p.astype(F32)) * T + row).astype(jnp.int16)
                 weight = weight.astype(BF16)
                 here = p == own_z * NX + lax.rem(own_x + (NX - k), NX)
@@ -99,14 +123,17 @@
         return carry
 
     lax.fori_loop(0, OWNERS // 4, of_four, 0, unroll=2)
-    copy = pltpu.make_async_copy(total.at[0], out_0, sem)
+    copy = pltpu.make_async_copy(total.at[0], out_0, sems.at[1])
     copy.start()
     for k, out in enumerate((out_1, out_2, out_3)):
         out[...] = total[NX - 1 - k]
     copy.wait()
 
 
-def dense_kernel(scalars, near_0, w_self_in, arrived, near_1, near_2, near_3, weights_t, features, features_t, w_agg, cotangent, hidden_ref, send_ref, keep_ref, agg_t, near, w_self, sems):
+def dense_kernel(
+    scalars, near_0, w_self_in, arrived, near_1, near_2, near_3, weights_t, features, features_t, w_agg, cotangent,
+    hidden_ref, send_ref, keep_ref, agg_t, near, w_self, sems,
+):
     own_c, own_x = scalars[0], scalars[1]
     degree = 1.0 + jnp.sum(weights_t[...], axis=0, keepdims=True)
     copy = pltpu.make_async_copy(near_0, near, sems.at[0])
@@ -134,22 +161,22 @@
     sigma = jax.nn.sigmoid(preact)
     hidden_ref[...] = (preact * sigma).astype(BF16)
     grad_pre = (cotangent[...].astype(F32) * sigma * (1.0 + preact * (1.0 - sigma))).astype(BF16)
-    of_agg = jnp.dot(agg_t[...], grad_pre, preferred_element_type=F32)
-    of_self = jnp.dot(features_t[...].reshape(NX * T, T), grad_pre, preferred_element_type=F32)
-
-    def lay(ref, product):
-        for j in range(NX):
-            ref[:, j] = product[:, j * T : (j + 1) * T].reshape(OWNERS, ref.shape[2], T).astype(ref.dtype)
-
-    @pl.when(own_c == 0)
-    def _():
-        lay(keep_ref, of_agg)
-        lay(send_ref, of_self)
-
-    @pl.when(own_c != 0)
-    def _():
-        lay(keep_ref, of_self)
-        lay(send_ref, of_agg)
+    for j in range(NX):
+        columns = grad_pre[:, j * T : (j + 1) * T]
+        keep_ref[NX + j] = columns
+        send_ref[NX + j] = columns
+        of_agg, of_self = agg_t[j * T : (j + 1) * T, :], features_t[j]
+        keep_ref[j] = jnp.where(own_c == 0, of_agg, of_self)
+        send_ref[j] = jnp.where(own_c == 0, of_self, of_agg)
+
+
+def grad_kernel(keep_ref, received_ref, grad_ref):
+    both = (keep_ref, received_ref)
+    left = jnp.concatenate([ref[0:NX].reshape(NX * T, T) for ref in both], axis=1)
+    for j in range(NX):
+        right = jnp.concatenate([ref[NX + j] for ref in both], axis=0)
+        product = jnp.dot(left, right, preferred_element_type=F32)
+        grad_ref[:, :, j * T : (j + 1) * T] = product.reshape(OWNERS, grad_ref.shape[1], T).astype(BF16)
 
 
 def add_kernel(parts_ref, sum_ref):
@@ -183,54 +210,66 @@
     told = jnp.pad(told, ((0, 3), (0, T - GROUPS * (1 + CAP))))
     block, row = (codes_t // T).astype(BF16), (codes_t % T).astype(BF16)
     gap = jnp.zeros((16 - K_LOC, T), BF16)
-    codes = [block[K_LOC:], row[K_LOC:], weights_t[K_LOC:], told]
-    codes += [block[:K_LOC], gap, row[:K_LOC], gap, weights_t[:K_LOC], gap]
-    codes = jnp.concatenate(codes, axis=0)
+    of_remote = jnp.concatenate([block[K_LOC:], row[K_LOC:], weights_t[K_LOC:], told], axis=0)
+    of_local = jnp.concatenate([block[:K_LOC], gap, row[:K_LOC], gap, weights_t[:K_LOC], gap], axis=0)
+    codes = jnp.concatenate([of_remote, of_local], axis=0)
     forward = [[(i, (i + k) % NX) for i in range(NX)] for k in range(NX)]
-    codes = jnp.stack([codes] + [lax.ppermute(codes, X, forward[k]) for k in range(1, NX)])
-    remote_codes = lax.all_gather(codes[:, :TOLD], Y + ("c",), axis=0)
+    codes = [codes] + [lax.ppermute(codes, X, forward[k]) for k in range(1, NX)]
+    remote_codes, local_codes = vmem_call(
+        split_kernel, "split", [], codes, [((NX, TOLD, T), BF16), ((NX, 48, T), BF16)],
+        scratch=[pltpu.SemaphoreType.DMA((NX,))], outside=1, bytes_accessed=100_000,
+    )
+    remote_codes = lax.all_gather(remote_codes, Y + ("c",), axis=0)
+    local_codes = pltpu.with_memory_space_constraint(local_codes, pltpu.HBM)
+    blocks, remote_codes = lax.optimization_barrier((blocks, remote_codes))
     told = remote_codes[:, :, 12].astype(jnp.int32)
     sources = jnp.arange(GROUPS, dtype=jnp.int32)[:, None, None]
-    group = y * NC + c
-    here = jnp.sum(jnp.where(sources == group, told, 0), axis=0)
-    start = jnp.sum(jnp.where(sources < group, told[:, :, :GROUPS], 0), axis=0)
-    lists = here[:, GROUPS : GROUPS * (1 + CAP)]
-    scalars = jnp.concatenate([lists.reshape(-1), start.reshape(-1), here[:, :GROUPS].reshape(-1)])
-
-    def remote_sums(core, blocks):
-        (sums,) = vmem_call(
-            remote_kernel, "remote_sums", [jnp.concatenate([core[None], x[None], scalars])], [blocks, remote_codes],
-            [((NX, NY, T, T), BF16)], flops=300_000_000, bytes_accessed=2_500_000,
-        )
-        return sums
-
-    received = lax.ppermute(remote_sums(1 - c, blocks), "c", swap)
-    keep = remote_sums(c, blocks)
-    chip_sum = (keep.astype(F32) + received.astype(F32)).astype(BF16)
+
+    def of_source(group):
+        here = jnp.sum(jnp.where(sources == group, told, 0), axis=0)
+        start = jnp.sum(jnp.where(sources < group, told[:, :, :GROUPS], 0), axis=0)
+        lists = here[:, GROUPS : GROUPS * (1 + CAP)]
+        return jnp.concatenate([c[None], x[None], lists.reshape(-1), start.reshape(-1), here[:, :GROUPS].reshape(-1)])
+
+    others = lax.ppermute(blocks, "c", swap)
+    (part,) = vmem_call(
+        first_kernel, "own_group", [of_source(y * NC + c)], [blocks, remote_codes], [((NX, NY, T, T), F32)],
+        flops=300_000_000, bytes_accessed=3_500_000,
+    )
+    (chip_sum,) = vmem_call(
+        second_kernel, "other_group", [of_source(y * NC + 1 - c)], [others, remote_codes, part], [((NX, NY, T, T), BF16)],
+        scratch=[pltpu.VMEM((NX, NY, T, T), BF16), pltpu.SemaphoreType.DMA((NY,))], outside=1,
+        flops=300_000_000, bytes_accessed=5_500_000,
+    )
     arrived = lax.all_to_all(chip_sum.reshape(NX * NY, T, T), X + Y, 0, 0, tiled=True)
 
     *near, near_0 = vmem_call(
-        local_kernel, "local_sums", [jnp.stack([z, x])], [blocks, codes], [((T, T), F32)] * NX,
-        scratch=[pltpu.VMEM((NX, 4 * T, T), BF16), pltpu.VMEM((NX, T, T), F32), pltpu.SemaphoreType.DMA], outside=1,
+        local_kernel, "local_sums", [jnp.stack([z, x])], [blocks], [((T, T), F32)] * NX,
+        scratch=[
+            pltpu.VMEM((NX, 4 * T, T), BF16), pltpu.VMEM((NX, T, T), F32), pltpu.VMEM((NX, 48, T), BF16), pltpu.SemaphoreType.DMA((2,)),
+        ],
+        anywhere=[local_codes], outside=1,
         flops=600_000_000, bytes_accessed=1_500_000,
     )
     near_0 = pltpu.with_memory_space_constraint(near_0, pltpu.HBM)
     moved = [lax.ppermute(near[k - 1], X, forward[k]) for k in range(1, NX)]
 
     share = width // OWNERS
+    operands = ((2 * NX, T, T), BF16)
     hidden, send, keep = vmem_call(
         dense_kernel, "dense", [jnp.stack([c, x])],
         [arrived.reshape(NX, NY, T, T), *moved, weights_t.astype(F32), features, features_t, w_agg, cotangent],
-        [((T, width), BF16), ((OWNERS, NX, share, T), BF16), ((OWNERS, NX, share, T), F32)],
+        [((T, width), BF16), operands, operands],
         scratch=[pltpu.VMEM((width, T), BF16), pltpu.VMEM((T, T), F32), pltpu.VMEM((width, width), BF16), pltpu.SemaphoreType.DMA((2,))],
-        anywhere=[near_0, w_self], flops=300_000_000, bytes_accessed=5_000_000, transcendentals=65536,
+        anywhere=[near_0, w_self], flops=150_000_000, bytes_accessed=3_500_000, transcendentals=65536,
     )
     received = lax.ppermute(send, "c", swap)
-    chip_grad = (keep + received.astype(F32)).astype(BF16).reshape(OWNERS, NX * share, T)
+    (chip_grad,) = vmem_call(
+        grad_kernel, "gradient", [], [keep, received], [((OWNERS, share, width), BF16)], flops=300_000_000, bytes_accessed=1_000_000
+    )
     plane = added(lax.all_to_all(chip_grad, ("z",) + X, 0, 0, tiled=True), BF16)
     planes = lax.all_to_all(jnp.broadcast_to(plane, (NY,) + plane.shape), Y, 0, 0, tiled=True)
     grads = lax.all_gather(added(planes, F32), "c", axis=0)
-    grads = grads.reshape(NC, NX, share, T).swapaxes(1, 2).reshape(NC, share, width)
     return hidden, grads[0], grads[1]
 
 

time: 145 us -> 143 us (0.986)
  waiting for transfers between devices: 11.7 us -> 8.56 us
  starting transfers between devices: 46.9 us -> 49.7 us
  other arithmetic: 3.28 us -> 0.55 us
  Pallas kernels: 15.5 us -> 17.6 us
  local copies, waits for them, and re-layouts: 4.58 us -> 2.78 us
    convert_element_type x2 -> x0, other arithmetic: 2.75 us -> none  [the longest x1 2.6 us: body(): chip_sum = (keep.astype(F32) + received.astype(F32)).astype(BF16)]
    ppermute x4, waiting for transfers between devices: 4.44 us -> 1.71 us  [the longest x3 1.71 us: body(): codes = [codes] + [lax.ppermute(codes, X, forward[k]) for k in range(1, NX)]]
    unnamed x24 -> x18, local copies, waits for them, and re-layouts: 3.64 us -> 0.94 us
    pallas_call x7 -> x9, Pallas kernels: 15.5 us -> 17.6 us  [vmem_call(): pl.pallas_call(kernel, in_specs=[pl.BlockSpec(memory_space=pltpu.SMEM)] *...]
    all_to_all x1, starting transfers between devices: 5 us -> 6.54 us  [body(): lax.all_to_all(chip_sum.reshape(NX * NY, T, T), X + Y, 0, 0, tiled=True)]
  transfers between devices with their start and end apart: 10 -> 10, of which waited for: 7 -> 5; matrix products, arithmetic and copies ran while one was open for 1% -> 1% of each run, Pallas kernels for 7% -> 8%
where the time goes in v8:
time: 143 us; the launch traced here: 142 us
  blocking collectives  61.7 us (43%)
  starting transfers between devices  49.7 us (35%)
  Pallas kernels  17.6 us (12%)
  waiting for transfers between devices  8.56 us (6%)
  local copies, waits for them, and re-layouts  2.78 us (2%)
    all_to_all x1, blocking collectives, body(): plane = added(lax.all_to_all(chip_grad, ('z',) + X, 0, 0, tiled=True), BF16)  23.5 us
    all_gather x1, blocking collectives, body(): remote_codes = lax.all_gather(remote_codes, Y + ('c',), axis=0)  21.1 us
    pallas_call x9, Pallas kernels, vmem_call(): pl.pallas_call(kernel, in_specs=[pl.BlockSpec(memory_space=pltpu.SMEM)] *...  17.6 us
    all_to_all x1, starting transfers between devices, body(): lax.all_to_all(quarters.reshape(OWNERS, T, T), ('z',) + X, 0, 0, tiled=True)  13.7 us
    all_to_all x1, blocking collectives, body(): lax.all_to_all(jnp.broadcast_to(plane, (NY,) + plane.shape), Y, 0, 0, til...  12 us
    ppermute x3, starting transfers between devices, body(): moved = [lax.ppermute(near[k - 1], X, forward[k]) for k in range(1, NX)]  10.5 us
    ppermute x3, starting transfers between devices, body(): codes = [codes] + [lax.ppermute(codes, X, forward[k]) for k in range(1, NX)]  10.5 us
    all_to_all x1, starting transfers between devices, body(): lax.all_to_all(chip_sum.reshape(NX * NY, T, T), X + Y, 0, 0, tiled=True)  6.54 us
  transfers between devices with their start and end apart: 10, of which 5 were waited for; matrix products, arithmetic and copies ran while one was open for 1% of the time, Pallas kernels for 8%

profile of v8, /device:TPU:1, one launch (start us, length us, event | category | flops | bytes accessed | tf_op | source)
XLA Modules:
  0.0 141.8 jit_solution(14260981451099390610)
XLA Ops:
  0.6 0.9 copy-done
  1.6 1.2 spread.1
  2.7 13.7 %all-to-all-start = ((bf16[32,128,128]{2,1,0:T(8,128)(2,1)}), bf16[32,128,128]{2,1,0:T(8,128)(2,1)S(1)}, u32[]{:S(2)}, u32[]{:S(2)}) async-start(bf16[32,128,128]{2,1,0:T(8,128)(2,1)} %bitcast.50), calls=%async_computation | async-start | bytes 2097152 | tf_op jit(solution)/shard_map/all_to_all | solution.py:205
  16.5 0.1 copy.13
  16.6 0.1 concatenate.26
  16.8 0.1 fusion.9
  16.8 0.2 concatenate.28.codes_0
  17.0 3.1 %collective-permute-start = (bf16[64,128]{1,0:T(8,128)(2,1)S(1)}, bf16[64,128]{1,0:T(8,128)(2,1)S(1)}, u32[]{:S(2)}, u32[]{:S(2)}) collective-permute-start(bf16[64,128]{1,0:T(8,128)(2,1)S(1)} %concatenate.28.codes_0), channel_id=1, source_target_pairs={{0,16},{16,32},{32,48},{48,0},{1,17},{17,33},{33,49},{49,1},{2,18}... | collective-permute-start | bytes 49160 | tf_op jit(solution)/shard_map/ppermute | solution.py:217
  20.2 4.3 %collective-permute-start.1 = (bf16[64,128]{1,0:T(8,128)(2,1)S(1)}, bf16[64,128]{1,0:T(8,128)(2,1)S(1)}, u32[]{:S(2)}, u32[]{:S(2)}) collective-permute-start(bf16[64,128]{1,0:T(8,128)(2,1)S(1)} %concatenate.28.codes_0), channel_id=1, source_target_pairs={{0,32},{16,48},{32,0},{48,16},{1,33},{17,49},{33,1},{49,17},{2,34}... | collective-permute-start | bytes 49160 | tf_op jit(solution)/shard_map/ppermute | solution.py:217
  24.5 3.1 %collective-permute-start.2 = (bf16[64,128]{1,0:T(8,128)(2,1)S(1)}, bf16[64,128]{1,0:T(8,128)(2,1)S(1)}, u32[]{:S(2)}, u32[]{:S(2)}) collective-permute-start(bf16[64,128]{1,0:T(8,128)(2,1)S(1)} %concatenate.28.codes_0), channel_id=1, source_target_pairs={{0,48},{16,0},{32,16},{48,32},{1,49},{17,1},{33,17},{49,33},{2,50}... | collective-permute-start | bytes 49160 | tf_op jit(solution)/shard_map/ppermute | solution.py:217
  27.6 1.7 %collective-permute-done.2.codes_3 = bf16[64,128]{1,0:T(8,128)(2,1)S(1)} collective-permute-done((bf16[64,128]{1,0:T(8,128)(2,1)S(1)}, bf16[64,128]{1,0:T(8,128)(2,1)S(1)}, u32[]{:S(2)}, u32[]{:S(2)}) %collective-permute-start.2) | collective-permute-done | bytes 16416 | tf_op jit(solution)/shard_map/ppermute | solution.py:217
  29.3 0.6 split.1
  29.9 21.1 %all-gather = bf16[64,16,128]{2,1,0:T(8,128)(2,1)S(1)} all-gather(bf16[4,16,128]{2,1,0:T(8,128)(2,1)S(1)} %get-tuple-element.18), channel_id=2, replica_groups=mesh['z'=8,'x1'=2,'x0'=2,'y2'=2,'y1'=2,'y0'=2,'c'=2] {'y2','y1','y0','c'}, dimensions={0}, use_global_device_ids=true | all-gather | bytes 278528 | tf_op jit(solution)/shard_map/all_gather | solution.py:222
  51.1 2.1 %collective-permute-start.3 = (bf16[32,128,128]{2,1,0:T(8,128)(2,1)S(1)}, bf16[32,128,128]{2,1,0:T(8,128)(2,1)S(1)}, u32[]{:S(2)}, u32[]{:S(2)}) collective-permute-start(bf16[32,128,128]{2,1,0:T(8,128)(2,1)S(1)} %all-to-all-done.blocks_ref), channel_id=1, source_target_pairs={{0,1},{1,0},{2,3},{3,2},{4,5},{5,4},{6,7},{7,6},{8,9},{9,8},{10,11... | collective-permute-start | bytes 3145736 | tf_op jit(solution)/shard_map/ppermute | solution.py:234
  53.2 0.1 slice_convert_fusion
  53.2 0.1 select_reduce_fusion.1
  53.4 0.1 slice.50
  53.4 0.1 reshape.94
  53.5 0.1 select_reduce_fusion
  53.6 0.1 reshape.95
  53.7 0.1 reshape.96
  53.8 0.1 slice.53
  53.9 0.1 reshape.97
  54.0 0.1 reshape.98
  54.0 0.1 reshape.99
  54.1 0.1 concatenate.29.scalars
  54.2 0.1 concatenate.30.scalars
  54.3 1.6 %own_group.1.part_ref = f32[4,8,128,128]{3,2,1,0:T(8,128)S(1)} custom-call(s32[258]{0:T(512)S(1)} %concatenate.30.scalars, bf16[32,128,128]{2,1,0:T(8,128)(2,1)S(1)} %all-to-all-done.blocks_ref, bf16[16,4,16,128]{3,2,1,0:T(8,128)(2,1)S(1)} %bitcast.47), custom_call_target="tpu_custom_call" | custom-call | flops 300000000 | bytes 3500000 | tf_op jit(solution)/shard_map/own_group/pallas_call | solution.py:26
  55.9 2.5 %other_group.1 = bf16[4,8,128,128]{3,2,1,0:T(8,128)(2,1)} custom-call(s32[258]{0:T(512)S(1)} %concatenate.29.scalars, bf16[32,128,128]{2,1,0:T(8,128)(2,1)S(1)} %collective-permute-done.3.blocks_ref, bf16[16,4,16,128]{3,2,1,0:T(8,128)(2,1)S(1)} %bitcast.48, f32[4,8,128,128]{3,2,1,0:T(8,128)S(1)} %own_group.1.part_ref), custom_call_target="tpu_custom_call" | custom-call | flops 300000000 | bytes 5500000 | tf_op jit(solution)/shard_map/other_group/pallas_call | solution.py:26
  58.4 6.5 %all-to-all-start.1 = ((bf16[32,128,128]{2,1,0:T(8,128)(2,1)}), bf16[32,128,128]{2,1,0:T(8,128)(2,1)S(1)}, u32[]{:S(2)}, u32[]{:S(2)}) async-start(bf16[32,128,128]{2,1,0:T(8,128)(2,1)} %bitcast.49), calls=%async_computation.1 | async-start | bytes 2097152 | tf_op jit(solution)/shard_map/all_to_all | solution.py:244
  64.9 0.1 pad_add_fusion.1.scalars
  65.0 8.8 %local_sums.1 = (f32[128,128]{1,0:T(8,128)S(1)}, f32[128,128]{1,0:T(8,128)S(1)}, f32[128,128]{1,0:T(8,128)S(1)}, f32[128,128]{1,0:T(8,128)}) custom-call(s32[2]{0:T(128)S(1)} %pad_add_fusion.1.scalars, bf16[4,48,128]{2,1,0:T(8,128)(2,1)} %get-tuple-element.16.codes_ref, bf16[32,128,128]{2,1,0:T(8,128)(2,1)S(1)} %all-to-all-done.blocks_ref), custom_call_target="tpu_custom_call" | custom-call | flops 600000000 | bytes 1500000 | tf_op jit(solution)/shard_map/local_sums/pallas_call | solution.py:26
  73.8 3.1 %collective-permute-start.4 = (f32[128,128]{1,0:T(8,128)S(1)}, f32[128,128]{1,0:T(8,128)S(1)}, u32[]{:S(2)}, u32[]{:S(2)}) collective-permute-start(f32[128,128]{1,0:T(8,128)S(1)} %get-tuple-element.22), channel_id=1, source_target_pairs={{0,16},{16,32},{32,48},{48,0},{1,17},{17,33},{33,49},{49,1},{2,18}... | collective-permute-start | bytes 196616 | tf_op jit(solution)/shard_map/ppermute | solution.py:255
  76.9 4.3 %collective-permute-start.5 = (f32[128,128]{1,0:T(8,128)S(1)}, f32[128,128]{1,0:T(8,128)S(1)}, u32[]{:S(2)}, u32[]{:S(2)}) collective-permute-start(f32[128,128]{1,0:T(8,128)S(1)} %get-tuple-element.23), channel_id=1, source_target_pairs={{0,32},{16,48},{32,0},{48,16},{1,33},{17,49},{33,1},{49,17},{2,34}... | collective-permute-start | bytes 196616 | tf_op jit(solution)/shard_map/ppermute | solution.py:255
  81.3 3.0 %collective-permute-start.6 = (f32[128,128]{1,0:T(8,128)S(1)}, f32[128,128]{1,0:T(8,128)S(1)}, u32[]{:S(2)}, u32[]{:S(2)}) collective-permute-start(f32[128,128]{1,0:T(8,128)S(1)} %get-tuple-element.24), channel_id=1, source_target_pairs={{0,48},{16,0},{32,16},{48,32},{1,49},{17,1},{33,17},{49,33},{2,50}... | collective-permute-start | bytes 196616 | tf_op jit(solution)/shard_map/ppermute | solution.py:255
  84.3 0.1 pad_add_fusion.scalars
  84.4 1.7 %collective-permute-done.5.near_2 = f32[128,128]{1,0:T(8,128)S(1)} collective-permute-done((f32[128,128]{1,0:T(8,128)S(1)}, f32[128,128]{1,0:T(8,128)S(1)}, u32[]{:S(2)}, u32[]{:S(2)}) %collective-permute-start.5) | collective-permute-done | bytes 65568 | tf_op jit(solution)/shard_map/ppermute | solution.py:255
  86.1 2.1 %collective-permute-done.6.near_3 = f32[128,128]{1,0:T(8,128)S(1)} collective-permute-done((f32[128,128]{1,0:T(8,128)S(1)}, f32[128,128]{1,0:T(8,128)S(1)}, u32[]{:S(2)}, u32[]{:S(2)}) %collective-permute-start.6) | collective-permute-done | bytes 65568 | tf_op jit(solution)/shard_map/ppermute | solution.py:255
  88.2 1.9 %all-to-all-done.1 = bf16[32,128,128]{2,1,0:T(8,128)(2,1)S(1)} async-done(((bf16[32,128,128]{2,1,0:T(8,128)(2,1)}), bf16[32,128,128]{2,1,0:T(8,128)(2,1)S(1)}, u32[]{:S(2)}, u32[]{:S(2)}) %all-to-all-start.1) | async-done | bytes 1048608 | tf_op jit(solution)/shard_map/all_to_all | solution.py:244
  90.2 2.5 %dense.1 = (bf16[128,512]{1,0:T(8,128)(2,1)}, bf16[8,128,128]{2,1,0:T(8,128)(2,1)S(1)}, bf16[8,128,128]{2,1,0:T(8,128)(2,1)S(1)}) custom-call(s32[2]{0:T(128)S(1)} %pad_add_fusion.scalars, f32[128,128]{1,0:T(8,128)} %get-tuple-element.20.near_0, bf16[512,512]{1,0:T(8,128)(2,1)S(1)} %copy-done.2, bf16[4,8,128,128]{3,2,1,0:T(8,128)(2,1)S(1)} %bitcast.45, ...), custom_call_target="tpu_custom_call" | custom-call | flops 150000000 | bytes 3500000 | tf_op jit(solution)/shard_map/dense/pallas_call | solution.py:26
  92.7 6.3 %collective-permute-start.7 = (bf16[8,128,128]{2,1,0:T(8,128)(2,1)S(1)}, bf16[8,128,128]{2,1,0:T(8,128)(2,1)S(1)}, u32[]{:S(2)}, u32[]{:S(2)}) collective-permute-start(bf16[8,128,128]{2,1,0:T(8,128)(2,1)S(1)} %get-tuple-element.28), channel_id=1, source_target_pairs={{0,1},{1,0},{2,3},{3,2},{4,5},{5,4},{6,7},{7,6},{8,9},{9,8},{10,11... | collective-permute-start | bytes 786440 | tf_op jit(solution)/shard_map/ppermute | solution.py:266
  99.0 1.1 collective-permute-done.7.received_ref
  100.1 0.4 gradient.1
  100.5 23.5 %all_to_all.20.parts_ref = bf16[32,16,512]{2,1,0:T(8,128)(2,1)S(1)} all-to-all(bf16[32,16,512]{2,1,0:T(8,128)(2,1)S(1)} %gradient.1), channel_id=1, replica_groups=mesh['z'=8,'x1'=2,'x0'=2,'y2'=2,'y1'=2,'y0'=2,'c'=2] {'z','x1','x0'}, dimensions={0} | all-to-all | bytes 1048576 | tf_op jit(solution)/shard_map/all_to_all | solution.py:270
  124.0 0.1 added.2
  124.2 12.0 %all_to_all.21.parts_ref = bf16[8,16,512]{2,1,0:T(8,128)(2,1)S(1)} all-to-all(bf16[8,16,512]{2,1,0:T(8,128)(2,1)S(1)} %broadcast_in_dim.54), channel_id=1, replica_groups=mesh['z'=8,'x1'=2,'x0'=2,'y2'=2,'y1'=2,'y0'=2,'c'=2] {'y2','y1','y0'}, dimensions={0} | all-to-all | bytes 262144 | tf_op jit(solution)/shard_map/all_to_all | solution.py:271
  136.2 5.0 %all-gather.1 = f32[32,512]{1,0:T(8,128)S(1)} all-gather(f32[16,512]{1,0:T(8,128)S(1)} %added.3), channel_id=3, replica_groups=mesh['z'=8,'x1'=2,'x0'=2,'y2'=2,'y1'=2,'y0'=2,'c'=2] {'c'}, dimensions={0}, use_global_device_ids=true | all-gather | bytes 98304 | tf_op jit(solution)/shard_map/all_gather | solution.py:272
  141.2 0.6 fusion.11
  (34 shorter events, 0.2 us)
Async XLA Ops:
  0.6 0.9 copy-start
  1.5 14.9 %copy-start.6 = (s32[128,16]{0,1:T(8,128)S(1)}, s32[128,16]{0,1:T(8,128)}, u32[]{:S(2)}) copy-start(s32[128,16]{0,1:T(8,128)} %param.10) | copy-start | bytes 24580
  1.5 15.0 %copy-start.5 = (bf16[128,16]{0,1:T(8,128)(2,1)S(1)}, bf16[128,16]{0,1:T(8,128)(2,1)}, u32[]{:S(2)}) copy-start(bf16[128,16]{0,1:T(8,128)(2,1)} %param.9) | copy-start | bytes 12292
  1.5 15.0 %copy-start.7 = (s32[1,1,16,2]{2,3,1,0:T(2,128)S(1)}, s32[1,1,16,2]{2,3,1,0:T(2,128)}, u32[]{:S(2)}) copy-start(s32[1,1,16,2]{2,3,1,0:T(2,128)} %param.11) | copy-start | bytes 388
  1.5 15.2 %copy-start.8 = (s32[1,1,16]{2,1,0:T(1,128)S(1)}, s32[1,1,16]{2,1,0:T(1,128)}, u32[]{:S(2)}) copy-start(s32[1,1,16]{2,1,0:T(1,128)} %param.12) | copy-start | bytes 196
  2.7 48.3 %all-to-all-start = ((bf16[32,128,128]{2,1,0:T(8,128)(2,1)}), bf16[32,128,128]{2,1,0:T(8,128)(2,1)S(1)}, u32[]{:S(2)}, u32[]{:S(2)}) async-start(bf16[32,128,128]{2,1,0:T(8,128)(2,1)} %bitcast.50), calls=%async_computation | async-start | bytes 2097152 | tf_op jit(solution)/shard_map/all_to_all | solution.py:205
  17.0 10.5 %collective-permute-start = (bf16[64,128]{1,0:T(8,128)(2,1)S(1)}, bf16[64,128]{1,0:T(8,128)(2,1)S(1)}, u32[]{:S(2)}, u32[]{:S(2)}) collective-permute-start(bf16[64,128]{1,0:T(8,128)(2,1)S(1)} %concatenate.28.codes_0), channel_id=1, source_target_pairs={{0,16},{16,32},{32,48},{48,0},{1,17},{17,33},{33,49},{49,1},{2,18}... | collective-permute-start | bytes 49160 | tf_op jit(solution)/shard_map/ppermute | solution.py:217
  20.2 7.4 %collective-permute-start.1 = (bf16[64,128]{1,0:T(8,128)(2,1)S(1)}, bf16[64,128]{1,0:T(8,128)(2,1)S(1)}, u32[]{:S(2)}, u32[]{:S(2)}) collective-permute-start(bf16[64,128]{1,0:T(8,128)(2,1)S(1)} %concatenate.28.codes_0), channel_id=1, source_target_pairs={{0,32},{16,48},{32,0},{48,16},{1,33},{17,49},{33,1},{49,17},{2,34}... | collective-permute-start | bytes 49160 | tf_op jit(solution)/shard_map/ppermute | solution.py:217
  24.5 4.8 %collective-permute-start.2 = (bf16[64,128]{1,0:T(8,128)(2,1)S(1)}, bf16[64,128]{1,0:T(8,128)(2,1)S(1)}, u32[]{:S(2)}, u32[]{:S(2)}) collective-permute-start(bf16[64,128]{1,0:T(8,128)(2,1)S(1)} %concatenate.28.codes_0), channel_id=1, source_target_pairs={{0,48},{16,0},{32,16},{48,32},{1,49},{17,1},{33,17},{49,33},{2,50}... | collective-permute-start | bytes 49160 | tf_op jit(solution)/shard_map/ppermute | solution.py:217
  51.1 4.8 %collective-permute-start.3 = (bf16[32,128,128]{2,1,0:T(8,128)(2,1)S(1)}, bf16[32,128,128]{2,1,0:T(8,128)(2,1)S(1)}, u32[]{:S(2)}, u32[]{:S(2)}) collective-permute-start(bf16[32,128,128]{2,1,0:T(8,128)(2,1)S(1)} %all-to-all-done.blocks_ref), channel_id=1, source_target_pairs={{0,1},{1,0},{2,3},{3,2},{4,5},{5,4},{6,7},{7,6},{8,9},{9,8},{10,11... | collective-permute-start | bytes 3145736 | tf_op jit(solution)/shard_map/ppermute | solution.py:234
  58.3 31.8 %copy-start.1 = (bf16[128,512]{1,0:T(8,128)(2,1)S(1)}, bf16[128,512]{1,0:T(8,128)(2,1)}, u32[]{:S(2)}) copy-start(bf16[128,512]{1,0:T(8,128)(2,1)} %features.1) | copy-start | bytes 393220
  58.4 31.8 %copy-start.2 = (bf16[512,512]{1,0:T(8,128)(2,1)S(1)}, bf16[512,512]{1,0:T(8,128)(2,1)}, u32[]{:S(2)}) copy-start(bf16[512,512]{1,0:T(8,128)(2,1)} %w_self_in.1) | copy-start | bytes 1572868
  58.4 31.8 %copy-start.3 = (bf16[512,512]{1,0:T(8,128)(2,1)S(1)}, bf16[512,512]{1,0:T(8,128)(2,1)}, u32[]{:S(2)}) copy-start(bf16[512,512]{1,0:T(8,128)(2,1)} %w_agg.1) | copy-start | bytes 1572868
  58.4 31.8 %copy-start.4 = (bf16[128,512]{1,0:T(8,128)(2,1)S(1)}, bf16[128,512]{1,0:T(8,128)(2,1)}, u32[]{:S(2)}) copy-start(bf16[128,512]{1,0:T(8,128)(2,1)} %cotangent.1) | copy-start | bytes 393220
  58.4 31.7 %all-to-all-start.1 = ((bf16[32,128,128]{2,1,0:T(8,128)(2,1)}), bf16[32,128,128]{2,1,0:T(8,128)(2,1)S(1)}, u32[]{:S(2)}, u32[]{:S(2)}) async-start(bf16[32,128,128]{2,1,0:T(8,128)(2,1)} %bitcast.49), calls=%async_computation.1 | async-start | bytes 2097152 | tf_op jit(solution)/shard_map/all_to_all | solution.py:244
  73.8 10.6 %collective-permute-start.4 = (f32[128,128]{1,0:T(8,128)S(1)}, f32[128,128]{1,0:T(8,128)S(1)}, u32[]{:S(2)}, u32[]{:S(2)}) collective-permute-start(f32[128,128]{1,0:T(8,128)S(1)} %get-tuple-element.22), channel_id=1, source_target_pairs={{0,16},{16,32},{32,48},{48,0},{1,17},{17,33},{33,49},{49,1},{2,18}... | collective-permute-start | bytes 196616 | tf_op jit(solution)/shard_map/ppermute | solution.py:255
  76.9 9.1 %collective-permute-start.5 = (f32[128,128]{1,0:T(8,128)S(1)}, f32[128,128]{1,0:T(8,128)S(1)}, u32[]{:S(2)}, u32[]{:S(2)}) collective-permute-start(f32[128,128]{1,0:T(8,128)S(1)} %get-tuple-element.23), channel_id=1, source_target_pairs={{0,32},{16,48},{32,0},{48,16},{1,33},{17,49},{33,1},{49,17},{2,34}... | collective-permute-start | bytes 196616 | tf_op jit(solution)/shard_map/ppermute | solution.py:255
  81.3 6.9 %collective-permute-start.6 = (f32[128,128]{1,0:T(8,128)S(1)}, f32[128,128]{1,0:T(8,128)S(1)}, u32[]{:S(2)}, u32[]{:S(2)}) collective-permute-start(f32[128,128]{1,0:T(8,128)S(1)} %get-tuple-element.24), channel_id=1, source_target_pairs={{0,48},{16,0},{32,16},{48,32},{1,49},{17,1},{33,17},{49,33},{2,50}... | collective-permute-start | bytes 196616 | tf_op jit(solution)/shard_map/ppermute | solution.py:255
  92.7 7.4 %collective-permute-start.7 = (bf16[8,128,128]{2,1,0:T(8,128)(2,1)S(1)}, bf16[8,128,128]{2,1,0:T(8,128)(2,1)S(1)}, u32[]{:S(2)}, u32[]{:S(2)}) collective-permute-start(bf16[8,128,128]{2,1,0:T(8,128)(2,1)S(1)} %get-tuple-element.28), channel_id=1, source_target_pairs={{0,1},{1,0},{2,3},{3,2},{4,5},{5,4},{6,7},{7,6},{8,9},{9,8},{10,11... | collective-permute-start | bytes 786440 | tf_op jit(solution)/shard_map/ppermute | solution.py:266

commit v9 on v8

v9 whole, which is shorter than its diff:
```python
import functools

import jax
import jax.numpy as jnp
from jax import lax
from jax.experimental import pallas as pl
from jax.experimental.pallas import tpu as pltpu
from jax.sharding import Mesh, PartitionSpec as P

NZ, NX, NY, NC = 8, 4, 8, 2
OWNERS = NZ * NX
GROUPS = NY * NC
T = 128
K_LOC = 12
K_REM = 4
CAP = 2
TOLD = 16
X, Y = ("x1", "x0"), ("y2", "y1", "y0")
F32 = jnp.float32
BF16 = jnp.bfloat16
VMEM_LIMIT = 16 * 1024 * 1024


def vmem_call(
    kernel, name, scalar_inputs, array_inputs, outputs, scratch=(), anywhere=(), outside=0, flops=0, bytes_accessed=0, transcendentals=0
):
    vmem = pl.BlockSpec(memory_space=pltpu.VMEM)
    return pl.pallas_call(
        kernel,
        in_specs=[pl.BlockSpec(memory_space=pltpu.SMEM)] * len(scalar_inputs)
        + [pl.BlockSpec(memory_space=pltpu.HBM)] * len(anywhere)
        + [vmem] * len(array_inputs),
        out_specs=[vmem] * (len(outputs) - outside) + [pl.BlockSpec(memory_space=pltpu.HBM)] * outside,
        out_shape=[jax.ShapeDtypeStruct(*of) for of in outputs[: len(outputs) - outside]]
        + [pltpu.HBM(*of) for of in outputs[len(outputs) - outside :]],
        scratch_shapes=list(scratch),
        compiler_params=pltpu.CompilerParams(vmem_limit_bytes=VMEM_LIMIT),
        cost_estimate=pl.CostEstimate(flops=flops, bytes_accessed=bytes_accessed, transcendentals=transcendentals),
        name=name,
    )(*scalar_inputs, *anywhere, *array_inputs)


def spread_kernel(features_in, features_out, quarters_ref, quarters, features_t, sems_in, sems):
    loads = [pltpu.make_async_copy(features_in.at[:, x * T : (x + 1) * T], quarters.at[x], sems_in.at[x]) for x in range(NX)]
    for load in loads:
        load.start()
    copies = []
    for x in range(NX):
        loads[x].wait()
        features_t[x] = quarters[x].astype(F32).T.astype(BF16)
        for z in range(NZ):
            copies.append(pltpu.make_async_copy(features_t.at[x], quarters_ref.at[z, x], sems.at[x, z]))
            copies[-1].start()
        copies.append(pltpu.make_async_copy(features_t.at[x], features_out.at[x], sems.at[x, NZ]))
        copies[-1].start()
    for copy in copies:
        copy.wait()


def split_kernel(codes_0, codes_1, codes_2, codes_3, remote_ref, local_ref, sems):
    copies = []
    for k, codes in enumerate((codes_0, codes_1, codes_2, codes_3)):
        copies.append(pltpu.make_async_copy(codes.at[TOLD:], local_ref.at[k], sems.at[k]))
        copies[-1].start()
        remote_ref[k] = codes[0:TOLD]
    for copy in copies:
        copy.wait()


def remote_product(own, here, before, blocks_ref, told_ref, k, y):
    group = y * NC + own[0]
    first = jnp.clip(here[k, GROUPS + group * CAP], 0, OWNERS - 1)
    second = jnp.clip(here[k, GROUPS + group * CAP + 1], 0, OWNERS - 1)
    start, count = before[k, group].astype(F32), here[k, group].astype(F32)
    told = told_ref[group, k].astype(F32)
    entry = told[0:K_REM] - start
    row = jnp.where(entry < count, entry * T + told[K_REM : 2 * K_REM], -1.0).astype(jnp.int16)
    weight = told[2 * K_REM : 3 * K_REM].astype(BF16)
    rows = lax.broadcasted_iota(jnp.int16, (CAP * T, T), 0)
    hot = jnp.zeros((CAP * T, T), BF16)
    for slot in range(K_REM):
        hot = jnp.where(rows == row[slot : slot + 1], weight[slot : slot + 1], hot)
    pair = jnp.concatenate([blocks_ref[first], blocks_ref[second]], axis=1)
    return jnp.dot(pair, hot, preferred_element_type=F32)


def first_kernel(own, here, before, blocks_ref, told_ref, part_ref):
    for y in range(NY):
        for k in range(NX):
            part_ref[lax.rem(own[1] + (NX - k), NX), y] = remote_product(own, here, before, blocks_ref, told_ref, k, y)


def second_kernel(own, here, before, blocks_ref, told_ref, part_ref, sums_ref, sums, sems):
    copies = []
    for y in range(NY):
        for k in range(NX):
            x = lax.rem(own[1] + (NX - k), NX)
            sums[x, y] = (part_ref[x, y] + remote_product(own, here, before, blocks_ref, told_ref, k, y)).astype(BF16)
        copies.append(pltpu.make_async_copy(sums.at[:, y], sums_ref.at[:, y], sems.at[y]))
        copies[-1].start()
    for copy in copies:
        copy.wait()


def local_kernel(k, outside, scalars, blocks_ref, told_ref, out, hot_ref, total=None, sem=None):
    owner = scalars[0] * NX + lax.rem(scalars[1] + (NX - k), NX)
    rows = lax.broadcasted_iota(jnp.int16, (T, T), 0)
    lanes = lax.broadcasted_iota(jnp.int32, (1, T), 1).astype(F32)
    ones, zeros = jnp.ones((T, T), BF16), jnp.zeros((T, T), BF16)
    block, row, weight = (told_ref[k, n * 16 : n * 16 + 16, :].astype(F32) for n in range(3))
    weight = weight.astype(BF16)

    def of_four(i, summed):
        for j in range(4):
            p = 4 * i + j
            code = ((block - p.astype(F32)) * T + row).astype(jnp.int16)
            own = (lanes - jnp.where(p == owner, 0.0, 1024.0)).astype(jnp.int16)
            hot = jnp.where(rows == own, ones, zeros)
            for slot in range(K_LOC):
                hot = jnp.where(rows == code[slot : slot + 1], weight[slot : slot + 1], hot)
            hot_ref[j * T : (j + 1) * T, :] = hot
        four = jnp.concatenate([blocks_ref[4 * i + j] for j in range(4)], axis=1)
        return summed + jnp.dot(four, hot_ref[...], preferred_element_type=F32)

    summed = lax.fori_loop(0, OWNERS // 4, of_four, jnp.zeros((T, T), F32), unroll=2)
    if outside:
        total[...] = summed
        copy = pltpu.make_async_copy(total, out, sem)
        copy.start()
        copy.wait()
    else:
        out[...] = summed.astype(out.dtype)


def dense_kernel(
    scalars, near_in, weights_in, w_agg_in, w_self_in, features_in, features_t_in, cotangent_in, arrived, near_1, near_2, near_3,
    hidden_ref, send_ref, keep_ref, agg_t, near_0, weights_t, w_agg, w_self, features, features_t, cotangent, sems,
):
    own_x, own_c = scalars[0], scalars[1]
    sources = (near_in, weights_in, w_agg_in, features_in, w_self_in, cotangent_in, features_t_in)
    targets = (near_0, weights_t, w_agg, features, w_self, cotangent, features_t)
    copies = [pltpu.make_async_copy(of, to, sems.at[i]) for i, (of, to) in enumerate(zip(sources, targets))]
    for copy in copies:
        copy.start()

    def total(k, own):
        quarter = lax.rem(own_x + (NX - k), NX)
        summed = arrived[quarter, 0].astype(F32)
        for y in range(1, NY):
            summed = summed + arrived[quarter, y].astype(F32)
        agg_t[pl.ds(pl.multiple_of(quarter * T, T), T), :] = summed + own[...].astype(F32)

    total(1, near_1)
    total(2, near_2)
    total(3, near_3)
    copies[0].wait()
    total(0, near_0)
    copies[1].wait()
    degree = 1.0 + jnp.sum(weights_t[...].astype(F32), axis=0, keepdims=True)
    aggregate = (agg_t[...] / degree).astype(BF16)
    contract = (((0,), (0,)), ((), ()))
    copies[2].wait()
    preact = lax.dot_general(aggregate, w_agg[...], contract, preferred_element_type=F32)
    copies[3].wait()
    copies[4].wait()
    preact = preact + jnp.dot(features[...], w_self[...], preferred_element_type=F32)
    sigma = jax.nn.sigmoid(preact)
    hidden_ref[...] = (preact * sigma).astype(BF16)
    copies[5].wait()
    grad_pre = (cotangent[...].astype(F32) * sigma * (1.0 + preact * (1.0 - sigma))).astype(BF16)
    copies[6].wait()
    for j in range(NX):
        columns = grad_pre[:, j * T : (j + 1) * T]
        keep_ref[NX + j] = columns
        send_ref[NX + j] = columns
        of_agg, of_self = aggregate[j * T : (j + 1) * T, :], features_t[j]
        keep_ref[j] = jnp.where(own_c == 0, of_agg, of_self)
        send_ref[j] = jnp.where(own_c == 0, of_self, of_agg)


def grad_kernel(keep_ref, received_ref, grad_ref):
    both = (keep_ref, received_ref)
    left = jnp.concatenate([ref[0:NX].reshape(NX * T, T) for ref in both], axis=1)
    for j in range(NX):
        right = jnp.concatenate([ref[NX + j] for ref in both], axis=0)
        product = jnp.dot(left, right, preferred_element_type=F32)
        grad_ref[:, :, j * T : (j + 1) * T] = product.reshape(OWNERS, grad_ref.shape[1], T).astype(BF16)


def add_kernel(parts_ref, sum_ref):
    summed = parts_ref[0].astype(F32)
    for i in range(1, parts_ref.shape[0]):
        summed = summed + parts_ref[i].astype(F32)
    sum_ref[...] = summed.astype(sum_ref.dtype)


def added(parts, dtype):
    (summed,) = vmem_call(
        add_kernel, "added", [], [parts], [(parts.shape[1:], dtype)], flops=parts.size, bytes_accessed=3 * parts.size
    )
    return summed


def body(features, edge_weights, neighbours, send_list, send_count, w_agg, w_self, cotangent):
    width = features.shape[1]
    z, x, y, c = (lax.axis_index(a).astype(jnp.int32) for a in ("z", X, Y, "c"))
    swap = [(0, 1), (1, 0)]

    features_t, quarters = vmem_call(
        spread_kernel, "spread", [], [], [((NX, T, T), BF16), ((NZ, NX, T, T), BF16)],
        scratch=[
            pltpu.VMEM((NX, T, T), BF16), pltpu.VMEM((NX, T, T), BF16),
            pltpu.SemaphoreType.DMA((NX,)), pltpu.SemaphoreType.DMA((NX, NZ + 1)),
        ],
        anywhere=[pltpu.with_memory_space_constraint(features, pltpu.HBM)], outside=2, bytes_accessed=1_500_000,
    )
    blocks = lax.all_to_all(quarters.reshape(OWNERS, T, T), ("z",) + X, 0, 0, tiled=True)

    codes_t = neighbours.T
    weights_t = edge_weights.T
    told = jnp.concatenate([send_count[0], send_list[0].reshape(1, GROUPS * CAP)], axis=1).astype(BF16)
    told = jnp.pad(told, ((0, 3), (0, T - GROUPS * (1 + CAP))))
    block, row = (codes_t // T).astype(BF16), (codes_t % T).astype(BF16)
    gap = jnp.zeros((16 - K_LOC, T), BF16)
    of_remote = jnp.concatenate([block[K_LOC:], row[K_LOC:], weights_t[K_LOC:], told], axis=0)
    of_local = jnp.concatenate([block[:K_LOC], gap, row[:K_LOC], gap, weights_t[:K_LOC], gap], axis=0)
    codes = jnp.concatenate([of_remote, of_local], axis=0)
    forward = [[(i, (i + k) % NX) for i in range(NX)] for k in range(NX)]
    codes = [codes] + [lax.ppermute(codes, X, forward[k]) for k in range(1, NX)]
    remote_codes, local_codes = vmem_call(
        split_kernel, "split", [], codes, [((NX, TOLD, T), BF16), ((NX, 48, T), BF16)],
        scratch=[pltpu.SemaphoreType.DMA((NX,))], outside=1, bytes_accessed=100_000,
    )
    remote_codes = lax.all_gather(remote_codes, Y + ("c",), axis=0)
    blocks, remote_codes = lax.optimization_barrier((blocks, remote_codes))
    told = remote_codes[:, :, 12].astype(jnp.int32)
    sources = jnp.arange(GROUPS, dtype=jnp.int32)[:, None, None]

    def of_source(group):
        here = jnp.sum(jnp.where(sources == group, told, 0), axis=0)
        return here, jnp.sum(jnp.where(sources < group, told[:, :, :GROUPS], 0), axis=0)

    own = jnp.stack([c, x])
    others = lax.ppermute(blocks, "c", swap)
    (part,) = vmem_call(
        first_kernel, "own_group", [own, *of_source(y * NC + c)], [blocks, remote_codes], [((NX, NY, T, T), F32)],
        flops=300_000_000, bytes_accessed=3_500_000,
    )
    (chip_sum,) = vmem_call(
        second_kernel, "other_group", [own, *of_source(y * NC + 1 - c)], [others, remote_codes, part], [((NX, NY, T, T), BF16)],
        scratch=[pltpu.VMEM((NX, NY, T, T), BF16), pltpu.SemaphoreType.DMA((NY,))], outside=1,
        flops=300_000_000, bytes_accessed=5_500_000,
    )
    arrived = lax.all_to_all(chip_sum.reshape(NX * NY, T, T), X + Y, 0, 0, tiled=True)

    near = []
    for k in (2, 1, 3, 0):
        (sums,) = vmem_call(
            functools.partial(local_kernel, k, k == 0), "local_sums", [jnp.stack([z, x])], [blocks, local_codes],
            [((T, T), BF16 if k else F32)],
            scratch=[pltpu.VMEM((4 * T, T), BF16)] + ([] if k else [pltpu.VMEM((T, T), F32), pltpu.SemaphoreType.DMA]),
            outside=int(k == 0), flops=150_000_000, bytes_accessed=1_200_000,
        )
        near.append(lax.ppermute(sums, X, forward[NX - k]) if k else sums)
    two, three, one, near_0 = near

    share = width // OWNERS
    operands = ((2 * NX, T, T), BF16)
    arrived, x, c = lax.optimization_barrier((arrived, x, c))
    outside = [near_0, weights_t, w_agg, w_self, features, features_t, cotangent]
    hidden, send, keep = vmem_call(
        dense_kernel, "dense", [jnp.stack([x, c])], [arrived.reshape(NX, NY, T, T), one, two, three],
        [((T, width), BF16), operands, operands],
        scratch=[pltpu.VMEM((width, T), F32)]
        + [pltpu.VMEM(of.shape, of.dtype) for of in outside]
        + [pltpu.SemaphoreType.DMA((len(outside),))],
        anywhere=[pltpu.with_memory_space_constraint(of, pltpu.HBM) for of in outside],
        flops=150_000_000, bytes_accessed=3_500_000, transcendentals=65536,
    )
    received = lax.ppermute(send, "c", swap)
    (chip_grad,) = vmem_call(
        grad_kernel, "gradient", [], [keep, received], [((OWNERS, share, width), BF16)], flops=300_000_000, bytes_accessed=1_000_000
    )
    plane = added(lax.all_to_all(chip_grad, ("z",) + X, 0, 0, tiled=True), BF16)
    planes = lax.all_to_all(jnp.broadcast_to(plane, (NY,) + plane.shape), Y, 0, 0, tiled=True)
    grads = lax.all_gather(added(planes, F32), "c", axis=0)
    return hidden, grads[0], grads[1]


def solution(mesh):
    axes = ("z",) + X + Y + ("c",)
    fine = Mesh(mesh.devices.reshape(NZ, 2, 2, 2, 2, 2, NC), axes)
    row, rep = ("z",) + X, Y + ("c",)
    nodes = P(row + rep, None)
    in_specs = (nodes, nodes, nodes, P(row, rep, None, None), P(row, rep, None), P(), P(), nodes)
    out_specs = (nodes, P(row, None), P(row, None))
    return jax.shard_map(body, mesh=fine, in_specs=in_specs, out_specs=out_specs, check_vma=False)
```

time: 143 us -> 142 us (level)
  Pallas kernels: 17.6 us -> 22.2 us
  starting transfers between devices: 49.7 us -> 47 us
  local copies, waits for them, and re-layouts: 2.78 us -> 1.06 us
    pallas_call x9 -> x12, Pallas kernels: 17.6 us -> 22.2 us  [vmem_call(): pl.pallas_call(kernel, in_specs=[pl.BlockSpec(memory_space=pltpu.SMEM)] *...]
    ppermute x3, waiting for transfers between devices: 3.77 us -> 0.01 us  [body(): near.append(lax.ppermute(sums, X, forward[NX - k]) if k else sums)]
    ppermute x3, waiting for transfers between devices: 1.71 us -> 3.55 us  [body(): codes = [codes] + [lax.ppermute(codes, X, forward[k]) for k in range(1, NX)]]
  transfers between devices with their start and end apart: 10 -> 10, of which waited for: 5 -> 5; matrix products, arithmetic and copies ran while one was open for 1% -> 1% of each run, Pallas kernels for 8% -> 10%
where the time goes in v9:
time: 142 us
  blocking collectives  61.7 us (43%)
  starting transfers between devices  47 us (33%)
  Pallas kernels  22.2 us (16%)
  waiting for transfers between devices  8.17 us (6%)
    all_to_all x1, blocking collectives, body(): plane = added(lax.all_to_all(chip_grad, ('z',) + X, 0, 0, tiled=True), BF16)  23.6 us
    pallas_call x12, Pallas kernels, vmem_call(): pl.pallas_call(kernel, in_specs=[pl.BlockSpec(memory_space=pltpu.SMEM)] *...  22.2 us
    all_gather x1, blocking collectives, body(): remote_codes = lax.all_gather(remote_codes, Y + ('c',), axis=0)  21.2 us
    all_to_all x1, starting transfers between devices, body(): lax.all_to_all(quarters.reshape(OWNERS, T, T), ('z',) + X, 0, 0, tiled=True)  13.7 us
    all_to_all x1, blocking collectives, body(): lax.all_to_all(jnp.broadcast_to(plane, (NY,) + plane.shape), Y, 0, 0, til...  12 us
    ppermute x3, starting transfers between devices, body(): near.append(lax.ppermute(sums, X, forward[NX - k]) if k else sums)  10.5 us
    ppermute x3, starting transfers between devices, body(): codes = [codes] + [lax.ppermute(codes, X, forward[k]) for k in range(1, NX)]  9.31 us
    ppermute x1, starting transfers between devices, body(): received = lax.ppermute(send, 'c', swap)  6.21 us
  transfers between devices with their start and end apart: 10, of which 5 were waited for; matrix products, arithmetic and copies ran while one was open for 1% of the time, Pallas kernels for 10%

profile of v9, /device:TPU:1, one launch (start us, length us, event | category | flops | bytes accessed | tf_op | source)
XLA Modules:
  0.0 141.7 jit_solution(5950054437108121351)
XLA Ops:
  0.6 0.0 copy-start.1
  0.7 2.3 %spread.1 = (bf16[4,128,128]{2,1,0:T(8,128)(2,1)}, bf16[8,4,128,128]{3,2,1,0:T(8,128)(2,1)}) custom-call(bf16[128,512]{1,0:T(8,128)(2,1)} %features_in.3), custom_call_target="tpu_custom_call" | custom-call | bytes 1500000 | tf_op jit(solution)/shard_map/spread/pallas_call | solution.py:28
  3.0 13.7 %all-to-all-start = ((bf16[32,128,128]{2,1,0:T(8,128)(2,1)}), bf16[32,128,128]{2,1,0:T(8,128)(2,1)S(1)}, u32[]{:S(2)}, u32[]{:S(2)}) async-start(bf16[32,128,128]{2,1,0:T(8,128)(2,1)} %bitcast.49), calls=%async_computation | async-start | bytes 2097152 | tf_op jit(solution)/shard_map/all_to_all | solution.py:217
  16.8 0.1 copy.13
  16.9 0.1 concatenate.20
  17.0 0.1 fusion.9
  17.1 0.2 concatenate.22.codes_0
  17.3 4.3 %collective-permute-start.2 = (bf16[64,128]{1,0:T(8,128)(2,1)S(1)}, bf16[64,128]{1,0:T(8,128)(2,1)S(1)}, u32[]{:S(2)}, u32[]{:S(2)}) collective-permute-start(bf16[64,128]{1,0:T(8,128)(2,1)S(1)} %concatenate.22.codes_0), channel_id=1, source_target_pairs={{0,48},{16,0},{32,16},{48,32},{1,49},{17,1},{33,17},{49,33},{2,50}... | collective-permute-start | bytes 49160 | tf_op jit(solution)/shard_map/ppermute | solution.py:229
  21.6 2.5 %collective-permute-start.1 = (bf16[64,128]{1,0:T(8,128)(2,1)S(1)}, bf16[64,128]{1,0:T(8,128)(2,1)S(1)}, u32[]{:S(2)}, u32[]{:S(2)}) collective-permute-start(bf16[64,128]{1,0:T(8,128)(2,1)S(1)} %concatenate.22.codes_0), channel_id=1, source_target_pairs={{0,32},{16,48},{32,0},{48,16},{1,33},{17,49},{33,1},{49,17},{2,34}... | collective-permute-start | bytes 49160 | tf_op jit(solution)/shard_map/ppermute | solution.py:229
  24.1 2.5 %collective-permute-start = (bf16[64,128]{1,0:T(8,128)(2,1)S(1)}, bf16[64,128]{1,0:T(8,128)(2,1)S(1)}, u32[]{:S(2)}, u32[]{:S(2)}) collective-permute-start(bf16[64,128]{1,0:T(8,128)(2,1)S(1)} %concatenate.22.codes_0), channel_id=1, source_target_pairs={{0,16},{16,32},{32,48},{48,0},{1,17},{17,33},{33,49},{49,1},{2,18}... | collective-permute-start | bytes 49160 | tf_op jit(solution)/shard_map/ppermute | solution.py:229
  26.6 0.0 collective-permute-done.2.codes_3
  26.6 1.4 collective-permute-done.1.codes_2
  28.0 2.2 %collective-permute-done.codes_1 = bf16[64,128]{1,0:T(8,128)(2,1)S(1)} collective-permute-done((bf16[64,128]{1,0:T(8,128)(2,1)S(1)}, bf16[64,128]{1,0:T(8,128)(2,1)S(1)}, u32[]{:S(2)}, u32[]{:S(2)}) %collective-permute-start) | collective-permute-done | bytes 16416 | tf_op jit(solution)/shard_map/ppermute | solution.py:229
  30.2 0.6 split.1
  30.8 21.2 %all-gather = bf16[64,16,128]{2,1,0:T(8,128)(2,1)S(1)} all-gather(bf16[4,16,128]{2,1,0:T(8,128)(2,1)S(1)} %get-tuple-element.16), channel_id=2, replica_groups=mesh['z'=8,'x1'=2,'x0'=2,'y2'=2,'y1'=2,'y0'=2,'c'=2] {'y2','y1','y0','c'}, dimensions={0}, use_global_device_ids=true | all-gather | bytes 278528 | tf_op jit(solution)/shard_map/all_gather | solution.py:234
  52.0 0.0 all-to-all-done.blocks_ref
  52.0 2.1 %collective-permute-start.3 = (bf16[32,128,128]{2,1,0:T(8,128)(2,1)S(1)}, bf16[32,128,128]{2,1,0:T(8,128)(2,1)S(1)}, u32[]{:S(2)}, u32[]{:S(2)}) collective-permute-start(bf16[32,128,128]{2,1,0:T(8,128)(2,1)S(1)} %all-to-all-done.blocks_ref), channel_id=1, source_target_pairs={{0,1},{1,0},{2,3},{3,2},{4,5},{5,4},{6,7},{7,6},{8,9},{9,8},{10,11... | collective-permute-start | bytes 3145736 | tf_op jit(solution)/shard_map/ppermute | solution.py:244
  54.1 0.1 pad_add_fusion.own
  54.2 0.1 slice_convert_fusion
  54.2 0.1 select_reduce_fusion
  54.4 0.1 select_reduce_fusion.1
  54.5 1.6 %own_group.1.part_ref = f32[4,8,128,128]{3,2,1,0:T(8,128)S(1)} custom-call(s32[2]{0:T(128)S(1)} %pad_add_fusion.own, s32[4,128]{1,0:T(4,128)S(1)} %get-tuple-element.29.here, s32[4,16]{1,0:T(4,128)S(1)} %get-tuple-element.27.before, bf16[32,128,128]{2,1,0:T(8,128)(2,1)S(1)} %all-to-all-done.blocks_ref, bf16[16,4,16,128]{3,2,1,0:T(8,128)(2,1)S(1)} %bitcast.46), custom_call_target="tpu_custom_call" | custom-call | flops 300000000 | bytes 3500000 | tf_op jit(solution)/shard_map/own_group/pallas_call | solution.py:28
  56.1 0.4 collective-permute-done.3.blocks_ref
  56.5 2.5 %other_group.1 = bf16[4,8,128,128]{3,2,1,0:T(8,128)(2,1)} custom-call(s32[2]{0:T(128)S(1)} %pad_add_fusion.own, s32[4,128]{1,0:T(4,128)S(1)} %get-tuple-element.30.here, s32[4,16]{1,0:T(4,128)S(1)} %get-tuple-element.28.before, bf16[32,128,128]{2,1,0:T(8,128)(2,1)S(1)} %collective-permute-done.3.blocks_ref, bf16[16,4,16,128]{3,2,1,0:T(8,128)(2,1)S(1)} %bitcast.47, ...), custom_call_target="tpu_custom_call" | custom-call | flops 300000000 | bytes 5500000 | tf_op jit(solution)/shard_map/other_group/pallas_call | solution.py:28
  59.0 0.0 copy-start
  59.1 5.1 %all-to-all-start.1 = ((bf16[32,128,128]{2,1,0:T(8,128)(2,1)}), bf16[32,128,128]{2,1,0:T(8,128)(2,1)S(1)}, u32[]{:S(2)}, u32[]{:S(2)}) async-start(bf16[32,128,128]{2,1,0:T(8,128)(2,1)} %bitcast.48), calls=%async_computation.1 | async-start | bytes 2097152 | tf_op jit(solution)/shard_map/all_to_all | solution.py:254
  64.2 0.1 pad_add_fusion.2.scalars
  64.3 2.7 %local_sums.5 = bf16[128,128]{1,0:T(8,128)(2,1)S(1)} custom-call(s32[2]{0:T(128)S(1)} %pad_add_fusion.2.scalars, bf16[32,128,128]{2,1,0:T(8,128)(2,1)S(1)} %all-to-all-done.blocks_ref, bf16[4,48,128]{2,1,0:T(8,128)(2,1)S(1)} %copy-done), custom_call_target="tpu_custom_call" | custom-call | flops 150000000 | bytes 1200000 | tf_op jit(solution)/shard_map/local_sums/pallas_call | solution.py:28
  67.0 3.1 %collective-permute-start.4 = (bf16[128,128]{1,0:T(8,128)(2,1)S(1)}, bf16[128,128]{1,0:T(8,128)(2,1)S(1)}, u32[]{:S(2)}, u32[]{:S(2)}) collective-permute-start(bf16[128,128]{1,0:T(8,128)(2,1)S(1)} %local_sums.5), channel_id=1, source_target_pairs={{0,16},{16,32},{32,48},{48,0},{1,17},{17,33},{33,49},{49,1},{2,18}... | collective-permute-start | bytes 98312 | tf_op jit(solution)/shard_map/ppermute | solution.py:264
  70.2 2.7 %local_sums.6 = bf16[128,128]{1,0:T(8,128)(2,1)S(1)} custom-call(s32[2]{0:T(128)S(1)} %pad_add_fusion.2.scalars, bf16[32,128,128]{2,1,0:T(8,128)(2,1)S(1)} %all-to-all-done.blocks_ref, bf16[4,48,128]{2,1,0:T(8,128)(2,1)S(1)} %copy-done), custom_call_target="tpu_custom_call" | custom-call | flops 150000000 | bytes 1200000 | tf_op jit(solution)/shard_map/local_sums/pallas_call | solution.py:28
  72.9 4.3 %collective-permute-start.5 = (bf16[128,128]{1,0:T(8,128)(2,1)S(1)}, bf16[128,128]{1,0:T(8,128)(2,1)S(1)}, u32[]{:S(2)}, u32[]{:S(2)}) collective-permute-start(bf16[128,128]{1,0:T(8,128)(2,1)S(1)} %local_sums.6), channel_id=1, source_target_pairs={{0,32},{16,48},{32,0},{48,16},{1,33},{17,49},{33,1},{49,17},{2,34}... | collective-permute-start | bytes 98312 | tf_op jit(solution)/shard_map/ppermute | solution.py:264
  77.3 2.7 %local_sums.7 = bf16[128,128]{1,0:T(8,128)(2,1)S(1)} custom-call(s32[2]{0:T(128)S(1)} %pad_add_fusion.2.scalars, bf16[32,128,128]{2,1,0:T(8,128)(2,1)S(1)} %all-to-all-done.blocks_ref, bf16[4,48,128]{2,1,0:T(8,128)(2,1)S(1)} %copy-done), custom_call_target="tpu_custom_call" | custom-call | flops 150000000 | bytes 1200000 | tf_op jit(solution)/shard_map/local_sums/pallas_call | solution.py:28
  80.0 3.0 %collective-permute-start.6 = (bf16[128,128]{1,0:T(8,128)(2,1)S(1)}, bf16[128,128]{1,0:T(8,128)(2,1)S(1)}, u32[]{:S(2)}, u32[]{:S(2)}) collective-permute-start(bf16[128,128]{1,0:T(8,128)(2,1)S(1)} %local_sums.7), channel_id=1, source_target_pairs={{0,48},{16,0},{32,16},{48,32},{1,49},{17,1},{33,17},{49,33},{2,50}... | collective-permute-start | bytes 98312 | tf_op jit(solution)/shard_map/ppermute | solution.py:264
  83.1 3.4 %local_sums.4.near_in = f32[128,128]{1,0:T(8,128)} custom-call(s32[2]{0:T(128)S(1)} %pad_add_fusion.2.scalars, bf16[32,128,128]{2,1,0:T(8,128)(2,1)S(1)} %all-to-all-done.blocks_ref, bf16[4,48,128]{2,1,0:T(8,128)(2,1)S(1)} %copy-done), custom_call_target="tpu_custom_call" | custom-call | flops 150000000 | bytes 1200000 | tf_op jit(solution)/shard_map/local_sums/pallas_call | solution.py:28
  86.5 3.0 %all-to-all-done.1 = bf16[32,128,128]{2,1,0:T(8,128)(2,1)S(1)} async-done(((bf16[32,128,128]{2,1,0:T(8,128)(2,1)}), bf16[32,128,128]{2,1,0:T(8,128)(2,1)S(1)}, u32[]{:S(2)}, u32[]{:S(2)}) %all-to-all-start.1) | async-done | bytes 1048608 | tf_op jit(solution)/shard_map/all_to_all | solution.py:254
  89.5 0.1 pad_add_fusion.1.scalars
  89.6 0.0 collective-permute-done.4.near_1
  89.6 0.0 collective-permute-done.5.near_2
  89.6 0.0 collective-permute-done.6.near_3
  89.6 3.0 %dense.1 = (bf16[128,512]{1,0:T(8,128)(2,1)}, bf16[8,128,128]{2,1,0:T(8,128)(2,1)S(1)}, bf16[8,128,128]{2,1,0:T(8,128)(2,1)S(1)}) custom-call(s32[2]{0:T(128)S(1)} %pad_add_fusion.1.scalars, f32[128,128]{1,0:T(8,128)} %local_sums.4.near_in, bf16[16,128]{1,0:T(8,128)(2,1)} %bitcast.52, bf16[512,512]{1,0:T(8,128)(2,1)} %w_agg_in.1, ...), custom_call_target="tpu_custom_call" | custom-call | flops 150000000 | bytes 3500000 | tf_op jit(solution)/shard_map/dense/pallas_call | solution.py:28
  92.6 6.2 %collective-permute-start.7 = (bf16[8,128,128]{2,1,0:T(8,128)(2,1)S(1)}, bf16[8,128,128]{2,1,0:T(8,128)(2,1)S(1)}, u32[]{:S(2)}, u32[]{:S(2)}) collective-permute-start(bf16[8,128,128]{2,1,0:T(8,128)(2,1)S(1)} %get-tuple-element.26), channel_id=1, source_target_pairs={{0,1},{1,0},{2,3},{3,2},{4,5},{5,4},{6,7},{7,6},{8,9},{9,8},{10,11... | collective-permute-start | bytes 786440 | tf_op jit(solution)/shard_map/ppermute | solution.py:280
  98.8 1.1 collective-permute-done.7.received_ref
  99.9 0.4 gradient.1
  100.3 23.6 %all_to_all.20.parts_ref = bf16[32,16,512]{2,1,0:T(8,128)(2,1)S(1)} all-to-all(bf16[32,16,512]{2,1,0:T(8,128)(2,1)S(1)} %gradient.1), channel_id=1, replica_groups=mesh['z'=8,'x1'=2,'x0'=2,'y2'=2,'y1'=2,'y0'=2,'c'=2] {'z','x1','x0'}, dimensions={0} | all-to-all | bytes 1048576 | tf_op jit(solution)/shard_map/all_to_all | solution.py:284
  123.9 0.1 added.2
  124.0 12.0 %all_to_all.21.parts_ref = bf16[8,16,512]{2,1,0:T(8,128)(2,1)S(1)} all-to-all(bf16[8,16,512]{2,1,0:T(8,128)(2,1)S(1)} %broadcast_in_dim.50), channel_id=1, replica_groups=mesh['z'=8,'x1'=2,'x0'=2,'y2'=2,'y1'=2,'y0'=2,'c'=2] {'y2','y1','y0'}, dimensions={0} | all-to-all | bytes 262144 | tf_op jit(solution)/shard_map/all_to_all | solution.py:285
  136.0 5.0 %all-gather.1 = f32[32,512]{1,0:T(8,128)S(1)} all-gather(f32[16,512]{1,0:T(8,128)S(1)} %added.3), channel_id=3, replica_groups=mesh['z'=8,'x1'=2,'x0'=2,'y2'=2,'y1'=2,'y0'=2,'c'=2] {'c'}, dimensions={0}, use_global_device_ids=true | all-gather | bytes 98304 | tf_op jit(solution)/shard_map/all_gather | solution.py:286
  141.1 0.6 fusion.11
  (19 shorter events, 0.1 us)
Async XLA Ops:
  0.6 16.1 %copy-start.3 = (s32[1,1,16,2]{2,3,1,0:T(2,128)S(1)}, s32[1,1,16,2]{2,3,1,0:T(2,128)}, u32[]{:S(2)}) copy-start(s32[1,1,16,2]{2,3,1,0:T(2,128)} %param.11) | copy-start | bytes 388
  0.6 16.1 %copy-start.1 = (bf16[128,16]{0,1:T(8,128)(2,1)S(1)}, bf16[128,16]{0,1:T(8,128)(2,1)}, u32[]{:S(2)}) copy-start(bf16[128,16]{0,1:T(8,128)(2,1)} %param.9) | copy-start | bytes 12292
  0.7 16.3 %copy-start.2 = (s32[128,16]{0,1:T(8,128)S(1)}, s32[128,16]{0,1:T(8,128)}, u32[]{:S(2)}) copy-start(s32[128,16]{0,1:T(8,128)} %param.10) | copy-start | bytes 24580
  0.7 16.4 %copy-start.4 = (s32[1,1,16]{2,1,0:T(1,128)S(1)}, s32[1,1,16]{2,1,0:T(1,128)}, u32[]{:S(2)}) copy-start(s32[1,1,16]{2,1,0:T(1,128)} %param.12) | copy-start | bytes 196
  3.0 49.0 %all-to-all-start = ((bf16[32,128,128]{2,1,0:T(8,128)(2,1)}), bf16[32,128,128]{2,1,0:T(8,128)(2,1)S(1)}, u32[]{:S(2)}, u32[]{:S(2)}) async-start(bf16[32,128,128]{2,1,0:T(8,128)(2,1)} %bitcast.49), calls=%async_computation | async-start | bytes 2097152 | tf_op jit(solution)/shard_map/all_to_all | solution.py:217
  17.3 9.3 %collective-permute-start.2 = (bf16[64,128]{1,0:T(8,128)(2,1)S(1)}, bf16[64,128]{1,0:T(8,128)(2,1)S(1)}, u32[]{:S(2)}, u32[]{:S(2)}) collective-permute-start(bf16[64,128]{1,0:T(8,128)(2,1)S(1)} %concatenate.22.codes_0), channel_id=1, source_target_pairs={{0,48},{16,0},{32,16},{48,32},{1,49},{17,1},{33,17},{49,33},{2,50}... | collective-permute-start | bytes 49160 | tf_op jit(solution)/shard_map/ppermute | solution.py:229
  21.6 6.4 %collective-permute-start.1 = (bf16[64,128]{1,0:T(8,128)(2,1)S(1)}, bf16[64,128]{1,0:T(8,128)(2,1)S(1)}, u32[]{:S(2)}, u32[]{:S(2)}) collective-permute-start(bf16[64,128]{1,0:T(8,128)(2,1)S(1)} %concatenate.22.codes_0), channel_id=1, source_target_pairs={{0,32},{16,48},{32,0},{48,16},{1,33},{17,49},{33,1},{49,17},{2,34}... | collective-permute-start | bytes 49160 | tf_op jit(solution)/shard_map/ppermute | solution.py:229
  24.1 6.1 %collective-permute-start = (bf16[64,128]{1,0:T(8,128)(2,1)S(1)}, bf16[64,128]{1,0:T(8,128)(2,1)S(1)}, u32[]{:S(2)}, u32[]{:S(2)}) collective-permute-start(bf16[64,128]{1,0:T(8,128)(2,1)S(1)} %concatenate.22.codes_0), channel_id=1, source_target_pairs={{0,16},{16,32},{32,48},{48,0},{1,17},{17,33},{33,49},{49,1},{2,18}... | collective-permute-start | bytes 49160 | tf_op jit(solution)/shard_map/ppermute | solution.py:229
  52.0 4.5 %collective-permute-start.3 = (bf16[32,128,128]{2,1,0:T(8,128)(2,1)S(1)}, bf16[32,128,128]{2,1,0:T(8,128)(2,1)S(1)}, u32[]{:S(2)}, u32[]{:S(2)}) collective-permute-start(bf16[32,128,128]{2,1,0:T(8,128)(2,1)S(1)} %all-to-all-done.blocks_ref), channel_id=1, source_target_pairs={{0,1},{1,0},{2,3},{3,2},{4,5},{5,4},{6,7},{7,6},{8,9},{9,8},{10,11... | collective-permute-start | bytes 3145736 | tf_op jit(solution)/shard_map/ppermute | solution.py:244
  59.0 5.2 %copy-start = (bf16[4,48,128]{2,1,0:T(8,128)(2,1)S(1)}, bf16[4,48,128]{2,1,0:T(8,128)(2,1)}, u32[]{:S(2)}) copy-start(bf16[4,48,128]{2,1,0:T(8,128)(2,1)} %get-tuple-element.21.told_ref) | copy-start | bytes 147460
  59.1 30.4 %all-to-all-start.1 = ((bf16[32,128,128]{2,1,0:T(8,128)(2,1)}), bf16[32,128,128]{2,1,0:T(8,128)(2,1)S(1)}, u32[]{:S(2)}, u32[]{:S(2)}) async-start(bf16[32,128,128]{2,1,0:T(8,128)(2,1)} %bitcast.48), calls=%async_computation.1 | async-start | bytes 2097152 | tf_op jit(solution)/shard_map/all_to_all | solution.py:254
  67.0 22.5 %collective-permute-start.4 = (bf16[128,128]{1,0:T(8,128)(2,1)S(1)}, bf16[128,128]{1,0:T(8,128)(2,1)S(1)}, u32[]{:S(2)}, u32[]{:S(2)}) collective-permute-start(bf16[128,128]{1,0:T(8,128)(2,1)S(1)} %local_sums.5), channel_id=1, source_target_pairs={{0,16},{16,32},{32,48},{48,0},{1,17},{17,33},{33,49},{49,1},{2,18}... | collective-permute-start | bytes 98312 | tf_op jit(solution)/shard_map/ppermute | solution.py:264
  72.9 16.6 %collective-permute-start.5 = (bf16[128,128]{1,0:T(8,128)(2,1)S(1)}, bf16[128,128]{1,0:T(8,128)(2,1)S(1)}, u32[]{:S(2)}, u32[]{:S(2)}) collective-permute-start(bf16[128,128]{1,0:T(8,128)(2,1)S(1)} %local_sums.6), channel_id=1, source_target_pairs={{0,32},{16,48},{32,0},{48,16},{1,33},{17,49},{33,1},{49,17},{2,34}... | collective-permute-start | bytes 98312 | tf_op jit(solution)/shard_map/ppermute | solution.py:264
  80.0 9.5 %collective-permute-start.6 = (bf16[128,128]{1,0:T(8,128)(2,1)S(1)}, bf16[128,128]{1,0:T(8,128)(2,1)S(1)}, u32[]{:S(2)}, u32[]{:S(2)}) collective-permute-start(bf16[128,128]{1,0:T(8,128)(2,1)S(1)} %local_sums.7), channel_id=1, source_target_pairs={{0,48},{16,0},{32,16},{48,32},{1,49},{17,1},{33,17},{49,33},{2,50}... | collective-permute-start | bytes 98312 | tf_op jit(solution)/shard_map/ppermute | solution.py:264
  92.6 7.4 %collective-permute-start.7 = (bf16[8,128,128]{2,1,0:T(8,128)(2,1)S(1)}, bf16[8,128,128]{2,1,0:T(8,128)(2,1)S(1)}, u32[]{:S(2)}, u32[]{:S(2)}) collective-permute-start(bf16[8,128,128]{2,1,0:T(8,128)(2,1)S(1)} %get-tuple-element.26), channel_id=1, source_target_pairs={{0,1},{1,0},{2,3},{3,2},{4,5},{5,4},{6,7},{7,6},{8,9},{9,8},{10,11... | collective-permute-start | bytes 786440 | tf_op jit(solution)/shard_map/ppermute | solution.py:280

commit v10 on v9

--- a/solution.py
+++ b/solution.py
@@ -40,19 +40,12 @@
     )(*scalar_inputs, *anywhere, *array_inputs)
 
 
-def spread_kernel(features_in, features_out, quarters_ref, quarters, features_t, sems_in, sems):
-    loads = [pltpu.make_async_copy(features_in.at[:, x * T : (x + 1) * T], quarters.at[x], sems_in.at[x]) for x in range(NX)]
-    for load in loads:
-        load.start()
-    copies = []
-    for x in range(NX):
-        loads[x].wait()
-        features_t[x] = quarters[x].astype(F32).T.astype(BF16)
-        for z in range(NZ):
-            copies.append(pltpu.make_async_copy(features_t.at[x], quarters_ref.at[z, x], sems.at[x, z]))
-            copies[-1].start()
-        copies.append(pltpu.make_async_copy(features_t.at[x], features_out.at[x], sems.at[x, NZ]))
-        copies[-1].start()
+def spread_kernel(features_ref, features_out, quarters_ref, features_t, sems):
+    features_t[...] = features_ref[...].astype(F32).T.astype(BF16).reshape(NX, T, T)
+    copies = [pltpu.make_async_copy(features_t, quarters_ref.at[z], sems.at[z]) for z in range(NZ)]
+    copies.append(pltpu.make_async_copy(features_t, features_out, sems.at[NZ]))
+    for copy in copies:
+        copy.start()
     for copy in copies:
         copy.wait()
 
@@ -129,46 +122,39 @@
         copy.start()
         copy.wait()
     else:
-        out[...] = summed.astype(out.dtype)
+        out[...] = summed
 
 
 def dense_kernel(
-    scalars, near_in, weights_in, w_agg_in, w_self_in, features_in, features_t_in, cotangent_in, arrived, near_1, near_2, near_3,
-    hidden_ref, send_ref, keep_ref, agg_t, near_0, weights_t, w_agg, w_self, features, features_t, cotangent, sems,
+    scalars, near_0_in, near_1_in, near_2_in, near_3_in, weights_in, features_t_in, arrived, features, w_agg, w_self, cotangent,
+    hidden_ref, send_ref, keep_ref, agg_t, near_0, near_1, near_2, near_3, weights_t, features_t, sems,
 ):
     own_x, own_c = scalars[0], scalars[1]
-    sources = (near_in, weights_in, w_agg_in, features_in, w_self_in, cotangent_in, features_t_in)
-    targets = (near_0, weights_t, w_agg, features, w_self, cotangent, features_t)
+    sources = (near_0_in, near_1_in, near_2_in, near_3_in, weights_in, features_t_in)
+    targets = (near_0, near_1, near_2, near_3, weights_t, features_t)
     copies = [pltpu.make_async_copy(of, to, sems.at[i]) for i, (of, to) in enumerate(zip(sources, targets))]
     for copy in copies:
         copy.start()
 
-    def total(k, own):
+    for x in range(NX):
+        summed = arrived[x, 0].astype(F32)
+        for y in range(1, NY):
+            summed = summed + arrived[x, y].astype(F32)
+        agg_t[x * T : (x + 1) * T, :] = summed
+    for k, near in enumerate((near_0, near_1, near_2, near_3)):
+        copies[k].wait()
         quarter = lax.rem(own_x + (NX - k), NX)
-        summed = arrived[quarter, 0].astype(F32)
-        for y in range(1, NY):
-            summed = summed + arrived[quarter, y].astype(F32)
-        agg_t[pl.ds(pl.multiple_of(quarter * T, T), T), :] = summed + own[...].astype(F32)
-
-    total(1, near_1)
-    total(2, near_2)
-    total(3, near_3)
-    copies[0].wait()
-    total(0, near_0)
-    copies[1].wait()
+        agg_t[pl.ds(pl.multiple_of(quarter * T, T), T), :] += near[...]
+    copies[4].wait()
     degree = 1.0 + jnp.sum(weights_t[...].astype(F32), axis=0, keepdims=True)
     aggregate = (agg_t[...] / degree).astype(BF16)
     contract = (((0,), (0,)), ((), ()))
-    copies[2].wait()
     preact = lax.dot_general(aggregate, w_agg[...], contract, preferred_element_type=F32)
-    copies[3].wait()
-    copies[4].wait()
     preact = preact + jnp.dot(features[...], w_self[...], preferred_element_type=F32)
     sigma = jax.nn.sigmoid(preact)
     hidden_ref[...] = (preact * sigma).astype(BF16)
+    grad_pre = (cotangent[...].astype(F32) * sigma * (1.0 + preact * (1.0 - sigma))).astype(BF16)
     copies[5].wait()
-    grad_pre = (cotangent[...].astype(F32) * sigma * (1.0 + preact * (1.0 - sigma))).astype(BF16)
-    copies[6].wait()
     for j in range(NX):
         columns = grad_pre[:, j * T : (j + 1) * T]
         keep_ref[NX + j] = columns
@@ -207,12 +193,8 @@
     swap = [(0, 1), (1, 0)]
 
     features_t, quarters = vmem_call(
-        spread_kernel, "spread", [], [], [((NX, T, T), BF16), ((NZ, NX, T, T), BF16)],
-        scratch=[
-            pltpu.VMEM((NX, T, T), BF16), pltpu.VMEM((NX, T, T), BF16),
-            pltpu.SemaphoreType.DMA((NX,)), pltpu.SemaphoreType.DMA((NX, NZ + 1)),
-        ],
-        anywhere=[pltpu.with_memory_space_constraint(features, pltpu.HBM)], outside=2, bytes_accessed=1_500_000,
+        spread_kernel, "spread", [], [features], [((NX, T, T), BF16), ((NZ, NX, T, T), BF16)],
+        scratch=[pltpu.VMEM((NX, T, T), BF16), pltpu.SemaphoreType.DMA((NZ + 1,))], outside=2, bytes_accessed=1_500_000,
     )
     blocks = lax.all_to_all(quarters.reshape(OWNERS, T, T), ("z",) + X, 0, 0, tiled=True)
 
@@ -257,7 +239,7 @@
     for k in (2, 1, 3, 0):
         (sums,) = vmem_call(
             functools.partial(local_kernel, k, k == 0), "local_sums", [jnp.stack([z, x])], [blocks, local_codes],
-            [((T, T), BF16 if k else F32)],
+            [((T, T), F32)],
             scratch=[pltpu.VMEM((4 * T, T), BF16)] + ([] if k else [pltpu.VMEM((T, T), F32), pltpu.SemaphoreType.DMA]),
             outside=int(k == 0), flops=150_000_000, bytes_accessed=1_200_000,
         )
@@ -267,9 +249,9 @@
     share = width // OWNERS
     operands = ((2 * NX, T, T), BF16)
     arrived, x, c = lax.optimization_barrier((arrived, x, c))
-    outside = [near_0, weights_t, w_agg, w_self, features, features_t, cotangent]
+    outside = [near_0, one, two, three, weights_t, features_t]
     hidden, send, keep = vmem_call(
-        dense_kernel, "dense", [jnp.stack([x, c])], [arrived.reshape(NX, NY, T, T), one, two, three],
+        dense_kernel, "dense", [jnp.stack([x, c])], [arrived.reshape(NX, NY, T, T), features, w_agg, w_self, cotangent],
         [((T, width), BF16), operands, operands],
         scratch=[pltpu.VMEM((width, T), F32)]
         + [pltpu.VMEM(of.shape, of.dtype) for of in outside]

time: 142 us -> 142 us (level)
  transfers between devices with their start and end apart: 10 -> 10, of which waited for: 5 -> 5; matrix products, arithmetic and copies ran while one was open for 1% -> 1% of each run, Pallas kernels for 10% -> 11%
where the time goes in v10:
time: 142 us; the launch traced here: 141 us
  blocking collectives  61.8 us (44%)
  starting transfers between devices  46.9 us (33%)
  Pallas kernels  21.9 us (15%)
  waiting for transfers between devices  6.95 us (5%)
  local copies, waits for them, and re-layouts  1.97 us (1%)
    all_to_all x1, blocking collectives, body(): plane = added(lax.all_to_all(chip_grad, ('z',) + X, 0, 0, tiled=True), BF16)  23.6 us
    pallas_call x12, Pallas kernels, vmem_call(): pl.pallas_call(kernel, in_specs=[pl.BlockSpec(memory_space=pltpu.SMEM)] *...  21.9 us
    all_gather x1, blocking collectives, body(): remote_codes = lax.all_gather(remote_codes, Y + ('c',), axis=0)  21.2 us
    all_to_all x1, starting transfers between devices, body(): lax.all_to_all(quarters.reshape(OWNERS, T, T), ('z',) + X, 0, 0, tiled=True)  13.7 us
    all_to_all x1, blocking collectives, body(): lax.all_to_all(jnp.broadcast_to(plane, (NY,) + plane.shape), Y, 0, 0, til...  12 us
    ppermute x3, starting transfers between devices, body(): near.append(lax.ppermute(sums, X, forward[NX - k]) if k else sums)  10.5 us
    ppermute x3, starting transfers between devices, body(): codes = [codes] + [lax.ppermute(codes, X, forward[k]) for k in range(1, NX)]  9.31 us
    ppermute x1, starting transfers between devices, body(): received = lax.ppermute(send, 'c', swap)  6.19 us
  transfers between devices with their start and end apart: 10, of which 5 were waited for; matrix products, arithmetic and copies ran while one was open for 1% of the time, Pallas kernels for 11%

profile of v10, /device:TPU:1, one launch (start us, length us, event | category | flops | bytes accessed | tf_op | source)
XLA Modules:
  0.0 141.1 jit_solution(14171947137991691847)
XLA Ops:
  0.6 0.0 copy-start.1
  0.6 0.9 copy-done.1
  1.5 1.2 spread.1
  2.8 13.7 %all-to-all-start = ((bf16[32,128,128]{2,1,0:T(8,128)(2,1)}), bf16[32,128,128]{2,1,0:T(8,128)(2,1)S(1)}, u32[]{:S(2)}, u32[]{:S(2)}) async-start(bf16[32,128,128]{2,1,0:T(8,128)(2,1)} %bitcast.49), calls=%async_computation | async-start | bytes 2097152 | tf_op jit(solution)/shard_map/all_to_all | solution.py:199
  16.6 0.1 copy.13
  16.7 0.1 concatenate.20
  16.8 0.1 fusion.9
  16.9 0.2 concatenate.22.codes_0
  17.1 4.3 %collective-permute-start.2 = (bf16[64,128]{1,0:T(8,128)(2,1)S(1)}, bf16[64,128]{1,0:T(8,128)(2,1)S(1)}, u32[]{:S(2)}, u32[]{:S(2)}) collective-permute-start(bf16[64,128]{1,0:T(8,128)(2,1)S(1)} %concatenate.22.codes_0), channel_id=1, source_target_pairs={{0,48},{16,0},{32,16},{48,32},{1,49},{17,1},{33,17},{49,33},{2,50}... | collective-permute-start | bytes 49160 | tf_op jit(solution)/shard_map/ppermute | solution.py:211
  21.5 2.5 %collective-permute-start.1 = (bf16[64,128]{1,0:T(8,128)(2,1)S(1)}, bf16[64,128]{1,0:T(8,128)(2,1)S(1)}, u32[]{:S(2)}, u32[]{:S(2)}) collective-permute-start(bf16[64,128]{1,0:T(8,128)(2,1)S(1)} %concatenate.22.codes_0), channel_id=1, source_target_pairs={{0,32},{16,48},{32,0},{48,16},{1,33},{17,49},{33,1},{49,17},{2,34}... | collective-permute-start | bytes 49160 | tf_op jit(solution)/shard_map/ppermute | solution.py:211
  23.9 2.5 %collective-permute-start = (bf16[64,128]{1,0:T(8,128)(2,1)S(1)}, bf16[64,128]{1,0:T(8,128)(2,1)S(1)}, u32[]{:S(2)}, u32[]{:S(2)}) collective-permute-start(bf16[64,128]{1,0:T(8,128)(2,1)S(1)} %concatenate.22.codes_0), channel_id=1, source_target_pairs={{0,16},{16,32},{32,48},{48,0},{1,17},{17,33},{33,49},{49,1},{2,18}... | collective-permute-start | bytes 49160 | tf_op jit(solution)/shard_map/ppermute | solution.py:211
  26.4 0.0 collective-permute-done.2.codes_3
  26.4 1.4 collective-permute-done.1.codes_2
  27.8 2.2 %collective-permute-done.codes_1 = bf16[64,128]{1,0:T(8,128)(2,1)S(1)} collective-permute-done((bf16[64,128]{1,0:T(8,128)(2,1)S(1)}, bf16[64,128]{1,0:T(8,128)(2,1)S(1)}, u32[]{:S(2)}, u32[]{:S(2)}) %collective-permute-start) | collective-permute-done | bytes 16416 | tf_op jit(solution)/shard_map/ppermute | solution.py:211
  30.0 0.6 split.1
  30.7 21.2 %all-gather = bf16[64,16,128]{2,1,0:T(8,128)(2,1)S(1)} all-gather(bf16[4,16,128]{2,1,0:T(8,128)(2,1)S(1)} %get-tuple-element.16), channel_id=2, replica_groups=mesh['z'=8,'x1'=2,'x0'=2,'y2'=2,'y1'=2,'y0'=2,'c'=2] {'y2','y1','y0','c'}, dimensions={0}, use_global_device_ids=true | all-gather | bytes 278528 | tf_op jit(solution)/shard_map/all_gather | solution.py:216
  51.8 0.0 all-to-all-done.blocks_ref
  51.8 2.1 %collective-permute-start.3 = (bf16[32,128,128]{2,1,0:T(8,128)(2,1)S(1)}, bf16[32,128,128]{2,1,0:T(8,128)(2,1)S(1)}, u32[]{:S(2)}, u32[]{:S(2)}) collective-permute-start(bf16[32,128,128]{2,1,0:T(8,128)(2,1)S(1)} %all-to-all-done.blocks_ref), channel_id=1, source_target_pairs={{0,1},{1,0},{2,3},{3,2},{4,5},{5,4},{6,7},{7,6},{8,9},{9,8},{10,11... | collective-permute-start | bytes 3145736 | tf_op jit(solution)/shard_map/ppermute | solution.py:226
  53.9 0.1 pad_add_fusion.own
  54.0 0.1 slice_convert_fusion
  54.1 0.1 select_reduce_fusion
  54.2 0.1 select_reduce_fusion.1
  54.3 1.6 %own_group.1.part_ref = f32[4,8,128,128]{3,2,1,0:T(8,128)S(1)} custom-call(s32[2]{0:T(128)S(1)} %pad_add_fusion.own, s32[4,128]{1,0:T(4,128)S(1)} %get-tuple-element.29.here, s32[4,16]{1,0:T(4,128)S(1)} %get-tuple-element.27.before, bf16[32,128,128]{2,1,0:T(8,128)(2,1)S(1)} %all-to-all-done.blocks_ref, bf16[16,4,16,128]{3,2,1,0:T(8,128)(2,1)S(1)} %bitcast.46), custom_call_target="tpu_custom_call" | custom-call | flops 300000000 | bytes 3500000 | tf_op jit(solution)/shard_map/own_group/pallas_call | solution.py:28
  55.9 0.4 collective-permute-done.3.blocks_ref
  56.4 2.5 %other_group.1 = bf16[4,8,128,128]{3,2,1,0:T(8,128)(2,1)} custom-call(s32[2]{0:T(128)S(1)} %pad_add_fusion.own, s32[4,128]{1,0:T(4,128)S(1)} %get-tuple-element.30.here, s32[4,16]{1,0:T(4,128)S(1)} %get-tuple-element.28.before, bf16[32,128,128]{2,1,0:T(8,128)(2,1)S(1)} %collective-permute-done.3.blocks_ref, bf16[16,4,16,128]{3,2,1,0:T(8,128)(2,1)S(1)} %bitcast.47, ...), custom_call_target="tpu_custom_call" | custom-call | flops 300000000 | bytes 5500000 | tf_op jit(solution)/shard_map/other_group/pallas_call | solution.py:28
  58.8 0.0 copy-start
  58.9 5.1 %all-to-all-start.1 = ((bf16[32,128,128]{2,1,0:T(8,128)(2,1)}), bf16[32,128,128]{2,1,0:T(8,128)(2,1)S(1)}, u32[]{:S(2)}, u32[]{:S(2)}) async-start(bf16[32,128,128]{2,1,0:T(8,128)(2,1)} %bitcast.48), calls=%async_computation.1 | async-start | bytes 2097152 | tf_op jit(solution)/shard_map/all_to_all | solution.py:236
  64.0 0.1 pad_add_fusion.2.scalars
  64.1 0.0 copy-start.5
  64.1 2.7 %local_sums.5 = f32[128,128]{1,0:T(8,128)S(1)} custom-call(s32[2]{0:T(128)S(1)} %pad_add_fusion.2.scalars, bf16[32,128,128]{2,1,0:T(8,128)(2,1)S(1)} %all-to-all-done.blocks_ref, bf16[4,48,128]{2,1,0:T(8,128)(2,1)S(1)} %copy-done), custom_call_target="tpu_custom_call" | custom-call | flops 150000000 | bytes 1200000 | tf_op jit(solution)/shard_map/local_sums/pallas_call | solution.py:28
  66.8 3.1 %collective-permute-start.4 = (f32[128,128]{1,0:T(8,128)S(1)}, f32[128,128]{1,0:T(8,128)}, u32[]{:S(2)}, u32[]{:S(2)}) collective-permute-start(f32[128,128]{1,0:T(8,128)S(1)} %local_sums.5), channel_id=1, source_target_pairs={{0,16},{16,32},{32,48},{48,0},{1,17},{17,33},{33,49},{49,1},{2,18}... | collective-permute-start | bytes 196616 | tf_op jit(solution)/shard_map/ppermute | solution.py:246
  70.0 3.4 %local_sums.6 = f32[128,128]{1,0:T(8,128)} custom-call(s32[2]{0:T(128)S(1)} %pad_add_fusion.2.scalars, bf16[32,128,128]{2,1,0:T(8,128)(2,1)S(1)} %all-to-all-done.blocks_ref, bf16[4,48,128]{2,1,0:T(8,128)(2,1)S(1)} %copy-done), custom_call_target="tpu_custom_call" | custom-call | flops 150000000 | bytes 1200000 | tf_op jit(solution)/shard_map/local_sums/pallas_call | solution.py:28
  73.4 4.3 %collective-permute-start.5 = (f32[128,128]{1,0:T(8,128)}, f32[128,128]{1,0:T(8,128)}, u32[]{:S(2)}, u32[]{:S(2)}) collective-permute-start(f32[128,128]{1,0:T(8,128)} %local_sums.6), channel_id=1, source_target_pairs={{0,32},{16,48},{32,0},{48,16},{1,33},{17,49},{33,1},{49,17},{2,34}... | collective-permute-start | bytes 196616 | tf_op jit(solution)/shard_map/ppermute | solution.py:246
  77.7 3.4 %local_sums.7 = f32[128,128]{1,0:T(8,128)} custom-call(s32[2]{0:T(128)S(1)} %pad_add_fusion.2.scalars, bf16[32,128,128]{2,1,0:T(8,128)(2,1)S(1)} %all-to-all-done.blocks_ref, bf16[4,48,128]{2,1,0:T(8,128)(2,1)S(1)} %copy-done), custom_call_target="tpu_custom_call" | custom-call | flops 150000000 | bytes 1200000 | tf_op jit(solution)/shard_map/local_sums/pallas_call | solution.py:28
  81.0 3.0 %collective-permute-start.6 = (f32[128,128]{1,0:T(8,128)}, f32[128,128]{1,0:T(8,128)}, u32[]{:S(2)}, u32[]{:S(2)}) collective-permute-start(f32[128,128]{1,0:T(8,128)} %local_sums.7), channel_id=1, source_target_pairs={{0,48},{16,0},{32,16},{48,32},{1,49},{17,1},{33,17},{49,33},{2,50}... | collective-permute-start | bytes 196616 | tf_op jit(solution)/shard_map/ppermute | solution.py:246
  84.1 3.4 %local_sums.4.near_0_in = f32[128,128]{1,0:T(8,128)} custom-call(s32[2]{0:T(128)S(1)} %pad_add_fusion.2.scalars, bf16[32,128,128]{2,1,0:T(8,128)(2,1)S(1)} %all-to-all-done.blocks_ref, bf16[4,48,128]{2,1,0:T(8,128)(2,1)S(1)} %copy-done), custom_call_target="tpu_custom_call" | custom-call | flops 150000000 | bytes 1200000 | tf_op jit(solution)/shard_map/local_sums/pallas_call | solution.py:28
  87.5 1.8 %all-to-all-done.1 = bf16[32,128,128]{2,1,0:T(8,128)(2,1)S(1)} async-done(((bf16[32,128,128]{2,1,0:T(8,128)(2,1)}), bf16[32,128,128]{2,1,0:T(8,128)(2,1)S(1)}, u32[]{:S(2)}, u32[]{:S(2)}) %all-to-all-start.1) | async-done | bytes 1048608 | tf_op jit(solution)/shard_map/all_to_all | solution.py:236
  89.3 0.1 pad_add_fusion.1.scalars
  89.4 0.0 collective-permute-done.4.near_1_in
  89.4 2.6 %dense.1 = (bf16[128,512]{1,0:T(8,128)(2,1)}, bf16[8,128,128]{2,1,0:T(8,128)(2,1)S(1)}, bf16[8,128,128]{2,1,0:T(8,128)(2,1)S(1)}) custom-call(s32[2]{0:T(128)S(1)} %pad_add_fusion.1.scalars, f32[128,128]{1,0:T(8,128)} %local_sums.4.near_0_in, f32[128,128]{1,0:T(8,128)} %collective-permute-done.4.near_1_in, f32[128,128]{1,0:T(8,128)} %collective-permute-done.5.near_2_in, ...), custom_call_target="tpu_custom_call" | custom-call | flops 150000000 | bytes 3500000 | tf_op jit(solution)/shard_map/dense/pallas_call | solution.py:28
  92.0 6.2 %collective-permute-start.7 = (bf16[8,128,128]{2,1,0:T(8,128)(2,1)S(1)}, bf16[8,128,128]{2,1,0:T(8,128)(2,1)S(1)}, u32[]{:S(2)}, u32[]{:S(2)}) collective-permute-start(bf16[8,128,128]{2,1,0:T(8,128)(2,1)S(1)} %get-tuple-element.26), channel_id=1, source_target_pairs={{0,1},{1,0},{2,3},{3,2},{4,5},{5,4},{6,7},{7,6},{8,9},{9,8},{10,11... | collective-permute-start | bytes 786440 | tf_op jit(solution)/shard_map/ppermute | solution.py:262
  98.2 1.1 collective-permute-done.7.received_ref
  99.3 0.4 gradient.1
  99.8 23.6 %all_to_all.20.parts_ref = bf16[32,16,512]{2,1,0:T(8,128)(2,1)S(1)} all-to-all(bf16[32,16,512]{2,1,0:T(8,128)(2,1)S(1)} %gradient.1), channel_id=1, replica_groups=mesh['z'=8,'x1'=2,'x0'=2,'y2'=2,'y1'=2,'y0'=2,'c'=2] {'z','x1','x0'}, dimensions={0} | all-to-all | bytes 1048576 | tf_op jit(solution)/shard_map/all_to_all | solution.py:266
  123.4 0.1 added.2
  123.5 12.0 %all_to_all.21.parts_ref = bf16[8,16,512]{2,1,0:T(8,128)(2,1)S(1)} all-to-all(bf16[8,16,512]{2,1,0:T(8,128)(2,1)S(1)} %broadcast_in_dim.50), channel_id=1, replica_groups=mesh['z'=8,'x1'=2,'x0'=2,'y2'=2,'y1'=2,'y0'=2,'c'=2] {'y2','y1','y0'}, dimensions={0} | all-to-all | bytes 262144 | tf_op jit(solution)/shard_map/all_to_all | solution.py:267
  135.5 5.0 %all-gather.1 = f32[32,512]{1,0:T(8,128)S(1)} all-gather(f32[16,512]{1,0:T(8,128)S(1)} %added.3), channel_id=3, replica_groups=mesh['z'=8,'x1'=2,'x0'=2,'y2'=2,'y1'=2,'y0'=2,'c'=2] {'c'}, dimensions={0}, use_global_device_ids=true | all-gather | bytes 98304 | tf_op jit(solution)/shard_map/all_gather | solution.py:268
  140.5 0.6 fusion.11
  (29 shorter events, 0.1 us)
Async XLA Ops:
  0.6 0.9 copy-start.1
  1.5 15.0 %copy-start.8 = (s32[1,1,16,2]{2,3,1,0:T(2,128)S(1)}, s32[1,1,16,2]{2,3,1,0:T(2,128)}, u32[]{:S(2)}) copy-start(s32[1,1,16,2]{2,3,1,0:T(2,128)} %param.11) | copy-start | bytes 388
  1.5 15.0 %copy-start.6 = (bf16[128,16]{0,1:T(8,128)(2,1)S(1)}, bf16[128,16]{0,1:T(8,128)(2,1)}, u32[]{:S(2)}) copy-start(bf16[128,16]{0,1:T(8,128)(2,1)} %param.9) | copy-start | bytes 12292
  1.5 15.2 %copy-start.7 = (s32[128,16]{0,1:T(8,128)S(1)}, s32[128,16]{0,1:T(8,128)}, u32[]{:S(2)}) copy-start(s32[128,16]{0,1:T(8,128)} %param.10) | copy-start | bytes 24580
  1.5 15.3 %copy-start.9 = (s32[1,1,16]{2,1,0:T(1,128)S(1)}, s32[1,1,16]{2,1,0:T(1,128)}, u32[]{:S(2)}) copy-start(s32[1,1,16]{2,1,0:T(1,128)} %param.12) | copy-start | bytes 196
  2.8 49.0 %all-to-all-start = ((bf16[32,128,128]{2,1,0:T(8,128)(2,1)}), bf16[32,128,128]{2,1,0:T(8,128)(2,1)S(1)}, u32[]{:S(2)}, u32[]{:S(2)}) async-start(bf16[32,128,128]{2,1,0:T(8,128)(2,1)} %bitcast.49), calls=%async_computation | async-start | bytes 2097152 | tf_op jit(solution)/shard_map/all_to_all | solution.py:199
  17.1 9.3 %collective-permute-start.2 = (bf16[64,128]{1,0:T(8,128)(2,1)S(1)}, bf16[64,128]{1,0:T(8,128)(2,1)S(1)}, u32[]{:S(2)}, u32[]{:S(2)}) collective-permute-start(bf16[64,128]{1,0:T(8,128)(2,1)S(1)} %concatenate.22.codes_0), channel_id=1, source_target_pairs={{0,48},{16,0},{32,16},{48,32},{1,49},{17,1},{33,17},{49,33},{2,50}... | collective-permute-start | bytes 49160 | tf_op jit(solution)/shard_map/ppermute | solution.py:211
  21.5 6.4 %collective-permute-start.1 = (bf16[64,128]{1,0:T(8,128)(2,1)S(1)}, bf16[64,128]{1,0:T(8,128)(2,1)S(1)}, u32[]{:S(2)}, u32[]{:S(2)}) collective-permute-start(bf16[64,128]{1,0:T(8,128)(2,1)S(1)} %concatenate.22.codes_0), channel_id=1, source_target_pairs={{0,32},{16,48},{32,0},{48,16},{1,33},{17,49},{33,1},{49,17},{2,34}... | collective-permute-start | bytes 49160 | tf_op jit(solution)/shard_map/ppermute | solution.py:211
  23.9 6.1 %collective-permute-start = (bf16[64,128]{1,0:T(8,128)(2,1)S(1)}, bf16[64,128]{1,0:T(8,128)(2,1)S(1)}, u32[]{:S(2)}, u32[]{:S(2)}) collective-permute-start(bf16[64,128]{1,0:T(8,128)(2,1)S(1)} %concatenate.22.codes_0), channel_id=1, source_target_pairs={{0,16},{16,32},{32,48},{48,0},{1,17},{17,33},{33,49},{49,1},{2,18}... | collective-permute-start | bytes 49160 | tf_op jit(solution)/shard_map/ppermute | solution.py:211
  51.8 4.5 %collective-permute-start.3 = (bf16[32,128,128]{2,1,0:T(8,128)(2,1)S(1)}, bf16[32,128,128]{2,1,0:T(8,128)(2,1)S(1)}, u32[]{:S(2)}, u32[]{:S(2)}) collective-permute-start(bf16[32,128,128]{2,1,0:T(8,128)(2,1)S(1)} %all-to-all-done.blocks_ref), channel_id=1, source_target_pairs={{0,1},{1,0},{2,3},{3,2},{4,5},{5,4},{6,7},{7,6},{8,9},{9,8},{10,11... | collective-permute-start | bytes 3145736 | tf_op jit(solution)/shard_map/ppermute | solution.py:226
  58.8 5.2 %copy-start = (bf16[4,48,128]{2,1,0:T(8,128)(2,1)S(1)}, bf16[4,48,128]{2,1,0:T(8,128)(2,1)}, u32[]{:S(2)}) copy-start(bf16[4,48,128]{2,1,0:T(8,128)(2,1)} %get-tuple-element.21.told_ref) | copy-start | bytes 147460
  58.9 30.4 %all-to-all-start.1 = ((bf16[32,128,128]{2,1,0:T(8,128)(2,1)}), bf16[32,128,128]{2,1,0:T(8,128)(2,1)S(1)}, u32[]{:S(2)}, u32[]{:S(2)}) async-start(bf16[32,128,128]{2,1,0:T(8,128)(2,1)} %bitcast.48), calls=%async_computation.1 | async-start | bytes 2097152 | tf_op jit(solution)/shard_map/all_to_all | solution.py:236
  64.1 25.3 %copy-start.2 = (bf16[128,512]{1,0:T(8,128)(2,1)S(1)}, bf16[128,512]{1,0:T(8,128)(2,1)}, u32[]{:S(2)}) copy-start(bf16[128,512]{1,0:T(8,128)(2,1)} %features.1) | copy-start | bytes 393220
  64.1 25.3 %copy-start.3 = (bf16[512,512]{1,0:T(8,128)(2,1)S(1)}, bf16[512,512]{1,0:T(8,128)(2,1)}, u32[]{:S(2)}) copy-start(bf16[512,512]{1,0:T(8,128)(2,1)} %w_agg.1) | copy-start | bytes 1572868
  64.1 25.3 %copy-start.4 = (bf16[512,512]{1,0:T(8,128)(2,1)S(1)}, bf16[512,512]{1,0:T(8,128)(2,1)}, u32[]{:S(2)}) copy-start(bf16[512,512]{1,0:T(8,128)(2,1)} %w_self.1) | copy-start | bytes 1572868
  64.1 25.3 %copy-start.5 = (bf16[128,512]{1,0:T(8,128)(2,1)S(1)}, bf16[128,512]{1,0:T(8,128)(2,1)}, u32[]{:S(2)}) copy-start(bf16[128,512]{1,0:T(8,128)(2,1)} %cotangent.1) | copy-start | bytes 393220
  66.8 22.5 %collective-permute-start.4 = (f32[128,128]{1,0:T(8,128)S(1)}, f32[128,128]{1,0:T(8,128)}, u32[]{:S(2)}, u32[]{:S(2)}) collective-permute-start(f32[128,128]{1,0:T(8,128)S(1)} %local_sums.5), channel_id=1, source_target_pairs={{0,16},{16,32},{32,48},{48,0},{1,17},{17,33},{33,49},{49,1},{2,18}... | collective-permute-start | bytes 196616 | tf_op jit(solution)/shard_map/ppermute | solution.py:246
  73.4 16.0 %collective-permute-start.5 = (f32[128,128]{1,0:T(8,128)}, f32[128,128]{1,0:T(8,128)}, u32[]{:S(2)}, u32[]{:S(2)}) collective-permute-start(f32[128,128]{1,0:T(8,128)} %local_sums.6), channel_id=1, source_target_pairs={{0,32},{16,48},{32,0},{48,16},{1,33},{17,49},{33,1},{49,17},{2,34}... | collective-permute-start | bytes 196616 | tf_op jit(solution)/shard_map/ppermute | solution.py:246
  81.0 8.3 %collective-permute-start.6 = (f32[128,128]{1,0:T(8,128)}, f32[128,128]{1,0:T(8,128)}, u32[]{:S(2)}, u32[]{:S(2)}) collective-permute-start(f32[128,128]{1,0:T(8,128)} %local_sums.7), channel_id=1, source_target_pairs={{0,48},{16,0},{32,16},{48,32},{1,49},{17,1},{33,17},{49,33},{2,50}... | collective-permute-start | bytes 196616 | tf_op jit(solution)/shard_map/ppermute | solution.py:246
  92.0 7.3 %collective-permute-start.7 = (bf16[8,128,128]{2,1,0:T(8,128)(2,1)S(1)}, bf16[8,128,128]{2,1,0:T(8,128)(2,1)S(1)}, u32[]{:S(2)}, u32[]{:S(2)}) collective-permute-start(bf16[8,128,128]{2,1,0:T(8,128)(2,1)S(1)} %get-tuple-element.26), channel_id=1, source_target_pairs={{0,1},{1,0},{2,3},{3,2},{4,5},{5,4},{6,7},{7,6},{8,9},{9,8},{10,11... | collective-permute-start | bytes 786440 | tf_op jit(solution)/shard_map/ppermute | solution.py:262

commit v11 on v10

--- a/solution.py
+++ b/solution.py
@@ -50,22 +50,23 @@
         copy.wait()
 
 
-def split_kernel(codes_0, codes_1, codes_2, codes_3, remote_ref, local_ref, sems):
+def split_kernel(codes_ref, remote_ref, local_ref, sems):
     copies = []
-    for k, codes in enumerate((codes_0, codes_1, codes_2, codes_3)):
-        copies.append(pltpu.make_async_copy(codes.at[TOLD:], local_ref.at[k], sems.at[k]))
+    for x in range(NX):
+        codes = codes_ref.at[x % 2, x // 2]
+        copies.append(pltpu.make_async_copy(codes.at[TOLD:], local_ref.at[x], sems.at[x]))
         copies[-1].start()
-        remote_ref[k] = codes[0:TOLD]
-    for copy in copies:
-        copy.wait()
-
-
-def remote_product(own, here, before, blocks_ref, told_ref, k, y):
-    group = y * NC + own[0]
-    first = jnp.clip(here[k, GROUPS + group * CAP], 0, OWNERS - 1)
-    second = jnp.clip(here[k, GROUPS + group * CAP + 1], 0, OWNERS - 1)
-    start, count = before[k, group].astype(F32), here[k, group].astype(F32)
-    told = told_ref[group, k].astype(F32)
+        remote_ref[x] = codes[0:TOLD]
+    for copy in copies:
+        copy.wait()
+
+
+def remote_product(core, here, before, blocks_ref, told_ref, x, y):
+    group = y * NC + core[0]
+    first = jnp.clip(here[x, GROUPS + group * CAP], 0, OWNERS - 1)
+    second = jnp.clip(here[x, GROUPS + group * CAP + 1], 0, OWNERS - 1)
+    start, count = before[x, group].astype(F32), here[x, group].astype(F32)
+    told = told_ref[group, x].astype(F32)
     entry = told[0:K_REM] - start
     row = jnp.where(entry < count, entry * T + told[K_REM : 2 * K_REM], -1.0).astype(jnp.int16)
     weight = told[2 * K_REM : 3 * K_REM].astype(BF16)
@@ -77,18 +78,17 @@
     return jnp.dot(pair, hot, preferred_element_type=F32)
 
 
-def first_kernel(own, here, before, blocks_ref, told_ref, part_ref):
+def first_kernel(core, here, before, blocks_ref, told_ref, part_ref):
     for y in range(NY):
-        for k in range(NX):
-            part_ref[lax.rem(own[1] + (NX - k), NX), y] = remote_product(own, here, before, blocks_ref, told_ref, k, y)
-
-
-def second_kernel(own, here, before, blocks_ref, told_ref, part_ref, sums_ref, sums, sems):
+        for x in range(NX):
+            part_ref[x, y] = remote_product(core, here, before, blocks_ref, told_ref, x, y)
+
+
+def second_kernel(core, here, before, blocks_ref, told_ref, part_ref, sums_ref, sums, sems):
     copies = []
     for y in range(NY):
-        for k in range(NX):
-            x = lax.rem(own[1] + (NX - k), NX)
-            sums[x, y] = (part_ref[x, y] + remote_product(own, here, before, blocks_ref, told_ref, k, y)).astype(BF16)
+        for x in range(NX):
+            sums[x, y] = (part_ref[x, y] + remote_product(core, here, before, blocks_ref, told_ref, x, y)).astype(BF16)
         copies.append(pltpu.make_async_copy(sums.at[:, y], sums_ref.at[:, y], sems.at[y]))
         copies[-1].start()
     for copy in copies:
@@ -96,11 +96,12 @@
 
 
 def local_kernel(k, outside, scalars, blocks_ref, told_ref, out, hot_ref, total=None, sem=None):
-    owner = scalars[0] * NX + lax.rem(scalars[1] + (NX - k), NX)
+    x = lax.rem(scalars[1] + (NX - k), NX)
+    owner = scalars[0] * NX + x
     rows = lax.broadcasted_iota(jnp.int16, (T, T), 0)
     lanes = lax.broadcasted_iota(jnp.int32, (1, T), 1).astype(F32)
     ones, zeros = jnp.ones((T, T), BF16), jnp.zeros((T, T), BF16)
-    block, row, weight = (told_ref[k, n * 16 : n * 16 + 16, :].astype(F32) for n in range(3))
+    block, row, weight = (told_ref[x, n * 16 : n * 16 + 16, :].astype(F32) for n in range(3))
     weight = weight.astype(BF16)
 
     def of_four(i, summed):
@@ -208,9 +209,9 @@
     of_local = jnp.concatenate([block[:K_LOC], gap, row[:K_LOC], gap, weights_t[:K_LOC], gap], axis=0)
     codes = jnp.concatenate([of_remote, of_local], axis=0)
     forward = [[(i, (i + k) % NX) for i in range(NX)] for k in range(NX)]
-    codes = [codes] + [lax.ppermute(codes, X, forward[k]) for k in range(1, NX)]
+    codes = lax.all_gather(lax.all_gather(codes, "x1", axis=0), "x0", axis=0)
     remote_codes, local_codes = vmem_call(
-        split_kernel, "split", [], codes, [((NX, TOLD, T), BF16), ((NX, 48, T), BF16)],
+        split_kernel, "split", [], [codes], [((NX, TOLD, T), BF16), ((NX, 48, T), BF16)],
         scratch=[pltpu.SemaphoreType.DMA((NX,))], outside=1, bytes_accessed=100_000,
     )
     remote_codes = lax.all_gather(remote_codes, Y + ("c",), axis=0)
@@ -222,14 +223,14 @@
         here = jnp.sum(jnp.where(sources == group, told, 0), axis=0)
         return here, jnp.sum(jnp.where(sources < group, told[:, :, :GROUPS], 0), axis=0)
 
-    own = jnp.stack([c, x])
+    core = c[None]
     others = lax.ppermute(blocks, "c", swap)
     (part,) = vmem_call(
-        first_kernel, "own_group", [own, *of_source(y * NC + c)], [blocks, remote_codes], [((NX, NY, T, T), F32)],
+        first_kernel, "own_group", [core, *of_source(y * NC + c)], [blocks, remote_codes], [((NX, NY, T, T), F32)],
         flops=300_000_000, bytes_accessed=3_500_000,
     )
     (chip_sum,) = vmem_call(
-        second_kernel, "other_group", [own, *of_source(y * NC + 1 - c)], [others, remote_codes, part], [((NX, NY, T, T), BF16)],
+        second_kernel, "other_group", [core, *of_source(y * NC + 1 - c)], [others, remote_codes, part], [((NX, NY, T, T), BF16)],
         scratch=[pltpu.VMEM((NX, NY, T, T), BF16), pltpu.SemaphoreType.DMA((NY,))], outside=1,
         flops=300_000_000, bytes_accessed=5_500_000,
     )

time: 142 us -> 140 us (0.986)
  blocking collectives: 61.8 us -> 70.2 us
  starting transfers between devices: 46.9 us -> 40.1 us
  waiting for transfers between devices: 6.95 us -> 3.45 us
    all_gather x0 -> x2, blocking collectives: none -> 9.62 us  [body(): codes = lax.all_gather(lax.all_gather(codes, 'x1', axis=0), 'x0', axis=0)]
    ppermute x3 -> x0, starting transfers between devices: 9.31 us -> none  [body(): codes = [codes] + [lax.ppermute(codes, X, forward[k]) for k in range(1, NX)]]
    ppermute x3 -> x0, waiting for transfers between devices: 3.55 us -> none  [body(): codes = [codes] + [lax.ppermute(codes, X, forward[k]) for k in range(1, NX)]]
    all_to_all x1, starting transfers between devices: 5.14 us -> 7.59 us  [body(): lax.all_to_all(chip_sum.reshape(NX * NY, T, T), X + Y, 0, 0, tiled=True)]
  transfers between devices with their start and end apart: 10 -> 7, of which waited for: 5 -> 3; matrix products, arithmetic and copies ran while one was open for 1% -> 1% of each run, Pallas kernels for 11% -> 11%
where the time goes in v11:
time: 140 us; the launch traced here: 139 us
  blocking collectives  70.2 us (50%)
  starting transfers between devices  40.1 us (29%)
  Pallas kernels  22 us (16%)
  waiting for transfers between devices  3.45 us (2%)
  local copies, waits for them, and re-layouts  1.97 us (1%)
    all_to_all x1, blocking collectives, body(): plane = added(lax.all_to_all(chip_grad, ('z',) + X, 0, 0, tiled=True), BF16)  22.9 us
    pallas_call x12, Pallas kernels, vmem_call(): pl.pallas_call(kernel, in_specs=[pl.BlockSpec(memory_space=pltpu.SMEM)] *...  22 us
    all_gather x1, blocking collectives, body(): remote_codes = lax.all_gather(remote_codes, Y + ('c',), axis=0)  20.6 us
    all_to_all x1, starting transfers between devices, body(): lax.all_to_all(quarters.reshape(OWNERS, T, T), ('z',) + X, 0, 0, tiled=True)  13.7 us
    all_to_all x1, blocking collectives, body(): lax.all_to_all(jnp.broadcast_to(plane, (NY,) + plane.shape), Y, 0, 0, til...  12 us
    ppermute x3, starting transfers between devices, body(): near.append(lax.ppermute(sums, X, forward[NX - k]) if k else sums)  10.5 us
    all_gather x2, blocking collectives, body(): codes = lax.all_gather(lax.all_gather(codes, 'x1', axis=0), 'x0', axis=0)  9.62 us
    all_to_all x1, starting transfers between devices, body(): lax.all_to_all(chip_sum.reshape(NX * NY, T, T), X + Y, 0, 0, tiled=True)  7.59 us
  transfers between devices with their start and end apart: 7, of which 3 were waited for; matrix products, arithmetic and copies ran while one was open for 1% of the time, Pallas kernels for 11%

profile of v11, /device:TPU:1, one launch (start us, length us, event | category | flops | bytes accessed | tf_op | source)
XLA Modules:
  0.0 139.2 jit_solution(1838289161257815705)
XLA Ops:
  0.6 0.0 copy-start.1
  0.6 0.9 copy-done.1
  1.5 1.2 spread.1
  2.8 13.7 %all-to-all-start = ((bf16[32,128,128]{2,1,0:T(8,128)(2,1)}), bf16[32,128,128]{2,1,0:T(8,128)(2,1)S(1)}, u32[]{:S(2)}, u32[]{:S(2)}) async-start(bf16[32,128,128]{2,1,0:T(8,128)(2,1)} %bitcast.52), calls=%async_computation | async-start | bytes 2097152 | tf_op jit(solution)/shard_map/all_to_all | solution.py:200
  16.6 0.1 copy.13
  16.6 0.1 concatenate.20
  16.7 0.0 copy-done.7
  16.8 0.1 fusion.9
  16.9 0.2 concatenate.22
  17.1 4.9 %all-gather = bf16[128,128]{1,0:T(8,128)(2,1)S(1)} all-gather(bf16[64,128]{1,0:T(8,128)(2,1)S(1)} %concatenate.22), channel_id=2, replica_groups=mesh['z'=8,'x1'=2,'x0'=2,'y2'=2,'y1'=2,'y0'=2,'c'=2] {'x1'}, dimensions={0}, use_global_device_ids=true | all-gather | bytes 49152 | tf_op jit(solution)/shard_map/all_gather | solution.py:212
  22.0 4.7 %all-gather.1 = bf16[4,64,128]{2,1,0:T(8,128)(2,1)S(1)} all-gather(bf16[2,64,128]{2,1,0:T(8,128)(2,1)S(1)} %bitcast.55), channel_id=3, replica_groups=mesh['z'=8,'x1'=2,'x0'=2,'y2'=2,'y1'=2,'y0'=2,'c'=2] {'x0'}, dimensions={0}, use_global_device_ids=true | all-gather | bytes 98304 | tf_op jit(solution)/shard_map/all_gather | solution.py:212
  26.7 0.6 split.1
  27.4 20.6 %all-gather.2 = bf16[64,16,128]{2,1,0:T(8,128)(2,1)S(1)} all-gather(bf16[4,16,128]{2,1,0:T(8,128)(2,1)S(1)} %get-tuple-element.16), channel_id=4, replica_groups=mesh['z'=8,'x1'=2,'x0'=2,'y2'=2,'y1'=2,'y0'=2,'c'=2] {'y2','y1','y0','c'}, dimensions={0}, use_global_device_ids=true | all-gather | bytes 278528 | tf_op jit(solution)/shard_map/all_gather | solution.py:217
  48.0 0.0 all-to-all-done.blocks_ref
  48.0 2.1 %collective-permute-start = (bf16[32,128,128]{2,1,0:T(8,128)(2,1)S(1)}, bf16[32,128,128]{2,1,0:T(8,128)(2,1)S(1)}, u32[]{:S(2)}, u32[]{:S(2)}) collective-permute-start(bf16[32,128,128]{2,1,0:T(8,128)(2,1)S(1)} %all-to-all-done.blocks_ref), channel_id=1, source_target_pairs={{0,1},{1,0},{2,3},{3,2},{4,5},{5,4},{6,7},{7,6},{8,9},{9,8},{10,11... | collective-permute-start | bytes 3145736 | tf_op jit(solution)/shard_map/ppermute | solution.py:227
  50.1 0.1 slice_convert_fusion
  50.2 0.1 select_reduce_fusion
  50.3 0.1 select_reduce_fusion.1
  50.4 1.6 %own_group.1.part_ref = f32[4,8,128,128]{3,2,1,0:T(8,128)S(1)} custom-call(s32[1]{0:T(128)} %bitcast.core, s32[4,128]{1,0:T(4,128)S(1)} %get-tuple-element.29.here, s32[4,16]{1,0:T(4,128)S(1)} %get-tuple-element.27.before, bf16[32,128,128]{2,1,0:T(8,128)(2,1)S(1)} %all-to-all-done.blocks_ref, bf16[16,4,16,128]{3,2,1,0:T(8,128)(2,1)S(1)} %bitcast.48), custom_call_target="tpu_custom_call" | custom-call | flops 300000000 | bytes 3500000 | tf_op jit(solution)/shard_map/own_group/pallas_call | solution.py:28
  52.0 0.5 collective-permute-done.blocks_ref
  52.6 2.6 %other_group.1 = bf16[4,8,128,128]{3,2,1,0:T(8,128)(2,1)} custom-call(s32[1]{0:T(128)} %bitcast.core, s32[4,128]{1,0:T(4,128)S(1)} %get-tuple-element.30.here, s32[4,16]{1,0:T(4,128)S(1)} %get-tuple-element.28.before, bf16[32,128,128]{2,1,0:T(8,128)(2,1)S(1)} %collective-permute-done.blocks_ref, bf16[16,4,16,128]{3,2,1,0:T(8,128)(2,1)S(1)} %bitcast.49, ...), custom_call_target="tpu_custom_call" | custom-call | flops 300000000 | bytes 5500000 | tf_op jit(solution)/shard_map/other_group/pallas_call | solution.py:28
  55.1 0.0 copy-start
  55.2 7.6 %all-to-all-start.1 = ((bf16[32,128,128]{2,1,0:T(8,128)(2,1)}), bf16[32,128,128]{2,1,0:T(8,128)(2,1)S(1)}, u32[]{:S(2)}, u32[]{:S(2)}) async-start(bf16[32,128,128]{2,1,0:T(8,128)(2,1)} %bitcast.51), calls=%async_computation.1 | async-start | bytes 2097152 | tf_op jit(solution)/shard_map/all_to_all | solution.py:237
  62.8 0.1 pad_add_fusion.1.scalars
  62.8 0.0 copy-done
  62.9 0.0 copy-start.5
  62.9 2.7 %local_sums.5 = f32[128,128]{1,0:T(8,128)S(1)} custom-call(s32[2]{0:T(128)S(1)} %pad_add_fusion.1.scalars, bf16[32,128,128]{2,1,0:T(8,128)(2,1)S(1)} %all-to-all-done.blocks_ref, bf16[4,48,128]{2,1,0:T(8,128)(2,1)S(1)} %copy-done), custom_call_target="tpu_custom_call" | custom-call | flops 150000000 | bytes 1200000 | tf_op jit(solution)/shard_map/local_sums/pallas_call | solution.py:28
  65.6 3.1 %collective-permute-start.1 = (f32[128,128]{1,0:T(8,128)S(1)}, f32[128,128]{1,0:T(8,128)}, u32[]{:S(2)}, u32[]{:S(2)}) collective-permute-start(f32[128,128]{1,0:T(8,128)S(1)} %local_sums.5), channel_id=1, source_target_pairs={{0,16},{16,32},{32,48},{48,0},{1,17},{17,33},{33,49},{49,1},{2,18}... | collective-permute-start | bytes 196616 | tf_op jit(solution)/shard_map/ppermute | solution.py:247
  68.8 3.4 %local_sums.6 = f32[128,128]{1,0:T(8,128)} custom-call(s32[2]{0:T(128)S(1)} %pad_add_fusion.1.scalars, bf16[32,128,128]{2,1,0:T(8,128)(2,1)S(1)} %all-to-all-done.blocks_ref, bf16[4,48,128]{2,1,0:T(8,128)(2,1)S(1)} %copy-done), custom_call_target="tpu_custom_call" | custom-call | flops 150000000 | bytes 1200000 | tf_op jit(solution)/shard_map/local_sums/pallas_call | solution.py:28
  72.1 4.3 %collective-permute-start.2 = (f32[128,128]{1,0:T(8,128)}, f32[128,128]{1,0:T(8,128)}, u32[]{:S(2)}, u32[]{:S(2)}) collective-permute-start(f32[128,128]{1,0:T(8,128)} %local_sums.6), channel_id=1, source_target_pairs={{0,32},{16,48},{32,0},{48,16},{1,33},{17,49},{33,1},{49,17},{2,34}... | collective-permute-start | bytes 196616 | tf_op jit(solution)/shard_map/ppermute | solution.py:247
  76.5 3.4 %local_sums.7 = f32[128,128]{1,0:T(8,128)} custom-call(s32[2]{0:T(128)S(1)} %pad_add_fusion.1.scalars, bf16[32,128,128]{2,1,0:T(8,128)(2,1)S(1)} %all-to-all-done.blocks_ref, bf16[4,48,128]{2,1,0:T(8,128)(2,1)S(1)} %copy-done), custom_call_target="tpu_custom_call" | custom-call | flops 150000000 | bytes 1200000 | tf_op jit(solution)/shard_map/local_sums/pallas_call | solution.py:28
  79.8 3.0 %collective-permute-start.3 = (f32[128,128]{1,0:T(8,128)}, f32[128,128]{1,0:T(8,128)}, u32[]{:S(2)}, u32[]{:S(2)}) collective-permute-start(f32[128,128]{1,0:T(8,128)} %local_sums.7), channel_id=1, source_target_pairs={{0,48},{16,0},{32,16},{48,32},{1,49},{17,1},{33,17},{49,33},{2,50}... | collective-permute-start | bytes 196616 | tf_op jit(solution)/shard_map/ppermute | solution.py:247
  82.9 3.4 %local_sums.4.near_0_in = f32[128,128]{1,0:T(8,128)} custom-call(s32[2]{0:T(128)S(1)} %pad_add_fusion.1.scalars, bf16[32,128,128]{2,1,0:T(8,128)(2,1)S(1)} %all-to-all-done.blocks_ref, bf16[4,48,128]{2,1,0:T(8,128)(2,1)S(1)} %copy-done), custom_call_target="tpu_custom_call" | custom-call | flops 150000000 | bytes 1200000 | tf_op jit(solution)/shard_map/local_sums/pallas_call | solution.py:28
  86.3 1.8 %all-to-all-done.1 = bf16[32,128,128]{2,1,0:T(8,128)(2,1)S(1)} async-done(((bf16[32,128,128]{2,1,0:T(8,128)(2,1)}), bf16[32,128,128]{2,1,0:T(8,128)(2,1)S(1)}, u32[]{:S(2)}, u32[]{:S(2)}) %all-to-all-start.1) | async-done | bytes 1048608 | tf_op jit(solution)/shard_map/all_to_all | solution.py:237
  88.0 0.1 pad_add_fusion.scalars
  88.1 0.0 collective-permute-done.1.near_1_in
  88.1 0.0 collective-permute-done.2.near_2_in
  88.1 0.0 collective-permute-done.3.near_3_in
  88.1 0.0 copy-done.2
  88.2 2.6 %dense.1 = (bf16[128,512]{1,0:T(8,128)(2,1)}, bf16[8,128,128]{2,1,0:T(8,128)(2,1)S(1)}, bf16[8,128,128]{2,1,0:T(8,128)(2,1)S(1)}) custom-call(s32[2]{0:T(128)S(1)} %pad_add_fusion.scalars, f32[128,128]{1,0:T(8,128)} %local_sums.4.near_0_in, f32[128,128]{1,0:T(8,128)} %collective-permute-done.1.near_1_in, f32[128,128]{1,0:T(8,128)} %collective-permute-done.2.near_2_in, ...), custom_call_target="tpu_custom_call" | custom-call | flops 150000000 | bytes 3500000 | tf_op jit(solution)/shard_map/dense/pallas_call | solution.py:28
  90.7 6.2 %collective-permute-start.4 = (bf16[8,128,128]{2,1,0:T(8,128)(2,1)S(1)}, bf16[8,128,128]{2,1,0:T(8,128)(2,1)S(1)}, u32[]{:S(2)}, u32[]{:S(2)}) collective-permute-start(bf16[8,128,128]{2,1,0:T(8,128)(2,1)S(1)} %get-tuple-element.26), channel_id=1, source_target_pairs={{0,1},{1,0},{2,3},{3,2},{4,5},{5,4},{6,7},{7,6},{8,9},{9,8},{10,11... | collective-permute-start | bytes 786440 | tf_op jit(solution)/shard_map/ppermute | solution.py:263
  97.0 1.1 collective-permute-done.4.received_ref
  98.1 0.4 gradient.1
  98.5 22.9 %all_to_all.20.parts_ref = bf16[32,16,512]{2,1,0:T(8,128)(2,1)S(1)} all-to-all(bf16[32,16,512]{2,1,0:T(8,128)(2,1)S(1)} %gradient.1), channel_id=1, replica_groups=mesh['z'=8,'x1'=2,'x0'=2,'y2'=2,'y1'=2,'y0'=2,'c'=2] {'z','x1','x0'}, dimensions={0} | all-to-all | bytes 1048576 | tf_op jit(solution)/shard_map/all_to_all | solution.py:267
  121.4 0.1 added.2
  121.5 12.0 %all_to_all.21.parts_ref = bf16[8,16,512]{2,1,0:T(8,128)(2,1)S(1)} all-to-all(bf16[8,16,512]{2,1,0:T(8,128)(2,1)S(1)} %broadcast_in_dim.54), channel_id=1, replica_groups=mesh['z'=8,'x1'=2,'x0'=2,'y2'=2,'y1'=2,'y0'=2,'c'=2] {'y2','y1','y0'}, dimensions={0} | all-to-all | bytes 262144 | tf_op jit(solution)/shard_map/all_to_all | solution.py:268
  133.6 5.0 %all-gather.3 = f32[32,512]{1,0:T(8,128)S(1)} all-gather(f32[16,512]{1,0:T(8,128)S(1)} %added.3), channel_id=5, replica_groups=mesh['z'=8,'x1'=2,'x0'=2,'y2'=2,'y1'=2,'y0'=2,'c'=2] {'c'}, dimensions={0}, use_global_device_ids=true | all-gather | bytes 98304 | tf_op jit(solution)/shard_map/all_gather | solution.py:269
  138.6 0.6 fusion.11
  (24 shorter events, 0.1 us)
Async XLA Ops:
  0.6 0.9 copy-start.1
  1.5 15.0 %copy-start.8 = (s32[1,1,16,2]{2,3,1,0:T(2,128)S(1)}, s32[1,1,16,2]{2,3,1,0:T(2,128)}, u32[]{:S(2)}) copy-start(s32[1,1,16,2]{2,3,1,0:T(2,128)} %param.11) | copy-start | bytes 388
  1.5 15.0 %copy-start.6 = (bf16[128,16]{0,1:T(8,128)(2,1)S(1)}, bf16[128,16]{0,1:T(8,128)(2,1)}, u32[]{:S(2)}) copy-start(bf16[128,16]{0,1:T(8,128)(2,1)} %param.9) | copy-start | bytes 12292
  1.5 15.2 %copy-start.7 = (s32[128,16]{0,1:T(8,128)S(1)}, s32[128,16]{0,1:T(8,128)}, u32[]{:S(2)}) copy-start(s32[128,16]{0,1:T(8,128)} %param.10) | copy-start | bytes 24580
  1.5 15.3 %copy-start.9 = (s32[1,1,16]{2,1,0:T(1,128)S(1)}, s32[1,1,16]{2,1,0:T(1,128)}, u32[]{:S(2)}) copy-start(s32[1,1,16]{2,1,0:T(1,128)} %param.12) | copy-start | bytes 196
  2.8 45.2 %all-to-all-start = ((bf16[32,128,128]{2,1,0:T(8,128)(2,1)}), bf16[32,128,128]{2,1,0:T(8,128)(2,1)S(1)}, u32[]{:S(2)}, u32[]{:S(2)}) async-start(bf16[32,128,128]{2,1,0:T(8,128)(2,1)} %bitcast.52), calls=%async_computation | async-start | bytes 2097152 | tf_op jit(solution)/shard_map/all_to_all | solution.py:200
  48.0 4.5 %collective-permute-start = (bf16[32,128,128]{2,1,0:T(8,128)(2,1)S(1)}, bf16[32,128,128]{2,1,0:T(8,128)(2,1)S(1)}, u32[]{:S(2)}, u32[]{:S(2)}) collective-permute-start(bf16[32,128,128]{2,1,0:T(8,128)(2,1)S(1)} %all-to-all-done.blocks_ref), channel_id=1, source_target_pairs={{0,1},{1,0},{2,3},{3,2},{4,5},{5,4},{6,7},{7,6},{8,9},{9,8},{10,11... | collective-permute-start | bytes 3145736 | tf_op jit(solution)/shard_map/ppermute | solution.py:227
  55.1 7.7 %copy-start = (bf16[4,48,128]{2,1,0:T(8,128)(2,1)S(1)}, bf16[4,48,128]{2,1,0:T(8,128)(2,1)}, u32[]{:S(2)}) copy-start(bf16[4,48,128]{2,1,0:T(8,128)(2,1)} %get-tuple-element.21.told_ref) | copy-start | bytes 147460
  55.2 32.9 %all-to-all-start.1 = ((bf16[32,128,128]{2,1,0:T(8,128)(2,1)}), bf16[32,128,128]{2,1,0:T(8,128)(2,1)S(1)}, u32[]{:S(2)}, u32[]{:S(2)}) async-start(bf16[32,128,128]{2,1,0:T(8,128)(2,1)} %bitcast.51), calls=%async_computation.1 | async-start | bytes 2097152 | tf_op jit(solution)/shard_map/all_to_all | solution.py:237
  62.8 25.3 %copy-start.2 = (bf16[128,512]{1,0:T(8,128)(2,1)S(1)}, bf16[128,512]{1,0:T(8,128)(2,1)}, u32[]{:S(2)}) copy-start(bf16[128,512]{1,0:T(8,128)(2,1)} %features.1) | copy-start | bytes 393220
  62.9 25.3 %copy-start.3 = (bf16[512,512]{1,0:T(8,128)(2,1)S(1)}, bf16[512,512]{1,0:T(8,128)(2,1)}, u32[]{:S(2)}) copy-start(bf16[512,512]{1,0:T(8,128)(2,1)} %w_agg.1) | copy-start | bytes 1572868
  62.9 25.3 %copy-start.4 = (bf16[512,512]{1,0:T(8,128)(2,1)S(1)}, bf16[512,512]{1,0:T(8,128)(2,1)}, u32[]{:S(2)}) copy-start(bf16[512,512]{1,0:T(8,128)(2,1)} %w_self.1) | copy-start | bytes 1572868
  62.9 25.3 %copy-start.5 = (bf16[128,512]{1,0:T(8,128)(2,1)S(1)}, bf16[128,512]{1,0:T(8,128)(2,1)}, u32[]{:S(2)}) copy-start(bf16[128,512]{1,0:T(8,128)(2,1)} %cotangent.1) | copy-start | bytes 393220
  65.6 22.5 %collective-permute-start.1 = (f32[128,128]{1,0:T(8,128)S(1)}, f32[128,128]{1,0:T(8,128)}, u32[]{:S(2)}, u32[]{:S(2)}) collective-permute-start(f32[128,128]{1,0:T(8,128)S(1)} %local_sums.5), channel_id=1, source_target_pairs={{0,16},{16,32},{32,48},{48,0},{1,17},{17,33},{33,49},{49,1},{2,18}... | collective-permute-start | bytes 196616 | tf_op jit(solution)/shard_map/ppermute | solution.py:247
  72.1 16.0 %collective-permute-start.2 = (f32[128,128]{1,0:T(8,128)}, f32[128,128]{1,0:T(8,128)}, u32[]{:S(2)}, u32[]{:S(2)}) collective-permute-start(f32[128,128]{1,0:T(8,128)} %local_sums.6), channel_id=1, source_target_pairs={{0,32},{16,48},{32,0},{48,16},{1,33},{17,49},{33,1},{49,17},{2,34}... | collective-permute-start | bytes 196616 | tf_op jit(solution)/shard_map/ppermute | solution.py:247
  79.8 8.3 %collective-permute-start.3 = (f32[128,128]{1,0:T(8,128)}, f32[128,128]{1,0:T(8,128)}, u32[]{:S(2)}, u32[]{:S(2)}) collective-permute-start(f32[128,128]{1,0:T(8,128)} %local_sums.7), channel_id=1, source_target_pairs={{0,48},{16,0},{32,16},{48,32},{1,49},{17,1},{33,17},{49,33},{2,50}... | collective-permute-start | bytes 196616 | tf_op jit(solution)/shard_map/ppermute | solution.py:247
  90.7 7.3 %collective-permute-start.4 = (bf16[8,128,128]{2,1,0:T(8,128)(2,1)S(1)}, bf16[8,128,128]{2,1,0:T(8,128)(2,1)S(1)}, u32[]{:S(2)}, u32[]{:S(2)}) collective-permute-start(bf16[8,128,128]{2,1,0:T(8,128)(2,1)S(1)} %get-tuple-element.26), channel_id=1, source_target_pairs={{0,1},{1,0},{2,3},{3,2},{4,5},{5,4},{6,7},{7,6},{8,9},{9,8},{10,11... | collective-permute-start | bytes 786440 | tf_op jit(solution)/shard_map/ppermute | solution.py:263

commit v12 on v11

--- a/solution.py
+++ b/solution.py
@@ -50,10 +50,10 @@
         copy.wait()
 
 
-def split_kernel(codes_ref, remote_ref, local_ref, sems):
+def split_kernel(scalars, codes_ref, remote_ref, local_ref, sems):
     copies = []
     for x in range(NX):
-        codes = codes_ref.at[x % 2, x // 2]
+        codes = codes_ref.at[x % 2, lax.rem(x // 2 + scalars[0], 2)]
         copies.append(pltpu.make_async_copy(codes.at[TOLD:], local_ref.at[x], sems.at[x]))
         copies[-1].start()
         remote_ref[x] = codes[0:TOLD]
@@ -193,12 +193,6 @@
     z, x, y, c = (lax.axis_index(a).astype(jnp.int32) for a in ("z", X, Y, "c"))
     swap = [(0, 1), (1, 0)]
 
-    features_t, quarters = vmem_call(
-        spread_kernel, "spread", [], [features], [((NX, T, T), BF16), ((NZ, NX, T, T), BF16)],
-        scratch=[pltpu.VMEM((NX, T, T), BF16), pltpu.SemaphoreType.DMA((NZ + 1,))], outside=2, bytes_accessed=1_500_000,
-    )
-    blocks = lax.all_to_all(quarters.reshape(OWNERS, T, T), ("z",) + X, 0, 0, tiled=True)
-
     codes_t = neighbours.T
     weights_t = edge_weights.T
     told = jnp.concatenate([send_count[0], send_list[0].reshape(1, GROUPS * CAP)], axis=1).astype(BF16)
@@ -208,10 +202,18 @@
     of_remote = jnp.concatenate([block[K_LOC:], row[K_LOC:], weights_t[K_LOC:], told], axis=0)
     of_local = jnp.concatenate([block[:K_LOC], gap, row[:K_LOC], gap, weights_t[:K_LOC], gap], axis=0)
     codes = jnp.concatenate([of_remote, of_local], axis=0)
+    features_after, codes = lax.optimization_barrier((features, codes))
+    features_t, quarters = vmem_call(
+        spread_kernel, "spread", [], [features_after], [((NX, T, T), BF16), ((NZ, NX, T, T), BF16)],
+        scratch=[pltpu.VMEM((NX, T, T), BF16), pltpu.SemaphoreType.DMA((NZ + 1,))], outside=2, bytes_accessed=1_500_000,
+    )
+    beside = lax.ppermute(codes, "x1", swap)
+    quarters, beside = lax.optimization_barrier((quarters, beside))
+    blocks = lax.all_to_all(quarters.reshape(OWNERS, T, T), ("z",) + X, 0, 0, tiled=True)
     forward = [[(i, (i + k) % NX) for i in range(NX)] for k in range(NX)]
-    codes = lax.all_gather(lax.all_gather(codes, "x1", axis=0), "x0", axis=0)
+    codes = lax.all_gather(jnp.stack([codes, beside]), "x0", axis=0)
     remote_codes, local_codes = vmem_call(
-        split_kernel, "split", [], [codes], [((NX, TOLD, T), BF16), ((NX, 48, T), BF16)],
+        split_kernel, "split", [lax.axis_index("x1").astype(jnp.int32)[None]], [codes], [((NX, TOLD, T), BF16), ((NX, 48, T), BF16)],
         scratch=[pltpu.SemaphoreType.DMA((NX,))], outside=1, bytes_accessed=100_000,
     )
     remote_codes = lax.all_gather(remote_codes, Y + ("c",), axis=0)

time: 140 us -> 144 us (1.029)
  starting transfers between devices: 40.1 us -> 48.2 us
  blocking collectives: 70.2 us -> 62.6 us
  other arithmetic: 0.54 us -> 2.58 us
    all_gather x2 -> x1, blocking collectives: 9.62 us -> 3.44 us  [body(): codes = lax.all_gather(jnp.stack([codes, beside]), 'x0', axis=0)]
    ppermute x0 -> x1, starting transfers between devices: none -> 5.47 us  [body(): beside = lax.ppermute(codes, 'x1', swap)]
    all_to_all x1, blocking collectives: 22.9 us -> 19.6 us  [body(): plane = added(lax.all_to_all(chip_grad, ('z',) + X, 0, 0, tiled=True), BF16)]
    all_to_all x1, starting transfers between devices: 7.59 us -> 10.1 us  [body(): lax.all_to_all(chip_sum.reshape(NX * NY, T, T), X + Y, 0, 0, tiled=True)]
    all_gather x1, blocking collectives: 20.6 us -> 23 us  [body(): remote_codes = lax.all_gather(remote_codes, Y + ('c',), axis=0)]
    ppermute x1, starting transfers between devices: 2.06 us -> 3.79 us  [body(): others = lax.ppermute(blocks, 'c', swap)]
    all_to_all x1, starting transfers between devices: 13.7 us -> 12.1 us  [body(): lax.all_to_all(quarters.reshape(OWNERS, T, T), ('z',) + X, 0, 0, tiled=True)]
  transfers between devices with their start and end apart: 7 -> 8, of which waited for: 3 -> 3; matrix products, arithmetic and copies ran while one was open for 1% -> 0% of each run, Pallas kernels for 11% -> 11%
where the time goes in v12:
time: 144 us; the launch traced here: 143 us
  blocking collectives  62.6 us (43%)
  starting transfers between devices  48.2 us (33%)
  Pallas kernels  22 us (15%)
  local copies, waits for them, and re-layouts  3.31 us (2%)
  waiting for transfers between devices  3.15 us (2%)
  other arithmetic  2.58 us (2%)
    all_gather x1, blocking collectives, body(): remote_codes = lax.all_gather(remote_codes, Y + ('c',), axis=0)  23 us
    pallas_call x12, Pallas kernels, vmem_call(): pl.pallas_call(kernel, in_specs=[pl.BlockSpec(memory_space=pltpu.SMEM)] *...  22 us
    all_to_all x1, blocking collectives, body(): plane = added(lax.all_to_all(chip_grad, ('z',) + X, 0, 0, tiled=True), BF16)  19.6 us
    all_to_all x1, starting transfers between devices, body(): lax.all_to_all(quarters.reshape(OWNERS, T, T), ('z',) + X, 0, 0, tiled=True)  12.1 us
    all_to_all x1, blocking collectives, body(): lax.all_to_all(jnp.broadcast_to(plane, (NY,) + plane.shape), Y, 0, 0, til...  11.5 us
    ppermute x3, starting transfers between devices, body(): near.append(lax.ppermute(sums, X, forward[NX - k]) if k else sums)  10.5 us
    all_to_all x1, starting transfers between devices, body(): lax.all_to_all(chip_sum.reshape(NX * NY, T, T), X + Y, 0, 0, tiled=True)  10.1 us
    ppermute x1, starting transfers between devices, body(): received = lax.ppermute(send, 'c', swap)  6.27 us
  transfers between devices with their start and end apart: 8, of which 3 were waited for; matrix products, arithmetic and copies ran while one was open for 0% of the time, Pallas kernels for 11%

profile of v12, /device:TPU:1, one launch (start us, length us, event | category | flops | bytes accessed | tf_op | source)
XLA Modules:
  0.0 142.8 jit_solution(5090659427069374741)
XLA Ops:
  0.6 0.7 convert.10
  1.3 0.7 convert_bitcast_fusion
  2.0 0.7 slice.45
  2.7 0.1 copy.13
  2.8 0.1 concatenate.20
  2.9 0.7 fusion.1
  3.6 0.1 fusion.9
  3.7 0.9 concatenate.22
  4.5 5.5 %collective-permute-start = (bf16[64,128]{1,0:T(8,128)(2,1)S(1)}, bf16[64,128]{1,0:T(8,128)(2,1)S(1)}, u32[]{:S(2)}, u32[]{:S(2)}) collective-permute-start(bf16[64,128]{1,0:T(8,128)(2,1)S(1)} %concatenate.22), channel_id=1, source_target_pairs={{0,32},{32,0},{1,33},{33,1},{2,34},{34,2},{3,35},{35,3},{4,36},{36... | collective-permute-start | bytes 49160 | tf_op jit(solution)/shard_map/ppermute | solution.py:210
  10.0 0.0 copy-start.1
  10.0 0.9 copy-done.1
  10.9 1.2 spread.1
  12.1 0.0 collective-permute-done
  12.1 12.1 %all-to-all-start = ((bf16[32,128,128]{2,1,0:T(8,128)(2,1)}), bf16[32,128,128]{2,1,0:T(8,128)(2,1)S(1)}, u32[]{:S(2)}, u32[]{:S(2)}) async-start(bf16[32,128,128]{2,1,0:T(8,128)(2,1)} %bitcast.54), calls=%async_computation | async-start | bytes 2097152 | tf_op jit(solution)/shard_map/all_to_all | solution.py:212
  24.2 3.4 %all-gather = bf16[4,64,128]{2,1,0:T(8,128)(2,1)S(1)} all-gather(bf16[2,64,128]{2,1,0:T(8,128)(2,1)S(1)} %pad_maximum_fusion), channel_id=2, replica_groups=mesh['z'=8,'x1'=2,'x0'=2,'y2'=2,'y1'=2,'y0'=2,'c'=2] {'x0'}, dimensions={0}, use_global_device_ids=true | all-gather | bytes 98304 | tf_op jit(solution)/shard_map/all_gather | solution.py:214
  27.7 0.6 split.1
  28.3 23.0 %all-gather.1 = bf16[64,16,128]{2,1,0:T(8,128)(2,1)S(1)} all-gather(bf16[4,16,128]{2,1,0:T(8,128)(2,1)S(1)} %get-tuple-element.24), channel_id=3, replica_groups=mesh['z'=8,'x1'=2,'x0'=2,'y2'=2,'y1'=2,'y0'=2,'c'=2] {'y2','y1','y0','c'}, dimensions={0}, use_global_device_ids=true | all-gather | bytes 278528 | tf_op jit(solution)/shard_map/all_gather | solution.py:219
  51.3 0.0 all-to-all-done.blocks_ref
  51.3 3.8 %collective-permute-start.1 = (bf16[32,128,128]{2,1,0:T(8,128)(2,1)S(1)}, bf16[32,128,128]{2,1,0:T(8,128)(2,1)S(1)}, u32[]{:S(2)}, u32[]{:S(2)}) collective-permute-start(bf16[32,128,128]{2,1,0:T(8,128)(2,1)S(1)} %all-to-all-done.blocks_ref), channel_id=1, source_target_pairs={{0,1},{1,0},{2,3},{3,2},{4,5},{5,4},{6,7},{7,6},{8,9},{9,8},{10,11... | collective-permute-start | bytes 3145736 | tf_op jit(solution)/shard_map/ppermute | solution.py:229
  55.2 0.1 slice_convert_fusion
  55.2 0.1 select_reduce_fusion
  55.4 0.1 select_reduce_fusion.1
  55.5 1.6 %own_group.1.part_ref = f32[4,8,128,128]{3,2,1,0:T(8,128)S(1)} custom-call(s32[1]{0:T(128)} %bitcast.core, s32[4,128]{1,0:T(4,128)S(1)} %get-tuple-element.37.here, s32[4,16]{1,0:T(4,128)S(1)} %get-tuple-element.35.before, bf16[32,128,128]{2,1,0:T(8,128)(2,1)S(1)} %all-to-all-done.blocks_ref, bf16[16,4,16,128]{3,2,1,0:T(8,128)(2,1)S(1)} %bitcast.50), custom_call_target="tpu_custom_call" | custom-call | flops 300000000 | bytes 3500000 | tf_op jit(solution)/shard_map/own_group/pallas_call | solution.py:28
  57.1 0.3 collective-permute-done.1.blocks_ref
  57.4 2.6 %other_group.1 = bf16[4,8,128,128]{3,2,1,0:T(8,128)(2,1)} custom-call(s32[1]{0:T(128)} %bitcast.core, s32[4,128]{1,0:T(4,128)S(1)} %get-tuple-element.38.here, s32[4,16]{1,0:T(4,128)S(1)} %get-tuple-element.36.before, bf16[32,128,128]{2,1,0:T(8,128)(2,1)S(1)} %collective-permute-done.1.blocks_ref, bf16[16,4,16,128]{3,2,1,0:T(8,128)(2,1)S(1)} %bitcast.51, ...), custom_call_target="tpu_custom_call" | custom-call | flops 300000000 | bytes 5500000 | tf_op jit(solution)/shard_map/other_group/pallas_call | solution.py:28
  60.0 0.0 copy-start
  60.0 10.1 %all-to-all-start.1 = ((bf16[32,128,128]{2,1,0:T(8,128)(2,1)}), bf16[32,128,128]{2,1,0:T(8,128)(2,1)S(1)}, u32[]{:S(2)}, u32[]{:S(2)}) async-start(bf16[32,128,128]{2,1,0:T(8,128)(2,1)} %bitcast.53), calls=%async_computation.1 | async-start | bytes 2097152 | tf_op jit(solution)/shard_map/all_to_all | solution.py:239
  70.1 0.1 pad_add_fusion.1.scalars
  70.2 0.0 copy-start.5
  70.2 2.7 %local_sums.5 = f32[128,128]{1,0:T(8,128)S(1)} custom-call(s32[2]{0:T(128)S(1)} %pad_add_fusion.1.scalars, bf16[32,128,128]{2,1,0:T(8,128)(2,1)S(1)} %all-to-all-done.blocks_ref, bf16[4,48,128]{2,1,0:T(8,128)(2,1)S(1)} %copy-done), custom_call_target="tpu_custom_call" | custom-call | flops 150000000 | bytes 1200000 | tf_op jit(solution)/shard_map/local_sums/pallas_call | solution.py:28
  73.0 3.1 %collective-permute-start.2 = (f32[128,128]{1,0:T(8,128)S(1)}, f32[128,128]{1,0:T(8,128)}, u32[]{:S(2)}, u32[]{:S(2)}) collective-permute-start(f32[128,128]{1,0:T(8,128)S(1)} %local_sums.5), channel_id=1, source_target_pairs={{0,16},{16,32},{32,48},{48,0},{1,17},{17,33},{33,49},{49,1},{2,18}... | collective-permute-start | bytes 196616 | tf_op jit(solution)/shard_map/ppermute | solution.py:249
  76.1 3.4 %local_sums.6 = f32[128,128]{1,0:T(8,128)} custom-call(s32[2]{0:T(128)S(1)} %pad_add_fusion.1.scalars, bf16[32,128,128]{2,1,0:T(8,128)(2,1)S(1)} %all-to-all-done.blocks_ref, bf16[4,48,128]{2,1,0:T(8,128)(2,1)S(1)} %copy-done), custom_call_target="tpu_custom_call" | custom-call | flops 150000000 | bytes 1200000 | tf_op jit(solution)/shard_map/local_sums/pallas_call | solution.py:28
  79.5 4.3 %collective-permute-start.3 = (f32[128,128]{1,0:T(8,128)}, f32[128,128]{1,0:T(8,128)}, u32[]{:S(2)}, u32[]{:S(2)}) collective-permute-start(f32[128,128]{1,0:T(8,128)} %local_sums.6), channel_id=1, source_target_pairs={{0,32},{16,48},{32,0},{48,16},{1,33},{17,49},{33,1},{49,17},{2,34}... | collective-permute-start | bytes 196616 | tf_op jit(solution)/shard_map/ppermute | solution.py:249
  83.8 3.4 %local_sums.7 = f32[128,128]{1,0:T(8,128)} custom-call(s32[2]{0:T(128)S(1)} %pad_add_fusion.1.scalars, bf16[32,128,128]{2,1,0:T(8,128)(2,1)S(1)} %all-to-all-done.blocks_ref, bf16[4,48,128]{2,1,0:T(8,128)(2,1)S(1)} %copy-done), custom_call_target="tpu_custom_call" | custom-call | flops 150000000 | bytes 1200000 | tf_op jit(solution)/shard_map/local_sums/pallas_call | solution.py:28
  87.2 3.0 %collective-permute-start.4 = (f32[128,128]{1,0:T(8,128)}, f32[128,128]{1,0:T(8,128)}, u32[]{:S(2)}, u32[]{:S(2)}) collective-permute-start(f32[128,128]{1,0:T(8,128)} %local_sums.7), channel_id=1, source_target_pairs={{0,48},{16,0},{32,16},{48,32},{1,49},{17,1},{33,17},{49,33},{2,50}... | collective-permute-start | bytes 196616 | tf_op jit(solution)/shard_map/ppermute | solution.py:249
  90.2 3.4 %local_sums.4.near_0_in = f32[128,128]{1,0:T(8,128)} custom-call(s32[2]{0:T(128)S(1)} %pad_add_fusion.1.scalars, bf16[32,128,128]{2,1,0:T(8,128)(2,1)S(1)} %all-to-all-done.blocks_ref, bf16[4,48,128]{2,1,0:T(8,128)(2,1)S(1)} %copy-done), custom_call_target="tpu_custom_call" | custom-call | flops 150000000 | bytes 1200000 | tf_op jit(solution)/shard_map/local_sums/pallas_call | solution.py:28
  93.6 1.7 %all-to-all-done.1 = bf16[32,128,128]{2,1,0:T(8,128)(2,1)S(1)} async-done(((bf16[32,128,128]{2,1,0:T(8,128)(2,1)}), bf16[32,128,128]{2,1,0:T(8,128)(2,1)S(1)}, u32[]{:S(2)}, u32[]{:S(2)}) %all-to-all-start.1) | async-done | bytes 1048608 | tf_op jit(solution)/shard_map/all_to_all | solution.py:239
  95.3 0.1 pad_add_fusion.scalars
  95.4 0.0 collective-permute-done.2.near_1_in
  95.4 2.6 %dense.1 = (bf16[128,512]{1,0:T(8,128)(2,1)}, bf16[8,128,128]{2,1,0:T(8,128)(2,1)S(1)}, bf16[8,128,128]{2,1,0:T(8,128)(2,1)S(1)}) custom-call(s32[2]{0:T(128)S(1)} %pad_add_fusion.scalars, f32[128,128]{1,0:T(8,128)} %local_sums.4.near_0_in, f32[128,128]{1,0:T(8,128)} %collective-permute-done.2.near_1_in, f32[128,128]{1,0:T(8,128)} %collective-permute-done.3.near_2_in, ...), custom_call_target="tpu_custom_call" | custom-call | flops 150000000 | bytes 3500000 | tf_op jit(solution)/shard_map/dense/pallas_call | solution.py:28
  98.0 6.3 %collective-permute-start.5 = (bf16[8,128,128]{2,1,0:T(8,128)(2,1)S(1)}, bf16[8,128,128]{2,1,0:T(8,128)(2,1)S(1)}, u32[]{:S(2)}, u32[]{:S(2)}) collective-permute-start(bf16[8,128,128]{2,1,0:T(8,128)(2,1)S(1)} %get-tuple-element.34), channel_id=1, source_target_pairs={{0,1},{1,0},{2,3},{3,2},{4,5},{5,4},{6,7},{7,6},{8,9},{9,8},{10,11... | collective-permute-start | bytes 786440 | tf_op jit(solution)/shard_map/ppermute | solution.py:265
  104.3 1.1 collective-permute-done.5.received_ref
  105.4 0.4 gradient.1
  105.9 19.6 %all_to_all.20.parts_ref = bf16[32,16,512]{2,1,0:T(8,128)(2,1)S(1)} all-to-all(bf16[32,16,512]{2,1,0:T(8,128)(2,1)S(1)} %gradient.1), channel_id=1, replica_groups=mesh['z'=8,'x1'=2,'x0'=2,'y2'=2,'y1'=2,'y0'=2,'c'=2] {'z','x1','x0'}, dimensions={0} | all-to-all | bytes 1048576 | tf_op jit(solution)/shard_map/all_to_all | solution.py:269
  125.5 0.1 added.2
  125.6 11.5 %all_to_all.21.parts_ref = bf16[8,16,512]{2,1,0:T(8,128)(2,1)S(1)} all-to-all(bf16[8,16,512]{2,1,0:T(8,128)(2,1)S(1)} %broadcast_in_dim.58), channel_id=1, replica_groups=mesh['z'=8,'x1'=2,'x0'=2,'y2'=2,'y1'=2,'y0'=2,'c'=2] {'y2','y1','y0'}, dimensions={0} | all-to-all | bytes 262144 | tf_op jit(solution)/shard_map/all_to_all | solution.py:270
  137.2 5.0 %all-gather.2 = f32[32,512]{1,0:T(8,128)S(1)} all-gather(f32[16,512]{1,0:T(8,128)S(1)} %added.3), channel_id=4, replica_groups=mesh['z'=8,'x1'=2,'x0'=2,'y2'=2,'y1'=2,'y0'=2,'c'=2] {'c'}, dimensions={0}, use_global_device_ids=true | all-gather | bytes 98304 | tf_op jit(solution)/shard_map/all_gather | solution.py:271
  142.2 0.6 fusion.11
  (18 shorter events, 0.1 us)
Async XLA Ops:
  4.5 7.6 %collective-permute-start = (bf16[64,128]{1,0:T(8,128)(2,1)S(1)}, bf16[64,128]{1,0:T(8,128)(2,1)S(1)}, u32[]{:S(2)}, u32[]{:S(2)}) collective-permute-start(bf16[64,128]{1,0:T(8,128)(2,1)S(1)} %concatenate.22), channel_id=1, source_target_pairs={{0,32},{32,0},{1,33},{33,1},{2,34},{34,2},{3,35},{35,3},{4,36},{36... | collective-permute-start | bytes 49160 | tf_op jit(solution)/shard_map/ppermute | solution.py:210
  10.0 0.9 copy-start.1
  12.1 39.2 %all-to-all-start = ((bf16[32,128,128]{2,1,0:T(8,128)(2,1)}), bf16[32,128,128]{2,1,0:T(8,128)(2,1)S(1)}, u32[]{:S(2)}, u32[]{:S(2)}) async-start(bf16[32,128,128]{2,1,0:T(8,128)(2,1)} %bitcast.54), calls=%async_computation | async-start | bytes 2097152 | tf_op jit(solution)/shard_map/all_to_all | solution.py:212
  51.3 6.1 %collective-permute-start.1 = (bf16[32,128,128]{2,1,0:T(8,128)(2,1)S(1)}, bf16[32,128,128]{2,1,0:T(8,128)(2,1)S(1)}, u32[]{:S(2)}, u32[]{:S(2)}) collective-permute-start(bf16[32,128,128]{2,1,0:T(8,128)(2,1)S(1)} %all-to-all-done.blocks_ref), channel_id=1, source_target_pairs={{0,1},{1,0},{2,3},{3,2},{4,5},{5,4},{6,7},{7,6},{8,9},{9,8},{10,11... | collective-permute-start | bytes 3145736 | tf_op jit(solution)/shard_map/ppermute | solution.py:229
  60.0 10.2 %copy-start = (bf16[4,48,128]{2,1,0:T(8,128)(2,1)S(1)}, bf16[4,48,128]{2,1,0:T(8,128)(2,1)}, u32[]{:S(2)}) copy-start(bf16[4,48,128]{2,1,0:T(8,128)(2,1)} %get-tuple-element.29.told_ref) | copy-start | bytes 147460
  60.0 35.3 %all-to-all-start.1 = ((bf16[32,128,128]{2,1,0:T(8,128)(2,1)}), bf16[32,128,128]{2,1,0:T(8,128)(2,1)S(1)}, u32[]{:S(2)}, u32[]{:S(2)}) async-start(bf16[32,128,128]{2,1,0:T(8,128)(2,1)} %bitcast.53), calls=%async_computation.1 | async-start | bytes 2097152 | tf_op jit(solution)/shard_map/all_to_all | solution.py:239
  70.2 25.2 %copy-start.2 = (bf16[128,512]{1,0:T(8,128)(2,1)S(1)}, bf16[128,512]{1,0:T(8,128)(2,1)}, u32[]{:S(2)}) copy-start(bf16[128,512]{1,0:T(8,128)(2,1)} %features.1) | copy-start | bytes 393220
  70.2 25.2 %copy-start.3 = (bf16[512,512]{1,0:T(8,128)(2,1)S(1)}, bf16[512,512]{1,0:T(8,128)(2,1)}, u32[]{:S(2)}) copy-start(bf16[512,512]{1,0:T(8,128)(2,1)} %w_agg.1) | copy-start | bytes 1572868
  70.2 25.2 %copy-start.4 = (bf16[512,512]{1,0:T(8,128)(2,1)S(1)}, bf16[512,512]{1,0:T(8,128)(2,1)}, u32[]{:S(2)}) copy-start(bf16[512,512]{1,0:T(8,128)(2,1)} %w_self.1) | copy-start | bytes 1572868
  70.2 25.2 %copy-start.5 = (bf16[128,512]{1,0:T(8,128)(2,1)S(1)}, bf16[128,512]{1,0:T(8,128)(2,1)}, u32[]{:S(2)}) copy-start(bf16[128,512]{1,0:T(8,128)(2,1)} %cotangent.1) | copy-start | bytes 393220
  73.0 22.4 %collective-permute-start.2 = (f32[128,128]{1,0:T(8,128)S(1)}, f32[128,128]{1,0:T(8,128)}, u32[]{:S(2)}, u32[]{:S(2)}) collective-permute-start(f32[128,128]{1,0:T(8,128)S(1)} %local_sums.5), channel_id=1, source_target_pairs={{0,16},{16,32},{32,48},{48,0},{1,17},{17,33},{33,49},{49,1},{2,18}... | collective-permute-start | bytes 196616 | tf_op jit(solution)/shard_map/ppermute | solution.py:249
  79.5 15.9 %collective-permute-start.3 = (f32[128,128]{1,0:T(8,128)}, f32[128,128]{1,0:T(8,128)}, u32[]{:S(2)}, u32[]{:S(2)}) collective-permute-start(f32[128,128]{1,0:T(8,128)} %local_sums.6), channel_id=1, source_target_pairs={{0,32},{16,48},{32,0},{48,16},{1,33},{17,49},{33,1},{49,17},{2,34}... | collective-permute-start | bytes 196616 | tf_op jit(solution)/shard_map/ppermute | solution.py:249
  87.2 8.2 %collective-permute-start.4 = (f32[128,128]{1,0:T(8,128)}, f32[128,128]{1,0:T(8,128)}, u32[]{:S(2)}, u32[]{:S(2)}) collective-permute-start(f32[128,128]{1,0:T(8,128)} %local_sums.7), channel_id=1, source_target_pairs={{0,48},{16,0},{32,16},{48,32},{1,49},{17,1},{33,17},{49,33},{2,50}... | collective-permute-start | bytes 196616 | tf_op jit(solution)/shard_map/ppermute | solution.py:249
  98.0 7.4 %collective-permute-start.5 = (bf16[8,128,128]{2,1,0:T(8,128)(2,1)S(1)}, bf16[8,128,128]{2,1,0:T(8,128)(2,1)S(1)}, u32[]{:S(2)}, u32[]{:S(2)}) collective-permute-start(bf16[8,128,128]{2,1,0:T(8,128)(2,1)S(1)} %get-tuple-element.34), channel_id=1, source_target_pairs={{0,1},{1,0},{2,3},{3,2},{4,5},{5,4},{6,7},{7,6},{8,9},{9,8},{10,11... | collective-permute-start | bytes 786440 | tf_op jit(solution)/shard_map/ppermute | solution.py:265

commit v13 on v11

--- a/solution.py
+++ b/solution.py
@@ -127,12 +127,12 @@
 
 
 def dense_kernel(
-    scalars, near_0_in, near_1_in, near_2_in, near_3_in, weights_in, features_t_in, arrived, features, w_agg, w_self, cotangent,
-    hidden_ref, send_ref, keep_ref, agg_t, near_0, near_1, near_2, near_3, weights_t, features_t, sems,
+    scalars, near_0_in, weights_in, from_self_in, features_t_in, arrived, near_1, near_2, near_3, w_agg, cotangent,
+    preact_ref, send_ref, keep_ref, agg_t, near_0, weights_t, from_self, features_t, sems,
 ):
     own_x, own_c = scalars[0], scalars[1]
-    sources = (near_0_in, near_1_in, near_2_in, near_3_in, weights_in, features_t_in)
-    targets = (near_0, near_1, near_2, near_3, weights_t, features_t)
+    sources = (near_0_in, weights_in, from_self_in, features_t_in)
+    targets = (near_0, weights_t, from_self, features_t)
     copies = [pltpu.make_async_copy(of, to, sems.at[i]) for i, (of, to) in enumerate(zip(sources, targets))]
     for copy in copies:
         copy.start()
@@ -142,20 +142,22 @@
         for y in range(1, NY):
             summed = summed + arrived[x, y].astype(F32)
         agg_t[x * T : (x + 1) * T, :] = summed
-    for k, near in enumerate((near_0, near_1, near_2, near_3)):
-        copies[k].wait()
+    for k, near in ((1, near_1), (2, near_2), (3, near_3), (0, near_0)):
+        if k == 0:
+            copies[0].wait()
         quarter = lax.rem(own_x + (NX - k), NX)
         agg_t[pl.ds(pl.multiple_of(quarter * T, T), T), :] += near[...]
-    copies[4].wait()
+    copies[1].wait()
     degree = 1.0 + jnp.sum(weights_t[...].astype(F32), axis=0, keepdims=True)
     aggregate = (agg_t[...] / degree).astype(BF16)
     contract = (((0,), (0,)), ((), ()))
     preact = lax.dot_general(aggregate, w_agg[...], contract, preferred_element_type=F32)
-    preact = preact + jnp.dot(features[...], w_self[...], preferred_element_type=F32)
+    copies[2].wait()
+    preact = preact + from_self[...]
+    preact_ref[...] = preact
     sigma = jax.nn.sigmoid(preact)
-    hidden_ref[...] = (preact * sigma).astype(BF16)
     grad_pre = (cotangent[...].astype(F32) * sigma * (1.0 + preact * (1.0 - sigma))).astype(BF16)
-    copies[5].wait()
+    copies[3].wait()
     for j in range(NX):
         columns = grad_pre[:, j * T : (j + 1) * T]
         keep_ref[NX + j] = columns
@@ -163,6 +165,18 @@
         of_agg, of_self = aggregate[j * T : (j + 1) * T, :], features_t[j]
         keep_ref[j] = jnp.where(own_c == 0, of_agg, of_self)
         send_ref[j] = jnp.where(own_c == 0, of_self, of_agg)
+
+
+def self_kernel(features, w_self, out_ref, product, sem):
+    product[...] = jnp.dot(features[...], w_self[...], preferred_element_type=F32)
+    copy = pltpu.make_async_copy(product, out_ref, sem)
+    copy.start()
+    copy.wait()
+
+
+def hidden_kernel(preact_ref, hidden_ref):
+    preact = preact_ref[...]
+    hidden_ref[...] = (preact * jax.nn.sigmoid(preact)).astype(BF16)
 
 
 def grad_kernel(keep_ref, received_ref, grad_ref):
@@ -236,6 +250,7 @@
     )
     arrived = lax.all_to_all(chip_sum.reshape(NX * NY, T, T), X + Y, 0, 0, tiled=True)
 
+    features_later, _ = lax.optimization_barrier((features, chip_sum))
     near = []
     for k in (2, 1, 3, 0):
         (sums,) = vmem_call(
@@ -249,11 +264,15 @@
 
     share = width // OWNERS
     operands = ((2 * NX, T, T), BF16)
+    (from_self,) = vmem_call(
+        self_kernel, "from_self", [], [features_later, w_self], [((T, width), F32)],
+        scratch=[pltpu.VMEM((T, width), F32), pltpu.SemaphoreType.DMA], outside=1, flops=67_000_000, bytes_accessed=900_000,
+    )
     arrived, x, c = lax.optimization_barrier((arrived, x, c))
-    outside = [near_0, one, two, three, weights_t, features_t]
-    hidden, send, keep = vmem_call(
-        dense_kernel, "dense", [jnp.stack([x, c])], [arrived.reshape(NX, NY, T, T), features, w_agg, w_self, cotangent],
-        [((T, width), BF16), operands, operands],
+    outside = [near_0, weights_t, from_self, features_t]
+    preact, send, keep = vmem_call(
+        dense_kernel, "dense", [jnp.stack([x, c])], [arrived.reshape(NX, NY, T, T), one, two, three, w_agg, cotangent],
+        [((T, width), F32), operands, operands],
         scratch=[pltpu.VMEM((width, T), F32)]
         + [pltpu.VMEM(of.shape, of.dtype) for of in outside]
         + [pltpu.SemaphoreType.DMA((len(outside),))],
@@ -261,6 +280,8 @@
         flops=150_000_000, bytes_accessed=3_500_000, transcendentals=65536,
     )
     received = lax.ppermute(send, "c", swap)
+    (hidden,) = vmem_call(hidden_kernel, "hidden", [], [preact], [((T, width), BF16)], flops=1_000_000, bytes_accessed=400_000, transcendentals=65536)
+    received, hidden = lax.optimization_barrier((received, hidden))
     (chip_grad,) = vmem_call(
         grad_kernel, "gradient", [], [keep, received], [((OWNERS, share, width), BF16)], flops=300_000_000, bytes_accessed=1_000_000
     )

time: 140 us -> 139 us (level)
    pallas_call x12 -> x14, Pallas kernels: 22 us -> 21.8 us  [vmem_call(): pl.pallas_call(kernel, in_specs=[pl.BlockSpec(memory_space=pltpu.SMEM)] *...]
where the time goes in v13:
time: 139 us
  blocking collectives  70.2 us (51%)
  starting transfers between devices  40.2 us (29%)
  Pallas kernels  21.8 us (16%)
  waiting for transfers between devices  2.83 us (2%)
  local copies, waits for them, and re-layouts  1.97 us (1%)
    all_to_all x1, blocking collectives, body(): plane = added(lax.all_to_all(chip_grad, ('z',) + X, 0, 0, tiled=True), BF16)  22.9 us
    pallas_call x14, Pallas kernels, vmem_call(): pl.pallas_call(kernel, in_specs=[pl.BlockSpec(memory_space=pltpu.SMEM)] *...  21.8 us
    all_gather x1, blocking collectives, body(): remote_codes = lax.all_gather(remote_codes, Y + ('c',), axis=0)  20.6 us
    all_to_all x1, starting transfers between devices, body(): lax.all_to_all(quarters.reshape(OWNERS, T, T), ('z',) + X, 0, 0, tiled=True)  13.7 us
    all_to_all x1, blocking collectives, body(): lax.all_to_all(jnp.broadcast_to(plane, (NY,) + plane.shape), Y, 0, 0, til...  12 us
    ppermute x3, starting transfers between devices, body(): near.append(lax.ppermute(sums, X, forward[NX - k]) if k else sums)  10.7 us
    all_gather x2, blocking collectives, body(): codes = lax.all_gather(lax.all_gather(codes, 'x1', axis=0), 'x0', axis=0)  9.62 us
    all_to_all x1, starting transfers between devices, body(): lax.all_to_all(chip_sum.reshape(NX * NY, T, T), X + Y, 0, 0, tiled=True)  7.6 us
  transfers between devices with their start and end apart: 7, of which 3 were waited for; matrix products, arithmetic and copies ran while one was open for 1% of the time, Pallas kernels for 11%

profile of v13, /device:TPU:1, one launch (start us, length us, event | category | flops | bytes accessed | tf_op | source)
XLA Modules:
  0.0 138.5 jit_solution(3394548586141584946)
XLA Ops:
  0.6 0.0 copy-start.2
  0.6 0.9 copy-done.2
  1.5 1.2 spread.1
  2.7 13.7 %all-to-all-start = ((bf16[32,128,128]{2,1,0:T(8,128)(2,1)}), bf16[32,128,128]{2,1,0:T(8,128)(2,1)S(1)}, u32[]{:S(2)}, u32[]{:S(2)}) async-start(bf16[32,128,128]{2,1,0:T(8,128)(2,1)} %bitcast.52), calls=%async_computation | async-start | bytes 2097152 | tf_op jit(solution)/shard_map/all_to_all | solution.py:214
  16.5 0.1 copy.13
  16.6 0.1 concatenate.20
  16.7 0.0 copy-done.7
  16.8 0.1 fusion.9
  16.9 0.2 concatenate.22
  17.1 4.9 %all-gather = bf16[128,128]{1,0:T(8,128)(2,1)S(1)} all-gather(bf16[64,128]{1,0:T(8,128)(2,1)S(1)} %concatenate.22), channel_id=2, replica_groups=mesh['z'=8,'x1'=2,'x0'=2,'y2'=2,'y1'=2,'y0'=2,'c'=2] {'x1'}, dimensions={0}, use_global_device_ids=true | all-gather | bytes 49152 | tf_op jit(solution)/shard_map/all_gather | solution.py:226
  21.9 4.7 %all-gather.1 = bf16[4,64,128]{2,1,0:T(8,128)(2,1)S(1)} all-gather(bf16[2,64,128]{2,1,0:T(8,128)(2,1)S(1)} %bitcast.55), channel_id=3, replica_groups=mesh['z'=8,'x1'=2,'x0'=2,'y2'=2,'y1'=2,'y0'=2,'c'=2] {'x0'}, dimensions={0}, use_global_device_ids=true | all-gather | bytes 98304 | tf_op jit(solution)/shard_map/all_gather | solution.py:226
  26.7 0.6 split.1
  27.3 20.6 %all-gather.2 = bf16[64,16,128]{2,1,0:T(8,128)(2,1)S(1)} all-gather(bf16[4,16,128]{2,1,0:T(8,128)(2,1)S(1)} %get-tuple-element.19), channel_id=4, replica_groups=mesh['z'=8,'x1'=2,'x0'=2,'y2'=2,'y1'=2,'y0'=2,'c'=2] {'y2','y1','y0','c'}, dimensions={0}, use_global_device_ids=true | all-gather | bytes 278528 | tf_op jit(solution)/shard_map/all_gather | solution.py:231
  48.0 0.0 all-to-all-done.blocks_ref
  48.0 2.1 %collective-permute-start = (bf16[32,128,128]{2,1,0:T(8,128)(2,1)S(1)}, bf16[32,128,128]{2,1,0:T(8,128)(2,1)S(1)}, u32[]{:S(2)}, u32[]{:S(2)}) collective-permute-start(bf16[32,128,128]{2,1,0:T(8,128)(2,1)S(1)} %all-to-all-done.blocks_ref), channel_id=1, source_target_pairs={{0,1},{1,0},{2,3},{3,2},{4,5},{5,4},{6,7},{7,6},{8,9},{9,8},{10,11... | collective-permute-start | bytes 3145736 | tf_op jit(solution)/shard_map/ppermute | solution.py:241
  50.1 0.1 slice_convert_fusion
  50.2 0.1 select_reduce_fusion
  50.3 0.1 select_reduce_fusion.1
  50.4 1.6 %own_group.1.part_ref = f32[4,8,128,128]{3,2,1,0:T(8,128)S(1)} custom-call(s32[1]{0:T(128)} %bitcast.core, s32[4,128]{1,0:T(4,128)S(1)} %get-tuple-element.35.here, s32[4,16]{1,0:T(4,128)S(1)} %get-tuple-element.33.before, bf16[32,128,128]{2,1,0:T(8,128)(2,1)S(1)} %all-to-all-done.blocks_ref, bf16[16,4,16,128]{3,2,1,0:T(8,128)(2,1)S(1)} %bitcast.48), custom_call_target="tpu_custom_call" | custom-call | flops 300000000 | bytes 3500000 | tf_op jit(solution)/shard_map/own_group/pallas_call | solution.py:28
  52.0 0.5 collective-permute-done.blocks_ref
  52.5 2.6 %other_group.1 = bf16[4,8,128,128]{3,2,1,0:T(8,128)(2,1)} custom-call(s32[1]{0:T(128)} %bitcast.core, s32[4,128]{1,0:T(4,128)S(1)} %get-tuple-element.36.here, s32[4,16]{1,0:T(4,128)S(1)} %get-tuple-element.34.before, bf16[32,128,128]{2,1,0:T(8,128)(2,1)S(1)} %collective-permute-done.blocks_ref, bf16[16,4,16,128]{3,2,1,0:T(8,128)(2,1)S(1)} %bitcast.49, ...), custom_call_target="tpu_custom_call" | custom-call | flops 300000000 | bytes 5500000 | tf_op jit(solution)/shard_map/other_group/pallas_call | solution.py:28
  55.1 7.6 %all-to-all-start.1 = ((bf16[32,128,128]{2,1,0:T(8,128)(2,1)}), bf16[32,128,128]{2,1,0:T(8,128)(2,1)S(1)}, u32[]{:S(2)}, u32[]{:S(2)}) async-start(bf16[32,128,128]{2,1,0:T(8,128)(2,1)} %bitcast.51), calls=%async_computation.1 | async-start | bytes 2097152 | tf_op jit(solution)/shard_map/all_to_all | solution.py:251
  62.7 0.1 pad_add_fusion.1.scalars
  62.8 2.7 %local_sums.5 = f32[128,128]{1,0:T(8,128)S(1)} custom-call(s32[2]{0:T(128)S(1)} %pad_add_fusion.1.scalars, bf16[32,128,128]{2,1,0:T(8,128)(2,1)S(1)} %all-to-all-done.blocks_ref, bf16[4,48,128]{2,1,0:T(8,128)(2,1)S(1)} %copy-done), custom_call_target="tpu_custom_call" | custom-call | flops 150000000 | bytes 1200000 | tf_op jit(solution)/shard_map/local_sums/pallas_call | solution.py:28
  65.6 0.0 copy-start.4
  65.6 0.0 copy-start.5
  65.6 3.3 %collective-permute-start.1 = (f32[128,128]{1,0:T(8,128)S(1)}, f32[128,128]{1,0:T(8,128)S(1)}, u32[]{:S(2)}, u32[]{:S(2)}) collective-permute-start(f32[128,128]{1,0:T(8,128)S(1)} %local_sums.5), channel_id=1, source_target_pairs={{0,16},{16,32},{32,48},{48,0},{1,17},{17,33},{33,49},{49,1},{2,18}... | collective-permute-start | bytes 196616 | tf_op jit(solution)/shard_map/ppermute | solution.py:262
  68.9 2.7 %local_sums.6 = f32[128,128]{1,0:T(8,128)S(1)} custom-call(s32[2]{0:T(128)S(1)} %pad_add_fusion.1.scalars, bf16[32,128,128]{2,1,0:T(8,128)(2,1)S(1)} %all-to-all-done.blocks_ref, bf16[4,48,128]{2,1,0:T(8,128)(2,1)S(1)} %copy-done), custom_call_target="tpu_custom_call" | custom-call | flops 150000000 | bytes 1200000 | tf_op jit(solution)/shard_map/local_sums/pallas_call | solution.py:28
  71.6 4.3 %collective-permute-start.2 = (f32[128,128]{1,0:T(8,128)S(1)}, f32[128,128]{1,0:T(8,128)S(1)}, u32[]{:S(2)}, u32[]{:S(2)}) collective-permute-start(f32[128,128]{1,0:T(8,128)S(1)} %local_sums.6), channel_id=1, source_target_pairs={{0,32},{16,48},{32,0},{48,16},{1,33},{17,49},{33,1},{49,17},{2,34}... | collective-permute-start | bytes 196616 | tf_op jit(solution)/shard_map/ppermute | solution.py:262
  76.0 2.7 %local_sums.7 = f32[128,128]{1,0:T(8,128)S(1)} custom-call(s32[2]{0:T(128)S(1)} %pad_add_fusion.1.scalars, bf16[32,128,128]{2,1,0:T(8,128)(2,1)S(1)} %all-to-all-done.blocks_ref, bf16[4,48,128]{2,1,0:T(8,128)(2,1)S(1)} %copy-done), custom_call_target="tpu_custom_call" | custom-call | flops 150000000 | bytes 1200000 | tf_op jit(solution)/shard_map/local_sums/pallas_call | solution.py:28
  78.7 3.1 %collective-permute-start.3 = (f32[128,128]{1,0:T(8,128)S(1)}, f32[128,128]{1,0:T(8,128)S(1)}, u32[]{:S(2)}, u32[]{:S(2)}) collective-permute-start(f32[128,128]{1,0:T(8,128)S(1)} %local_sums.7), channel_id=1, source_target_pairs={{0,48},{16,0},{32,16},{48,32},{1,49},{17,1},{33,17},{49,33},{2,50}... | collective-permute-start | bytes 196616 | tf_op jit(solution)/shard_map/ppermute | solution.py:262
  81.8 3.4 %local_sums.4.near_0_in = f32[128,128]{1,0:T(8,128)} custom-call(s32[2]{0:T(128)S(1)} %pad_add_fusion.1.scalars, bf16[32,128,128]{2,1,0:T(8,128)(2,1)S(1)} %all-to-all-done.blocks_ref, bf16[4,48,128]{2,1,0:T(8,128)(2,1)S(1)} %copy-done), custom_call_target="tpu_custom_call" | custom-call | flops 150000000 | bytes 1200000 | tf_op jit(solution)/shard_map/local_sums/pallas_call | solution.py:28
  85.2 1.0 from_self.1.from_self_in
  86.2 1.9 %all-to-all-done.1 = bf16[32,128,128]{2,1,0:T(8,128)(2,1)S(1)} async-done(((bf16[32,128,128]{2,1,0:T(8,128)(2,1)}), bf16[32,128,128]{2,1,0:T(8,128)(2,1)S(1)}, u32[]{:S(2)}, u32[]{:S(2)}) %all-to-all-start.1) | async-done | bytes 1048608 | tf_op jit(solution)/shard_map/all_to_all | solution.py:251
  88.0 0.1 pad_add_fusion.scalars
  88.1 0.0 collective-permute-done.1.near_1
  88.1 0.0 collective-permute-done.2.near_2
  88.1 0.0 collective-permute-done.3.near_3
  88.1 2.0 %dense.1 = (f32[128,512]{1,0:T(8,128)S(1)}, bf16[8,128,128]{2,1,0:T(8,128)(2,1)S(1)}, bf16[8,128,128]{2,1,0:T(8,128)(2,1)S(1)}) custom-call(s32[2]{0:T(128)S(1)} %pad_add_fusion.scalars, f32[128,128]{1,0:T(8,128)} %local_sums.4.near_0_in, bf16[16,128]{1,0:T(8,128)(2,1)} %bitcast.58, f32[128,512]{1,0:T(8,128)} %from_self.1.from_self_in, ...), custom_call_target="tpu_custom_call" | custom-call | flops 150000000 | bytes 3500000 | tf_op jit(solution)/shard_map/dense/pallas_call | solution.py:28
  90.1 6.2 %collective-permute-start.4 = (bf16[8,128,128]{2,1,0:T(8,128)(2,1)S(1)}, bf16[8,128,128]{2,1,0:T(8,128)(2,1)S(1)}, u32[]{:S(2)}, u32[]{:S(2)}) collective-permute-start(bf16[8,128,128]{2,1,0:T(8,128)(2,1)S(1)} %get-tuple-element.28), channel_id=1, source_target_pairs={{0,1},{1,0},{2,3},{3,2},{4,5},{5,4},{6,7},{7,6},{8,9},{9,8},{10,11... | collective-permute-start | bytes 786440 | tf_op jit(solution)/shard_map/ppermute | solution.py:282
  96.3 0.7 hidden.1
  97.0 0.4 collective-permute-done.4.received_ref
  97.4 0.4 gradient.1
  97.9 22.9 %all_to_all.20.parts_ref = bf16[32,16,512]{2,1,0:T(8,128)(2,1)S(1)} all-to-all(bf16[32,16,512]{2,1,0:T(8,128)(2,1)S(1)} %gradient.1), channel_id=1, replica_groups=mesh['z'=8,'x1'=2,'x0'=2,'y2'=2,'y1'=2,'y0'=2,'c'=2] {'z','x1','x0'}, dimensions={0} | all-to-all | bytes 1048576 | tf_op jit(solution)/shard_map/all_to_all | solution.py:288
  120.7 0.1 added.2
  120.8 12.0 %all_to_all.21.parts_ref = bf16[8,16,512]{2,1,0:T(8,128)(2,1)S(1)} all-to-all(bf16[8,16,512]{2,1,0:T(8,128)(2,1)S(1)} %broadcast_in_dim.54), channel_id=1, replica_groups=mesh['z'=8,'x1'=2,'x0'=2,'y2'=2,'y1'=2,'y0'=2,'c'=2] {'y2','y1','y0'}, dimensions={0} | all-to-all | bytes 262144 | tf_op jit(solution)/shard_map/all_to_all | solution.py:289
  132.9 5.0 %all-gather.3 = f32[32,512]{1,0:T(8,128)S(1)} all-gather(f32[16,512]{1,0:T(8,128)S(1)} %added.3), channel_id=5, replica_groups=mesh['z'=8,'x1'=2,'x0'=2,'y2'=2,'y1'=2,'y0'=2,'c'=2] {'c'}, dimensions={0}, use_global_device_ids=true | all-gather | bytes 98304 | tf_op jit(solution)/shard_map/all_gather | solution.py:290
  137.9 0.6 fusion.11
  (26 shorter events, 0.1 us)
Async XLA Ops:
  0.6 0.9 copy-start.2
  1.5 14.9 %copy-start.8 = (s32[1,1,16,2]{2,3,1,0:T(2,128)S(1)}, s32[1,1,16,2]{2,3,1,0:T(2,128)}, u32[]{:S(2)}) copy-start(s32[1,1,16,2]{2,3,1,0:T(2,128)} %param.11) | copy-start | bytes 388
  1.5 15.0 %copy-start.6 = (bf16[128,16]{0,1:T(8,128)(2,1)S(1)}, bf16[128,16]{0,1:T(8,128)(2,1)}, u32[]{:S(2)}) copy-start(bf16[128,16]{0,1:T(8,128)(2,1)} %param.9) | copy-start | bytes 12292
  1.5 15.2 %copy-start.7 = (s32[128,16]{0,1:T(8,128)S(1)}, s32[128,16]{0,1:T(8,128)}, u32[]{:S(2)}) copy-start(s32[128,16]{0,1:T(8,128)} %param.10) | copy-start | bytes 24580
  1.5 15.2 %copy-start.9 = (s32[1,1,16]{2,1,0:T(1,128)S(1)}, s32[1,1,16]{2,1,0:T(1,128)}, u32[]{:S(2)}) copy-start(s32[1,1,16]{2,1,0:T(1,128)} %param.12) | copy-start | bytes 196
  2.7 45.2 %all-to-all-start = ((bf16[32,128,128]{2,1,0:T(8,128)(2,1)}), bf16[32,128,128]{2,1,0:T(8,128)(2,1)S(1)}, u32[]{:S(2)}, u32[]{:S(2)}) async-start(bf16[32,128,128]{2,1,0:T(8,128)(2,1)} %bitcast.52), calls=%async_computation | async-start | bytes 2097152 | tf_op jit(solution)/shard_map/all_to_all | solution.py:214
  48.0 4.5 %collective-permute-start = (bf16[32,128,128]{2,1,0:T(8,128)(2,1)S(1)}, bf16[32,128,128]{2,1,0:T(8,128)(2,1)S(1)}, u32[]{:S(2)}, u32[]{:S(2)}) collective-permute-start(bf16[32,128,128]{2,1,0:T(8,128)(2,1)S(1)} %all-to-all-done.blocks_ref), channel_id=1, source_target_pairs={{0,1},{1,0},{2,3},{3,2},{4,5},{5,4},{6,7},{7,6},{8,9},{9,8},{10,11... | collective-permute-start | bytes 3145736 | tf_op jit(solution)/shard_map/ppermute | solution.py:241
  55.1 7.7 %copy-start = (bf16[4,48,128]{2,1,0:T(8,128)(2,1)S(1)}, bf16[4,48,128]{2,1,0:T(8,128)(2,1)}, u32[]{:S(2)}) copy-start(bf16[4,48,128]{2,1,0:T(8,128)(2,1)} %get-tuple-element.24.told_ref) | copy-start | bytes 147460
  55.1 32.9 %all-to-all-start.1 = ((bf16[32,128,128]{2,1,0:T(8,128)(2,1)}), bf16[32,128,128]{2,1,0:T(8,128)(2,1)S(1)}, u32[]{:S(2)}, u32[]{:S(2)}) async-start(bf16[32,128,128]{2,1,0:T(8,128)(2,1)} %bitcast.51), calls=%async_computation.1 | async-start | bytes 2097152 | tf_op jit(solution)/shard_map/all_to_all | solution.py:251
  62.8 22.3 %copy-start.1 = (bf16[512,512]{1,0:T(8,128)(2,1)S(1)}, bf16[512,512]{1,0:T(8,128)(2,1)}, u32[]{:S(2)}) copy-start(bf16[512,512]{1,0:T(8,128)(2,1)} %w_self.1) | copy-start | bytes 1572868
  62.8 22.3 %copy-start.3 = (bf16[128,512]{1,0:T(8,128)(2,1)S(1)}, bf16[128,512]{1,0:T(8,128)(2,1)}, u32[]{:S(2)}) copy-start(bf16[128,512]{1,0:T(8,128)(2,1)} %features) | copy-start | bytes 393220
  65.6 22.5 %copy-start.4 = (bf16[512,512]{1,0:T(8,128)(2,1)S(1)}, bf16[512,512]{1,0:T(8,128)(2,1)}, u32[]{:S(2)}) copy-start(bf16[512,512]{1,0:T(8,128)(2,1)} %w_agg.1) | copy-start | bytes 1572868
  65.6 22.5 %copy-start.5 = (bf16[128,512]{1,0:T(8,128)(2,1)S(1)}, bf16[128,512]{1,0:T(8,128)(2,1)}, u32[]{:S(2)}) copy-start(bf16[128,512]{1,0:T(8,128)(2,1)} %cotangent.1) | copy-start | bytes 393220
  65.6 22.5 %collective-permute-start.1 = (f32[128,128]{1,0:T(8,128)S(1)}, f32[128,128]{1,0:T(8,128)S(1)}, u32[]{:S(2)}, u32[]{:S(2)}) collective-permute-start(f32[128,128]{1,0:T(8,128)S(1)} %local_sums.5), channel_id=1, source_target_pairs={{0,16},{16,32},{32,48},{48,0},{1,17},{17,33},{33,49},{49,1},{2,18}... | collective-permute-start | bytes 196616 | tf_op jit(solution)/shard_map/ppermute | solution.py:262
  71.6 16.5 %collective-permute-start.2 = (f32[128,128]{1,0:T(8,128)S(1)}, f32[128,128]{1,0:T(8,128)S(1)}, u32[]{:S(2)}, u32[]{:S(2)}) collective-permute-start(f32[128,128]{1,0:T(8,128)S(1)} %local_sums.6), channel_id=1, source_target_pairs={{0,32},{16,48},{32,0},{48,16},{1,33},{17,49},{33,1},{49,17},{2,34}... | collective-permute-start | bytes 196616 | tf_op jit(solution)/shard_map/ppermute | solution.py:262
  78.7 9.4 %collective-permute-start.3 = (f32[128,128]{1,0:T(8,128)S(1)}, f32[128,128]{1,0:T(8,128)S(1)}, u32[]{:S(2)}, u32[]{:S(2)}) collective-permute-start(f32[128,128]{1,0:T(8,128)S(1)} %local_sums.7), channel_id=1, source_target_pairs={{0,48},{16,0},{32,16},{48,32},{1,49},{17,1},{33,17},{49,33},{2,50}... | collective-permute-start | bytes 196616 | tf_op jit(solution)/shard_map/ppermute | solution.py:262
  90.1 7.3 %collective-permute-start.4 = (bf16[8,128,128]{2,1,0:T(8,128)(2,1)S(1)}, bf16[8,128,128]{2,1,0:T(8,128)(2,1)S(1)}, u32[]{:S(2)}, u32[]{:S(2)}) collective-permute-start(bf16[8,128,128]{2,1,0:T(8,128)(2,1)S(1)} %get-tuple-element.28), channel_id=1, source_target_pairs={{0,1},{1,0},{2,3},{3,2},{4,5},{5,4},{6,7},{7,6},{8,9},{9,8},{10,11... | collective-permute-start | bytes 786440 | tf_op jit(solution)/shard_map/ppermute | solution.py:282

commit v14 on v13

--- a/solution.py
+++ b/solution.py
@@ -88,8 +88,8 @@
     copies = []
     for y in range(NY):
         for x in range(NX):
-            sums[x, y] = (part_ref[x, y] + remote_product(core, here, before, blocks_ref, told_ref, x, y)).astype(BF16)
-        copies.append(pltpu.make_async_copy(sums.at[:, y], sums_ref.at[:, y], sems.at[y]))
+            sums[y, x] = (part_ref[x, y] + remote_product(core, here, before, blocks_ref, told_ref, x, y)).astype(BF16)
+        copies.append(pltpu.make_async_copy(sums.at[y], sums_ref.at[y], sems.at[y]))
         copies[-1].start()
     for copy in copies:
         copy.wait()
@@ -138,9 +138,9 @@
         copy.start()
 
     for x in range(NX):
-        summed = arrived[x, 0].astype(F32)
+        summed = arrived[0, x].astype(F32)
         for y in range(1, NY):
-            summed = summed + arrived[x, y].astype(F32)
+            summed = summed + arrived[y, x].astype(F32)
         agg_t[x * T : (x + 1) * T, :] = summed
     for k, near in ((1, near_1), (2, near_2), (3, near_3), (0, near_0)):
         if k == 0:
@@ -244,11 +244,11 @@
         flops=300_000_000, bytes_accessed=3_500_000,
     )
     (chip_sum,) = vmem_call(
-        second_kernel, "other_group", [core, *of_source(y * NC + 1 - c)], [others, remote_codes, part], [((NX, NY, T, T), BF16)],
-        scratch=[pltpu.VMEM((NX, NY, T, T), BF16), pltpu.SemaphoreType.DMA((NY,))], outside=1,
+        second_kernel, "other_group", [core, *of_source(y * NC + 1 - c)], [others, remote_codes, part], [((NY, NX, T, T), BF16)],
+        scratch=[pltpu.VMEM((NY, NX, T, T), BF16), pltpu.SemaphoreType.DMA((NY,))], outside=1,
         flops=300_000_000, bytes_accessed=5_500_000,
     )
-    arrived = lax.all_to_all(chip_sum.reshape(NX * NY, T, T), X + Y, 0, 0, tiled=True)
+    arrived = lax.all_to_all(chip_sum.reshape(NX * NY, T, T), Y + X, 0, 0, tiled=True)
 
     features_later, _ = lax.optimization_barrier((features, chip_sum))
     near = []
@@ -271,7 +271,7 @@
     arrived, x, c = lax.optimization_barrier((arrived, x, c))
     outside = [near_0, weights_t, from_self, features_t]
     preact, send, keep = vmem_call(
-        dense_kernel, "dense", [jnp.stack([x, c])], [arrived.reshape(NX, NY, T, T), one, two, three, w_agg, cotangent],
+        dense_kernel, "dense", [jnp.stack([x, c])], [arrived.reshape(NY, NX, T, T), one, two, three, w_agg, cotangent],
         [((T, width), F32), operands, operands],
         scratch=[pltpu.VMEM((width, T), F32)]
         + [pltpu.VMEM(of.shape, of.dtype) for of in outside]

time: 139 us -> 139 us (level)
  starting transfers between devices: 40.2 us -> 37.9 us
  waiting for transfers between devices: 2.83 us -> 4.61 us
    all_to_all x1, blocking collectives: 22.9 us -> 25.4 us  [body(): plane = added(lax.all_to_all(chip_grad, ('z',) + X, 0, 0, tiled=True), BF16)]
    ppermute x1, starting transfers between devices: 6.19 us -> 3.85 us  [body(): received = lax.ppermute(send, 'c', swap)]
    all_to_all x1, waiting for transfers between devices: 1.86 us -> 3.64 us  [body(): lax.all_to_all(chip_sum.reshape(NX * NY, T, T), Y + X, 0, 0, tiled=True)]
    all_to_all x1, blocking collectives: 12 us -> 10.4 us  [body(): lax.all_to_all(jnp.broadcast_to(plane, (NY,) + plane.shape), Y, 0, 0, til...]
where the time goes in v14:
time: 139 us
  blocking collectives  70.8 us (51%)
  starting transfers between devices  37.9 us (27%)
  Pallas kernels  21.8 us (16%)
  waiting for transfers between devices  4.61 us (3%)
  local copies, waits for them, and re-layouts  1.97 us (1%)
    all_to_all x1, blocking collectives, body(): plane = added(lax.all_to_all(chip_grad, ('z',) + X, 0, 0, tiled=True), BF16)  25.4 us
    pallas_call x14, Pallas kernels, vmem_call(): pl.pallas_call(kernel, in_specs=[pl.BlockSpec(memory_space=pltpu.SMEM)] *...  21.8 us
    all_gather x1, blocking collectives, body(): remote_codes = lax.all_gather(remote_codes, Y + ('c',), axis=0)  20.6 us
    all_to_all x1, starting transfers between devices, body(): lax.all_to_all(quarters.reshape(OWNERS, T, T), ('z',) + X, 0, 0, tiled=True)  13.7 us
    ppermute x3, starting transfers between devices, body(): near.append(lax.ppermute(sums, X, forward[NX - k]) if k else sums)  10.7 us
    all_to_all x1, blocking collectives, body(): lax.all_to_all(jnp.broadcast_to(plane, (NY,) + plane.shape), Y, 0, 0, til...  10.4 us
    all_gather x2, blocking collectives, body(): codes = lax.all_gather(lax.all_gather(codes, 'x1', axis=0), 'x0', axis=0)  9.62 us
    all_to_all x1, starting transfers between devices, body(): lax.all_to_all(chip_sum.reshape(NX * NY, T, T), Y + X, 0, 0, tiled=True)  7.62 us
  transfers between devices with their start and end apart: 7, of which 3 were waited for; matrix products, arithmetic and copies ran while one was open for 1% of the time, Pallas kernels for 11%

profile of v14, /device:TPU:1, one launch (start us, length us, event | category | flops | bytes accessed | tf_op | source)
XLA Modules:
  0.0 138.6 jit_solution(9884412683531477531)
XLA Ops:
  0.6 0.0 copy-start.2
  0.6 0.9 copy-done.2
  1.5 1.2 spread.1
  2.7 13.7 %all-to-all-start = ((bf16[32,128,128]{2,1,0:T(8,128)(2,1)}), bf16[32,128,128]{2,1,0:T(8,128)(2,1)S(1)}, u32[]{:S(2)}, u32[]{:S(2)}) async-start(bf16[32,128,128]{2,1,0:T(8,128)(2,1)} %bitcast.52), calls=%async_computation | async-start | bytes 2097152 | tf_op jit(solution)/shard_map/all_to_all | solution.py:214
  16.5 0.1 copy.13
  16.6 0.1 concatenate.20
  16.7 0.0 copy-done.7
  16.8 0.1 fusion.9
  16.9 0.2 concatenate.22
  17.1 4.9 %all-gather = bf16[128,128]{1,0:T(8,128)(2,1)S(1)} all-gather(bf16[64,128]{1,0:T(8,128)(2,1)S(1)} %concatenate.22), channel_id=2, replica_groups=mesh['z'=8,'x1'=2,'x0'=2,'y2'=2,'y1'=2,'y0'=2,'c'=2] {'x1'}, dimensions={0}, use_global_device_ids=true | all-gather | bytes 49152 | tf_op jit(solution)/shard_map/all_gather | solution.py:226
  21.9 4.7 %all-gather.1 = bf16[4,64,128]{2,1,0:T(8,128)(2,1)S(1)} all-gather(bf16[2,64,128]{2,1,0:T(8,128)(2,1)S(1)} %bitcast.55), channel_id=3, replica_groups=mesh['z'=8,'x1'=2,'x0'=2,'y2'=2,'y1'=2,'y0'=2,'c'=2] {'x0'}, dimensions={0}, use_global_device_ids=true | all-gather | bytes 98304 | tf_op jit(solution)/shard_map/all_gather | solution.py:226
  26.7 0.6 split.1
  27.3 20.6 %all-gather.2 = bf16[64,16,128]{2,1,0:T(8,128)(2,1)S(1)} all-gather(bf16[4,16,128]{2,1,0:T(8,128)(2,1)S(1)} %get-tuple-element.19), channel_id=4, replica_groups=mesh['z'=8,'x1'=2,'x0'=2,'y2'=2,'y1'=2,'y0'=2,'c'=2] {'y2','y1','y0','c'}, dimensions={0}, use_global_device_ids=true | all-gather | bytes 278528 | tf_op jit(solution)/shard_map/all_gather | solution.py:231
  48.0 0.0 all-to-all-done.blocks_ref
  48.0 2.1 %collective-permute-start = (bf16[32,128,128]{2,1,0:T(8,128)(2,1)S(1)}, bf16[32,128,128]{2,1,0:T(8,128)(2,1)S(1)}, u32[]{:S(2)}, u32[]{:S(2)}) collective-permute-start(bf16[32,128,128]{2,1,0:T(8,128)(2,1)S(1)} %all-to-all-done.blocks_ref), channel_id=1, source_target_pairs={{0,1},{1,0},{2,3},{3,2},{4,5},{5,4},{6,7},{7,6},{8,9},{9,8},{10,11... | collective-permute-start | bytes 3145736 | tf_op jit(solution)/shard_map/ppermute | solution.py:241
  50.1 0.1 slice_convert_fusion
  50.2 0.1 select_reduce_fusion
  50.3 0.1 select_reduce_fusion.1
  50.4 1.6 %own_group.1.part_ref = f32[4,8,128,128]{3,2,1,0:T(8,128)S(1)} custom-call(s32[1]{0:T(128)} %bitcast.core, s32[4,128]{1,0:T(4,128)S(1)} %get-tuple-element.35.here, s32[4,16]{1,0:T(4,128)S(1)} %get-tuple-element.33.before, bf16[32,128,128]{2,1,0:T(8,128)(2,1)S(1)} %all-to-all-done.blocks_ref, bf16[16,4,16,128]{3,2,1,0:T(8,128)(2,1)S(1)} %bitcast.48), custom_call_target="tpu_custom_call" | custom-call | flops 300000000 | bytes 3500000 | tf_op jit(solution)/shard_map/own_group/pallas_call | solution.py:28
  52.0 0.5 collective-permute-done.blocks_ref
  52.5 2.6 %other_group.1 = bf16[8,4,128,128]{3,2,1,0:T(8,128)(2,1)} custom-call(s32[1]{0:T(128)} %bitcast.core, s32[4,128]{1,0:T(4,128)S(1)} %get-tuple-element.36.here, s32[4,16]{1,0:T(4,128)S(1)} %get-tuple-element.34.before, bf16[32,128,128]{2,1,0:T(8,128)(2,1)S(1)} %collective-permute-done.blocks_ref, bf16[16,4,16,128]{3,2,1,0:T(8,128)(2,1)S(1)} %bitcast.49, ...), custom_call_target="tpu_custom_call" | custom-call | flops 300000000 | bytes 5500000 | tf_op jit(solution)/shard_map/other_group/pallas_call | solution.py:28
  55.1 7.6 %all-to-all-start.1 = ((bf16[32,128,128]{2,1,0:T(8,128)(2,1)}), bf16[32,128,128]{2,1,0:T(8,128)(2,1)S(1)}, u32[]{:S(2)}, u32[]{:S(2)}) async-start(bf16[32,128,128]{2,1,0:T(8,128)(2,1)} %bitcast.51), calls=%async_computation.1 | async-start | bytes 2097152 | tf_op jit(solution)/shard_map/all_to_all | solution.py:251
  62.8 0.1 pad_add_fusion.1.scalars
  62.8 2.7 %local_sums.5 = f32[128,128]{1,0:T(8,128)S(1)} custom-call(s32[2]{0:T(128)S(1)} %pad_add_fusion.1.scalars, bf16[32,128,128]{2,1,0:T(8,128)(2,1)S(1)} %all-to-all-done.blocks_ref, bf16[4,48,128]{2,1,0:T(8,128)(2,1)S(1)} %copy-done), custom_call_target="tpu_custom_call" | custom-call | flops 150000000 | bytes 1200000 | tf_op jit(solution)/shard_map/local_sums/pallas_call | solution.py:28
  65.6 0.0 copy-start.4
  65.6 0.0 copy-start.5
  65.6 3.3 %collective-permute-start.1 = (f32[128,128]{1,0:T(8,128)S(1)}, f32[128,128]{1,0:T(8,128)S(1)}, u32[]{:S(2)}, u32[]{:S(2)}) collective-permute-start(f32[128,128]{1,0:T(8,128)S(1)} %local_sums.5), channel_id=1, source_target_pairs={{0,16},{16,32},{32,48},{48,0},{1,17},{17,33},{33,49},{49,1},{2,18}... | collective-permute-start | bytes 196616 | tf_op jit(solution)/shard_map/ppermute | solution.py:262
  68.9 2.7 %local_sums.6 = f32[128,128]{1,0:T(8,128)S(1)} custom-call(s32[2]{0:T(128)S(1)} %pad_add_fusion.1.scalars, bf16[32,128,128]{2,1,0:T(8,128)(2,1)S(1)} %all-to-all-done.blocks_ref, bf16[4,48,128]{2,1,0:T(8,128)(2,1)S(1)} %copy-done), custom_call_target="tpu_custom_call" | custom-call | flops 150000000 | bytes 1200000 | tf_op jit(solution)/shard_map/local_sums/pallas_call | solution.py:28
  71.6 4.3 %collective-permute-start.2 = (f32[128,128]{1,0:T(8,128)S(1)}, f32[128,128]{1,0:T(8,128)S(1)}, u32[]{:S(2)}, u32[]{:S(2)}) collective-permute-start(f32[128,128]{1,0:T(8,128)S(1)} %local_sums.6), channel_id=1, source_target_pairs={{0,32},{16,48},{32,0},{48,16},{1,33},{17,49},{33,1},{49,17},{2,34}... | collective-permute-start | bytes 196616 | tf_op jit(solution)/shard_map/ppermute | solution.py:262
  75.9 2.7 %local_sums.7 = f32[128,128]{1,0:T(8,128)S(1)} custom-call(s32[2]{0:T(128)S(1)} %pad_add_fusion.1.scalars, bf16[32,128,128]{2,1,0:T(8,128)(2,1)S(1)} %all-to-all-done.blocks_ref, bf16[4,48,128]{2,1,0:T(8,128)(2,1)S(1)} %copy-done), custom_call_target="tpu_custom_call" | custom-call | flops 150000000 | bytes 1200000 | tf_op jit(solution)/shard_map/local_sums/pallas_call | solution.py:28
  78.7 3.1 %collective-permute-start.3 = (f32[128,128]{1,0:T(8,128)S(1)}, f32[128,128]{1,0:T(8,128)S(1)}, u32[]{:S(2)}, u32[]{:S(2)}) collective-permute-start(f32[128,128]{1,0:T(8,128)S(1)} %local_sums.7), channel_id=1, source_target_pairs={{0,48},{16,0},{32,16},{48,32},{1,49},{17,1},{33,17},{49,33},{2,50}... | collective-permute-start | bytes 196616 | tf_op jit(solution)/shard_map/ppermute | solution.py:262
  81.8 3.4 %local_sums.4.near_0_in = f32[128,128]{1,0:T(8,128)} custom-call(s32[2]{0:T(128)S(1)} %pad_add_fusion.1.scalars, bf16[32,128,128]{2,1,0:T(8,128)(2,1)S(1)} %all-to-all-done.blocks_ref, bf16[4,48,128]{2,1,0:T(8,128)(2,1)S(1)} %copy-done), custom_call_target="tpu_custom_call" | custom-call | flops 150000000 | bytes 1200000 | tf_op jit(solution)/shard_map/local_sums/pallas_call | solution.py:28
  85.2 1.0 from_self.1.from_self_in
  86.2 3.6 %all-to-all-done.1 = bf16[32,128,128]{2,1,0:T(8,128)(2,1)S(1)} async-done(((bf16[32,128,128]{2,1,0:T(8,128)(2,1)}), bf16[32,128,128]{2,1,0:T(8,128)(2,1)S(1)}, u32[]{:S(2)}, u32[]{:S(2)}) %all-to-all-start.1) | async-done | bytes 1048608 | tf_op jit(solution)/shard_map/all_to_all | solution.py:251
  89.8 0.1 pad_add_fusion.scalars
  89.9 0.0 collective-permute-done.1.near_1
  89.9 0.0 collective-permute-done.2.near_2
  89.9 0.0 collective-permute-done.3.near_3
  89.9 2.0 %dense.1 = (f32[128,512]{1,0:T(8,128)S(1)}, bf16[8,128,128]{2,1,0:T(8,128)(2,1)S(1)}, bf16[8,128,128]{2,1,0:T(8,128)(2,1)S(1)}) custom-call(s32[2]{0:T(128)S(1)} %pad_add_fusion.scalars, f32[128,128]{1,0:T(8,128)} %local_sums.4.near_0_in, bf16[16,128]{1,0:T(8,128)(2,1)} %bitcast.58, f32[128,512]{1,0:T(8,128)} %from_self.1.from_self_in, ...), custom_call_target="tpu_custom_call" | custom-call | flops 150000000 | bytes 3500000 | tf_op jit(solution)/shard_map/dense/pallas_call | solution.py:28
  91.9 3.9 %collective-permute-start.4 = (bf16[8,128,128]{2,1,0:T(8,128)(2,1)S(1)}, bf16[8,128,128]{2,1,0:T(8,128)(2,1)S(1)}, u32[]{:S(2)}, u32[]{:S(2)}) collective-permute-start(bf16[8,128,128]{2,1,0:T(8,128)(2,1)S(1)} %get-tuple-element.28), channel_id=1, source_target_pairs={{0,1},{1,0},{2,3},{3,2},{4,5},{5,4},{6,7},{7,6},{8,9},{9,8},{10,11... | collective-permute-start | bytes 786440 | tf_op jit(solution)/shard_map/ppermute | solution.py:282
  95.7 0.7 hidden.1
  96.4 0.4 collective-permute-done.4.received_ref
  96.9 0.4 gradient.1
  97.3 25.4 %all_to_all.20.parts_ref = bf16[32,16,512]{2,1,0:T(8,128)(2,1)S(1)} all-to-all(bf16[32,16,512]{2,1,0:T(8,128)(2,1)S(1)} %gradient.1), channel_id=1, replica_groups=mesh['z'=8,'x1'=2,'x0'=2,'y2'=2,'y1'=2,'y0'=2,'c'=2] {'z','x1','x0'}, dimensions={0} | all-to-all | bytes 1048576 | tf_op jit(solution)/shard_map/all_to_all | solution.py:288
  122.7 0.1 added.2
  122.8 10.4 %all_to_all.21.parts_ref = bf16[8,16,512]{2,1,0:T(8,128)(2,1)S(1)} all-to-all(bf16[8,16,512]{2,1,0:T(8,128)(2,1)S(1)} %broadcast_in_dim.54), channel_id=1, replica_groups=mesh['z'=8,'x1'=2,'x0'=2,'y2'=2,'y1'=2,'y0'=2,'c'=2] {'y2','y1','y0'}, dimensions={0} | all-to-all | bytes 262144 | tf_op jit(solution)/shard_map/all_to_all | solution.py:289
  133.2 4.7 %all-gather.3 = f32[32,512]{1,0:T(8,128)S(1)} all-gather(f32[16,512]{1,0:T(8,128)S(1)} %added.3), channel_id=5, replica_groups=mesh['z'=8,'x1'=2,'x0'=2,'y2'=2,'y1'=2,'y0'=2,'c'=2] {'c'}, dimensions={0}, use_global_device_ids=true | all-gather | bytes 98304 | tf_op jit(solution)/shard_map/all_gather | solution.py:290
  137.9 0.6 fusion.11
  (26 shorter events, 0.1 us)
Async XLA Ops:
  0.6 0.9 copy-start.2
  1.5 14.9 %copy-start.8 = (s32[1,1,16,2]{2,3,1,0:T(2,128)S(1)}, s32[1,1,16,2]{2,3,1,0:T(2,128)}, u32[]{:S(2)}) copy-start(s32[1,1,16,2]{2,3,1,0:T(2,128)} %param.11) | copy-start | bytes 388
  1.5 15.0 %copy-start.6 = (bf16[128,16]{0,1:T(8,128)(2,1)S(1)}, bf16[128,16]{0,1:T(8,128)(2,1)}, u32[]{:S(2)}) copy-start(bf16[128,16]{0,1:T(8,128)(2,1)} %param.9) | copy-start | bytes 12292
  1.5 15.2 %copy-start.7 = (s32[128,16]{0,1:T(8,128)S(1)}, s32[128,16]{0,1:T(8,128)}, u32[]{:S(2)}) copy-start(s32[128,16]{0,1:T(8,128)} %param.10) | copy-start | bytes 24580
  1.5 15.2 %copy-start.9 = (s32[1,1,16]{2,1,0:T(1,128)S(1)}, s32[1,1,16]{2,1,0:T(1,128)}, u32[]{:S(2)}) copy-start(s32[1,1,16]{2,1,0:T(1,128)} %param.12) | copy-start | bytes 196
  2.7 45.2 %all-to-all-start = ((bf16[32,128,128]{2,1,0:T(8,128)(2,1)}), bf16[32,128,128]{2,1,0:T(8,128)(2,1)S(1)}, u32[]{:S(2)}, u32[]{:S(2)}) async-start(bf16[32,128,128]{2,1,0:T(8,128)(2,1)} %bitcast.52), calls=%async_computation | async-start | bytes 2097152 | tf_op jit(solution)/shard_map/all_to_all | solution.py:214
  48.0 4.5 %collective-permute-start = (bf16[32,128,128]{2,1,0:T(8,128)(2,1)S(1)}, bf16[32,128,128]{2,1,0:T(8,128)(2,1)S(1)}, u32[]{:S(2)}, u32[]{:S(2)}) collective-permute-start(bf16[32,128,128]{2,1,0:T(8,128)(2,1)S(1)} %all-to-all-done.blocks_ref), channel_id=1, source_target_pairs={{0,1},{1,0},{2,3},{3,2},{4,5},{5,4},{6,7},{7,6},{8,9},{9,8},{10,11... | collective-permute-start | bytes 3145736 | tf_op jit(solution)/shard_map/ppermute | solution.py:241
  55.1 7.7 %copy-start = (bf16[4,48,128]{2,1,0:T(8,128)(2,1)S(1)}, bf16[4,48,128]{2,1,0:T(8,128)(2,1)}, u32[]{:S(2)}) copy-start(bf16[4,48,128]{2,1,0:T(8,128)(2,1)} %get-tuple-element.24.told_ref) | copy-start | bytes 147460
  55.1 34.7 %all-to-all-start.1 = ((bf16[32,128,128]{2,1,0:T(8,128)(2,1)}), bf16[32,128,128]{2,1,0:T(8,128)(2,1)S(1)}, u32[]{:S(2)}, u32[]{:S(2)}) async-start(bf16[32,128,128]{2,1,0:T(8,128)(2,1)} %bitcast.51), calls=%async_computation.1 | async-start | bytes 2097152 | tf_op jit(solution)/shard_map/all_to_all | solution.py:251
  62.8 22.3 %copy-start.1 = (bf16[512,512]{1,0:T(8,128)(2,1)S(1)}, bf16[512,512]{1,0:T(8,128)(2,1)}, u32[]{:S(2)}) copy-start(bf16[512,512]{1,0:T(8,128)(2,1)} %w_self.1) | copy-start | bytes 1572868
  62.8 22.3 %copy-start.3 = (bf16[128,512]{1,0:T(8,128)(2,1)S(1)}, bf16[128,512]{1,0:T(8,128)(2,1)}, u32[]{:S(2)}) copy-start(bf16[128,512]{1,0:T(8,128)(2,1)} %features) | copy-start | bytes 393220
  65.6 24.3 %copy-start.4 = (bf16[512,512]{1,0:T(8,128)(2,1)S(1)}, bf16[512,512]{1,0:T(8,128)(2,1)}, u32[]{:S(2)}) copy-start(bf16[512,512]{1,0:T(8,128)(2,1)} %w_agg.1) | copy-start | bytes 1572868
  65.6 24.3 %copy-start.5 = (bf16[128,512]{1,0:T(8,128)(2,1)S(1)}, bf16[128,512]{1,0:T(8,128)(2,1)}, u32[]{:S(2)}) copy-start(bf16[128,512]{1,0:T(8,128)(2,1)} %cotangent.1) | copy-start | bytes 393220
  65.6 24.3 %collective-permute-start.1 = (f32[128,128]{1,0:T(8,128)S(1)}, f32[128,128]{1,0:T(8,128)S(1)}, u32[]{:S(2)}, u32[]{:S(2)}) collective-permute-start(f32[128,128]{1,0:T(8,128)S(1)} %local_sums.5), channel_id=1, source_target_pairs={{0,16},{16,32},{32,48},{48,0},{1,17},{17,33},{33,49},{49,1},{2,18}... | collective-permute-start | bytes 196616 | tf_op jit(solution)/shard_map/ppermute | solution.py:262
  71.6 18.3 %collective-permute-start.2 = (f32[128,128]{1,0:T(8,128)S(1)}, f32[128,128]{1,0:T(8,128)S(1)}, u32[]{:S(2)}, u32[]{:S(2)}) collective-permute-start(f32[128,128]{1,0:T(8,128)S(1)} %local_sums.6), channel_id=1, source_target_pairs={{0,32},{16,48},{32,0},{48,16},{1,33},{17,49},{33,1},{49,17},{2,34}... | collective-permute-start | bytes 196616 | tf_op jit(solution)/shard_map/ppermute | solution.py:262
  78.7 11.2 %collective-permute-start.3 = (f32[128,128]{1,0:T(8,128)S(1)}, f32[128,128]{1,0:T(8,128)S(1)}, u32[]{:S(2)}, u32[]{:S(2)}) collective-permute-start(f32[128,128]{1,0:T(8,128)S(1)} %local_sums.7), channel_id=1, source_target_pairs={{0,48},{16,0},{32,16},{48,32},{1,49},{17,1},{33,17},{49,33},{2,50}... | collective-permute-start | bytes 196616 | tf_op jit(solution)/shard_map/ppermute | solution.py:262
  91.9 5.0 %collective-permute-start.4 = (bf16[8,128,128]{2,1,0:T(8,128)(2,1)S(1)}, bf16[8,128,128]{2,1,0:T(8,128)(2,1)S(1)}, u32[]{:S(2)}, u32[]{:S(2)}) collective-permute-start(bf16[8,128,128]{2,1,0:T(8,128)(2,1)S(1)} %get-tuple-element.28), channel_id=1, source_target_pairs={{0,1},{1,0},{2,3},{3,2},{4,5},{5,4},{6,7},{7,6},{8,9},{9,8},{10,11... | collective-permute-start | bytes 786440 | tf_op jit(solution)/shard_map/ppermute | solution.py:282

commit v15 on v14

--- a/solution.py
+++ b/solution.py
@@ -185,7 +185,9 @@
     for j in range(NX):
         right = jnp.concatenate([ref[NX + j] for ref in both], axis=0)
         product = jnp.dot(left, right, preferred_element_type=F32)
-        grad_ref[:, :, j * T : (j + 1) * T] = product.reshape(OWNERS, grad_ref.shape[1], T).astype(BF16)
+        shares = product.astype(BF16).reshape(NZ, NX, grad_ref.shape[1], T)
+        for x in range(NX):
+            grad_ref[x * NZ : (x + 1) * NZ, :, j * T : (j + 1) * T] = shares[:, x]
 
 
 def add_kernel(parts_ref, sum_ref):
@@ -285,7 +287,7 @@
     (chip_grad,) = vmem_call(
         grad_kernel, "gradient", [], [keep, received], [((OWNERS, share, width), BF16)], flops=300_000_000, bytes_accessed=1_000_000
     )
-    plane = added(lax.all_to_all(chip_grad, ("z",) + X, 0, 0, tiled=True), BF16)
+    plane = added(lax.all_to_all(chip_grad, X + ("z",), 0, 0, tiled=True), BF16)
     planes = lax.all_to_all(jnp.broadcast_to(plane, (NY,) + plane.shape), Y, 0, 0, tiled=True)
     grads = lax.all_gather(added(planes, F32), "c", axis=0)
     return hidden, grads[0], grads[1]

time: 139 us -> 138 us (level)
    all_to_all x1, blocking collectives: 25.4 us -> 22.9 us  [body(): plane = added(lax.all_to_all(chip_grad, X + ('z',), 0, 0, tiled=True), BF16)]
    all_gather x1, blocking collectives: 4.73 us -> 6.19 us  [body(): grads = lax.all_gather(added(planes, F32), 'c', axis=0)]
where the time goes in v15:
time: 138 us
  blocking collectives  69.7 us (51%)
  starting transfers between devices  37.9 us (27%)
  Pallas kernels  21.8 us (16%)
  waiting for transfers between devices  4.61 us (3%)
  local copies, waits for them, and re-layouts  1.97 us (1%)
    all_to_all x1, blocking collectives, body(): plane = added(lax.all_to_all(chip_grad, X + ('z',), 0, 0, tiled=True), BF16)  22.9 us
    pallas_call x14, Pallas kernels, vmem_call(): pl.pallas_call(kernel, in_specs=[pl.BlockSpec(memory_space=pltpu.SMEM)] *...  21.8 us
    all_gather x1, blocking collectives, body(): remote_codes = lax.all_gather(remote_codes, Y + ('c',), axis=0)  20.6 us
    all_to_all x1, starting transfers between devices, body(): lax.all_to_all(quarters.reshape(OWNERS, T, T), ('z',) + X, 0, 0, tiled=True)  13.7 us
    ppermute x3, starting transfers between devices, body(): near.append(lax.ppermute(sums, X, forward[NX - k]) if k else sums)  10.7 us
    all_to_all x1, blocking collectives, body(): lax.all_to_all(jnp.broadcast_to(plane, (NY,) + plane.shape), Y, 0, 0, til...  10.3 us
    all_gather x2, blocking collectives, body(): codes = lax.all_gather(lax.all_gather(codes, 'x1', axis=0), 'x0', axis=0)  9.62 us
    all_to_all x1, starting transfers between devices, body(): lax.all_to_all(chip_sum.reshape(NX * NY, T, T), Y + X, 0, 0, tiled=True)  7.62 us
  transfers between devices with their start and end apart: 7, of which 3 were waited for; matrix products, arithmetic and copies ran while one was open for 1% of the time, Pallas kernels for 11%

profile of v15, /device:TPU:1, one launch (start us, length us, event | category | flops | bytes accessed | tf_op | source)
XLA Modules:
  0.0 137.5 jit_solution(10572345254797493622)
XLA Ops:
  0.6 0.0 copy-start.2
  0.6 0.9 copy-done.2
  1.5 1.2 spread.1
  2.7 13.7 %all-to-all-start = ((bf16[32,128,128]{2,1,0:T(8,128)(2,1)}), bf16[32,128,128]{2,1,0:T(8,128)(2,1)S(1)}, u32[]{:S(2)}, u32[]{:S(2)}) async-start(bf16[32,128,128]{2,1,0:T(8,128)(2,1)} %bitcast.52), calls=%async_computation | async-start | bytes 2097152 | tf_op jit(solution)/shard_map/all_to_all | solution.py:216
  16.5 0.1 copy.13
  16.6 0.1 concatenate.20
  16.7 0.0 copy-done.7
  16.8 0.1 fusion.9
  16.9 0.2 concatenate.22
  17.1 4.9 %all-gather = bf16[128,128]{1,0:T(8,128)(2,1)S(1)} all-gather(bf16[64,128]{1,0:T(8,128)(2,1)S(1)} %concatenate.22), channel_id=2, replica_groups=mesh['z'=8,'x1'=2,'x0'=2,'y2'=2,'y1'=2,'y0'=2,'c'=2] {'x1'}, dimensions={0}, use_global_device_ids=true | all-gather | bytes 49152 | tf_op jit(solution)/shard_map/all_gather | solution.py:228
  21.9 4.7 %all-gather.1 = bf16[4,64,128]{2,1,0:T(8,128)(2,1)S(1)} all-gather(bf16[2,64,128]{2,1,0:T(8,128)(2,1)S(1)} %bitcast.55), channel_id=3, replica_groups=mesh['z'=8,'x1'=2,'x0'=2,'y2'=2,'y1'=2,'y0'=2,'c'=2] {'x0'}, dimensions={0}, use_global_device_ids=true | all-gather | bytes 98304 | tf_op jit(solution)/shard_map/all_gather | solution.py:228
  26.7 0.6 split.1
  27.3 20.6 %all-gather.2 = bf16[64,16,128]{2,1,0:T(8,128)(2,1)S(1)} all-gather(bf16[4,16,128]{2,1,0:T(8,128)(2,1)S(1)} %get-tuple-element.19), channel_id=4, replica_groups=mesh['z'=8,'x1'=2,'x0'=2,'y2'=2,'y1'=2,'y0'=2,'c'=2] {'y2','y1','y0','c'}, dimensions={0}, use_global_device_ids=true | all-gather | bytes 278528 | tf_op jit(solution)/shard_map/all_gather | solution.py:233
  48.0 0.0 all-to-all-done.blocks_ref
  48.0 2.1 %collective-permute-start = (bf16[32,128,128]{2,1,0:T(8,128)(2,1)S(1)}, bf16[32,128,128]{2,1,0:T(8,128)(2,1)S(1)}, u32[]{:S(2)}, u32[]{:S(2)}) collective-permute-start(bf16[32,128,128]{2,1,0:T(8,128)(2,1)S(1)} %all-to-all-done.blocks_ref), channel_id=1, source_target_pairs={{0,1},{1,0},{2,3},{3,2},{4,5},{5,4},{6,7},{7,6},{8,9},{9,8},{10,11... | collective-permute-start | bytes 3145736 | tf_op jit(solution)/shard_map/ppermute | solution.py:243
  50.1 0.1 slice_convert_fusion
  50.2 0.1 select_reduce_fusion
  50.3 0.1 select_reduce_fusion.1
  50.4 1.6 %own_group.1.part_ref = f32[4,8,128,128]{3,2,1,0:T(8,128)S(1)} custom-call(s32[1]{0:T(128)} %bitcast.core, s32[4,128]{1,0:T(4,128)S(1)} %get-tuple-element.35.here, s32[4,16]{1,0:T(4,128)S(1)} %get-tuple-element.33.before, bf16[32,128,128]{2,1,0:T(8,128)(2,1)S(1)} %all-to-all-done.blocks_ref, bf16[16,4,16,128]{3,2,1,0:T(8,128)(2,1)S(1)} %bitcast.48), custom_call_target="tpu_custom_call" | custom-call | flops 300000000 | bytes 3500000 | tf_op jit(solution)/shard_map/own_group/pallas_call | solution.py:28
  52.0 0.5 collective-permute-done.blocks_ref
  52.5 2.6 %other_group.1 = bf16[8,4,128,128]{3,2,1,0:T(8,128)(2,1)} custom-call(s32[1]{0:T(128)} %bitcast.core, s32[4,128]{1,0:T(4,128)S(1)} %get-tuple-element.36.here, s32[4,16]{1,0:T(4,128)S(1)} %get-tuple-element.34.before, bf16[32,128,128]{2,1,0:T(8,128)(2,1)S(1)} %collective-permute-done.blocks_ref, bf16[16,4,16,128]{3,2,1,0:T(8,128)(2,1)S(1)} %bitcast.49, ...), custom_call_target="tpu_custom_call" | custom-call | flops 300000000 | bytes 5500000 | tf_op jit(solution)/shard_map/other_group/pallas_call | solution.py:28
  55.1 7.6 %all-to-all-start.1 = ((bf16[32,128,128]{2,1,0:T(8,128)(2,1)}), bf16[32,128,128]{2,1,0:T(8,128)(2,1)S(1)}, u32[]{:S(2)}, u32[]{:S(2)}) async-start(bf16[32,128,128]{2,1,0:T(8,128)(2,1)} %bitcast.51), calls=%async_computation.1 | async-start | bytes 2097152 | tf_op jit(solution)/shard_map/all_to_all | solution.py:253
  62.8 0.1 pad_add_fusion.1.scalars
  62.8 2.7 %local_sums.5 = f32[128,128]{1,0:T(8,128)S(1)} custom-call(s32[2]{0:T(128)S(1)} %pad_add_fusion.1.scalars, bf16[32,128,128]{2,1,0:T(8,128)(2,1)S(1)} %all-to-all-done.blocks_ref, bf16[4,48,128]{2,1,0:T(8,128)(2,1)S(1)} %copy-done), custom_call_target="tpu_custom_call" | custom-call | flops 150000000 | bytes 1200000 | tf_op jit(solution)/shard_map/local_sums/pallas_call | solution.py:28
  65.6 0.0 copy-start.4
  65.6 0.0 copy-start.5
  65.6 3.3 %collective-permute-start.1 = (f32[128,128]{1,0:T(8,128)S(1)}, f32[128,128]{1,0:T(8,128)S(1)}, u32[]{:S(2)}, u32[]{:S(2)}) collective-permute-start(f32[128,128]{1,0:T(8,128)S(1)} %local_sums.5), channel_id=1, source_target_pairs={{0,16},{16,32},{32,48},{48,0},{1,17},{17,33},{33,49},{49,1},{2,18}... | collective-permute-start | bytes 196616 | tf_op jit(solution)/shard_map/ppermute | solution.py:264
  68.9 2.7 %local_sums.6 = f32[128,128]{1,0:T(8,128)S(1)} custom-call(s32[2]{0:T(128)S(1)} %pad_add_fusion.1.scalars, bf16[32,128,128]{2,1,0:T(8,128)(2,1)S(1)} %all-to-all-done.blocks_ref, bf16[4,48,128]{2,1,0:T(8,128)(2,1)S(1)} %copy-done), custom_call_target="tpu_custom_call" | custom-call | flops 150000000 | bytes 1200000 | tf_op jit(solution)/shard_map/local_sums/pallas_call | solution.py:28
  71.6 4.3 %collective-permute-start.2 = (f32[128,128]{1,0:T(8,128)S(1)}, f32[128,128]{1,0:T(8,128)S(1)}, u32[]{:S(2)}, u32[]{:S(2)}) collective-permute-start(f32[128,128]{1,0:T(8,128)S(1)} %local_sums.6), channel_id=1, source_target_pairs={{0,32},{16,48},{32,0},{48,16},{1,33},{17,49},{33,1},{49,17},{2,34}... | collective-permute-start | bytes 196616 | tf_op jit(solution)/shard_map/ppermute | solution.py:264
  75.9 2.7 %local_sums.7 = f32[128,128]{1,0:T(8,128)S(1)} custom-call(s32[2]{0:T(128)S(1)} %pad_add_fusion.1.scalars, bf16[32,128,128]{2,1,0:T(8,128)(2,1)S(1)} %all-to-all-done.blocks_ref, bf16[4,48,128]{2,1,0:T(8,128)(2,1)S(1)} %copy-done), custom_call_target="tpu_custom_call" | custom-call | flops 150000000 | bytes 1200000 | tf_op jit(solution)/shard_map/local_sums/pallas_call | solution.py:28
  78.7 3.1 %collective-permute-start.3 = (f32[128,128]{1,0:T(8,128)S(1)}, f32[128,128]{1,0:T(8,128)S(1)}, u32[]{:S(2)}, u32[]{:S(2)}) collective-permute-start(f32[128,128]{1,0:T(8,128)S(1)} %local_sums.7), channel_id=1, source_target_pairs={{0,48},{16,0},{32,16},{48,32},{1,49},{17,1},{33,17},{49,33},{2,50}... | collective-permute-start | bytes 196616 | tf_op jit(solution)/shard_map/ppermute | solution.py:264
  81.8 3.4 %local_sums.4.near_0_in = f32[128,128]{1,0:T(8,128)} custom-call(s32[2]{0:T(128)S(1)} %pad_add_fusion.1.scalars, bf16[32,128,128]{2,1,0:T(8,128)(2,1)S(1)} %all-to-all-done.blocks_ref, bf16[4,48,128]{2,1,0:T(8,128)(2,1)S(1)} %copy-done), custom_call_target="tpu_custom_call" | custom-call | flops 150000000 | bytes 1200000 | tf_op jit(solution)/shard_map/local_sums/pallas_call | solution.py:28
  85.2 1.0 from_self.1.from_self_in
  86.2 3.6 %all-to-all-done.1 = bf16[32,128,128]{2,1,0:T(8,128)(2,1)S(1)} async-done(((bf16[32,128,128]{2,1,0:T(8,128)(2,1)}), bf16[32,128,128]{2,1,0:T(8,128)(2,1)S(1)}, u32[]{:S(2)}, u32[]{:S(2)}) %all-to-all-start.1) | async-done | bytes 1048608 | tf_op jit(solution)/shard_map/all_to_all | solution.py:253
  89.8 0.1 pad_add_fusion.scalars
  89.9 0.0 collective-permute-done.1.near_1
  89.9 0.0 collective-permute-done.2.near_2
  89.9 0.0 collective-permute-done.3.near_3
  89.9 2.0 %dense.1 = (f32[128,512]{1,0:T(8,128)S(1)}, bf16[8,128,128]{2,1,0:T(8,128)(2,1)S(1)}, bf16[8,128,128]{2,1,0:T(8,128)(2,1)S(1)}) custom-call(s32[2]{0:T(128)S(1)} %pad_add_fusion.scalars, f32[128,128]{1,0:T(8,128)} %local_sums.4.near_0_in, bf16[16,128]{1,0:T(8,128)(2,1)} %bitcast.58, f32[128,512]{1,0:T(8,128)} %from_self.1.from_self_in, ...), custom_call_target="tpu_custom_call" | custom-call | flops 150000000 | bytes 3500000 | tf_op jit(solution)/shard_map/dense/pallas_call | solution.py:28
  91.9 3.9 %collective-permute-start.4 = (bf16[8,128,128]{2,1,0:T(8,128)(2,1)S(1)}, bf16[8,128,128]{2,1,0:T(8,128)(2,1)S(1)}, u32[]{:S(2)}, u32[]{:S(2)}) collective-permute-start(bf16[8,128,128]{2,1,0:T(8,128)(2,1)S(1)} %get-tuple-element.28), channel_id=1, source_target_pairs={{0,1},{1,0},{2,3},{3,2},{4,5},{5,4},{6,7},{7,6},{8,9},{9,8},{10,11... | collective-permute-start | bytes 786440 | tf_op jit(solution)/shard_map/ppermute | solution.py:284
  95.7 0.7 hidden.1
  96.4 0.4 collective-permute-done.4.received_ref
  96.9 0.4 gradient.1
  97.3 22.9 %all_to_all.20.parts_ref = bf16[32,16,512]{2,1,0:T(8,128)(2,1)S(1)} all-to-all(bf16[32,16,512]{2,1,0:T(8,128)(2,1)S(1)} %gradient.1), channel_id=1, replica_groups=mesh['z'=8,'x1'=2,'x0'=2,'y2'=2,'y1'=2,'y0'=2,'c'=2] {'x1','x0','z'}, dimensions={0} | all-to-all | bytes 1048576 | tf_op jit(solution)/shard_map/all_to_all | solution.py:290
  120.2 0.1 added.2
  120.3 10.3 %all_to_all.21.parts_ref = bf16[8,16,512]{2,1,0:T(8,128)(2,1)S(1)} all-to-all(bf16[8,16,512]{2,1,0:T(8,128)(2,1)S(1)} %broadcast_in_dim.54), channel_id=1, replica_groups=mesh['z'=8,'x1'=2,'x0'=2,'y2'=2,'y1'=2,'y0'=2,'c'=2] {'y2','y1','y0'}, dimensions={0} | all-to-all | bytes 262144 | tf_op jit(solution)/shard_map/all_to_all | solution.py:291
  130.7 6.2 %all-gather.3 = f32[32,512]{1,0:T(8,128)S(1)} all-gather(f32[16,512]{1,0:T(8,128)S(1)} %added.3), channel_id=5, replica_groups=mesh['z'=8,'x1'=2,'x0'=2,'y2'=2,'y1'=2,'y0'=2,'c'=2] {'c'}, dimensions={0}, use_global_device_ids=true | all-gather | bytes 98304 | tf_op jit(solution)/shard_map/all_gather | solution.py:292
  136.9 0.6 fusion.11
  (26 shorter events, 0.1 us)
Async XLA Ops:
  0.6 0.9 copy-start.2
  1.5 14.9 %copy-start.8 = (s32[1,1,16,2]{2,3,1,0:T(2,128)S(1)}, s32[1,1,16,2]{2,3,1,0:T(2,128)}, u32[]{:S(2)}) copy-start(s32[1,1,16,2]{2,3,1,0:T(2,128)} %param.11) | copy-start | bytes 388
  1.5 15.0 %copy-start.6 = (bf16[128,16]{0,1:T(8,128)(2,1)S(1)}, bf16[128,16]{0,1:T(8,128)(2,1)}, u32[]{:S(2)}) copy-start(bf16[128,16]{0,1:T(8,128)(2,1)} %param.9) | copy-start | bytes 12292
  1.5 15.2 %copy-start.7 = (s32[128,16]{0,1:T(8,128)S(1)}, s32[128,16]{0,1:T(8,128)}, u32[]{:S(2)}) copy-start(s32[128,16]{0,1:T(8,128)} %param.10) | copy-start | bytes 24580
  1.5 15.2 %copy-start.9 = (s32[1,1,16]{2,1,0:T(1,128)S(1)}, s32[1,1,16]{2,1,0:T(1,128)}, u32[]{:S(2)}) copy-start(s32[1,1,16]{2,1,0:T(1,128)} %param.12) | copy-start | bytes 196
  2.7 45.2 %all-to-all-start = ((bf16[32,128,128]{2,1,0:T(8,128)(2,1)}), bf16[32,128,128]{2,1,0:T(8,128)(2,1)S(1)}, u32[]{:S(2)}, u32[]{:S(2)}) async-start(bf16[32,128,128]{2,1,0:T(8,128)(2,1)} %bitcast.52), calls=%async_computation | async-start | bytes 2097152 | tf_op jit(solution)/shard_map/all_to_all | solution.py:216
  48.0 4.5 %collective-permute-start = (bf16[32,128,128]{2,1,0:T(8,128)(2,1)S(1)}, bf16[32,128,128]{2,1,0:T(8,128)(2,1)S(1)}, u32[]{:S(2)}, u32[]{:S(2)}) collective-permute-start(bf16[32,128,128]{2,1,0:T(8,128)(2,1)S(1)} %all-to-all-done.blocks_ref), channel_id=1, source_target_pairs={{0,1},{1,0},{2,3},{3,2},{4,5},{5,4},{6,7},{7,6},{8,9},{9,8},{10,11... | collective-permute-start | bytes 3145736 | tf_op jit(solution)/shard_map/ppermute | solution.py:243
  55.1 7.7 %copy-start = (bf16[4,48,128]{2,1,0:T(8,128)(2,1)S(1)}, bf16[4,48,128]{2,1,0:T(8,128)(2,1)}, u32[]{:S(2)}) copy-start(bf16[4,48,128]{2,1,0:T(8,128)(2,1)} %get-tuple-element.24.told_ref) | copy-start | bytes 147460
  55.1 34.7 %all-to-all-start.1 = ((bf16[32,128,128]{2,1,0:T(8,128)(2,1)}), bf16[32,128,128]{2,1,0:T(8,128)(2,1)S(1)}, u32[]{:S(2)}, u32[]{:S(2)}) async-start(bf16[32,128,128]{2,1,0:T(8,128)(2,1)} %bitcast.51), calls=%async_computation.1 | async-start | bytes 2097152 | tf_op jit(solution)/shard_map/all_to_all | solution.py:253
  62.8 22.3 %copy-start.1 = (bf16[512,512]{1,0:T(8,128)(2,1)S(1)}, bf16[512,512]{1,0:T(8,128)(2,1)}, u32[]{:S(2)}) copy-start(bf16[512,512]{1,0:T(8,128)(2,1)} %w_self.1) | copy-start | bytes 1572868
  62.8 22.3 %copy-start.3 = (bf16[128,512]{1,0:T(8,128)(2,1)S(1)}, bf16[128,512]{1,0:T(8,128)(2,1)}, u32[]{:S(2)}) copy-start(bf16[128,512]{1,0:T(8,128)(2,1)} %features) | copy-start | bytes 393220
  65.6 24.3 %copy-start.4 = (bf16[512,512]{1,0:T(8,128)(2,1)S(1)}, bf16[512,512]{1,0:T(8,128)(2,1)}, u32[]{:S(2)}) copy-start(bf16[512,512]{1,0:T(8,128)(2,1)} %w_agg.1) | copy-start | bytes 1572868
  65.6 24.3 %copy-start.5 = (bf16[128,512]{1,0:T(8,128)(2,1)S(1)}, bf16[128,512]{1,0:T(8,128)(2,1)}, u32[]{:S(2)}) copy-start(bf16[128,512]{1,0:T(8,128)(2,1)} %cotangent.1) | copy-start | bytes 393220
  65.6 24.3 %collective-permute-start.1 = (f32[128,128]{1,0:T(8,128)S(1)}, f32[128,128]{1,0:T(8,128)S(1)}, u32[]{:S(2)}, u32[]{:S(2)}) collective-permute-start(f32[128,128]{1,0:T(8,128)S(1)} %local_sums.5), channel_id=1, source_target_pairs={{0,16},{16,32},{32,48},{48,0},{1,17},{17,33},{33,49},{49,1},{2,18}... | collective-permute-start | bytes 196616 | tf_op jit(solution)/shard_map/ppermute | solution.py:264
  71.6 18.3 %collective-permute-start.2 = (f32[128,128]{1,0:T(8,128)S(1)}, f32[128,128]{1,0:T(8,128)S(1)}, u32[]{:S(2)}, u32[]{:S(2)}) collective-permute-start(f32[128,128]{1,0:T(8,128)S(1)} %local_sums.6), channel_id=1, source_target_pairs={{0,32},{16,48},{32,0},{48,16},{1,33},{17,49},{33,1},{49,17},{2,34}... | collective-permute-start | bytes 196616 | tf_op jit(solution)/shard_map/ppermute | solution.py:264
  78.7 11.2 %collective-permute-start.3 = (f32[128,128]{1,0:T(8,128)S(1)}, f32[128,128]{1,0:T(8,128)S(1)}, u32[]{:S(2)}, u32[]{:S(2)}) collective-permute-start(f32[128,128]{1,0:T(8,128)S(1)} %local_sums.7), channel_id=1, source_target_pairs={{0,48},{16,0},{32,16},{48,32},{1,49},{17,1},{33,17},{49,33},{2,50}... | collective-permute-start | bytes 196616 | tf_op jit(solution)/shard_map/ppermute | solution.py:264
  91.9 5.0 %collective-permute-start.4 = (bf16[8,128,128]{2,1,0:T(8,128)(2,1)S(1)}, bf16[8,128,128]{2,1,0:T(8,128)(2,1)S(1)}, u32[]{:S(2)}, u32[]{:S(2)}) collective-permute-start(bf16[8,128,128]{2,1,0:T(8,128)(2,1)S(1)} %get-tuple-element.28), channel_id=1, source_target_pairs={{0,1},{1,0},{2,3},{3,2},{4,5},{5,4},{6,7},{7,6},{8,9},{9,8},{10,11... | collective-permute-start | bytes 786440 | tf_op jit(solution)/shard_map/ppermute | solution.py:284

commit v16 on v15

--- a/solution.py
+++ b/solution.py
@@ -42,7 +42,7 @@
 
 def spread_kernel(features_ref, features_out, quarters_ref, features_t, sems):
     features_t[...] = features_ref[...].astype(F32).T.astype(BF16).reshape(NX, T, T)
-    copies = [pltpu.make_async_copy(features_t, quarters_ref.at[z], sems.at[z]) for z in range(NZ)]
+    copies = [pltpu.make_async_copy(features_t, quarters_ref.at[:, z], sems.at[z]) for z in range(NZ)]
     copies.append(pltpu.make_async_copy(features_t, features_out, sems.at[NZ]))
     for copy in copies:
         copy.start()
@@ -74,6 +74,7 @@
     hot = jnp.zeros((CAP * T, T), BF16)
     for slot in range(K_REM):
         hot = jnp.where(rows == row[slot : slot + 1], weight[slot : slot + 1], hot)
+    first, second = (lax.rem(p, NX) * NZ + lax.div(p, NX) for p in (first, second))
     pair = jnp.concatenate([blocks_ref[first], blocks_ref[second]], axis=1)
     return jnp.dot(pair, hot, preferred_element_type=F32)
 
@@ -106,7 +107,7 @@
 
     def of_four(i, summed):
         for j in range(4):
-            p = 4 * i + j
+            p = lax.rem(4 * i + j, NZ) * NX + lax.div(4 * i + j, NZ)
             code = ((block - p.astype(F32)) * T + row).astype(jnp.int16)
             own = (lanes - jnp.where(p == owner, 0.0, 1024.0)).astype(jnp.int16)
             hot = jnp.where(rows == own, ones, zeros)
@@ -210,10 +211,10 @@
     swap = [(0, 1), (1, 0)]
 
     features_t, quarters = vmem_call(
-        spread_kernel, "spread", [], [features], [((NX, T, T), BF16), ((NZ, NX, T, T), BF16)],
+        spread_kernel, "spread", [], [features], [((NX, T, T), BF16), ((NX, NZ, T, T), BF16)],
         scratch=[pltpu.VMEM((NX, T, T), BF16), pltpu.SemaphoreType.DMA((NZ + 1,))], outside=2, bytes_accessed=1_500_000,
     )
-    blocks = lax.all_to_all(quarters.reshape(OWNERS, T, T), ("z",) + X, 0, 0, tiled=True)
+    blocks = lax.all_to_all(quarters.reshape(OWNERS, T, T), X + ("z",), 0, 0, tiled=True)
 
     codes_t = neighbours.T
     weights_t = edge_weights.T

time: 138 us -> 139 us (level)
  no operation moved by 1% of the time
where the time goes in v16:
time: 139 us; the launch traced here: 138 us
  blocking collectives  70.9 us (51%)
  starting transfers between devices  37.1 us (27%)
  Pallas kernels  21.9 us (16%)
  waiting for transfers between devices  4.53 us (3%)
  local copies, waits for them, and re-layouts  1.97 us (1%)
    all_to_all x1, blocking collectives, body(): plane = added(lax.all_to_all(chip_grad, X + ('z',), 0, 0, tiled=True), BF16)  24.1 us
    pallas_call x14, Pallas kernels, vmem_call(): pl.pallas_call(kernel, in_specs=[pl.BlockSpec(memory_space=pltpu.SMEM)] *...  21.9 us
    all_gather x1, blocking collectives, body(): remote_codes = lax.all_gather(remote_codes, Y + ('c',), axis=0)  21.4 us
    all_to_all x1, starting transfers between devices, body(): lax.all_to_all(quarters.reshape(OWNERS, T, T), X + ('z',), 0, 0, tiled=True)  13.7 us
    ppermute x3, starting transfers between devices, body(): near.append(lax.ppermute(sums, X, forward[NX - k]) if k else sums)  10.7 us
    all_to_all x1, blocking collectives, body(): lax.all_to_all(jnp.broadcast_to(plane, (NY,) + plane.shape), Y, 0, 0, til...  10.3 us
    all_gather x2, blocking collectives, body(): codes = lax.all_gather(lax.all_gather(codes, 'x1', axis=0), 'x0', axis=0)  8.87 us
    all_to_all x1, starting transfers between devices, body(): lax.all_to_all(chip_sum.reshape(NX * NY, T, T), Y + X, 0, 0, tiled=True)  6.85 us
  transfers between devices with their start and end apart: 7, of which 3 were waited for; matrix products, arithmetic and copies ran while one was open for 1% of the time, Pallas kernels for 11%

profile of v16, /device:TPU:1, one launch (start us, length us, event | category | flops | bytes accessed | tf_op | source)
XLA Modules:
  0.0 138.0 jit_solution(17584806720771208207)
XLA Ops:
  0.6 0.0 copy-start.2
  0.6 0.9 copy-done.2
  1.5 1.2 spread.1
  2.7 13.7 %all-to-all-start = ((bf16[32,128,128]{2,1,0:T(8,128)(2,1)}), bf16[32,128,128]{2,1,0:T(8,128)(2,1)S(1)}, u32[]{:S(2)}, u32[]{:S(2)}) async-start(bf16[32,128,128]{2,1,0:T(8,128)(2,1)} %bitcast.52), calls=%async_computation | async-start | bytes 2097152 | tf_op jit(solution)/shard_map/all_to_all | solution.py:217
  16.5 0.1 copy.13
  16.6 0.1 concatenate.20
  16.7 0.0 copy-done.7
  16.8 0.1 fusion.9
  16.9 0.2 concatenate.22
  17.1 4.9 %all-gather = bf16[128,128]{1,0:T(8,128)(2,1)S(1)} all-gather(bf16[64,128]{1,0:T(8,128)(2,1)S(1)} %concatenate.22), channel_id=2, replica_groups=mesh['z'=8,'x1'=2,'x0'=2,'y2'=2,'y1'=2,'y0'=2,'c'=2] {'x1'}, dimensions={0}, use_global_device_ids=true | all-gather | bytes 49152 | tf_op jit(solution)/shard_map/all_gather | solution.py:229
  21.9 4.0 %all-gather.1 = bf16[4,64,128]{2,1,0:T(8,128)(2,1)S(1)} all-gather(bf16[2,64,128]{2,1,0:T(8,128)(2,1)S(1)} %bitcast.55), channel_id=3, replica_groups=mesh['z'=8,'x1'=2,'x0'=2,'y2'=2,'y1'=2,'y0'=2,'c'=2] {'x0'}, dimensions={0}, use_global_device_ids=true | all-gather | bytes 98304 | tf_op jit(solution)/shard_map/all_gather | solution.py:229
  25.9 0.6 split.1
  26.6 21.4 %all-gather.2 = bf16[64,16,128]{2,1,0:T(8,128)(2,1)S(1)} all-gather(bf16[4,16,128]{2,1,0:T(8,128)(2,1)S(1)} %get-tuple-element.19), channel_id=4, replica_groups=mesh['z'=8,'x1'=2,'x0'=2,'y2'=2,'y1'=2,'y0'=2,'c'=2] {'y2','y1','y0','c'}, dimensions={0}, use_global_device_ids=true | all-gather | bytes 278528 | tf_op jit(solution)/shard_map/all_gather | solution.py:234
  48.0 0.0 all-to-all-done.blocks_ref
  48.0 2.1 %collective-permute-start = (bf16[32,128,128]{2,1,0:T(8,128)(2,1)S(1)}, bf16[32,128,128]{2,1,0:T(8,128)(2,1)S(1)}, u32[]{:S(2)}, u32[]{:S(2)}) collective-permute-start(bf16[32,128,128]{2,1,0:T(8,128)(2,1)S(1)} %all-to-all-done.blocks_ref), channel_id=1, source_target_pairs={{0,1},{1,0},{2,3},{3,2},{4,5},{5,4},{6,7},{7,6},{8,9},{9,8},{10,11... | collective-permute-start | bytes 3145736 | tf_op jit(solution)/shard_map/ppermute | solution.py:244
  50.1 0.1 slice_convert_fusion
  50.2 0.1 select_reduce_fusion
  50.3 0.1 select_reduce_fusion.1
  50.4 1.6 %own_group.1.part_ref = f32[4,8,128,128]{3,2,1,0:T(8,128)S(1)} custom-call(s32[1]{0:T(128)} %bitcast.core, s32[4,128]{1,0:T(4,128)S(1)} %get-tuple-element.35.here, s32[4,16]{1,0:T(4,128)S(1)} %get-tuple-element.33.before, bf16[32,128,128]{2,1,0:T(8,128)(2,1)S(1)} %all-to-all-done.blocks_ref, bf16[16,4,16,128]{3,2,1,0:T(8,128)(2,1)S(1)} %bitcast.48), custom_call_target="tpu_custom_call" | custom-call | flops 300000000 | bytes 3500000 | tf_op jit(solution)/shard_map/own_group/pallas_call | solution.py:28
  52.0 0.5 collective-permute-done.blocks_ref
  52.5 2.6 %other_group.1 = bf16[8,4,128,128]{3,2,1,0:T(8,128)(2,1)} custom-call(s32[1]{0:T(128)} %bitcast.core, s32[4,128]{1,0:T(4,128)S(1)} %get-tuple-element.36.here, s32[4,16]{1,0:T(4,128)S(1)} %get-tuple-element.34.before, bf16[32,128,128]{2,1,0:T(8,128)(2,1)S(1)} %collective-permute-done.blocks_ref, bf16[16,4,16,128]{3,2,1,0:T(8,128)(2,1)S(1)} %bitcast.49, ...), custom_call_target="tpu_custom_call" | custom-call | flops 300000000 | bytes 5500000 | tf_op jit(solution)/shard_map/other_group/pallas_call | solution.py:28
  55.1 6.9 %all-to-all-start.1 = ((bf16[32,128,128]{2,1,0:T(8,128)(2,1)}), bf16[32,128,128]{2,1,0:T(8,128)(2,1)S(1)}, u32[]{:S(2)}, u32[]{:S(2)}) async-start(bf16[32,128,128]{2,1,0:T(8,128)(2,1)} %bitcast.51), calls=%async_computation.1 | async-start | bytes 2097152 | tf_op jit(solution)/shard_map/all_to_all | solution.py:254
  62.0 0.1 pad_add_fusion.1.scalars
  62.1 2.8 %local_sums.5 = f32[128,128]{1,0:T(8,128)S(1)} custom-call(s32[2]{0:T(128)S(1)} %pad_add_fusion.1.scalars, bf16[32,128,128]{2,1,0:T(8,128)(2,1)S(1)} %all-to-all-done.blocks_ref, bf16[4,48,128]{2,1,0:T(8,128)(2,1)S(1)} %copy-done), custom_call_target="tpu_custom_call" | custom-call | flops 150000000 | bytes 1200000 | tf_op jit(solution)/shard_map/local_sums/pallas_call | solution.py:28
  64.9 0.0 copy-start.4
  64.9 0.0 copy-start.5
  64.9 3.3 %collective-permute-start.1 = (f32[128,128]{1,0:T(8,128)S(1)}, f32[128,128]{1,0:T(8,128)S(1)}, u32[]{:S(2)}, u32[]{:S(2)}) collective-permute-start(f32[128,128]{1,0:T(8,128)S(1)} %local_sums.5), channel_id=1, source_target_pairs={{0,16},{16,32},{32,48},{48,0},{1,17},{17,33},{33,49},{49,1},{2,18}... | collective-permute-start | bytes 196616 | tf_op jit(solution)/shard_map/ppermute | solution.py:265
  68.2 2.8 %local_sums.6 = f32[128,128]{1,0:T(8,128)S(1)} custom-call(s32[2]{0:T(128)S(1)} %pad_add_fusion.1.scalars, bf16[32,128,128]{2,1,0:T(8,128)(2,1)S(1)} %all-to-all-done.blocks_ref, bf16[4,48,128]{2,1,0:T(8,128)(2,1)S(1)} %copy-done), custom_call_target="tpu_custom_call" | custom-call | flops 150000000 | bytes 1200000 | tf_op jit(solution)/shard_map/local_sums/pallas_call | solution.py:28
  70.9 4.3 %collective-permute-start.2 = (f32[128,128]{1,0:T(8,128)S(1)}, f32[128,128]{1,0:T(8,128)S(1)}, u32[]{:S(2)}, u32[]{:S(2)}) collective-permute-start(f32[128,128]{1,0:T(8,128)S(1)} %local_sums.6), channel_id=1, source_target_pairs={{0,32},{16,48},{32,0},{48,16},{1,33},{17,49},{33,1},{49,17},{2,34}... | collective-permute-start | bytes 196616 | tf_op jit(solution)/shard_map/ppermute | solution.py:265
  75.2 2.8 %local_sums.7 = f32[128,128]{1,0:T(8,128)S(1)} custom-call(s32[2]{0:T(128)S(1)} %pad_add_fusion.1.scalars, bf16[32,128,128]{2,1,0:T(8,128)(2,1)S(1)} %all-to-all-done.blocks_ref, bf16[4,48,128]{2,1,0:T(8,128)(2,1)S(1)} %copy-done), custom_call_target="tpu_custom_call" | custom-call | flops 150000000 | bytes 1200000 | tf_op jit(solution)/shard_map/local_sums/pallas_call | solution.py:28
  78.0 3.1 %collective-permute-start.3 = (f32[128,128]{1,0:T(8,128)S(1)}, f32[128,128]{1,0:T(8,128)S(1)}, u32[]{:S(2)}, u32[]{:S(2)}) collective-permute-start(f32[128,128]{1,0:T(8,128)S(1)} %local_sums.7), channel_id=1, source_target_pairs={{0,48},{16,0},{32,16},{48,32},{1,49},{17,1},{33,17},{49,33},{2,50}... | collective-permute-start | bytes 196616 | tf_op jit(solution)/shard_map/ppermute | solution.py:265
  81.1 3.4 %local_sums.4.near_0_in = f32[128,128]{1,0:T(8,128)} custom-call(s32[2]{0:T(128)S(1)} %pad_add_fusion.1.scalars, bf16[32,128,128]{2,1,0:T(8,128)(2,1)S(1)} %all-to-all-done.blocks_ref, bf16[4,48,128]{2,1,0:T(8,128)(2,1)S(1)} %copy-done), custom_call_target="tpu_custom_call" | custom-call | flops 150000000 | bytes 1200000 | tf_op jit(solution)/shard_map/local_sums/pallas_call | solution.py:28
  84.5 1.0 from_self.1.from_self_in
  85.5 3.6 %all-to-all-done.1 = bf16[32,128,128]{2,1,0:T(8,128)(2,1)S(1)} async-done(((bf16[32,128,128]{2,1,0:T(8,128)(2,1)}), bf16[32,128,128]{2,1,0:T(8,128)(2,1)S(1)}, u32[]{:S(2)}, u32[]{:S(2)}) %all-to-all-start.1) | async-done | bytes 1048608 | tf_op jit(solution)/shard_map/all_to_all | solution.py:254
  89.1 0.1 pad_add_fusion.scalars
  89.2 0.0 collective-permute-done.1.near_1
  89.2 0.0 collective-permute-done.2.near_2
  89.2 0.0 collective-permute-done.3.near_3
  89.2 2.0 %dense.1 = (f32[128,512]{1,0:T(8,128)S(1)}, bf16[8,128,128]{2,1,0:T(8,128)(2,1)S(1)}, bf16[8,128,128]{2,1,0:T(8,128)(2,1)S(1)}) custom-call(s32[2]{0:T(128)S(1)} %pad_add_fusion.scalars, f32[128,128]{1,0:T(8,128)} %local_sums.4.near_0_in, bf16[16,128]{1,0:T(8,128)(2,1)} %bitcast.58, f32[128,512]{1,0:T(8,128)} %from_self.1.from_self_in, ...), custom_call_target="tpu_custom_call" | custom-call | flops 150000000 | bytes 3500000 | tf_op jit(solution)/shard_map/dense/pallas_call | solution.py:28
  91.2 3.8 %collective-permute-start.4 = (bf16[8,128,128]{2,1,0:T(8,128)(2,1)S(1)}, bf16[8,128,128]{2,1,0:T(8,128)(2,1)S(1)}, u32[]{:S(2)}, u32[]{:S(2)}) collective-permute-start(bf16[8,128,128]{2,1,0:T(8,128)(2,1)S(1)} %get-tuple-element.28), channel_id=1, source_target_pairs={{0,1},{1,0},{2,3},{3,2},{4,5},{5,4},{6,7},{7,6},{8,9},{9,8},{10,11... | collective-permute-start | bytes 786440 | tf_op jit(solution)/shard_map/ppermute | solution.py:285
  95.0 0.7 hidden.1
  95.7 0.4 collective-permute-done.4.received_ref
  96.1 0.4 gradient.1
  96.6 24.1 %all_to_all.20.parts_ref = bf16[32,16,512]{2,1,0:T(8,128)(2,1)S(1)} all-to-all(bf16[32,16,512]{2,1,0:T(8,128)(2,1)S(1)} %gradient.1), channel_id=1, replica_groups=mesh['z'=8,'x1'=2,'x0'=2,'y2'=2,'y1'=2,'y0'=2,'c'=2] {'x1','x0','z'}, dimensions={0} | all-to-all | bytes 1048576 | tf_op jit(solution)/shard_map/all_to_all | solution.py:291
  120.7 0.1 added.2
  120.8 10.3 %all_to_all.21.parts_ref = bf16[8,16,512]{2,1,0:T(8,128)(2,1)S(1)} all-to-all(bf16[8,16,512]{2,1,0:T(8,128)(2,1)S(1)} %broadcast_in_dim.54), channel_id=1, replica_groups=mesh['z'=8,'x1'=2,'x0'=2,'y2'=2,'y1'=2,'y0'=2,'c'=2] {'y2','y1','y0'}, dimensions={0} | all-to-all | bytes 262144 | tf_op jit(solution)/shard_map/all_to_all | solution.py:292
  131.1 6.2 %all-gather.3 = f32[32,512]{1,0:T(8,128)S(1)} all-gather(f32[16,512]{1,0:T(8,128)S(1)} %added.3), channel_id=5, replica_groups=mesh['z'=8,'x1'=2,'x0'=2,'y2'=2,'y1'=2,'y0'=2,'c'=2] {'c'}, dimensions={0}, use_global_device_ids=true | all-gather | bytes 98304 | tf_op jit(solution)/shard_map/all_gather | solution.py:293
  137.3 0.6 fusion.11
  (26 shorter events, 0.1 us)
Async XLA Ops:
  0.6 0.9 copy-start.2
  1.5 14.9 %copy-start.8 = (s32[1,1,16,2]{2,3,1,0:T(2,128)S(1)}, s32[1,1,16,2]{2,3,1,0:T(2,128)}, u32[]{:S(2)}) copy-start(s32[1,1,16,2]{2,3,1,0:T(2,128)} %param.11) | copy-start | bytes 388
  1.5 15.0 %copy-start.6 = (bf16[128,16]{0,1:T(8,128)(2,1)S(1)}, bf16[128,16]{0,1:T(8,128)(2,1)}, u32[]{:S(2)}) copy-start(bf16[128,16]{0,1:T(8,128)(2,1)} %param.9) | copy-start | bytes 12292
  1.5 15.2 %copy-start.7 = (s32[128,16]{0,1:T(8,128)S(1)}, s32[128,16]{0,1:T(8,128)}, u32[]{:S(2)}) copy-start(s32[128,16]{0,1:T(8,128)} %param.10) | copy-start | bytes 24580
  1.5 15.2 %copy-start.9 = (s32[1,1,16]{2,1,0:T(1,128)S(1)}, s32[1,1,16]{2,1,0:T(1,128)}, u32[]{:S(2)}) copy-start(s32[1,1,16]{2,1,0:T(1,128)} %param.12) | copy-start | bytes 196
  2.7 45.2 %all-to-all-start = ((bf16[32,128,128]{2,1,0:T(8,128)(2,1)}), bf16[32,128,128]{2,1,0:T(8,128)(2,1)S(1)}, u32[]{:S(2)}, u32[]{:S(2)}) async-start(bf16[32,128,128]{2,1,0:T(8,128)(2,1)} %bitcast.52), calls=%async_computation | async-start | bytes 2097152 | tf_op jit(solution)/shard_map/all_to_all | solution.py:217
  48.0 4.5 %collective-permute-start = (bf16[32,128,128]{2,1,0:T(8,128)(2,1)S(1)}, bf16[32,128,128]{2,1,0:T(8,128)(2,1)S(1)}, u32[]{:S(2)}, u32[]{:S(2)}) collective-permute-start(bf16[32,128,128]{2,1,0:T(8,128)(2,1)S(1)} %all-to-all-done.blocks_ref), channel_id=1, source_target_pairs={{0,1},{1,0},{2,3},{3,2},{4,5},{5,4},{6,7},{7,6},{8,9},{9,8},{10,11... | collective-permute-start | bytes 3145736 | tf_op jit(solution)/shard_map/ppermute | solution.py:244
  55.1 7.0 %copy-start = (bf16[4,48,128]{2,1,0:T(8,128)(2,1)S(1)}, bf16[4,48,128]{2,1,0:T(8,128)(2,1)}, u32[]{:S(2)}) copy-start(bf16[4,48,128]{2,1,0:T(8,128)(2,1)} %get-tuple-element.24.told_ref) | copy-start | bytes 147460
  55.1 33.9 %all-to-all-start.1 = ((bf16[32,128,128]{2,1,0:T(8,128)(2,1)}), bf16[32,128,128]{2,1,0:T(8,128)(2,1)S(1)}, u32[]{:S(2)}, u32[]{:S(2)}) async-start(bf16[32,128,128]{2,1,0:T(8,128)(2,1)} %bitcast.51), calls=%async_computation.1 | async-start | bytes 2097152 | tf_op jit(solution)/shard_map/all_to_all | solution.py:254
  62.1 22.4 %copy-start.1 = (bf16[512,512]{1,0:T(8,128)(2,1)S(1)}, bf16[512,512]{1,0:T(8,128)(2,1)}, u32[]{:S(2)}) copy-start(bf16[512,512]{1,0:T(8,128)(2,1)} %w_self.1) | copy-start | bytes 1572868
  62.1 22.4 %copy-start.3 = (bf16[128,512]{1,0:T(8,128)(2,1)S(1)}, bf16[128,512]{1,0:T(8,128)(2,1)}, u32[]{:S(2)}) copy-start(bf16[128,512]{1,0:T(8,128)(2,1)} %features) | copy-start | bytes 393220
  64.9 24.3 %copy-start.4 = (bf16[512,512]{1,0:T(8,128)(2,1)S(1)}, bf16[512,512]{1,0:T(8,128)(2,1)}, u32[]{:S(2)}) copy-start(bf16[512,512]{1,0:T(8,128)(2,1)} %w_agg.1) | copy-start | bytes 1572868
  64.9 24.3 %copy-start.5 = (bf16[128,512]{1,0:T(8,128)(2,1)S(1)}, bf16[128,512]{1,0:T(8,128)(2,1)}, u32[]{:S(2)}) copy-start(bf16[128,512]{1,0:T(8,128)(2,1)} %cotangent.1) | copy-start | bytes 393220
  64.9 24.3 %collective-permute-start.1 = (f32[128,128]{1,0:T(8,128)S(1)}, f32[128,128]{1,0:T(8,128)S(1)}, u32[]{:S(2)}, u32[]{:S(2)}) collective-permute-start(f32[128,128]{1,0:T(8,128)S(1)} %local_sums.5), channel_id=1, source_target_pairs={{0,16},{16,32},{32,48},{48,0},{1,17},{17,33},{33,49},{49,1},{2,18}... | collective-permute-start | bytes 196616 | tf_op jit(solution)/shard_map/ppermute | solution.py:265
  70.9 18.2 %collective-permute-start.2 = (f32[128,128]{1,0:T(8,128)S(1)}, f32[128,128]{1,0:T(8,128)S(1)}, u32[]{:S(2)}, u32[]{:S(2)}) collective-permute-start(f32[128,128]{1,0:T(8,128)S(1)} %local_sums.6), channel_id=1, source_target_pairs={{0,32},{16,48},{32,0},{48,16},{1,33},{17,49},{33,1},{49,17},{2,34}... | collective-permute-start | bytes 196616 | tf_op jit(solution)/shard_map/ppermute | solution.py:265
  78.0 11.2 %collective-permute-start.3 = (f32[128,128]{1,0:T(8,128)S(1)}, f32[128,128]{1,0:T(8,128)S(1)}, u32[]{:S(2)}, u32[]{:S(2)}) collective-permute-start(f32[128,128]{1,0:T(8,128)S(1)} %local_sums.7), channel_id=1, source_target_pairs={{0,48},{16,0},{32,16},{48,32},{1,49},{17,1},{33,17},{49,33},{2,50}... | collective-permute-start | bytes 196616 | tf_op jit(solution)/shard_map/ppermute | solution.py:265
  91.2 5.0 %collective-permute-start.4 = (bf16[8,128,128]{2,1,0:T(8,128)(2,1)S(1)}, bf16[8,128,128]{2,1,0:T(8,128)(2,1)S(1)}, u32[]{:S(2)}, u32[]{:S(2)}) collective-permute-start(bf16[8,128,128]{2,1,0:T(8,128)(2,1)S(1)} %get-tuple-element.28), channel_id=1, source_target_pairs={{0,1},{1,0},{2,3},{3,2},{4,5},{5,4},{6,7},{7,6},{8,9},{9,8},{10,11... | collective-permute-start | bytes 786440 | tf_op jit(solution)/shard_map/ppermute | solution.py:285

commit v17 on v15

--- a/solution.py
+++ b/solution.py
@@ -51,12 +51,11 @@
 
 
 def split_kernel(codes_ref, remote_ref, local_ref, sems):
-    copies = []
+    copies = [pltpu.make_async_copy(codes_ref.at[i, :, TOLD:], local_ref.at[i], sems.at[i]) for i in range(2)]
+    for copy in copies:
+        copy.start()
     for x in range(NX):
-        codes = codes_ref.at[x % 2, x // 2]
-        copies.append(pltpu.make_async_copy(codes.at[TOLD:], local_ref.at[x], sems.at[x]))
-        copies[-1].start()
-        remote_ref[x] = codes[0:TOLD]
+        remote_ref[x] = codes_ref[x % 2, x // 2, 0:TOLD]
     for copy in copies:
         copy.wait()
 
@@ -101,7 +100,7 @@
     rows = lax.broadcasted_iota(jnp.int16, (T, T), 0)
     lanes = lax.broadcasted_iota(jnp.int32, (1, T), 1).astype(F32)
     ones, zeros = jnp.ones((T, T), BF16), jnp.zeros((T, T), BF16)
-    block, row, weight = (told_ref[x, n * 16 : n * 16 + 16, :].astype(F32) for n in range(3))
+    block, row, weight = (told_ref[lax.rem(x, 2), lax.div(x, 2), n * 16 : n * 16 + 16, :].astype(F32) for n in range(3))
     weight = weight.astype(BF16)
 
     def of_four(i, summed):
@@ -194,12 +193,12 @@
     summed = parts_ref[0].astype(F32)
     for i in range(1, parts_ref.shape[0]):
         summed = summed + parts_ref[i].astype(F32)
-    sum_ref[...] = summed.astype(sum_ref.dtype)
-
-
-def added(parts, dtype):
+    sum_ref[...] = jnp.broadcast_to(summed.astype(sum_ref.dtype), sum_ref.shape)
+
+
+def added(parts, dtype, copies=()):
     (summed,) = vmem_call(
-        add_kernel, "added", [], [parts], [(parts.shape[1:], dtype)], flops=parts.size, bytes_accessed=3 * parts.size
+        add_kernel, "added", [], [parts], [(copies + parts.shape[1:], dtype)], flops=parts.size, bytes_accessed=3 * parts.size
     )
     return summed
 
@@ -227,8 +226,8 @@
     forward = [[(i, (i + k) % NX) for i in range(NX)] for k in range(NX)]
     codes = lax.all_gather(lax.all_gather(codes, "x1", axis=0), "x0", axis=0)
     remote_codes, local_codes = vmem_call(
-        split_kernel, "split", [], [codes], [((NX, TOLD, T), BF16), ((NX, 48, T), BF16)],
-        scratch=[pltpu.SemaphoreType.DMA((NX,))], outside=1, bytes_accessed=100_000,
+        split_kernel, "split", [], [codes], [((NX, TOLD, T), BF16), ((2, 2, 48, T), BF16)],
+        scratch=[pltpu.SemaphoreType.DMA((2,))], outside=1, bytes_accessed=100_000,
     )
     remote_codes = lax.all_gather(remote_codes, Y + ("c",), axis=0)
     blocks, remote_codes = lax.optimization_barrier((blocks, remote_codes))
@@ -287,8 +286,8 @@
     (chip_grad,) = vmem_call(
         grad_kernel, "gradient", [], [keep, received], [((OWNERS, share, width), BF16)], flops=300_000_000, bytes_accessed=1_000_000
     )
-    plane = added(lax.all_to_all(chip_grad, X + ("z",), 0, 0, tiled=True), BF16)
-    planes = lax.all_to_all(jnp.broadcast_to(plane, (NY,) + plane.shape), Y, 0, 0, tiled=True)
+    planes = added(lax.all_to_all(chip_grad, X + ("z",), 0, 0, tiled=True), BF16, (NY,))
+    planes = lax.all_to_all(planes, Y, 0, 0, tiled=True)
     grads = lax.all_gather(added(planes, F32), "c", axis=0)
     return hidden, grads[0], grads[1]
 

time: 138 us -> 138 us (level)
  no operation moved by 1% of the time
where the time goes in v17:
time: 138 us; the launch traced here: 137 us
  blocking collectives  69.7 us (51%)
  starting transfers between devices  37.9 us (27%)
  Pallas kernels  21.8 us (16%)
  waiting for transfers between devices  4.63 us (3%)
  local copies, waits for them, and re-layouts  1.96 us (1%)
    all_to_all x1, blocking collectives, body(): lax.all_to_all(chip_grad, X + ('z',), 0, 0, tiled=True)  22.9 us
    pallas_call x14, Pallas kernels, vmem_call(): pl.pallas_call(kernel, in_specs=[pl.BlockSpec(memory_space=pltpu.SMEM)] *...  21.8 us
    all_gather x1, blocking collectives, body(): remote_codes = lax.all_gather(remote_codes, Y + ('c',), axis=0)  20.6 us
    all_to_all x1, starting transfers between devices, body(): lax.all_to_all(quarters.reshape(OWNERS, T, T), ('z',) + X, 0, 0, tiled=True)  13.7 us
    ppermute x3, starting transfers between devices, body(): near.append(lax.ppermute(sums, X, forward[NX - k]) if k else sums)  10.7 us
    all_to_all x1, blocking collectives, body(): planes = lax.all_to_all(planes, Y, 0, 0, tiled=True)  10.3 us
    all_gather x2, blocking collectives, body(): codes = lax.all_gather(lax.all_gather(codes, 'x1', axis=0), 'x0', axis=0)  9.62 us
    all_to_all x1, starting transfers between devices, body(): lax.all_to_all(chip_sum.reshape(NX * NY, T, T), Y + X, 0, 0, tiled=True)  7.62 us
  transfers between devices with their start and end apart: 7, of which 3 were waited for; matrix products, arithmetic and copies ran while one was open for 1% of the time, Pallas kernels for 11%

profile of v17, /device:TPU:1, one launch (start us, length us, event | category | flops | bytes accessed | tf_op | source)
XLA Modules:
  0.0 137.5 jit_solution(11255231076266180154)
XLA Ops:
  0.6 0.0 copy-start.2
  0.6 0.9 copy-done.2
  1.5 1.2 spread.1
  2.7 13.7 %all-to-all-start = ((bf16[32,128,128]{2,1,0:T(8,128)(2,1)}), bf16[32,128,128]{2,1,0:T(8,128)(2,1)S(1)}, u32[]{:S(2)}, u32[]{:S(2)}) async-start(bf16[32,128,128]{2,1,0:T(8,128)(2,1)} %bitcast.52), calls=%async_computation | async-start | bytes 2097152 | tf_op jit(solution)/shard_map/all_to_all | solution.py:215
  16.5 0.1 copy.13
  16.6 0.1 concatenate.20
  16.7 0.0 copy-done.7
  16.8 0.1 fusion.9
  16.9 0.2 concatenate.22
  17.1 4.9 %all-gather = bf16[128,128]{1,0:T(8,128)(2,1)S(1)} all-gather(bf16[64,128]{1,0:T(8,128)(2,1)S(1)} %concatenate.22), channel_id=2, replica_groups=mesh['z'=8,'x1'=2,'x0'=2,'y2'=2,'y1'=2,'y0'=2,'c'=2] {'x1'}, dimensions={0}, use_global_device_ids=true | all-gather | bytes 49152 | tf_op jit(solution)/shard_map/all_gather | solution.py:227
  21.9 4.7 %all-gather.1 = bf16[4,64,128]{2,1,0:T(8,128)(2,1)S(1)} all-gather(bf16[2,64,128]{2,1,0:T(8,128)(2,1)S(1)} %bitcast.55), channel_id=3, replica_groups=mesh['z'=8,'x1'=2,'x0'=2,'y2'=2,'y1'=2,'y0'=2,'c'=2] {'x0'}, dimensions={0}, use_global_device_ids=true | all-gather | bytes 98304 | tf_op jit(solution)/shard_map/all_gather | solution.py:227
  26.7 0.6 split.1
  27.3 20.6 %all-gather.2 = bf16[64,16,128]{2,1,0:T(8,128)(2,1)S(1)} all-gather(bf16[4,16,128]{2,1,0:T(8,128)(2,1)S(1)} %get-tuple-element.19), channel_id=4, replica_groups=mesh['z'=8,'x1'=2,'x0'=2,'y2'=2,'y1'=2,'y0'=2,'c'=2] {'y2','y1','y0','c'}, dimensions={0}, use_global_device_ids=true | all-gather | bytes 278528 | tf_op jit(solution)/shard_map/all_gather | solution.py:232
  48.0 0.0 all-to-all-done.blocks_ref
  48.0 2.1 %collective-permute-start = (bf16[32,128,128]{2,1,0:T(8,128)(2,1)S(1)}, bf16[32,128,128]{2,1,0:T(8,128)(2,1)S(1)}, u32[]{:S(2)}, u32[]{:S(2)}) collective-permute-start(bf16[32,128,128]{2,1,0:T(8,128)(2,1)S(1)} %all-to-all-done.blocks_ref), channel_id=1, source_target_pairs={{0,1},{1,0},{2,3},{3,2},{4,5},{5,4},{6,7},{7,6},{8,9},{9,8},{10,11... | collective-permute-start | bytes 3145736 | tf_op jit(solution)/shard_map/ppermute | solution.py:242
  50.1 0.1 slice_convert_fusion
  50.1 0.1 select_reduce_fusion
  50.3 0.1 select_reduce_fusion.1
  50.4 1.6 %own_group.1.part_ref = f32[4,8,128,128]{3,2,1,0:T(8,128)S(1)} custom-call(s32[1]{0:T(128)} %bitcast.core, s32[4,128]{1,0:T(4,128)S(1)} %get-tuple-element.35.here, s32[4,16]{1,0:T(4,128)S(1)} %get-tuple-element.33.before, bf16[32,128,128]{2,1,0:T(8,128)(2,1)S(1)} %all-to-all-done.blocks_ref, bf16[16,4,16,128]{3,2,1,0:T(8,128)(2,1)S(1)} %bitcast.48), custom_call_target="tpu_custom_call" | custom-call | flops 300000000 | bytes 3500000 | tf_op jit(solution)/shard_map/own_group/pallas_call | solution.py:28
  52.0 0.5 collective-permute-done.blocks_ref
  52.5 2.6 %other_group.1 = bf16[8,4,128,128]{3,2,1,0:T(8,128)(2,1)} custom-call(s32[1]{0:T(128)} %bitcast.core, s32[4,128]{1,0:T(4,128)S(1)} %get-tuple-element.36.here, s32[4,16]{1,0:T(4,128)S(1)} %get-tuple-element.34.before, bf16[32,128,128]{2,1,0:T(8,128)(2,1)S(1)} %collective-permute-done.blocks_ref, bf16[16,4,16,128]{3,2,1,0:T(8,128)(2,1)S(1)} %bitcast.49, ...), custom_call_target="tpu_custom_call" | custom-call | flops 300000000 | bytes 5500000 | tf_op jit(solution)/shard_map/other_group/pallas_call | solution.py:28
  55.1 7.6 %all-to-all-start.1 = ((bf16[32,128,128]{2,1,0:T(8,128)(2,1)}), bf16[32,128,128]{2,1,0:T(8,128)(2,1)S(1)}, u32[]{:S(2)}, u32[]{:S(2)}) async-start(bf16[32,128,128]{2,1,0:T(8,128)(2,1)} %bitcast.51), calls=%async_computation.1 | async-start | bytes 2097152 | tf_op jit(solution)/shard_map/all_to_all | solution.py:252
  62.7 0.1 pad_add_fusion.1.scalars
  62.8 2.7 %local_sums.5 = f32[128,128]{1,0:T(8,128)S(1)} custom-call(s32[2]{0:T(128)S(1)} %pad_add_fusion.1.scalars, bf16[32,128,128]{2,1,0:T(8,128)(2,1)S(1)} %all-to-all-done.blocks_ref, bf16[2,2,48,128]{3,2,1,0:T(8,128)(2,1)S(1)} %copy-done), custom_call_target="tpu_custom_call" | custom-call | flops 150000000 | bytes 1200000 | tf_op jit(solution)/shard_map/local_sums/pallas_call | solution.py:28
  65.6 0.0 copy-start.4
  65.6 0.0 copy-start.5
  65.6 3.3 %collective-permute-start.1 = (f32[128,128]{1,0:T(8,128)S(1)}, f32[128,128]{1,0:T(8,128)S(1)}, u32[]{:S(2)}, u32[]{:S(2)}) collective-permute-start(f32[128,128]{1,0:T(8,128)S(1)} %local_sums.5), channel_id=1, source_target_pairs={{0,16},{16,32},{32,48},{48,0},{1,17},{17,33},{33,49},{49,1},{2,18}... | collective-permute-start | bytes 196616 | tf_op jit(solution)/shard_map/ppermute | solution.py:263
  68.9 2.7 %local_sums.6 = f32[128,128]{1,0:T(8,128)S(1)} custom-call(s32[2]{0:T(128)S(1)} %pad_add_fusion.1.scalars, bf16[32,128,128]{2,1,0:T(8,128)(2,1)S(1)} %all-to-all-done.blocks_ref, bf16[2,2,48,128]{3,2,1,0:T(8,128)(2,1)S(1)} %copy-done), custom_call_target="tpu_custom_call" | custom-call | flops 150000000 | bytes 1200000 | tf_op jit(solution)/shard_map/local_sums/pallas_call | solution.py:28
  71.6 4.3 %collective-permute-start.2 = (f32[128,128]{1,0:T(8,128)S(1)}, f32[128,128]{1,0:T(8,128)S(1)}, u32[]{:S(2)}, u32[]{:S(2)}) collective-permute-start(f32[128,128]{1,0:T(8,128)S(1)} %local_sums.6), channel_id=1, source_target_pairs={{0,32},{16,48},{32,0},{48,16},{1,33},{17,49},{33,1},{49,17},{2,34}... | collective-permute-start | bytes 196616 | tf_op jit(solution)/shard_map/ppermute | solution.py:263
  75.9 2.7 %local_sums.7 = f32[128,128]{1,0:T(8,128)S(1)} custom-call(s32[2]{0:T(128)S(1)} %pad_add_fusion.1.scalars, bf16[32,128,128]{2,1,0:T(8,128)(2,1)S(1)} %all-to-all-done.blocks_ref, bf16[2,2,48,128]{3,2,1,0:T(8,128)(2,1)S(1)} %copy-done), custom_call_target="tpu_custom_call" | custom-call | flops 150000000 | bytes 1200000 | tf_op jit(solution)/shard_map/local_sums/pallas_call | solution.py:28
  78.7 3.1 %collective-permute-start.3 = (f32[128,128]{1,0:T(8,128)S(1)}, f32[128,128]{1,0:T(8,128)S(1)}, u32[]{:S(2)}, u32[]{:S(2)}) collective-permute-start(f32[128,128]{1,0:T(8,128)S(1)} %local_sums.7), channel_id=1, source_target_pairs={{0,48},{16,0},{32,16},{48,32},{1,49},{17,1},{33,17},{49,33},{2,50}... | collective-permute-start | bytes 196616 | tf_op jit(solution)/shard_map/ppermute | solution.py:263
  81.8 3.4 %local_sums.4.near_0_in = f32[128,128]{1,0:T(8,128)} custom-call(s32[2]{0:T(128)S(1)} %pad_add_fusion.1.scalars, bf16[32,128,128]{2,1,0:T(8,128)(2,1)S(1)} %all-to-all-done.blocks_ref, bf16[2,2,48,128]{3,2,1,0:T(8,128)(2,1)S(1)} %copy-done), custom_call_target="tpu_custom_call" | custom-call | flops 150000000 | bytes 1200000 | tf_op jit(solution)/shard_map/local_sums/pallas_call | solution.py:28
  85.2 1.0 from_self.1.from_self_in
  86.2 3.7 %all-to-all-done.1 = bf16[32,128,128]{2,1,0:T(8,128)(2,1)S(1)} async-done(((bf16[32,128,128]{2,1,0:T(8,128)(2,1)}), bf16[32,128,128]{2,1,0:T(8,128)(2,1)S(1)}, u32[]{:S(2)}, u32[]{:S(2)}) %all-to-all-start.1) | async-done | bytes 1048608 | tf_op jit(solution)/shard_map/all_to_all | solution.py:252
  89.8 0.1 pad_add_fusion.scalars
  89.9 0.0 collective-permute-done.1.near_1
  89.9 0.0 collective-permute-done.2.near_2
  89.9 0.0 collective-permute-done.3.near_3
  89.9 2.0 %dense.1 = (f32[128,512]{1,0:T(8,128)S(1)}, bf16[8,128,128]{2,1,0:T(8,128)(2,1)S(1)}, bf16[8,128,128]{2,1,0:T(8,128)(2,1)S(1)}) custom-call(s32[2]{0:T(128)S(1)} %pad_add_fusion.scalars, f32[128,128]{1,0:T(8,128)} %local_sums.4.near_0_in, bf16[16,128]{1,0:T(8,128)(2,1)} %bitcast.58, f32[128,512]{1,0:T(8,128)} %from_self.1.from_self_in, ...), custom_call_target="tpu_custom_call" | custom-call | flops 150000000 | bytes 3500000 | tf_op jit(solution)/shard_map/dense/pallas_call | solution.py:28
  91.9 3.8 %collective-permute-start.4 = (bf16[8,128,128]{2,1,0:T(8,128)(2,1)S(1)}, bf16[8,128,128]{2,1,0:T(8,128)(2,1)S(1)}, u32[]{:S(2)}, u32[]{:S(2)}) collective-permute-start(bf16[8,128,128]{2,1,0:T(8,128)(2,1)S(1)} %get-tuple-element.28), channel_id=1, source_target_pairs={{0,1},{1,0},{2,3},{3,2},{4,5},{5,4},{6,7},{7,6},{8,9},{9,8},{10,11... | collective-permute-start | bytes 786440 | tf_op jit(solution)/shard_map/ppermute | solution.py:283
  95.7 0.7 hidden.1
  96.4 0.4 collective-permute-done.4.received_ref
  96.9 0.4 gradient.1
  97.3 22.9 %all_to_all.20.parts_ref = bf16[32,16,512]{2,1,0:T(8,128)(2,1)S(1)} all-to-all(bf16[32,16,512]{2,1,0:T(8,128)(2,1)S(1)} %gradient.1), channel_id=1, replica_groups=mesh['z'=8,'x1'=2,'x0'=2,'y2'=2,'y1'=2,'y0'=2,'c'=2] {'x1','x0','z'}, dimensions={0} | all-to-all | bytes 1048576 | tf_op jit(solution)/shard_map/all_to_all | solution.py:289
  120.2 0.1 added.2
  120.3 10.3 %all_to_all.21.parts_ref = bf16[8,16,512]{2,1,0:T(8,128)(2,1)S(1)} all-to-all(bf16[8,16,512]{2,1,0:T(8,128)(2,1)S(1)} %added.2), channel_id=1, replica_groups=mesh['z'=8,'x1'=2,'x0'=2,'y2'=2,'y1'=2,'y0'=2,'c'=2] {'y2','y1','y0'}, dimensions={0} | all-to-all | bytes 262144 | tf_op jit(solution)/shard_map/all_to_all | solution.py:290
  130.6 6.2 %all-gather.3 = f32[32,512]{1,0:T(8,128)S(1)} all-gather(f32[16,512]{1,0:T(8,128)S(1)} %added.3), channel_id=5, replica_groups=mesh['z'=8,'x1'=2,'x0'=2,'y2'=2,'y1'=2,'y0'=2,'c'=2] {'c'}, dimensions={0}, use_global_device_ids=true | all-gather | bytes 98304 | tf_op jit(solution)/shard_map/all_gather | solution.py:291
  136.8 0.6 fusion.11
  (25 shorter events, 0.1 us)
Async XLA Ops:
  0.6 0.9 copy-start.2
  1.5 14.9 %copy-start.8 = (s32[1,1,16,2]{2,3,1,0:T(2,128)S(1)}, s32[1,1,16,2]{2,3,1,0:T(2,128)}, u32[]{:S(2)}) copy-start(s32[1,1,16,2]{2,3,1,0:T(2,128)} %param.11) | copy-start | bytes 388
  1.5 15.0 %copy-start.6 = (bf16[128,16]{0,1:T(8,128)(2,1)S(1)}, bf16[128,16]{0,1:T(8,128)(2,1)}, u32[]{:S(2)}) copy-start(bf16[128,16]{0,1:T(8,128)(2,1)} %param.9) | copy-start | bytes 12292
  1.5 15.2 %copy-start.7 = (s32[128,16]{0,1:T(8,128)S(1)}, s32[128,16]{0,1:T(8,128)}, u32[]{:S(2)}) copy-start(s32[128,16]{0,1:T(8,128)} %param.10) | copy-start | bytes 24580
  1.5 15.2 %copy-start.9 = (s32[1,1,16]{2,1,0:T(1,128)S(1)}, s32[1,1,16]{2,1,0:T(1,128)}, u32[]{:S(2)}) copy-start(s32[1,1,16]{2,1,0:T(1,128)} %param.12) | copy-start | bytes 196
  2.7 45.2 %all-to-all-start = ((bf16[32,128,128]{2,1,0:T(8,128)(2,1)}), bf16[32,128,128]{2,1,0:T(8,128)(2,1)S(1)}, u32[]{:S(2)}, u32[]{:S(2)}) async-start(bf16[32,128,128]{2,1,0:T(8,128)(2,1)} %bitcast.52), calls=%async_computation | async-start | bytes 2097152 | tf_op jit(solution)/shard_map/all_to_all | solution.py:215
  48.0 4.5 %collective-permute-start = (bf16[32,128,128]{2,1,0:T(8,128)(2,1)S(1)}, bf16[32,128,128]{2,1,0:T(8,128)(2,1)S(1)}, u32[]{:S(2)}, u32[]{:S(2)}) collective-permute-start(bf16[32,128,128]{2,1,0:T(8,128)(2,1)S(1)} %all-to-all-done.blocks_ref), channel_id=1, source_target_pairs={{0,1},{1,0},{2,3},{3,2},{4,5},{5,4},{6,7},{7,6},{8,9},{9,8},{10,11... | collective-permute-start | bytes 3145736 | tf_op jit(solution)/shard_map/ppermute | solution.py:242
  55.1 7.7 %copy-start = (bf16[2,2,48,128]{3,2,1,0:T(8,128)(2,1)S(1)}, bf16[2,2,48,128]{3,2,1,0:T(8,128)(2,1)}, u32[]{:S(2)}) copy-start(bf16[2,2,48,128]{3,2,1,0:T(8,128)(2,1)} %get-tuple-element.24.told_ref) | copy-start | bytes 147460
  55.1 34.7 %all-to-all-start.1 = ((bf16[32,128,128]{2,1,0:T(8,128)(2,1)}), bf16[32,128,128]{2,1,0:T(8,128)(2,1)S(1)}, u32[]{:S(2)}, u32[]{:S(2)}) async-start(bf16[32,128,128]{2,1,0:T(8,128)(2,1)} %bitcast.51), calls=%async_computation.1 | async-start | bytes 2097152 | tf_op jit(solution)/shard_map/all_to_all | solution.py:252
  62.8 22.3 %copy-start.1 = (bf16[512,512]{1,0:T(8,128)(2,1)S(1)}, bf16[512,512]{1,0:T(8,128)(2,1)}, u32[]{:S(2)}) copy-start(bf16[512,512]{1,0:T(8,128)(2,1)} %w_self.1) | copy-start | bytes 1572868
  62.8 22.3 %copy-start.3 = (bf16[128,512]{1,0:T(8,128)(2,1)S(1)}, bf16[128,512]{1,0:T(8,128)(2,1)}, u32[]{:S(2)}) copy-start(bf16[128,512]{1,0:T(8,128)(2,1)} %features) | copy-start | bytes 393220
  65.6 24.3 %copy-start.4 = (bf16[512,512]{1,0:T(8,128)(2,1)S(1)}, bf16[512,512]{1,0:T(8,128)(2,1)}, u32[]{:S(2)}) copy-start(bf16[512,512]{1,0:T(8,128)(2,1)} %w_agg.1) | copy-start | bytes 1572868
  65.6 24.3 %copy-start.5 = (bf16[128,512]{1,0:T(8,128)(2,1)S(1)}, bf16[128,512]{1,0:T(8,128)(2,1)}, u32[]{:S(2)}) copy-start(bf16[128,512]{1,0:T(8,128)(2,1)} %cotangent.1) | copy-start | bytes 393220
  65.6 24.3 %collective-permute-start.1 = (f32[128,128]{1,0:T(8,128)S(1)}, f32[128,128]{1,0:T(8,128)S(1)}, u32[]{:S(2)}, u32[]{:S(2)}) collective-permute-start(f32[128,128]{1,0:T(8,128)S(1)} %local_sums.5), channel_id=1, source_target_pairs={{0,16},{16,32},{32,48},{48,0},{1,17},{17,33},{33,49},{49,1},{2,18}... | collective-permute-start | bytes 196616 | tf_op jit(solution)/shard_map/ppermute | solution.py:263
  71.6 18.3 %collective-permute-start.2 = (f32[128,128]{1,0:T(8,128)S(1)}, f32[128,128]{1,0:T(8,128)S(1)}, u32[]{:S(2)}, u32[]{:S(2)}) collective-permute-start(f32[128,128]{1,0:T(8,128)S(1)} %local_sums.6), channel_id=1, source_target_pairs={{0,32},{16,48},{32,0},{48,16},{1,33},{17,49},{33,1},{49,17},{2,34}... | collective-permute-start | bytes 196616 | tf_op jit(solution)/shard_map/ppermute | solution.py:263
  78.7 11.2 %collective-permute-start.3 = (f32[128,128]{1,0:T(8,128)S(1)}, f32[128,128]{1,0:T(8,128)S(1)}, u32[]{:S(2)}, u32[]{:S(2)}) collective-permute-start(f32[128,128]{1,0:T(8,128)S(1)} %local_sums.7), channel_id=1, source_target_pairs={{0,48},{16,0},{32,16},{48,32},{1,49},{17,1},{33,17},{49,33},{2,50}... | collective-permute-start | bytes 196616 | tf_op jit(solution)/shard_map/ppermute | solution.py:263
  91.9 5.0 %collective-permute-start.4 = (bf16[8,128,128]{2,1,0:T(8,128)(2,1)S(1)}, bf16[8,128,128]{2,1,0:T(8,128)(2,1)S(1)}, u32[]{:S(2)}, u32[]{:S(2)}) collective-permute-start(bf16[8,128,128]{2,1,0:T(8,128)(2,1)S(1)} %get-tuple-element.28), channel_id=1, source_target_pairs={{0,1},{1,0},{2,3},{3,2},{4,5},{5,4},{6,7},{7,6},{8,9},{9,8},{10,11... | collective-permute-start | bytes 786440 | tf_op jit(solution)/shard_map/ppermute | solution.py:283

commit v18 on v17

--- a/solution.py
+++ b/solution.py
@@ -287,7 +287,7 @@
         grad_kernel, "gradient", [], [keep, received], [((OWNERS, share, width), BF16)], flops=300_000_000, bytes_accessed=1_000_000
     )
     planes = added(lax.all_to_all(chip_grad, X + ("z",), 0, 0, tiled=True), BF16, (NY,))
-    planes = lax.all_to_all(planes, Y, 0, 0, tiled=True)
+    planes = lax.all_to_all(planes, Y[::-1], 0, 0, tiled=True)
     grads = lax.all_gather(added(planes, F32), "c", axis=0)
     return hidden, grads[0], grads[1]
 

time: 138 us -> 137 us (level)
  no operation moved by 1% of the time
where the time goes in v18:
time: 137 us; the launch traced here: 136 us
  blocking collectives  68.5 us (50%)
  starting transfers between devices  37.9 us (28%)
  Pallas kernels  21.8 us (16%)
  waiting for transfers between devices  4.63 us (3%)
  local copies, waits for them, and re-layouts  1.96 us (1%)
    all_to_all x1, blocking collectives, body(): lax.all_to_all(chip_grad, X + ('z',), 0, 0, tiled=True)  22.9 us
    pallas_call x14, Pallas kernels, vmem_call(): pl.pallas_call(kernel, in_specs=[pl.BlockSpec(memory_space=pltpu.SMEM)] *...  21.8 us
    all_gather x1, blocking collectives, body(): remote_codes = lax.all_gather(remote_codes, Y + ('c',), axis=0)  20.6 us
    all_to_all x1, starting transfers between devices, body(): lax.all_to_all(quarters.reshape(OWNERS, T, T), ('z',) + X, 0, 0, tiled=True)  13.7 us
    ppermute x3, starting transfers between devices, body(): near.append(lax.ppermute(sums, X, forward[NX - k]) if k else sums)  10.7 us
    all_gather x2, blocking collectives, body(): codes = lax.all_gather(lax.all_gather(codes, 'x1', axis=0), 'x0', axis=0)  9.62 us
    all_to_all x1, blocking collectives, body(): planes = lax.all_to_all(planes, Y[::-1], 0, 0, tiled=True)  9.09 us
    all_to_all x1, starting transfers between devices, body(): lax.all_to_all(chip_sum.reshape(NX * NY, T, T), Y + X, 0, 0, tiled=True)  7.62 us
  transfers between devices with their start and end apart: 7, of which 3 were waited for; matrix products, arithmetic and copies ran while one was open for 1% of the time, Pallas kernels for 11%

profile of v18, /device:TPU:1, one launch (start us, length us, event | category | flops | bytes accessed | tf_op | source)
XLA Modules:
  0.0 136.2 jit_solution(5441102538254286727)
XLA Ops:
  0.6 0.0 copy-start.2
  0.6 0.9 copy-done.2
  1.5 1.2 spread.1
  2.7 13.7 %all-to-all-start = ((bf16[32,128,128]{2,1,0:T(8,128)(2,1)}), bf16[32,128,128]{2,1,0:T(8,128)(2,1)S(1)}, u32[]{:S(2)}, u32[]{:S(2)}) async-start(bf16[32,128,128]{2,1,0:T(8,128)(2,1)} %bitcast.52), calls=%async_computation | async-start | bytes 2097152 | tf_op jit(solution)/shard_map/all_to_all | solution.py:215
  16.5 0.0 copy-done.8
  16.5 0.1 copy.13
  16.6 0.1 concatenate.20
  16.8 0.1 fusion.9
  16.9 0.2 concatenate.22
  17.1 4.9 %all-gather = bf16[128,128]{1,0:T(8,128)(2,1)S(1)} all-gather(bf16[64,128]{1,0:T(8,128)(2,1)S(1)} %concatenate.22), channel_id=2, replica_groups=mesh['z'=8,'x1'=2,'x0'=2,'y2'=2,'y1'=2,'y0'=2,'c'=2] {'x1'}, dimensions={0}, use_global_device_ids=true | all-gather | bytes 49152 | tf_op jit(solution)/shard_map/all_gather | solution.py:227
  21.9 4.7 %all-gather.1 = bf16[4,64,128]{2,1,0:T(8,128)(2,1)S(1)} all-gather(bf16[2,64,128]{2,1,0:T(8,128)(2,1)S(1)} %bitcast.55), channel_id=3, replica_groups=mesh['z'=8,'x1'=2,'x0'=2,'y2'=2,'y1'=2,'y0'=2,'c'=2] {'x0'}, dimensions={0}, use_global_device_ids=true | all-gather | bytes 98304 | tf_op jit(solution)/shard_map/all_gather | solution.py:227
  26.7 0.6 split.1
  27.3 20.6 %all-gather.2 = bf16[64,16,128]{2,1,0:T(8,128)(2,1)S(1)} all-gather(bf16[4,16,128]{2,1,0:T(8,128)(2,1)S(1)} %get-tuple-element.19), channel_id=4, replica_groups=mesh['z'=8,'x1'=2,'x0'=2,'y2'=2,'y1'=2,'y0'=2,'c'=2] {'y2','y1','y0','c'}, dimensions={0}, use_global_device_ids=true | all-gather | bytes 278528 | tf_op jit(solution)/shard_map/all_gather | solution.py:232
  48.0 0.0 all-to-all-done.blocks_ref
  48.0 2.1 %collective-permute-start = (bf16[32,128,128]{2,1,0:T(8,128)(2,1)S(1)}, bf16[32,128,128]{2,1,0:T(8,128)(2,1)S(1)}, u32[]{:S(2)}, u32[]{:S(2)}) collective-permute-start(bf16[32,128,128]{2,1,0:T(8,128)(2,1)S(1)} %all-to-all-done.blocks_ref), channel_id=1, source_target_pairs={{0,1},{1,0},{2,3},{3,2},{4,5},{5,4},{6,7},{7,6},{8,9},{9,8},{10,11... | collective-permute-start | bytes 3145736 | tf_op jit(solution)/shard_map/ppermute | solution.py:242
  50.1 0.1 slice_convert_fusion
  50.1 0.1 select_reduce_fusion
  50.3 0.1 select_reduce_fusion.1
  50.4 1.6 %own_group.1.part_ref = f32[4,8,128,128]{3,2,1,0:T(8,128)S(1)} custom-call(s32[1]{0:T(128)} %bitcast.core, s32[4,128]{1,0:T(4,128)S(1)} %get-tuple-element.35.here, s32[4,16]{1,0:T(4,128)S(1)} %get-tuple-element.33.before, bf16[32,128,128]{2,1,0:T(8,128)(2,1)S(1)} %all-to-all-done.blocks_ref, bf16[16,4,16,128]{3,2,1,0:T(8,128)(2,1)S(1)} %bitcast.48), custom_call_target="tpu_custom_call" | custom-call | flops 300000000 | bytes 3500000 | tf_op jit(solution)/shard_map/own_group/pallas_call | solution.py:28
  52.0 0.5 collective-permute-done.blocks_ref
  52.5 2.6 %other_group.1 = bf16[8,4,128,128]{3,2,1,0:T(8,128)(2,1)} custom-call(s32[1]{0:T(128)} %bitcast.core, s32[4,128]{1,0:T(4,128)S(1)} %get-tuple-element.36.here, s32[4,16]{1,0:T(4,128)S(1)} %get-tuple-element.34.before, bf16[32,128,128]{2,1,0:T(8,128)(2,1)S(1)} %collective-permute-done.blocks_ref, bf16[16,4,16,128]{3,2,1,0:T(8,128)(2,1)S(1)} %bitcast.49, ...), custom_call_target="tpu_custom_call" | custom-call | flops 300000000 | bytes 5500000 | tf_op jit(solution)/shard_map/other_group/pallas_call | solution.py:28
  55.1 7.6 %all-to-all-start.1 = ((bf16[32,128,128]{2,1,0:T(8,128)(2,1)}), bf16[32,128,128]{2,1,0:T(8,128)(2,1)S(1)}, u32[]{:S(2)}, u32[]{:S(2)}) async-start(bf16[32,128,128]{2,1,0:T(8,128)(2,1)} %bitcast.51), calls=%async_computation.1 | async-start | bytes 2097152 | tf_op jit(solution)/shard_map/all_to_all | solution.py:252
  62.7 0.1 pad_add_fusion.1.scalars
  62.8 2.7 %local_sums.5 = f32[128,128]{1,0:T(8,128)S(1)} custom-call(s32[2]{0:T(128)S(1)} %pad_add_fusion.1.scalars, bf16[32,128,128]{2,1,0:T(8,128)(2,1)S(1)} %all-to-all-done.blocks_ref, bf16[2,2,48,128]{3,2,1,0:T(8,128)(2,1)S(1)} %copy-done), custom_call_target="tpu_custom_call" | custom-call | flops 150000000 | bytes 1200000 | tf_op jit(solution)/shard_map/local_sums/pallas_call | solution.py:28
  65.6 0.0 copy-start.4
  65.6 0.0 copy-start.5
  65.6 3.3 %collective-permute-start.1 = (f32[128,128]{1,0:T(8,128)S(1)}, f32[128,128]{1,0:T(8,128)S(1)}, u32[]{:S(2)}, u32[]{:S(2)}) collective-permute-start(f32[128,128]{1,0:T(8,128)S(1)} %local_sums.5), channel_id=1, source_target_pairs={{0,16},{16,32},{32,48},{48,0},{1,17},{17,33},{33,49},{49,1},{2,18}... | collective-permute-start | bytes 196616 | tf_op jit(solution)/shard_map/ppermute | solution.py:263
  68.9 2.7 %local_sums.6 = f32[128,128]{1,0:T(8,128)S(1)} custom-call(s32[2]{0:T(128)S(1)} %pad_add_fusion.1.scalars, bf16[32,128,128]{2,1,0:T(8,128)(2,1)S(1)} %all-to-all-done.blocks_ref, bf16[2,2,48,128]{3,2,1,0:T(8,128)(2,1)S(1)} %copy-done), custom_call_target="tpu_custom_call" | custom-call | flops 150000000 | bytes 1200000 | tf_op jit(solution)/shard_map/local_sums/pallas_call | solution.py:28
  71.6 4.3 %collective-permute-start.2 = (f32[128,128]{1,0:T(8,128)S(1)}, f32[128,128]{1,0:T(8,128)S(1)}, u32[]{:S(2)}, u32[]{:S(2)}) collective-permute-start(f32[128,128]{1,0:T(8,128)S(1)} %local_sums.6), channel_id=1, source_target_pairs={{0,32},{16,48},{32,0},{48,16},{1,33},{17,49},{33,1},{49,17},{2,34}... | collective-permute-start | bytes 196616 | tf_op jit(solution)/shard_map/ppermute | solution.py:263
  75.9 2.7 %local_sums.7 = f32[128,128]{1,0:T(8,128)S(1)} custom-call(s32[2]{0:T(128)S(1)} %pad_add_fusion.1.scalars, bf16[32,128,128]{2,1,0:T(8,128)(2,1)S(1)} %all-to-all-done.blocks_ref, bf16[2,2,48,128]{3,2,1,0:T(8,128)(2,1)S(1)} %copy-done), custom_call_target="tpu_custom_call" | custom-call | flops 150000000 | bytes 1200000 | tf_op jit(solution)/shard_map/local_sums/pallas_call | solution.py:28
  78.7 3.1 %collective-permute-start.3 = (f32[128,128]{1,0:T(8,128)S(1)}, f32[128,128]{1,0:T(8,128)S(1)}, u32[]{:S(2)}, u32[]{:S(2)}) collective-permute-start(f32[128,128]{1,0:T(8,128)S(1)} %local_sums.7), channel_id=1, source_target_pairs={{0,48},{16,0},{32,16},{48,32},{1,49},{17,1},{33,17},{49,33},{2,50}... | collective-permute-start | bytes 196616 | tf_op jit(solution)/shard_map/ppermute | solution.py:263
  81.8 3.4 %local_sums.4.near_0_in = f32[128,128]{1,0:T(8,128)} custom-call(s32[2]{0:T(128)S(1)} %pad_add_fusion.1.scalars, bf16[32,128,128]{2,1,0:T(8,128)(2,1)S(1)} %all-to-all-done.blocks_ref, bf16[2,2,48,128]{3,2,1,0:T(8,128)(2,1)S(1)} %copy-done), custom_call_target="tpu_custom_call" | custom-call | flops 150000000 | bytes 1200000 | tf_op jit(solution)/shard_map/local_sums/pallas_call | solution.py:28
  85.2 1.0 from_self.1.from_self_in
  86.2 3.7 %all-to-all-done.1 = bf16[32,128,128]{2,1,0:T(8,128)(2,1)S(1)} async-done(((bf16[32,128,128]{2,1,0:T(8,128)(2,1)}), bf16[32,128,128]{2,1,0:T(8,128)(2,1)S(1)}, u32[]{:S(2)}, u32[]{:S(2)}) %all-to-all-start.1) | async-done | bytes 1048608 | tf_op jit(solution)/shard_map/all_to_all | solution.py:252
  89.8 0.1 pad_add_fusion.scalars
  89.9 0.0 collective-permute-done.1.near_1
  89.9 0.0 collective-permute-done.2.near_2
  89.9 0.0 collective-permute-done.3.near_3
  89.9 2.0 %dense.1 = (f32[128,512]{1,0:T(8,128)S(1)}, bf16[8,128,128]{2,1,0:T(8,128)(2,1)S(1)}, bf16[8,128,128]{2,1,0:T(8,128)(2,1)S(1)}) custom-call(s32[2]{0:T(128)S(1)} %pad_add_fusion.scalars, f32[128,128]{1,0:T(8,128)} %local_sums.4.near_0_in, bf16[16,128]{1,0:T(8,128)(2,1)} %bitcast.58, f32[128,512]{1,0:T(8,128)} %from_self.1.from_self_in, ...), custom_call_target="tpu_custom_call" | custom-call | flops 150000000 | bytes 3500000 | tf_op jit(solution)/shard_map/dense/pallas_call | solution.py:28
  91.9 3.8 %collective-permute-start.4 = (bf16[8,128,128]{2,1,0:T(8,128)(2,1)S(1)}, bf16[8,128,128]{2,1,0:T(8,128)(2,1)S(1)}, u32[]{:S(2)}, u32[]{:S(2)}) collective-permute-start(bf16[8,128,128]{2,1,0:T(8,128)(2,1)S(1)} %get-tuple-element.28), channel_id=1, source_target_pairs={{0,1},{1,0},{2,3},{3,2},{4,5},{5,4},{6,7},{7,6},{8,9},{9,8},{10,11... | collective-permute-start | bytes 786440 | tf_op jit(solution)/shard_map/ppermute | solution.py:283
  95.7 0.7 hidden.1
  96.4 0.4 collective-permute-done.4.received_ref
  96.9 0.4 gradient.1
  97.3 22.9 %all_to_all.20.parts_ref = bf16[32,16,512]{2,1,0:T(8,128)(2,1)S(1)} all-to-all(bf16[32,16,512]{2,1,0:T(8,128)(2,1)S(1)} %gradient.1), channel_id=1, replica_groups=mesh['z'=8,'x1'=2,'x0'=2,'y2'=2,'y1'=2,'y0'=2,'c'=2] {'x1','x0','z'}, dimensions={0} | all-to-all | bytes 1048576 | tf_op jit(solution)/shard_map/all_to_all | solution.py:289
  120.2 0.1 added.2
  120.3 9.1 %all_to_all.21.parts_ref = bf16[8,16,512]{2,1,0:T(8,128)(2,1)S(1)} all-to-all(bf16[8,16,512]{2,1,0:T(8,128)(2,1)S(1)} %added.2), channel_id=1, replica_groups=mesh['z'=8,'x1'=2,'x0'=2,'y2'=2,'y1'=2,'y0'=2,'c'=2] {'y0','y1','y2'}, dimensions={0} | all-to-all | bytes 262144 | tf_op jit(solution)/shard_map/all_to_all | solution.py:290
  129.4 6.2 %all-gather.3 = f32[32,512]{1,0:T(8,128)S(1)} all-gather(f32[16,512]{1,0:T(8,128)S(1)} %added.3), channel_id=5, replica_groups=mesh['z'=8,'x1'=2,'x0'=2,'y2'=2,'y1'=2,'y0'=2,'c'=2] {'c'}, dimensions={0}, use_global_device_ids=true | all-gather | bytes 98304 | tf_op jit(solution)/shard_map/all_gather | solution.py:291
  135.6 0.6 fusion.11
  (25 shorter events, 0.1 us)
Async XLA Ops:
  0.6 0.9 copy-start.2
  1.5 14.9 %copy-start.8 = (s32[1,1,16,2]{2,3,1,0:T(2,128)S(1)}, s32[1,1,16,2]{2,3,1,0:T(2,128)}, u32[]{:S(2)}) copy-start(s32[1,1,16,2]{2,3,1,0:T(2,128)} %param.11) | copy-start | bytes 388
  1.5 15.0 %copy-start.6 = (bf16[128,16]{0,1:T(8,128)(2,1)S(1)}, bf16[128,16]{0,1:T(8,128)(2,1)}, u32[]{:S(2)}) copy-start(bf16[128,16]{0,1:T(8,128)(2,1)} %param.9) | copy-start | bytes 12292
  1.5 15.2 %copy-start.7 = (s32[128,16]{0,1:T(8,128)S(1)}, s32[128,16]{0,1:T(8,128)}, u32[]{:S(2)}) copy-start(s32[128,16]{0,1:T(8,128)} %param.10) | copy-start | bytes 24580
  1.5 15.2 %copy-start.9 = (s32[1,1,16]{2,1,0:T(1,128)S(1)}, s32[1,1,16]{2,1,0:T(1,128)}, u32[]{:S(2)}) copy-start(s32[1,1,16]{2,1,0:T(1,128)} %param.12) | copy-start | bytes 196
  2.7 45.2 %all-to-all-start = ((bf16[32,128,128]{2,1,0:T(8,128)(2,1)}), bf16[32,128,128]{2,1,0:T(8,128)(2,1)S(1)}, u32[]{:S(2)}, u32[]{:S(2)}) async-start(bf16[32,128,128]{2,1,0:T(8,128)(2,1)} %bitcast.52), calls=%async_computation | async-start | bytes 2097152 | tf_op jit(solution)/shard_map/all_to_all | solution.py:215
  48.0 4.5 %collective-permute-start = (bf16[32,128,128]{2,1,0:T(8,128)(2,1)S(1)}, bf16[32,128,128]{2,1,0:T(8,128)(2,1)S(1)}, u32[]{:S(2)}, u32[]{:S(2)}) collective-permute-start(bf16[32,128,128]{2,1,0:T(8,128)(2,1)S(1)} %all-to-all-done.blocks_ref), channel_id=1, source_target_pairs={{0,1},{1,0},{2,3},{3,2},{4,5},{5,4},{6,7},{7,6},{8,9},{9,8},{10,11... | collective-permute-start | bytes 3145736 | tf_op jit(solution)/shard_map/ppermute | solution.py:242
  55.1 7.7 %copy-start = (bf16[2,2,48,128]{3,2,1,0:T(8,128)(2,1)S(1)}, bf16[2,2,48,128]{3,2,1,0:T(8,128)(2,1)}, u32[]{:S(2)}) copy-start(bf16[2,2,48,128]{3,2,1,0:T(8,128)(2,1)} %get-tuple-element.24.told_ref) | copy-start | bytes 147460
  55.1 34.7 %all-to-all-start.1 = ((bf16[32,128,128]{2,1,0:T(8,128)(2,1)}), bf16[32,128,128]{2,1,0:T(8,128)(2,1)S(1)}, u32[]{:S(2)}, u32[]{:S(2)}) async-start(bf16[32,128,128]{2,1,0:T(8,128)(2,1)} %bitcast.51), calls=%async_computation.1 | async-start | bytes 2097152 | tf_op jit(solution)/shard_map/all_to_all | solution.py:252
  62.8 22.3 %copy-start.1 = (bf16[512,512]{1,0:T(8,128)(2,1)S(1)}, bf16[512,512]{1,0:T(8,128)(2,1)}, u32[]{:S(2)}) copy-start(bf16[512,512]{1,0:T(8,128)(2,1)} %w_self.1) | copy-start | bytes 1572868
  62.8 22.3 %copy-start.3 = (bf16[128,512]{1,0:T(8,128)(2,1)S(1)}, bf16[128,512]{1,0:T(8,128)(2,1)}, u32[]{:S(2)}) copy-start(bf16[128,512]{1,0:T(8,128)(2,1)} %features) | copy-start | bytes 393220
  65.6 24.3 %copy-start.4 = (bf16[512,512]{1,0:T(8,128)(2,1)S(1)}, bf16[512,512]{1,0:T(8,128)(2,1)}, u32[]{:S(2)}) copy-start(bf16[512,512]{1,0:T(8,128)(2,1)} %w_agg.1) | copy-start | bytes 1572868
  65.6 24.3 %copy-start.5 = (bf16[128,512]{1,0:T(8,128)(2,1)S(1)}, bf16[128,512]{1,0:T(8,128)(2,1)}, u32[]{:S(2)}) copy-start(bf16[128,512]{1,0:T(8,128)(2,1)} %cotangent.1) | copy-start | bytes 393220
  65.6 24.3 %collective-permute-start.1 = (f32[128,128]{1,0:T(8,128)S(1)}, f32[128,128]{1,0:T(8,128)S(1)}, u32[]{:S(2)}, u32[]{:S(2)}) collective-permute-start(f32[128,128]{1,0:T(8,128)S(1)} %local_sums.5), channel_id=1, source_target_pairs={{0,16},{16,32},{32,48},{48,0},{1,17},{17,33},{33,49},{49,1},{2,18}... | collective-permute-start | bytes 196616 | tf_op jit(solution)/shard_map/ppermute | solution.py:263
  71.6 18.3 %collective-permute-start.2 = (f32[128,128]{1,0:T(8,128)S(1)}, f32[128,128]{1,0:T(8,128)S(1)}, u32[]{:S(2)}, u32[]{:S(2)}) collective-permute-start(f32[128,128]{1,0:T(8,128)S(1)} %local_sums.6), channel_id=1, source_target_pairs={{0,32},{16,48},{32,0},{48,16},{1,33},{17,49},{33,1},{49,17},{2,34}... | collective-permute-start | bytes 196616 | tf_op jit(solution)/shard_map/ppermute | solution.py:263
  78.7 11.2 %collective-permute-start.3 = (f32[128,128]{1,0:T(8,128)S(1)}, f32[128,128]{1,0:T(8,128)S(1)}, u32[]{:S(2)}, u32[]{:S(2)}) collective-permute-start(f32[128,128]{1,0:T(8,128)S(1)} %local_sums.7), channel_id=1, source_target_pairs={{0,48},{16,0},{32,16},{48,32},{1,49},{17,1},{33,17},{49,33},{2,50}... | collective-permute-start | bytes 196616 | tf_op jit(solution)/shard_map/ppermute | solution.py:263
  91.9 5.0 %collective-permute-start.4 = (bf16[8,128,128]{2,1,0:T(8,128)(2,1)S(1)}, bf16[8,128,128]{2,1,0:T(8,128)(2,1)S(1)}, u32[]{:S(2)}, u32[]{:S(2)}) collective-permute-start(bf16[8,128,128]{2,1,0:T(8,128)(2,1)S(1)} %get-tuple-element.28), channel_id=1, source_target_pairs={{0,1},{1,0},{2,3},{3,2},{4,5},{5,4},{6,7},{7,6},{8,9},{9,8},{10,11... | collective-permute-start | bytes 786440 | tf_op jit(solution)/shard_map/ppermute | solution.py:283
